TPU v7x, 32 devices: a whole 2x2x4 slice. The times are simulated.
32 devices in a mesh: row: 4 (over z), group: 8 (over y, x, core).
Axes of the slice: x: 2, y: 2, z: 4, core: 2. Of those that a mesh axis runs over, the one named last changes fastest.
Arguments:
- states: bfloat16 [8192, 8192], P('row', 'group'), may hold values from -1 to 1, as said below
- targets: float32 [8192, 128], P('row'), may hold values from -6 to 6
- ridge: float32 [128], replicated, may hold values from 0.5 to 8
Outputs:
- weights: float32 [8192, 128], P(('group', 'row'))
- residual: float32 [8192, 128], P('row')
Inputs may be any that keep to these rules, and one draw needn't show every extreme that they name: Final hidden states of the model, one row a token.
All inputs are finite; a program needn't handle non-finite values.
Results may differ from a plain program's by a relative error of at most 0.0026.
Values may be sent and summed in bfloat16 or wider, within the bound.
No kernel may reach another device: no remote copies, remote signals or barrier semaphores. Data moves between devices by JAX's collectives and lax.ppermute only.
A program may use at most 64 MiB of HBM per device.

v0:
```python
import jax
import jax.numpy as jnp
from jax import lax
from jax.sharding import PartitionSpec as P

ITERS = 3


def contract_rows(left, right):
    return lax.dot_general(
        left, right, (((0,), (0,)), ((), ())), preferred_element_type=jnp.float32
    )


def shards(states, targets, ridge):
    n_row = lax.axis_size("row")
    n_group = lax.axis_size("group")
    share = states.shape[1] // n_row
    tok_share = states.shape[0] // n_group
    row_start = lax.axis_index("row") * share
    tok_start = lax.axis_index("group") * tok_share

    def transposed(resid_b):
        return lax.psum(contract_rows(states, resid_b), "row")

    def own_rows(values):
        return lax.dynamic_slice_in_dim(values, row_start, share, 0)

    def grad_norm(grad):
        mine = own_rows(grad)
        return lax.psum(jnp.sum(mine * mine, axis=0), ("row", "group"))

    grad = transposed(targets.astype(jnp.bfloat16))
    residual = targets
    weights = jnp.zeros_like(grad)
    direction = grad
    gamma = grad_norm(grad)
    for step in range(ITERS):
        full_dir = direction.astype(jnp.bfloat16)
        local_image = jnp.dot(states, full_dir, preferred_element_type=jnp.float32)
        image = lax.psum(local_image, "group")
        rows_mine = lax.dynamic_slice_in_dim(image, tok_start, tok_share, 0)
        image_sq = jnp.sum(rows_mine * rows_mine, axis=0)
        mine = own_rows(direction)
        dir_part = ridge * jnp.sum(mine * mine, axis=0)
        image_part = lax.psum(image_sq, ("row", "group"))
        delta = image_part + lax.psum(dir_part, ("row", "group"))
        alpha = gamma / delta
        weights = weights + alpha * direction
        residual = residual - alpha * image
        if step + 1 < ITERS:
            resid_b = residual.astype(jnp.bfloat16)
            grad = transposed(resid_b) - ridge * weights
            gamma_new = grad_norm(grad)
            direction = grad + gamma_new / gamma * direction
            gamma = gamma_new
    return (own_rows(weights), residual)


def solution(mesh):
    placed = (P("row", "group"), P("row", None), P())
    return jax.shard_map(
        shards,
        mesh=mesh,
        in_specs=placed,
        out_specs=(P(("group", "row"), None), P("row", None)),
        check_vma=False,
    )
```

profile of v0, /device:TPU:0, one launch (start us, length us, event | category | flops | bytes accessed | tf_op | source)
XLA Modules:
  0.0 539.3 jit_solution(12081938226730381501)
XLA Ops:
  7.2 0.0 all-reduce.8.cloned.1.call-start
  7.2 4.6 fusion.2
  11.8 0.0 copy-start.2
  11.8 0.0 all-reduce.8.cloned.1.call-update
  11.8 0.0 copy-start.3
  11.8 0.0 all-reduce.10.cloned.1.call-start
  11.9 41.1 %all-reduce.8.cloned.1.call-done = f32[1024,128]{1,0:T(8,128)} async-done(((f32[1024,128]{1,0:T(8,128)}), f32[1024,128]{1,0:T(8,128)}) %all-reduce.8.cloned.1.call-update) | async-done | bytes 524304 | tf_op jit(solution)/shard_map/psum | solution.py:24
  53.0 0.0 copy-start.1
  53.0 4.9 convolution_bitcast_fusion.2
  57.9 0.0 all-reduce.10.cloned.1.call-update
  57.9 0.0 all-reduce.12.cloned.1.call-start
  57.9 0.0 copy-done.2
  58.0 0.3 copy.5
  58.3 0.0 copy-done.1
  58.3 0.1 multiply_reduce_fusion.7
  58.4 56.3 %all-reduce.10.cloned.1.call-done = f32[2048,128]{0,1:T(8,128)} async-done(((f32[2048,128]{0,1:T(8,128)}), f32[2048,128]{0,1:T(8,128)}) %all-reduce.10.cloned.1.call-update) | async-done | bytes 1048592 | tf_op jit(solution)/shard_map/psum | solution.py:41
  114.6 1.0 multiply_reduce_fusion.6
  115.6 0.0 copy-done.3
  115.7 39.2 %all-reduce = (f32[128]{0:T(128)S(1)}, f32[128]{0:T(128)S(1)}) all-reduce(f32[128]{0:T(128)S(1)} %multiply_reduce_fusion.7, f32[128]{0:T(128)S(1)} %multiply_add_fusion.5), channel_id=1, replica_groups=mesh['row'=4,'group'=8] {'row','group'}, use_global_device_ids=true, to_apply=%region_2.0 | all-reduce | flops 256 | bytes 2048 | tf_op jit(solution)/shard_map/psum | solution.py:31
  154.9 5.1 convolution_bitcast_fusion.4
  159.9 0.0 all-reduce.12.cloned.1.call-update
  160.0 0.0 all-reduce.14.cloned.1.call-start
  160.0 38.3 %all-reduce.12.cloned.1.call-done = f32[1024,128]{1,0:T(8,128)} async-done(((f32[1024,128]{1,0:T(8,128)}), f32[1024,128]{1,0:T(8,128)}) %all-reduce.12.cloned.1.call-update) | async-done | bytes 524304 | tf_op jit(solution)/shard_map/psum | solution.py:24
  198.3 1.1 multiply_subtract_fusion.4
  199.4 0.1 multiply_reduce_fusion.5
  199.4 39.9 %psum.111 = f32[128]{0:T(128)S(1)} all-reduce(f32[128]{0:T(128)S(1)} %multiply_reduce_fusion.5), channel_id=1, replica_groups=mesh['row'=4,'group'=8] {'row','group'}, use_global_device_ids=true, to_apply=%region_9.0 | all-reduce | flops 128 | bytes 1024 | tf_op jit(solution)/shard_map/psum | solution.py:31
  239.4 0.1 multiply_add_fusion.2
  239.4 4.7 convolution_bitcast_fusion.1
  244.1 0.0 all-reduce.14.cloned.1.call-update
  244.1 0.0 all-reduce.16.cloned.1.call-start
  244.2 0.1 multiply_reduce_fusion.3
  244.2 56.4 %all-reduce.14.cloned.1.call-done = f32[2048,128]{0,1:T(8,128)} async-done(((f32[2048,128]{0,1:T(8,128)}), f32[2048,128]{0,1:T(8,128)}) %all-reduce.14.cloned.1.call-update) | async-done | bytes 1048592 | tf_op jit(solution)/shard_map/psum | solution.py:41
  300.6 1.0 multiply_reduce_fusion.4
  301.6 39.2 %psum.121 = f32[128]{0:T(128)S(1)} all-reduce(f32[128]{0:T(128)S(1)} %multiply_add_fusion.4), channel_id=1, replica_groups=mesh['row'=4,'group'=8] {'row','group'}, use_global_device_ids=true, to_apply=%region_12.0 | all-reduce | flops 128 | bytes 1024 | tf_op jit(solution)/shard_map/psum | solution.py:46
  340.8 0.0 copy-start
  340.9 2.0 multiply_subtract_fusion.1
  342.9 0.8 copy-done
  343.7 2.6 convolution_bitcast_fusion.3
  346.2 0.0 all-reduce.16.cloned.1.call-update
  346.3 0.0 all-reduce.18.cloned.1.call-start
  346.3 38.3 %all-reduce.16.cloned.1.call-done = f32[1024,128]{1,0:T(8,128)} async-done(((f32[1024,128]{1,0:T(8,128)}), f32[1024,128]{1,0:T(8,128)}) %all-reduce.16.cloned.1.call-update) | async-done | bytes 524304 | tf_op jit(solution)/shard_map/psum | solution.py:24
  384.6 2.0 multiply_subtract_fusion.3
  386.6 40.1 %psum.116 = f32[128]{0:T(128)S(1)} all-reduce(f32[128]{0:T(128)S(1)} %multiply_reduce_fusion.2), channel_id=1, replica_groups=mesh['row'=4,'group'=8] {'row','group'}, use_global_device_ids=true, to_apply=%region_17.0 | all-reduce | flops 128 | bytes 1024 | tf_op jit(solution)/shard_map/psum | solution.py:31
  426.7 0.1 multiply_add_fusion
  426.8 4.7 convolution_bitcast_fusion
  431.4 0.0 all-reduce.18.cloned.1.call-update
  431.5 0.1 multiply_reduce_fusion
  431.5 56.4 %all-reduce.18.cloned.1.call-done = f32[2048,128]{0,1:T(8,128)} async-done(((f32[2048,128]{0,1:T(8,128)}), f32[2048,128]{0,1:T(8,128)}) %all-reduce.18.cloned.1.call-update) | async-done | bytes 1048592 | tf_op jit(solution)/shard_map/psum | solution.py:41
  487.9 1.0 multiply_reduce_fusion.1
  489.0 39.2 %psum.122 = f32[128]{0:T(128)S(1)} all-reduce(f32[128]{0:T(128)S(1)} %multiply_add_fusion.3), channel_id=1, replica_groups=mesh['row'=4,'group'=8] {'row','group'}, use_global_device_ids=true, to_apply=%region_20.0 | all-reduce | flops 128 | bytes 1024 | tf_op jit(solution)/shard_map/psum | solution.py:46
  528.2 1.4 multiply_subtract_fusion
  529.6 1.3 copy.8
  530.9 1.6 dynamic-slice_add_fusion
  (9 shorter events, 0.1 us)
Async XLA Ops:
  7.2 45.8 %all-reduce.8.cloned.1.call-start = ((), (), s32[]{:S(2)}) async-start(), calls=%async_computation | async-start | bytes 1048576 | tf_op jit(solution)/shard_map/psum | solution.py:24
  11.8 46.2 %copy-start.2 = (f32[2048,128]{1,0:T(8,128)S(1)}, f32[2048,128]{1,0:T(8,128)}, u32[]{:S(2)}) copy-start(f32[2048,128]{1,0:T(8,128)} %param.4) | copy-start | bytes 3145732
  11.8 103.8 %copy-start.3 = (f32[128]{0:T(128)S(1)}, f32[128]{0:T(128)}, u32[]{:S(2)}) copy-start(f32[128]{0:T(128)} %param.5) | copy-start | bytes 1540
  11.8 102.8 %all-reduce.10.cloned.1.call-start = ((), (), s32[]{:S(2)}) async-start(), calls=%async_computation.1 | async-start | bytes 2097152 | tf_op jit(solution)/shard_map/psum | solution.py:41
  53.0 5.3 copy-start.1
  57.9 140.4 %all-reduce.12.cloned.1.call-start = ((), (), s32[]{:S(2)}) async-start(), calls=%async_computation.2 | async-start | bytes 1048576 | tf_op jit(solution)/shard_map/psum | solution.py:24
  160.0 140.6 %all-reduce.14.cloned.1.call-start = ((), (), s32[]{:S(2)}) async-start(), calls=%async_computation.3 | async-start | bytes 2097152 | tf_op jit(solution)/shard_map/psum | solution.py:41
  244.1 140.4 %all-reduce.16.cloned.1.call-start = ((), (), s32[]{:S(2)}) async-start(), calls=%async_computation.4 | async-start | bytes 1048576 | tf_op jit(solution)/shard_map/psum | solution.py:24
  340.8 2.8 copy-start
  346.3 141.7 %all-reduce.18.cloned.1.call-start = ((), (), s32[]{:S(2)}) async-start(), calls=%async_computation.5 | async-start | bytes 2097152 | tf_op jit(solution)/shard_map/psum | solution.py:41
Sparse Core Ops, SparseCore 0:
  11.9 40.9 all-reduce.7
  58.0 56.5 all-reduce.9
  160.1 38.1 all-reduce.11
  244.3 56.3 all-reduce.13
  346.4 38.1 all-reduce.15
  431.6 56.3 all-reduce.17
where the time goes:
time: 540 us; the launch traced here: 539 us
  waiting for transfers between devices  287 us (53%)
  blocking collectives  198 us (37%)
  matrix products  26.5 us (5%)
  between operations  14.2 us (3%)
  other arithmetic  11.5 us (2%)
    psum x3, waiting for transfers between devices, shards(): image = lax.psum(local_image, 'group')  169 us
    psum x3, blocking collectives, grad_norm(): return lax.psum(jnp.sum(mine * mine, axis=0), ('row', 'group'))  119 us
    psum x3, waiting for transfers between devices, transposed(): return lax.psum(contract_rows(states, resid_b), 'row')  118 us
    psum x2, blocking collectives, shards(): image_part = lax.psum(image_sq, ('row', 'group'))  78.4 us
    dot_general x3, matrix products, shards(): local_image = jnp.dot(states, full_dir, preferred_element_type=jnp.float32)  14.3 us
    dot_general x3, matrix products, contract_rows(): lax.dot_general(left, right, (((0,), (0,)), ((), ())), preferred_element_...  12.2 us
  transfers between devices with their start and end apart: 6, of which 6 were waited for; matrix products, arithmetic and copies ran while one was open for 0% of the time, Pallas kernels for 0%

commit v1 on v0

v1 whole, which is shorter than its diff:
```python
import functools

import jax
import jax.numpy as jnp
from jax import lax
from jax.experimental import pallas as pl
from jax.experimental.pallas import tpu as pltpu
from jax.sharding import PartitionSpec as P

ITERS = 3
PAD = 16
F32 = jnp.float32
BF16 = jnp.bfloat16
ROW_WIRE = (F32, F32, F32)
CORE_WIRE = (F32, F32, F32)
CHIP_WIRE = (F32, F32, F32)
LIMIT = 24 * 1024 * 1024


def tree_sum(terms):
    terms = list(terms)
    while len(terms) > 1:
        terms = [terms[i] + terms[i + 1] for i in range(0, len(terms), 2)]
    return terms[0]


def put_row(ref, value):
    rows = ref.shape[0] - PAD
    if ref.dtype == F32:
        parts = [value]
    else:
        high = value.astype(BF16).astype(F32)
        middle = (value - high).astype(BF16).astype(F32)
        parts = [high, middle, value - high - middle]
    shape = (PAD, ref.shape[1])
    index = lax.broadcasted_iota(jnp.int32, shape, 0)
    block = jnp.zeros(shape, F32)
    for place, part in enumerate(parts):
        block = jnp.where(index == place, jnp.broadcast_to(part, shape), block)
    ref[pl.ds(rows, PAD), :] = block.astype(ref.dtype)


def get_row(ref):
    rows = ref.shape[0] - PAD
    return jnp.sum(ref[pl.ds(rows, PAD), :].astype(F32), axis=0, keepdims=True)


def body_of(ref):
    return ref[pl.ds(0, ref.shape[0] - PAD), :]


def column_sum(values):
    return jnp.sum(values, axis=0, keepdims=True)


def spread(ref, value):
    ref[...] = jnp.broadcast_to(value, ref.shape)


def call(kernel, outs, *operands):
    vmem = pl.BlockSpec(memory_space=pltpu.VMEM)
    return pl.pallas_call(
        kernel,
        out_shape=[jax.ShapeDtypeStruct(shape, dtype) for shape, dtype in outs],
        in_specs=[vmem] * len(operands),
        out_specs=[vmem] * len(outs),
        compiler_params=pltpu.CompilerParams(vmem_limit_bytes=LIMIT),
    )(*operands)


def call_scratch(kernel, outs, scratch, *operands):
    vmem = pl.BlockSpec(memory_space=pltpu.VMEM)
    return pl.pallas_call(
        kernel,
        out_shape=[jax.ShapeDtypeStruct(shape, dtype) for shape, dtype in outs],
        in_specs=[vmem] * len(operands),
        out_specs=[vmem] * len(outs),
        scratch_shapes=scratch,
        compiler_params=pltpu.CompilerParams(vmem_limit_bytes=LIMIT),
    )(*operands)


def shards(states, targets, ridge):
    n_row = lax.axis_size("row")
    n_group = lax.axis_size("group")
    n_chip = n_group // 2
    tokens, feats = states.shape
    outs = targets.shape[1]
    feat_share = feats // n_row
    tok_share = tokens // n_group
    half = tokens // 2
    ridge = ridge.reshape(1, outs)
    scalar = ((8, outs), F32)

    def over_row(step, value):
        return lax.ppermute(value, "row", [(i, i ^ step) for i in range(n_row)])

    def over_group(step, value):
        return lax.ppermute(value, "group", [(i, i ^ step) for i in range(n_group)])

    def row_place(step):
        return pl.multiple_of((lax.axis_index("row") ^ step) * feat_share, feat_share)

    def token_place(core_step, chip_step):
        me = lax.axis_index("group")
        core = (me % 2) ^ core_step
        chip = (me // 2) ^ chip_step
        return pl.multiple_of((core * n_chip + chip) * tok_share, tok_share)

    def backward(wire, from_targets, *blocks):
        def kernel(a_ref, *refs):
            ins = refs[: len(blocks)]
            own_ref, delta_ref, *msg_refs, vec, prod = refs[len(blocks) :]
            if from_targets:
                vec[...] = ins[0][...].astype(BF16)
                delta = jnp.zeros((1, outs), F32)
            else:
                for core_step in range(2):
                    for chip_step in range(n_chip):
                        ref = ins[core_step * n_chip + chip_step]
                        vec[pl.ds(token_place(core_step, chip_step), tok_share), :] = body_of(ref)
                delta = tree_sum([get_row(ref) for ref in ins])
            spread(delta_ref, delta)
            turned = vec[...].T
            for start in range(0, feats, 256):
                part = jnp.dot(turned, a_ref[:, start : start + 256], preferred_element_type=F32)
                prod[start : start + 256, :] = part.T
            own_ref[...] = prod[pl.ds(row_place(0), feat_share), :]
            for step, ref in enumerate(msg_refs, 1):
                ref[pl.ds(0, feat_share), :] = prod[pl.ds(row_place(step), feat_share), :].astype(wire)
                put_row(ref, delta)

        msgs = [((feat_share + PAD, outs), wire)] * (n_row - 1)
        result = call_scratch(
            kernel,
            [((feat_share, outs), F32), scalar] + msgs,
            [pltpu.VMEM((tokens, outs), BF16), pltpu.VMEM((feats, outs), F32)],
            states,
            *blocks,
        )
        own, delta, *sends = result
        got = [over_row(step, send) for step, send in enumerate(sends, 1)]
        return own, delta, got

    def begin(own, got):
        def kernel(own_ref, *refs):
            ins, (grad_ref, msg_ref) = refs[: n_row - 1], refs[n_row - 1 :]
            grad = own_ref[...]
            for ref in ins:
                grad = grad + body_of(ref).astype(F32)
            grad_ref[...] = grad
            msg_ref[pl.ds(0, feat_share), :] = grad.astype(BF16)
            put_row(msg_ref, column_sum(grad * grad))

        return call(
            kernel, [((feat_share, outs), F32), ((feat_share + PAD, outs), BF16)], own, *got
        )

    def advance(own, delta, got, gamma, grad, direction, image, weights, residual):
        def kernel(own_ref, delta_ref, *refs):
            ins = refs[: n_row - 1]
            gamma_ref, grad_ref, dir_ref, image_ref, w_ref, r_ref, ridge_ref = refs[n_row - 1 : n_row + 6]
            w_out, r_out, grad_out, msg_ref = refs[n_row + 6 :]
            delta_all = tree_sum([delta_ref[0:1, :]] + [get_row(ref) for ref in ins])
            alpha = gamma_ref[0:1, :] / delta_all
            prod = own_ref[...]
            for ref in ins:
                prod = prod + body_of(ref).astype(F32)
            w_out[...] = w_ref[...] + alpha * dir_ref[...]
            r_out[...] = r_ref[...] - alpha * image_ref[...]
            new = grad_ref[...] - alpha * (prod + ridge_ref[...] * dir_ref[...])
            grad_out[...] = new
            msg_ref[pl.ds(0, feat_share), :] = new.astype(BF16)
            put_row(msg_ref, column_sum(new * new))

        return call(
            kernel,
            [((feat_share, outs), F32), ((tok_share, outs), F32), ((feat_share, outs), F32),
             ((feat_share + PAD, outs), BF16)],
            own, delta, *got, gamma, grad, direction, image, weights, residual, ridge,
        )

    def forward(wire, msg):
        blocks = [msg] + [over_row(step, msg) for step in range(1, n_row)]

        def kernel(a_ref, *refs):
            ins = refs[:n_row]
            own_ref, gamma_ref, peer_ref, vec = refs[n_row:]
            for step, ref in enumerate(ins):
                vec[pl.ds(row_place(step), feat_share), :] = body_of(ref)
            gamma = tree_sum([get_row(ref) for ref in ins])
            spread(gamma_ref, gamma)
            for core_step, ref in ((1, peer_ref), (0, own_ref)):
                for chip_step in range(n_chip):
                    part = jnp.dot(
                        a_ref[pl.ds(token_place(core_step, chip_step), tok_share), :],
                        vec[...],
                        preferred_element_type=F32,
                    )
                    ref[pl.ds(chip_step * tok_share, tok_share), :] = part.astype(ref.dtype)
            put_row(peer_ref, gamma)

        own, gamma, peer = call_scratch(
            kernel,
            [((half, outs), F32), scalar, ((half + PAD, outs), wire)],
            [pltpu.VMEM((feats, outs), BF16)],
            states,
            *blocks,
        )
        return own, gamma, over_group(1, peer)

    def join_cores(wire, own, gamma, got):
        def kernel(own_ref, gamma_ref, got_ref, out_ref, gamma_out, *msg_refs):
            total = gamma_ref[0:1, :] + get_row(got_ref)
            spread(gamma_out, total)
            for step, ref in enumerate((out_ref,) + msg_refs):
                place = pl.ds(step * tok_share, tok_share)
                both = own_ref[place, :] + got_ref[place, :].astype(F32)
                ref[pl.ds(0, tok_share), :] = both.astype(ref.dtype)
                if step:
                    put_row(ref, total)

        msgs = [((tok_share + PAD, outs), wire)] * (n_chip - 1)
        own, gamma, *sends = call(
            kernel, [((tok_share, outs), F32), scalar] + msgs, own, gamma, got
        )
        return own, gamma, [over_group(2 * step, send) for step, send in enumerate(sends, 1)]

    def image_of(wire, own, gamma, got, grad, before):
        def kernel(own_ref, gamma_ref, *refs):
            ins = refs[: n_chip - 1]
            grad_ref, ridge_ref, *rest = refs[n_chip - 1 :]
            gamma_out, dir_out, image_out, msg_ref = rest[-4:]
            gamma_all = tree_sum([gamma_ref[0:1, :]] + [get_row(ref) for ref in ins])
            spread(gamma_out, gamma_all)
            image = own_ref[...]
            for ref in ins:
                image = image + body_of(ref).astype(F32)
            direction = grad_ref[...]
            if before:
                old_gamma, old_dir, old_image = rest[:3]
                beta = gamma_all / old_gamma[0:1, :]
                image = image + beta * old_image[...]
                direction = direction + beta * old_dir[...]
            image_out[...] = image
            dir_out[...] = direction
            msg_ref[pl.ds(0, tok_share), :] = image.astype(msg_ref.dtype)
            put_row(
                msg_ref,
                column_sum(image * image) + ridge_ref[...] * column_sum(direction * direction),
            )

        return call(
            kernel,
            [scalar, ((feat_share, outs), F32), ((tok_share, outs), F32),
             ((tok_share + PAD, outs), wire)],
            own, gamma, *got, grad, ridge, *before,
        )

    def gathered(msg):
        mine = [msg] + [over_group(2 * step, msg) for step in range(1, n_chip)]
        return mine + [over_group(1, block) for block in mine]

    def own_targets():
        me = lax.axis_index("group")
        place = ((me % 2) * n_chip + me // 2) * tok_share
        return lax.dynamic_slice_in_dim(targets, place, tok_share, 0)

    weights = jnp.zeros((feat_share, outs), F32)
    residual = own_targets()
    own, _, got = backward(ROW_WIRE[0], True, targets)
    grad, msg = begin(own, got)
    before = ()
    for step in range(ITERS):
        own, gamma, got = forward(CORE_WIRE[step], msg)
        own, gamma, got = join_cores(CHIP_WIRE[step], own, gamma, got)
        last = step + 1 == ITERS
        gamma, direction, image, msg = image_of(
            F32 if last else BF16, own, gamma, got, grad, before
        )
        blocks = gathered(msg)
        if not last:
            own, delta, got = backward(ROW_WIRE[step + 1], False, *blocks)
            weights, residual, grad, msg = advance(
                own, delta, got, gamma, grad, direction, image, weights, residual
            )
            before = (gamma, direction, image)

    def last_delta(*refs):
        *ins, out_ref = refs
        spread(out_ref, tree_sum([get_row(ref) for ref in ins]))

    (delta,) = call(last_delta, [scalar], *blocks)
    deltas = [delta] + [over_row(step, delta) for step in range(1, n_row)]
    kept = gathered(residual)

    def finish(*refs):
        delta_refs, refs = refs[:n_row], refs[n_row:]
        image_refs, refs = refs[:n_group], refs[n_group:]
        kept_refs, refs = refs[:n_group], refs[n_group:]
        gamma_ref, dir_ref, w_ref, w_out, r_out = refs
        alpha = gamma_ref[0:1, :] / tree_sum([ref[0:1, :] for ref in delta_refs])
        w_out[...] = w_ref[...] + alpha * dir_ref[...]
        for core_step in range(2):
            for chip_step in range(n_chip):
                index = core_step * n_chip + chip_step
                place = pl.ds(token_place(core_step, chip_step), tok_share)
                r_out[place, :] = kept_refs[index][...] - alpha * body_of(image_refs[index]).astype(F32)

    weights, residual = call(
        finish,
        [((feat_share, outs), F32), ((tokens, outs), F32)],
        *deltas, *blocks, *kept, gamma, direction, weights,
    )
    return weights, residual


def solution(mesh):
    placed = (P("row", "group"), P("row", None), P())
    return jax.shard_map(
        shards,
        mesh=mesh,
        in_specs=placed,
        out_specs=(P(("group", "row"), None), P("row", None)),
        check_vma=False,
    )
```

time: 540 us -> 167 us (0.31)
  blocking collectives: 198 us -> 0 us
  waiting for transfers between devices: 287 us -> 90.2 us
  starting transfers between devices: 0.25 us -> 59 us
  matrix products: 26.5 us -> 0 us
  between operations: 14.2 us -> 0.79 us
  other arithmetic: 11.5 us -> 0 us
  Pallas kernels: 0 us -> 9.78 us
    psum x6 -> x0, waiting for transfers between devices: 287 us -> none  [the longest x3 169 us: shards(): image = lax.psum(local_image, 'group')]
    psum x5 -> x0, blocking collectives: 198 us -> none  [the longest x3 119 us: grad_norm(): return lax.psum(jnp.sum(mine * mine, axis=0), ('row', 'group'))]
    ppermute x0 -> x61, waiting for transfers between devices: none -> 90.2 us  [the longest x21 45.3 us: over_row(): return lax.ppermute(value, 'row', [(i, i ^ step) for i in range(n_row)])]
    ppermute x0 -> x61, starting transfers between devices: none -> 59 us  [the longest x21 32.4 us: over_row(): return lax.ppermute(value, 'row', [(i, i ^ step) for i in range(n_row)])]
    dot_general x6 -> x0, matrix products: 26.5 us -> none  [the longest x3 14.3 us: shards(): local_image = jnp.dot(states, full_dir, preferred_element_type=jnp.float32)]
    pallas_call x0 -> x17, Pallas kernels: none -> 9.78 us  [the longest x6 7.15 us: call_scratch(): pl.pallas_call(kernel, out_shape=[jax.ShapeDtypeStruct(shape, dtype) for...]
    sub x4 -> x0, other arithmetic: 6.45 us -> none  [the longest x2 3.4 us: shards(): residual = residual - alpha * image]
  transfers between devices with their start and end apart: 6 -> 61, of which waited for: 6 -> 39; matrix products, arithmetic and copies ran while one was open for 0% -> 1% of each run, Pallas kernels for 0% -> 0%
where the time goes in v1:
time: 167 us; the launch traced here: 166 us
  waiting for transfers between devices  90.2 us (54%)
  starting transfers between devices  59 us (35%)
  Pallas kernels  9.78 us (6%)
  local copies, waits for them, and re-layouts  6.53 us (4%)
    ppermute x21, waiting for transfers between devices, over_row(): return lax.ppermute(value, 'row', [(i, i ^ step) for i in range(n_row)])  45.3 us
    ppermute x40, waiting for transfers between devices, over_group(): return lax.ppermute(value, 'group', [(i, i ^ step) for i in range(n_group)])  44.9 us
    ppermute x21, starting transfers between devices, over_row(): return lax.ppermute(value, 'row', [(i, i ^ step) for i in range(n_row)])  32.4 us
    ppermute x40, starting transfers between devices, over_group(): return lax.ppermute(value, 'group', [(i, i ^ step) for i in range(n_group)])  26.6 us
    pallas_call x6, Pallas kernels, call_scratch(): pl.pallas_call(kernel, out_shape=[jax.ShapeDtypeStruct(shape, dtype) for...  7.15 us
    unnamed x12, local copies, waits for them, and re-layouts  5.61 us
  transfers between devices with their start and end apart: 61, of which 39 were waited for; matrix products, arithmetic and copies ran while one was open for 1% of the time, Pallas kernels for 0%

profile of v1, /device:TPU:0, one launch (start us, length us, event | category | flops | bytes accessed | tf_op | source)
XLA Modules:
  0.0 166.3 jit_solution(337292374461594237)
XLA Ops:
  0.6 2.2 %copy-done = bf16[2048,1024]{1,0:T(8,128)(2,1)S(1)} copy-done((bf16[2048,1024]{1,0:T(8,128)(2,1)S(1)}, bf16[2048,1024]{1,0:T(8,128)(2,1)}, u32[]{:S(2)}) %copy-start) | copy-done | bytes 4194328
  2.8 1.2 copy-done.4
  4.0 1.4 shard_map.50
  5.4 3.0 %collective-permute-start = (f32[272,128]{1,0:T(8,128)S(1)}, f32[272,128]{1,0:T(8,128)S(1)}, u32[]{:S(2)}, u32[]{:S(2)}) collective-permute-start(f32[272,128]{1,0:T(8,128)S(1)} %get-tuple-element.62), channel_id=1, source_target_pairs={{0,8},{8,0},{16,24},{24,16},{1,9},{9,1},{17,25},{25,17},{2,10},{10... | collective-permute-start | bytes 417800 | tf_op jit(solution)/shard_map/ppermute | solution.py:96
  8.5 2.6 %collective-permute-start.1 = (f32[272,128]{1,0:T(8,128)S(1)}, f32[272,128]{1,0:T(8,128)S(1)}, u32[]{:S(2)}, u32[]{:S(2)}) collective-permute-start(f32[272,128]{1,0:T(8,128)S(1)} %get-tuple-element.63), channel_id=1, source_target_pairs={{0,16},{8,24},{16,0},{24,8},{1,17},{9,25},{17,1},{25,9},{2,18},{10... | collective-permute-start | bytes 417800 | tf_op jit(solution)/shard_map/ppermute | solution.py:96
  11.0 2.8 %collective-permute-done.refs_0_ = f32[272,128]{1,0:T(8,128)S(1)} collective-permute-done((f32[272,128]{1,0:T(8,128)S(1)}, f32[272,128]{1,0:T(8,128)S(1)}, u32[]{:S(2)}, u32[]{:S(2)}) %collective-permute-start) | collective-permute-done | bytes 139296 | tf_op jit(solution)/shard_map/ppermute | solution.py:96
  13.9 8.0 %collective-permute-done.1.refs_1_ = f32[272,128]{1,0:T(8,128)S(1)} collective-permute-done((f32[272,128]{1,0:T(8,128)S(1)}, f32[272,128]{1,0:T(8,128)S(1)}, u32[]{:S(2)}, u32[]{:S(2)}) %collective-permute-start.1) | collective-permute-done | bytes 139296 | tf_op jit(solution)/shard_map/ppermute | solution.py:96
  22.0 2.3 %collective-permute-start.5 = (bf16[272,128]{1,0:T(8,128)(2,1)S(1)}, bf16[272,128]{1,0:T(8,128)(2,1)S(1)}, u32[]{:S(2)}, u32[]{:S(2)}) collective-permute-start(bf16[272,128]{1,0:T(8,128)(2,1)S(1)} %get-tuple-element.65.refs_0_), channel_id=1, source_target_pairs={{0,24},{8,16},{16,8},{24,0},{1,25},{9,17},{17,9},{25,1},{2,26},{10... | collective-permute-start | bytes 208904 | tf_op jit(solution)/shard_map/ppermute | solution.py:96
  24.3 1.7 %collective-permute-start.4 = (bf16[272,128]{1,0:T(8,128)(2,1)S(1)}, bf16[272,128]{1,0:T(8,128)(2,1)S(1)}, u32[]{:S(2)}, u32[]{:S(2)}) collective-permute-start(bf16[272,128]{1,0:T(8,128)(2,1)S(1)} %get-tuple-element.65.refs_0_), channel_id=1, source_target_pairs={{0,16},{8,24},{16,0},{24,8},{1,17},{9,25},{17,1},{25,9},{2,18},{10... | collective-permute-start | bytes 208904 | tf_op jit(solution)/shard_map/ppermute | solution.py:96
  26.5 2.4 %collective-permute-done.5.refs_3_ = bf16[272,128]{1,0:T(8,128)(2,1)S(1)} collective-permute-done((bf16[272,128]{1,0:T(8,128)(2,1)S(1)}, bf16[272,128]{1,0:T(8,128)(2,1)S(1)}, u32[]{:S(2)}, u32[]{:S(2)}) %collective-permute-start.5) | collective-permute-done | bytes 69664 | tf_op jit(solution)/shard_map/ppermute | solution.py:96
  28.9 1.4 collective-permute-done.4.refs_2_
  31.0 1.3 shard_map.52
  32.4 1.9 %collective-permute-done.6.got_ref = f32[1040,128]{1,0:T(8,128)S(1)} collective-permute-done((f32[1040,128]{1,0:T(8,128)S(1)}, f32[1040,128]{1,0:T(8,128)S(1)}, u32[]{:S(2)}, u32[]{:S(2)}) %collective-permute-start.6) | collective-permute-done | bytes 532512 | tf_op jit(solution)/shard_map/ppermute | solution.py:99
  34.4 1.6 collective-permute-start.7
  35.9 1.4 collective-permute-start.8
  37.9 2.7 %collective-permute-done.7.refs_0_ = f32[272,128]{1,0:T(8,128)S(1)} collective-permute-done((f32[272,128]{1,0:T(8,128)S(1)}, f32[272,128]{1,0:T(8,128)S(1)}, u32[]{:S(2)}, u32[]{:S(2)}) %collective-permute-start.7) | collective-permute-done | bytes 139296 | tf_op jit(solution)/shard_map/ppermute | solution.py:99
  40.6 3.7 %collective-permute-done.8.refs_1_ = f32[272,128]{1,0:T(8,128)S(1)} collective-permute-done((f32[272,128]{1,0:T(8,128)S(1)}, f32[272,128]{1,0:T(8,128)S(1)}, u32[]{:S(2)}, u32[]{:S(2)}) %collective-permute-start.8) | collective-permute-done | bytes 139296 | tf_op jit(solution)/shard_map/ppermute | solution.py:99
  44.5 1.5 collective-permute-start.12
  46.0 1.1 collective-permute-start.11
  48.0 2.1 %collective-permute-done.12.refs_3_ = bf16[272,128]{1,0:T(8,128)(2,1)S(1)} collective-permute-done((bf16[272,128]{1,0:T(8,128)(2,1)S(1)}, bf16[272,128]{1,0:T(8,128)(2,1)S(1)}, u32[]{:S(2)}, u32[]{:S(2)}) %collective-permute-start.12) | collective-permute-done | bytes 69664 | tf_op jit(solution)/shard_map/ppermute | solution.py:99
  53.9 2.7 %collective-permute-start.18 = (f32[272,128]{1,0:T(8,128)S(1)}, f32[272,128]{1,0:T(8,128)S(1)}, u32[]{:S(2)}, u32[]{:S(2)}) collective-permute-start(f32[272,128]{1,0:T(8,128)S(1)} %get-tuple-element.79), channel_id=1, source_target_pairs={{0,16},{8,24},{16,0},{24,8},{1,17},{9,25},{17,1},{25,9},{2,18},{10... | collective-permute-start | bytes 417800 | tf_op jit(solution)/shard_map/ppermute | solution.py:96
  56.6 1.5 collective-permute-start.19
  59.0 2.9 %collective-permute-done.17.refs_0_ = f32[272,128]{1,0:T(8,128)S(1)} collective-permute-done((f32[272,128]{1,0:T(8,128)S(1)}, f32[272,128]{1,0:T(8,128)S(1)}, u32[]{:S(2)}, u32[]{:S(2)}) %collective-permute-start.17) | collective-permute-done | bytes 139296 | tf_op jit(solution)/shard_map/ppermute | solution.py:96
  61.9 5.5 %collective-permute-done.18.refs_1_ = f32[272,128]{1,0:T(8,128)S(1)} collective-permute-done((f32[272,128]{1,0:T(8,128)S(1)}, f32[272,128]{1,0:T(8,128)S(1)}, u32[]{:S(2)}, u32[]{:S(2)}) %collective-permute-start.18) | collective-permute-done | bytes 139296 | tf_op jit(solution)/shard_map/ppermute | solution.py:96
  67.5 2.2 %collective-permute-start.22 = (bf16[272,128]{1,0:T(8,128)(2,1)S(1)}, bf16[272,128]{1,0:T(8,128)(2,1)S(1)}, u32[]{:S(2)}, u32[]{:S(2)}) collective-permute-start(bf16[272,128]{1,0:T(8,128)(2,1)S(1)} %get-tuple-element.84.refs_0_), channel_id=1, source_target_pairs={{0,24},{8,16},{16,8},{24,0},{1,25},{9,17},{17,9},{25,1},{2,26},{10... | collective-permute-start | bytes 208904 | tf_op jit(solution)/shard_map/ppermute | solution.py:96
  69.7 1.9 %collective-permute-start.21 = (bf16[272,128]{1,0:T(8,128)(2,1)S(1)}, bf16[272,128]{1,0:T(8,128)(2,1)S(1)}, u32[]{:S(2)}, u32[]{:S(2)}) collective-permute-start(bf16[272,128]{1,0:T(8,128)(2,1)S(1)} %get-tuple-element.84.refs_0_), channel_id=1, source_target_pairs={{0,16},{8,24},{16,0},{24,8},{1,17},{9,25},{17,1},{25,9},{2,18},{10... | collective-permute-start | bytes 208904 | tf_op jit(solution)/shard_map/ppermute | solution.py:96
  71.9 1.9 %collective-permute-done.22.refs_3_ = bf16[272,128]{1,0:T(8,128)(2,1)S(1)} collective-permute-done((bf16[272,128]{1,0:T(8,128)(2,1)S(1)}, bf16[272,128]{1,0:T(8,128)(2,1)S(1)}, u32[]{:S(2)}, u32[]{:S(2)}) %collective-permute-start.22) | collective-permute-done | bytes 69664 | tf_op jit(solution)/shard_map/ppermute | solution.py:96
  73.8 2.9 %collective-permute-done.21.refs_2_ = bf16[272,128]{1,0:T(8,128)(2,1)S(1)} collective-permute-done((bf16[272,128]{1,0:T(8,128)(2,1)S(1)}, bf16[272,128]{1,0:T(8,128)(2,1)S(1)}, u32[]{:S(2)}, u32[]{:S(2)}) %collective-permute-start.21) | collective-permute-done | bytes 69664 | tf_op jit(solution)/shard_map/ppermute | solution.py:96
  76.7 2.2 %copy-done.2 = bf16[2048,1024]{1,0:T(8,128)(2,1)S(1)} copy-done((bf16[2048,1024]{1,0:T(8,128)(2,1)S(1)}, bf16[2048,1024]{1,0:T(8,128)(2,1)}, u32[]{:S(2)}) %copy-start.2) | copy-done | bytes 4194328
  78.9 1.3 shard_map.57
  80.3 1.9 %collective-permute-done.23.got_ref = f32[1040,128]{1,0:T(8,128)S(1)} collective-permute-done((f32[1040,128]{1,0:T(8,128)S(1)}, f32[1040,128]{1,0:T(8,128)S(1)}, u32[]{:S(2)}, u32[]{:S(2)}) %collective-permute-start.23) | collective-permute-done | bytes 532512 | tf_op jit(solution)/shard_map/ppermute | solution.py:99
  82.2 1.4 collective-permute-start.24
  84.5 1.3 collective-permute-start.26
  85.8 2.9 %collective-permute-done.24.refs_0_ = f32[272,128]{1,0:T(8,128)S(1)} collective-permute-done((f32[272,128]{1,0:T(8,128)S(1)}, f32[272,128]{1,0:T(8,128)S(1)}, u32[]{:S(2)}, u32[]{:S(2)}) %collective-permute-start.24) | collective-permute-done | bytes 139296 | tf_op jit(solution)/shard_map/ppermute | solution.py:99
  88.7 3.3 %collective-permute-done.25.refs_1_ = f32[272,128]{1,0:T(8,128)S(1)} collective-permute-done((f32[272,128]{1,0:T(8,128)S(1)}, f32[272,128]{1,0:T(8,128)S(1)}, u32[]{:S(2)}, u32[]{:S(2)}) %collective-permute-start.25) | collective-permute-done | bytes 139296 | tf_op jit(solution)/shard_map/ppermute | solution.py:99
  92.2 1.5 collective-permute-start.29
  94.4 1.3 collective-permute-start.27
  95.7 2.1 %collective-permute-done.29.refs_3_ = bf16[272,128]{1,0:T(8,128)(2,1)S(1)} collective-permute-done((bf16[272,128]{1,0:T(8,128)(2,1)S(1)}, bf16[272,128]{1,0:T(8,128)(2,1)S(1)}, u32[]{:S(2)}, u32[]{:S(2)}) %collective-permute-start.29) | collective-permute-done | bytes 69664 | tf_op jit(solution)/shard_map/ppermute | solution.py:99
  101.3 2.9 %collective-permute-start.35 = (f32[272,128]{1,0:T(8,128)S(1)}, f32[272,128]{1,0:T(8,128)S(1)}, u32[]{:S(2)}, u32[]{:S(2)}) collective-permute-start(f32[272,128]{1,0:T(8,128)S(1)} %get-tuple-element.98), channel_id=1, source_target_pairs={{0,16},{8,24},{16,0},{24,8},{1,17},{9,25},{17,1},{25,9},{2,18},{10... | collective-permute-start | bytes 417800 | tf_op jit(solution)/shard_map/ppermute | solution.py:96
  104.2 1.2 collective-permute-start.36
  105.4 3.9 %collective-permute-done.34.refs_0_ = f32[272,128]{1,0:T(8,128)S(1)} collective-permute-done((f32[272,128]{1,0:T(8,128)S(1)}, f32[272,128]{1,0:T(8,128)S(1)}, u32[]{:S(2)}, u32[]{:S(2)}) %collective-permute-start.34) | collective-permute-done | bytes 139296 | tf_op jit(solution)/shard_map/ppermute | solution.py:96
  109.3 5.5 %collective-permute-done.35.refs_1_ = f32[272,128]{1,0:T(8,128)S(1)} collective-permute-done((f32[272,128]{1,0:T(8,128)S(1)}, f32[272,128]{1,0:T(8,128)S(1)}, u32[]{:S(2)}, u32[]{:S(2)}) %collective-permute-start.35) | collective-permute-done | bytes 139296 | tf_op jit(solution)/shard_map/ppermute | solution.py:96
  114.9 2.5 %collective-permute-start.39 = (bf16[272,128]{1,0:T(8,128)(2,1)S(1)}, bf16[272,128]{1,0:T(8,128)(2,1)S(1)}, u32[]{:S(2)}, u32[]{:S(2)}) collective-permute-start(bf16[272,128]{1,0:T(8,128)(2,1)S(1)} %get-tuple-element.105.refs_0_), channel_id=1, source_target_pairs={{0,24},{8,16},{16,8},{24,0},{1,25},{9,17},{17,9},{25,1},{2,26},{10... | collective-permute-start | bytes 208904 | tf_op jit(solution)/shard_map/ppermute | solution.py:96
  117.3 1.8 %collective-permute-start.38 = (bf16[272,128]{1,0:T(8,128)(2,1)S(1)}, bf16[272,128]{1,0:T(8,128)(2,1)S(1)}, u32[]{:S(2)}, u32[]{:S(2)}) collective-permute-start(bf16[272,128]{1,0:T(8,128)(2,1)S(1)} %get-tuple-element.105.refs_0_), channel_id=1, source_target_pairs={{0,16},{8,24},{16,0},{24,8},{1,17},{9,25},{17,1},{25,9},{2,18},{10... | collective-permute-start | bytes 208904 | tf_op jit(solution)/shard_map/ppermute | solution.py:96
  119.3 1.9 %collective-permute-done.39.refs_3_ = bf16[272,128]{1,0:T(8,128)(2,1)S(1)} collective-permute-done((bf16[272,128]{1,0:T(8,128)(2,1)S(1)}, bf16[272,128]{1,0:T(8,128)(2,1)S(1)}, u32[]{:S(2)}, u32[]{:S(2)}) %collective-permute-start.39) | collective-permute-done | bytes 69664 | tf_op jit(solution)/shard_map/ppermute | solution.py:96
  121.2 3.0 %collective-permute-done.38.refs_2_ = bf16[272,128]{1,0:T(8,128)(2,1)S(1)} collective-permute-done((bf16[272,128]{1,0:T(8,128)(2,1)S(1)}, bf16[272,128]{1,0:T(8,128)(2,1)S(1)}, u32[]{:S(2)}, u32[]{:S(2)}) %collective-permute-start.38) | collective-permute-done | bytes 69664 | tf_op jit(solution)/shard_map/ppermute | solution.py:96
  124.2 1.3 shard_map.62
  125.6 1.9 %collective-permute-done.40.got_ref = f32[1040,128]{1,0:T(8,128)S(1)} collective-permute-done((f32[1040,128]{1,0:T(8,128)S(1)}, f32[1040,128]{1,0:T(8,128)S(1)}, u32[]{:S(2)}, u32[]{:S(2)}) %collective-permute-start.40) | collective-permute-done | bytes 532512 | tf_op jit(solution)/shard_map/ppermute | solution.py:99
  127.6 1.1 collective-permute-start.41
  129.6 1.5 collective-permute-start.43
  131.1 3.0 %collective-permute-done.41.refs_0_ = f32[272,128]{1,0:T(8,128)S(1)} collective-permute-done((f32[272,128]{1,0:T(8,128)S(1)}, f32[272,128]{1,0:T(8,128)S(1)}, u32[]{:S(2)}, u32[]{:S(2)}) %collective-permute-start.41) | collective-permute-done | bytes 139296 | tf_op jit(solution)/shard_map/ppermute | solution.py:99
  134.2 3.0 %collective-permute-done.42.refs_1_ = f32[272,128]{1,0:T(8,128)S(1)} collective-permute-done((f32[272,128]{1,0:T(8,128)S(1)}, f32[272,128]{1,0:T(8,128)S(1)}, u32[]{:S(2)}, u32[]{:S(2)}) %collective-permute-start.42) | collective-permute-done | bytes 139296 | tf_op jit(solution)/shard_map/ppermute | solution.py:99
  137.8 1.5 collective-permute-start.46
  140.3 1.4 collective-permute-start.56
  141.7 1.1 collective-permute-start.55
  143.8 4.3 %collective-permute-done.56.refs_15_ = f32[256,128]{1,0:T(8,128)S(1)} collective-permute-done((f32[256,128]{1,0:T(8,128)S(1)}, f32[256,128]{1,0:T(8,128)S(1)}, u32[]{:S(2)}, u32[]{:S(2)}) %collective-permute-start.56) | collective-permute-done | bytes 131104 | tf_op jit(solution)/shard_map/ppermute | solution.py:99
  148.6 1.1 collective-permute-done.45.refs_2_.refs_6_
  149.6 2.3 %collective-permute-done.55.refs_14_ = f32[256,128]{1,0:T(8,128)S(1)} collective-permute-done((f32[256,128]{1,0:T(8,128)S(1)}, f32[256,128]{1,0:T(8,128)S(1)}, u32[]{:S(2)}, u32[]{:S(2)}) %collective-permute-start.55) | collective-permute-done | bytes 131104 | tf_op jit(solution)/shard_map/ppermute | solution.py:99
  152.9 4.1 %collective-permute-done.54.refs_13_ = f32[256,128]{1,0:T(8,128)S(1)} collective-permute-done((f32[256,128]{1,0:T(8,128)S(1)}, f32[256,128]{1,0:T(8,128)S(1)}, u32[]{:S(2)}, u32[]{:S(2)}) %collective-permute-start.54) | collective-permute-done | bytes 131104 | tf_op jit(solution)/shard_map/ppermute | solution.py:99
  158.1 2.5 %collective-permute-start.53 = (f32[8,128]{1,0:T(8,128)S(1)}, f32[8,128]{1,0:T(8,128)S(1)}, u32[]{:S(2)}, u32[]{:S(2)}) collective-permute-start(f32[8,128]{1,0:T(8,128)S(1)} %shard_map.65.refs_0_), channel_id=1, source_target_pairs={{0,24},{8,16},{16,8},{24,0},{1,25},{9,17},{17,9},{25,1},{2,26},{10... | collective-permute-start | bytes 12296 | tf_op jit(solution)/shard_map/ppermute | solution.py:96
  160.6 1.9 %collective-permute-start.51 = (f32[8,128]{1,0:T(8,128)S(1)}, f32[8,128]{1,0:T(8,128)S(1)}, u32[]{:S(2)}, u32[]{:S(2)}) collective-permute-start(f32[8,128]{1,0:T(8,128)S(1)} %shard_map.65.refs_0_), channel_id=1, source_target_pairs={{0,8},{8,0},{16,24},{24,16},{1,9},{9,1},{17,25},{25,17},{2,10},{10... | collective-permute-start | bytes 12296 | tf_op jit(solution)/shard_map/ppermute | solution.py:96
  162.6 1.0 collective-permute-done.53.refs_3_
  163.6 1.5 collective-permute-done.52.refs_2_
  165.1 1.2 shard_map.66
  (89 shorter events, 19.9 us)
Async XLA Ops:
  4.0 27.0 %copy-start.1 = (bf16[2048,1024]{1,0:T(8,128)(2,1)S(1)}, bf16[2048,1024]{1,0:T(8,128)(2,1)}, u32[]{:S(2)}) copy-start(bf16[2048,1024]{1,0:T(8,128)(2,1)} %a_ref.11) | copy-start | bytes 12582916
  5.4 38.9 %copy-start.5 = (f32[128]{0:T(128)S(1)}, f32[128]{0:T(128)}, u32[]{:S(2)}) copy-start(f32[128]{0:T(128)} %param.5) | copy-start | bytes 1540
  5.4 8.4 %collective-permute-start = (f32[272,128]{1,0:T(8,128)S(1)}, f32[272,128]{1,0:T(8,128)S(1)}, u32[]{:S(2)}, u32[]{:S(2)}) collective-permute-start(f32[272,128]{1,0:T(8,128)S(1)} %get-tuple-element.62), channel_id=1, source_target_pairs={{0,8},{8,0},{16,24},{24,16},{1,9},{9,1},{17,25},{25,17},{2,10},{10... | collective-permute-start | bytes 417800 | tf_op jit(solution)/shard_map/ppermute | solution.py:96
  8.5 13.5 %collective-permute-start.1 = (f32[272,128]{1,0:T(8,128)S(1)}, f32[272,128]{1,0:T(8,128)S(1)}, u32[]{:S(2)}, u32[]{:S(2)}) collective-permute-start(f32[272,128]{1,0:T(8,128)S(1)} %get-tuple-element.63), channel_id=1, source_target_pairs={{0,16},{8,24},{16,0},{24,8},{1,17},{9,25},{17,1},{25,9},{2,18},{10... | collective-permute-start | bytes 417800 | tf_op jit(solution)/shard_map/ppermute | solution.py:96
  11.0 10.9 %collective-permute-start.2 = (f32[272,128]{1,0:T(8,128)S(1)}, f32[272,128]{1,0:T(8,128)S(1)}, u32[]{:S(2)}, u32[]{:S(2)}) collective-permute-start(f32[272,128]{1,0:T(8,128)S(1)} %get-tuple-element.64), channel_id=1, source_target_pairs={{0,24},{8,16},{16,8},{24,0},{1,25},{9,17},{17,9},{25,1},{2,26},{10... | collective-permute-start | bytes 417800 | tf_op jit(solution)/shard_map/ppermute | solution.py:96
  22.0 6.9 %collective-permute-start.5 = (bf16[272,128]{1,0:T(8,128)(2,1)S(1)}, bf16[272,128]{1,0:T(8,128)(2,1)S(1)}, u32[]{:S(2)}, u32[]{:S(2)}) collective-permute-start(bf16[272,128]{1,0:T(8,128)(2,1)S(1)} %get-tuple-element.65.refs_0_), channel_id=1, source_target_pairs={{0,24},{8,16},{16,8},{24,0},{1,25},{9,17},{17,9},{25,1},{2,26},{10... | collective-permute-start | bytes 208904 | tf_op jit(solution)/shard_map/ppermute | solution.py:96
  24.3 6.0 %collective-permute-start.4 = (bf16[272,128]{1,0:T(8,128)(2,1)S(1)}, bf16[272,128]{1,0:T(8,128)(2,1)S(1)}, u32[]{:S(2)}, u32[]{:S(2)}) collective-permute-start(bf16[272,128]{1,0:T(8,128)(2,1)S(1)} %get-tuple-element.65.refs_0_), channel_id=1, source_target_pairs={{0,16},{8,24},{16,0},{24,8},{1,17},{9,25},{17,1},{25,9},{2,18},{10... | collective-permute-start | bytes 208904 | tf_op jit(solution)/shard_map/ppermute | solution.py:96
  26.0 5.0 %collective-permute-start.3 = (bf16[272,128]{1,0:T(8,128)(2,1)S(1)}, bf16[272,128]{1,0:T(8,128)(2,1)S(1)}, u32[]{:S(2)}, u32[]{:S(2)}) collective-permute-start(bf16[272,128]{1,0:T(8,128)(2,1)S(1)} %get-tuple-element.65.refs_0_), channel_id=1, source_target_pairs={{0,8},{8,0},{16,24},{24,16},{1,9},{9,1},{17,25},{25,17},{2,10},{10... | collective-permute-start | bytes 208904 | tf_op jit(solution)/shard_map/ppermute | solution.py:96
  32.3 2.0 %collective-permute-start.6 = (f32[1040,128]{1,0:T(8,128)S(1)}, f32[1040,128]{1,0:T(8,128)S(1)}, u32[]{:S(2)}, u32[]{:S(2)}) collective-permute-start(f32[1040,128]{1,0:T(8,128)S(1)} %get-tuple-element.68), channel_id=1, source_target_pairs={{0,1},{1,0},{2,3},{3,2},{4,5},{5,4},{6,7},{7,6},{8,9},{9,8},{10,11... | collective-permute-start | bytes 1597448 | tf_op jit(solution)/shard_map/ppermute | solution.py:99
  34.4 6.3 %collective-permute-start.7 = (f32[272,128]{1,0:T(8,128)S(1)}, f32[272,128]{1,0:T(8,128)S(1)}, u32[]{:S(2)}, u32[]{:S(2)}) collective-permute-start(f32[272,128]{1,0:T(8,128)S(1)} %get-tuple-element.71), channel_id=1, source_target_pairs={{0,2},{1,3},{2,0},{3,1},{4,6},{5,7},{6,4},{7,5},{8,10},{9,11},{10,... | collective-permute-start | bytes 417800 | tf_op jit(solution)/shard_map/ppermute | solution.py:99
  35.9 8.4 %collective-permute-start.8 = (f32[272,128]{1,0:T(8,128)S(1)}, f32[272,128]{1,0:T(8,128)S(1)}, u32[]{:S(2)}, u32[]{:S(2)}) collective-permute-start(f32[272,128]{1,0:T(8,128)S(1)} %get-tuple-element.72), channel_id=1, source_target_pairs={{0,4},{1,5},{2,6},{3,7},{4,0},{5,1},{6,2},{7,3},{8,12},{9,13},{10,... | collective-permute-start | bytes 417800 | tf_op jit(solution)/shard_map/ppermute | solution.py:99
  37.3 7.0 %collective-permute-start.9 = (f32[272,128]{1,0:T(8,128)S(1)}, f32[272,128]{1,0:T(8,128)S(1)}, u32[]{:S(2)}, u32[]{:S(2)}) collective-permute-start(f32[272,128]{1,0:T(8,128)S(1)} %get-tuple-element.73), channel_id=1, source_target_pairs={{0,6},{1,7},{2,4},{3,5},{4,2},{5,3},{6,0},{7,1},{8,14},{9,15},{10,... | collective-permute-start | bytes 417800 | tf_op jit(solution)/shard_map/ppermute | solution.py:99
  44.5 5.7 %collective-permute-start.12 = (bf16[272,128]{1,0:T(8,128)(2,1)S(1)}, bf16[272,128]{1,0:T(8,128)(2,1)S(1)}, u32[]{:S(2)}, u32[]{:S(2)}) collective-permute-start(bf16[272,128]{1,0:T(8,128)(2,1)S(1)} %get-tuple-element.75.refs_0_), channel_id=1, source_target_pairs={{0,6},{1,7},{2,4},{3,5},{4,2},{5,3},{6,0},{7,1},{8,14},{9,15},{10,... | collective-permute-start | bytes 208904 | tf_op jit(solution)/shard_map/ppermute | solution.py:99
  46.0 4.7 %collective-permute-start.11 = (bf16[272,128]{1,0:T(8,128)(2,1)S(1)}, bf16[272,128]{1,0:T(8,128)(2,1)S(1)}, u32[]{:S(2)}, u32[]{:S(2)}) collective-permute-start(bf16[272,128]{1,0:T(8,128)(2,1)S(1)} %get-tuple-element.75.refs_0_), channel_id=1, source_target_pairs={{0,4},{1,5},{2,6},{3,7},{4,0},{5,1},{6,2},{7,3},{8,12},{9,13},{10,... | collective-permute-start | bytes 208904 | tf_op jit(solution)/shard_map/ppermute | solution.py:99
  47.1 4.3 %collective-permute-start.10 = (bf16[272,128]{1,0:T(8,128)(2,1)S(1)}, bf16[272,128]{1,0:T(8,128)(2,1)S(1)}, u32[]{:S(2)}, u32[]{:S(2)}) collective-permute-start(bf16[272,128]{1,0:T(8,128)(2,1)S(1)} %get-tuple-element.75.refs_0_), channel_id=1, source_target_pairs={{0,2},{1,3},{2,0},{3,1},{4,6},{5,7},{6,4},{7,5},{8,10},{9,11},{10,... | collective-permute-start | bytes 208904 | tf_op jit(solution)/shard_map/ppermute | solution.py:99
  48.0 3.4 %collective-permute-start.13 = (bf16[272,128]{1,0:T(8,128)(2,1)S(1)}, bf16[272,128]{1,0:T(8,128)(2,1)S(1)}, u32[]{:S(2)}, u32[]{:S(2)}) collective-permute-start(bf16[272,128]{1,0:T(8,128)(2,1)S(1)} %get-tuple-element.75.refs_0_), channel_id=1, source_target_pairs={{0,1},{1,0},{2,3},{3,2},{4,5},{5,4},{6,7},{7,6},{8,9},{9,8},{10,11... | collective-permute-start | bytes 208904 | tf_op jit(solution)/shard_map/ppermute | solution.py:99
  50.1 1.3 collective-permute-start.16
  50.7 1.3 collective-permute-start.15
  51.4 1.3 collective-permute-start.14
  53.6 8.2 %collective-permute-start.17 = (f32[272,128]{1,0:T(8,128)S(1)}, f32[272,128]{1,0:T(8,128)S(1)}, u32[]{:S(2)}, u32[]{:S(2)}) collective-permute-start(f32[272,128]{1,0:T(8,128)S(1)} %get-tuple-element.78), channel_id=1, source_target_pairs={{0,8},{8,0},{16,24},{24,16},{1,9},{9,1},{17,25},{25,17},{2,10},{10... | collective-permute-start | bytes 417800 | tf_op jit(solution)/shard_map/ppermute | solution.py:96
  53.9 13.4 %collective-permute-start.18 = (f32[272,128]{1,0:T(8,128)S(1)}, f32[272,128]{1,0:T(8,128)S(1)}, u32[]{:S(2)}, u32[]{:S(2)}) collective-permute-start(f32[272,128]{1,0:T(8,128)S(1)} %get-tuple-element.79), channel_id=1, source_target_pairs={{0,16},{8,24},{16,0},{24,8},{1,17},{9,25},{17,1},{25,9},{2,18},{10... | collective-permute-start | bytes 417800 | tf_op jit(solution)/shard_map/ppermute | solution.py:96
  56.6 10.8 %collective-permute-start.19 = (f32[272,128]{1,0:T(8,128)S(1)}, f32[272,128]{1,0:T(8,128)S(1)}, u32[]{:S(2)}, u32[]{:S(2)}) collective-permute-start(f32[272,128]{1,0:T(8,128)S(1)} %get-tuple-element.80), channel_id=1, source_target_pairs={{0,24},{8,16},{16,8},{24,0},{1,25},{9,17},{17,9},{25,1},{2,26},{10... | collective-permute-start | bytes 417800 | tf_op jit(solution)/shard_map/ppermute | solution.py:96
  67.5 6.3 %collective-permute-start.22 = (bf16[272,128]{1,0:T(8,128)(2,1)S(1)}, bf16[272,128]{1,0:T(8,128)(2,1)S(1)}, u32[]{:S(2)}, u32[]{:S(2)}) collective-permute-start(bf16[272,128]{1,0:T(8,128)(2,1)S(1)} %get-tuple-element.84.refs_0_), channel_id=1, source_target_pairs={{0,24},{8,16},{16,8},{24,0},{1,25},{9,17},{17,9},{25,1},{2,26},{10... | collective-permute-start | bytes 208904 | tf_op jit(solution)/shard_map/ppermute | solution.py:96
  69.7 7.0 %collective-permute-start.21 = (bf16[272,128]{1,0:T(8,128)(2,1)S(1)}, bf16[272,128]{1,0:T(8,128)(2,1)S(1)}, u32[]{:S(2)}, u32[]{:S(2)}) collective-permute-start(bf16[272,128]{1,0:T(8,128)(2,1)S(1)} %get-tuple-element.84.refs_0_), channel_id=1, source_target_pairs={{0,16},{8,24},{16,0},{24,8},{1,17},{9,25},{17,1},{25,9},{2,18},{10... | collective-permute-start | bytes 208904 | tf_op jit(solution)/shard_map/ppermute | solution.py:96
  71.6 5.1 %collective-permute-start.20 = (bf16[272,128]{1,0:T(8,128)(2,1)S(1)}, bf16[272,128]{1,0:T(8,128)(2,1)S(1)}, u32[]{:S(2)}, u32[]{:S(2)}) collective-permute-start(bf16[272,128]{1,0:T(8,128)(2,1)S(1)} %get-tuple-element.84.refs_0_), channel_id=1, source_target_pairs={{0,8},{8,0},{16,24},{24,16},{1,9},{9,1},{17,25},{25,17},{2,10},{10... | collective-permute-start | bytes 208904 | tf_op jit(solution)/shard_map/ppermute | solution.py:96
  78.9 21.1 %copy-start.3 = (bf16[2048,1024]{1,0:T(8,128)(2,1)S(1)}, bf16[2048,1024]{1,0:T(8,128)(2,1)}, u32[]{:S(2)}) copy-start(bf16[2048,1024]{1,0:T(8,128)(2,1)} %a_ref.11) | copy-start | bytes 12582916
  80.2 2.0 %collective-permute-start.23 = (f32[1040,128]{1,0:T(8,128)S(1)}, f32[1040,128]{1,0:T(8,128)S(1)}, u32[]{:S(2)}, u32[]{:S(2)}) collective-permute-start(f32[1040,128]{1,0:T(8,128)S(1)} %get-tuple-element.87), channel_id=1, source_target_pairs={{0,1},{1,0},{2,3},{3,2},{4,5},{5,4},{6,7},{7,6},{8,9},{9,8},{10,11... | collective-permute-start | bytes 1597448 | tf_op jit(solution)/shard_map/ppermute | solution.py:99
  82.2 6.5 %collective-permute-start.24 = (f32[272,128]{1,0:T(8,128)S(1)}, f32[272,128]{1,0:T(8,128)S(1)}, u32[]{:S(2)}, u32[]{:S(2)}) collective-permute-start(f32[272,128]{1,0:T(8,128)S(1)} %get-tuple-element.90), channel_id=1, source_target_pairs={{0,2},{1,3},{2,0},{3,1},{4,6},{5,7},{6,4},{7,5},{8,10},{9,11},{10,... | collective-permute-start | bytes 417800 | tf_op jit(solution)/shard_map/ppermute | solution.py:99
  83.6 8.4 %collective-permute-start.25 = (f32[272,128]{1,0:T(8,128)S(1)}, f32[272,128]{1,0:T(8,128)S(1)}, u32[]{:S(2)}, u32[]{:S(2)}) collective-permute-start(f32[272,128]{1,0:T(8,128)S(1)} %get-tuple-element.91), channel_id=1, source_target_pairs={{0,4},{1,5},{2,6},{3,7},{4,0},{5,1},{6,2},{7,3},{8,12},{9,13},{10,... | collective-permute-start | bytes 417800 | tf_op jit(solution)/shard_map/ppermute | solution.py:99
  84.5 7.5 %collective-permute-start.26 = (f32[272,128]{1,0:T(8,128)S(1)}, f32[272,128]{1,0:T(8,128)S(1)}, u32[]{:S(2)}, u32[]{:S(2)}) collective-permute-start(f32[272,128]{1,0:T(8,128)S(1)} %get-tuple-element.92), channel_id=1, source_target_pairs={{0,6},{1,7},{2,4},{3,5},{4,2},{5,3},{6,0},{7,1},{8,14},{9,15},{10,... | collective-permute-start | bytes 417800 | tf_op jit(solution)/shard_map/ppermute | solution.py:99
  92.2 5.7 %collective-permute-start.29 = (bf16[272,128]{1,0:T(8,128)(2,1)S(1)}, bf16[272,128]{1,0:T(8,128)(2,1)S(1)}, u32[]{:S(2)}, u32[]{:S(2)}) collective-permute-start(bf16[272,128]{1,0:T(8,128)(2,1)S(1)} %get-tuple-element.94.refs_0_), channel_id=1, source_target_pairs={{0,6},{1,7},{2,4},{3,5},{4,2},{5,3},{6,0},{7,1},{8,14},{9,15},{10,... | collective-permute-start | bytes 208904 | tf_op jit(solution)/shard_map/ppermute | solution.py:99
  93.7 4.7 %collective-permute-start.28 = (bf16[272,128]{1,0:T(8,128)(2,1)S(1)}, bf16[272,128]{1,0:T(8,128)(2,1)S(1)}, u32[]{:S(2)}, u32[]{:S(2)}) collective-permute-start(bf16[272,128]{1,0:T(8,128)(2,1)S(1)} %get-tuple-element.94.refs_0_), channel_id=1, source_target_pairs={{0,4},{1,5},{2,6},{3,7},{4,0},{5,1},{6,2},{7,3},{8,12},{9,13},{10,... | collective-permute-start | bytes 208904 | tf_op jit(solution)/shard_map/ppermute | solution.py:99
  94.4 4.3 %collective-permute-start.27 = (bf16[272,128]{1,0:T(8,128)(2,1)S(1)}, bf16[272,128]{1,0:T(8,128)(2,1)S(1)}, u32[]{:S(2)}, u32[]{:S(2)}) collective-permute-start(bf16[272,128]{1,0:T(8,128)(2,1)S(1)} %get-tuple-element.94.refs_0_), channel_id=1, source_target_pairs={{0,2},{1,3},{2,0},{3,1},{4,6},{5,7},{6,4},{7,5},{8,10},{9,11},{10,... | collective-permute-start | bytes 208904 | tf_op jit(solution)/shard_map/ppermute | solution.py:99
  95.7 3.2 %collective-permute-start.30 = (bf16[272,128]{1,0:T(8,128)(2,1)S(1)}, bf16[272,128]{1,0:T(8,128)(2,1)S(1)}, u32[]{:S(2)}, u32[]{:S(2)}) collective-permute-start(bf16[272,128]{1,0:T(8,128)(2,1)S(1)} %get-tuple-element.94.refs_0_), channel_id=1, source_target_pairs={{0,1},{1,0},{2,3},{3,2},{4,5},{5,4},{6,7},{7,6},{8,9},{9,8},{10,11... | collective-permute-start | bytes 208904 | tf_op jit(solution)/shard_map/ppermute | solution.py:99
  97.8 1.3 collective-permute-start.33
  98.4 1.3 collective-permute-start.32
  98.7 1.3 collective-permute-start.31
  100.9 8.3 %collective-permute-start.34 = (f32[272,128]{1,0:T(8,128)S(1)}, f32[272,128]{1,0:T(8,128)S(1)}, u32[]{:S(2)}, u32[]{:S(2)}) collective-permute-start(f32[272,128]{1,0:T(8,128)S(1)} %get-tuple-element.97), channel_id=1, source_target_pairs={{0,8},{8,0},{16,24},{24,16},{1,9},{9,1},{17,25},{25,17},{2,10},{10... | collective-permute-start | bytes 417800 | tf_op jit(solution)/shard_map/ppermute | solution.py:96
  101.3 13.4 %collective-permute-start.35 = (f32[272,128]{1,0:T(8,128)S(1)}, f32[272,128]{1,0:T(8,128)S(1)}, u32[]{:S(2)}, u32[]{:S(2)}) collective-permute-start(f32[272,128]{1,0:T(8,128)S(1)} %get-tuple-element.98), channel_id=1, source_target_pairs={{0,16},{8,24},{16,0},{24,8},{1,17},{9,25},{17,1},{25,9},{2,18},{10... | collective-permute-start | bytes 417800 | tf_op jit(solution)/shard_map/ppermute | solution.py:96
  104.2 10.6 %collective-permute-start.36 = (f32[272,128]{1,0:T(8,128)S(1)}, f32[272,128]{1,0:T(8,128)S(1)}, u32[]{:S(2)}, u32[]{:S(2)}) collective-permute-start(f32[272,128]{1,0:T(8,128)S(1)} %get-tuple-element.99), channel_id=1, source_target_pairs={{0,24},{8,16},{16,8},{24,0},{1,25},{9,17},{17,9},{25,1},{2,26},{10... | collective-permute-start | bytes 417800 | tf_op jit(solution)/shard_map/ppermute | solution.py:96
  114.9 6.4 %collective-permute-start.39 = (bf16[272,128]{1,0:T(8,128)(2,1)S(1)}, bf16[272,128]{1,0:T(8,128)(2,1)S(1)}, u32[]{:S(2)}, u32[]{:S(2)}) collective-permute-start(bf16[272,128]{1,0:T(8,128)(2,1)S(1)} %get-tuple-element.105.refs_0_), channel_id=1, source_target_pairs={{0,24},{8,16},{16,8},{24,0},{1,25},{9,17},{17,9},{25,1},{2,26},{10... | collective-permute-start | bytes 208904 | tf_op jit(solution)/shard_map/ppermute | solution.py:96
  117.3 6.9 %collective-permute-start.38 = (bf16[272,128]{1,0:T(8,128)(2,1)S(1)}, bf16[272,128]{1,0:T(8,128)(2,1)S(1)}, u32[]{:S(2)}, u32[]{:S(2)}) collective-permute-start(bf16[272,128]{1,0:T(8,128)(2,1)S(1)} %get-tuple-element.105.refs_0_), channel_id=1, source_target_pairs={{0,16},{8,24},{16,0},{24,8},{1,17},{9,25},{17,1},{25,9},{2,18},{10... | collective-permute-start | bytes 208904 | tf_op jit(solution)/shard_map/ppermute | solution.py:96
  119.1 5.1 %collective-permute-start.37 = (bf16[272,128]{1,0:T(8,128)(2,1)S(1)}, bf16[272,128]{1,0:T(8,128)(2,1)S(1)}, u32[]{:S(2)}, u32[]{:S(2)}) collective-permute-start(bf16[272,128]{1,0:T(8,128)(2,1)S(1)} %get-tuple-element.105.refs_0_), channel_id=1, source_target_pairs={{0,8},{8,0},{16,24},{24,16},{1,9},{9,1},{17,25},{25,17},{2,10},{10... | collective-permute-start | bytes 208904 | tf_op jit(solution)/shard_map/ppermute | solution.py:96
  125.5 2.0 %collective-permute-start.40 = (f32[1040,128]{1,0:T(8,128)S(1)}, f32[1040,128]{1,0:T(8,128)S(1)}, u32[]{:S(2)}, u32[]{:S(2)}) collective-permute-start(f32[1040,128]{1,0:T(8,128)S(1)} %get-tuple-element.108), channel_id=1, source_target_pairs={{0,1},{1,0},{2,3},{3,2},{4,5},{5,4},{6,7},{7,6},{8,9},{9,8},{10,11... | collective-permute-start | bytes 1597448 | tf_op jit(solution)/shard_map/ppermute | solution.py:99
  127.6 6.6 %collective-permute-start.41 = (f32[272,128]{1,0:T(8,128)S(1)}, f32[272,128]{1,0:T(8,128)S(1)}, u32[]{:S(2)}, u32[]{:S(2)}) collective-permute-start(f32[272,128]{1,0:T(8,128)S(1)} %get-tuple-element.111), channel_id=1, source_target_pairs={{0,2},{1,3},{2,0},{3,1},{4,6},{5,7},{6,4},{7,5},{8,10},{9,11},{10,... | collective-permute-start | bytes 417800 | tf_op jit(solution)/shard_map/ppermute | solution.py:99
  128.7 8.4 %collective-permute-start.42 = (f32[272,128]{1,0:T(8,128)S(1)}, f32[272,128]{1,0:T(8,128)S(1)}, u32[]{:S(2)}, u32[]{:S(2)}) collective-permute-start(f32[272,128]{1,0:T(8,128)S(1)} %get-tuple-element.112), channel_id=1, source_target_pairs={{0,4},{1,5},{2,6},{3,7},{4,0},{5,1},{6,2},{7,3},{8,12},{9,13},{10,... | collective-permute-start | bytes 417800 | tf_op jit(solution)/shard_map/ppermute | solution.py:99
  129.6 7.5 %collective-permute-start.43 = (f32[272,128]{1,0:T(8,128)S(1)}, f32[272,128]{1,0:T(8,128)S(1)}, u32[]{:S(2)}, u32[]{:S(2)}) collective-permute-start(f32[272,128]{1,0:T(8,128)S(1)} %get-tuple-element.113), channel_id=1, source_target_pairs={{0,6},{1,7},{2,4},{3,5},{4,2},{5,3},{6,0},{7,1},{8,14},{9,15},{10,... | collective-permute-start | bytes 417800 | tf_op jit(solution)/shard_map/ppermute | solution.py:99
  137.8 10.2 %collective-permute-start.46 = (f32[272,128]{1,0:T(8,128)S(1)}, f32[272,128]{1,0:T(8,128)S(1)}, u32[]{:S(2)}, u32[]{:S(2)}) collective-permute-start(f32[272,128]{1,0:T(8,128)S(1)} %get-tuple-element.115.refs_0_.refs_4_), channel_id=1, source_target_pairs={{0,6},{1,7},{2,4},{3,5},{4,2},{5,3},{6,0},{7,1},{8,14},{9,15},{10,... | collective-permute-start | bytes 417800 | tf_op jit(solution)/shard_map/ppermute | solution.py:99
  139.3 10.3 %collective-permute-start.45 = (f32[272,128]{1,0:T(8,128)S(1)}, f32[272,128]{1,0:T(8,128)S(1)}, u32[]{:S(2)}, u32[]{:S(2)}) collective-permute-start(f32[272,128]{1,0:T(8,128)S(1)} %get-tuple-element.115.refs_0_.refs_4_), channel_id=1, source_target_pairs={{0,4},{1,5},{2,6},{3,7},{4,0},{5,1},{6,2},{7,3},{8,12},{9,13},{10,... | collective-permute-start | bytes 417800 | tf_op jit(solution)/shard_map/ppermute | solution.py:99
  140.3 7.8 %collective-permute-start.56 = (f32[256,128]{1,0:T(8,128)S(1)}, f32[256,128]{1,0:T(8,128)S(1)}, u32[]{:S(2)}, u32[]{:S(2)}) collective-permute-start(f32[256,128]{1,0:T(8,128)S(1)} %get-tuple-element.116.refs_12_), channel_id=1, source_target_pairs={{0,6},{1,7},{2,4},{3,5},{4,2},{5,3},{6,0},{7,1},{8,14},{9,15},{10,... | collective-permute-start | bytes 393224 | tf_op jit(solution)/shard_map/ppermute | solution.py:99
  141.7 10.3 %collective-permute-start.55 = (f32[256,128]{1,0:T(8,128)S(1)}, f32[256,128]{1,0:T(8,128)S(1)}, u32[]{:S(2)}, u32[]{:S(2)}) collective-permute-start(f32[256,128]{1,0:T(8,128)S(1)} %get-tuple-element.116.refs_12_), channel_id=1, source_target_pairs={{0,4},{1,5},{2,6},{3,7},{4,0},{5,1},{6,2},{7,3},{8,12},{9,13},{10,... | collective-permute-start | bytes 393224 | tf_op jit(solution)/shard_map/ppermute | solution.py:99
  142.8 10.1 %collective-permute-start.44 = (f32[272,128]{1,0:T(8,128)S(1)}, f32[272,128]{1,0:T(8,128)S(1)}, u32[]{:S(2)}, u32[]{:S(2)}) collective-permute-start(f32[272,128]{1,0:T(8,128)S(1)} %get-tuple-element.115.refs_0_.refs_4_), channel_id=1, source_target_pairs={{0,2},{1,3},{2,0},{3,1},{4,6},{5,7},{6,4},{7,5},{8,10},{9,11},{10,... | collective-permute-start | bytes 417800 | tf_op jit(solution)/shard_map/ppermute | solution.py:99
  148.0 9.0 %collective-permute-start.47 = (f32[272,128]{1,0:T(8,128)S(1)}, f32[272,128]{1,0:T(8,128)S(1)}, u32[]{:S(2)}, u32[]{:S(2)}) collective-permute-start(f32[272,128]{1,0:T(8,128)S(1)} %get-tuple-element.115.refs_0_.refs_4_), channel_id=1, source_target_pairs={{0,1},{1,0},{2,3},{3,2},{4,5},{5,4},{6,7},{7,6},{8,9},{9,8},{10,11... | collective-permute-start | bytes 417800 | tf_op jit(solution)/shard_map/ppermute | solution.py:99
  148.1 9.5 %collective-permute-start.50 = (f32[272,128]{1,0:T(8,128)S(1)}, f32[272,128]{1,0:T(8,128)S(1)}, u32[]{:S(2)}, u32[]{:S(2)}) collective-permute-start(f32[272,128]{1,0:T(8,128)S(1)} %collective-permute-done.46.refs_3_.refs_7_), channel_id=1, source_target_pairs={{0,1},{1,0},{2,3},{3,2},{4,5},{5,4},{6,7},{7,6},{8,9},{9,8},{10,11... | collective-permute-start | bytes 417800 | tf_op jit(solution)/shard_map/ppermute | solution.py:99
  149.6 8.0 %collective-permute-start.49 = (f32[272,128]{1,0:T(8,128)S(1)}, f32[272,128]{1,0:T(8,128)S(1)}, u32[]{:S(2)}, u32[]{:S(2)}) collective-permute-start(f32[272,128]{1,0:T(8,128)S(1)} %collective-permute-done.45.refs_2_.refs_6_), channel_id=1, source_target_pairs={{0,1},{1,0},{2,3},{3,2},{4,5},{5,4},{6,7},{7,6},{8,9},{9,8},{10,11... | collective-permute-start | bytes 417800 | tf_op jit(solution)/shard_map/ppermute | solution.py:99
  152.0 5.1 %collective-permute-start.54 = (f32[256,128]{1,0:T(8,128)S(1)}, f32[256,128]{1,0:T(8,128)S(1)}, u32[]{:S(2)}, u32[]{:S(2)}) collective-permute-start(f32[256,128]{1,0:T(8,128)S(1)} %get-tuple-element.116.refs_12_), channel_id=1, source_target_pairs={{0,2},{1,3},{2,0},{3,1},{4,6},{5,7},{6,4},{7,5},{8,10},{9,11},{10,... | collective-permute-start | bytes 393224 | tf_op jit(solution)/shard_map/ppermute | solution.py:99
  152.9 5.1 %collective-permute-start.48 = (f32[272,128]{1,0:T(8,128)S(1)}, f32[272,128]{1,0:T(8,128)S(1)}, u32[]{:S(2)}, u32[]{:S(2)}) collective-permute-start(f32[272,128]{1,0:T(8,128)S(1)} %collective-permute-done.44.refs_1_.refs_5_), channel_id=1, source_target_pairs={{0,1},{1,0},{2,3},{3,2},{4,5},{5,4},{6,7},{7,6},{8,9},{9,8},{10,11... | collective-permute-start | bytes 417800 | tf_op jit(solution)/shard_map/ppermute | solution.py:99
  157.0 3.6 %collective-permute-start.57 = (f32[256,128]{1,0:T(8,128)S(1)}, f32[256,128]{1,0:T(8,128)S(1)}, u32[]{:S(2)}, u32[]{:S(2)}) collective-permute-start(f32[256,128]{1,0:T(8,128)S(1)} %get-tuple-element.116.refs_12_), channel_id=1, source_target_pairs={{0,1},{1,0},{2,3},{3,2},{4,5},{5,4},{6,7},{7,6},{8,9},{9,8},{10,11... | collective-permute-start | bytes 393224 | tf_op jit(solution)/shard_map/ppermute | solution.py:99
  157.0 3.6 %collective-permute-start.60 = (f32[256,128]{1,0:T(8,128)S(1)}, f32[256,128]{1,0:T(8,128)S(1)}, u32[]{:S(2)}, u32[]{:S(2)}) collective-permute-start(f32[256,128]{1,0:T(8,128)S(1)} %collective-permute-done.56.refs_15_), channel_id=1, source_target_pairs={{0,1},{1,0},{2,3},{3,2},{4,5},{5,4},{6,7},{7,6},{8,9},{9,8},{10,11... | collective-permute-start | bytes 393224 | tf_op jit(solution)/shard_map/ppermute | solution.py:99
  157.6 5.0 %collective-permute-start.59 = (f32[256,128]{1,0:T(8,128)S(1)}, f32[256,128]{1,0:T(8,128)S(1)}, u32[]{:S(2)}, u32[]{:S(2)}) collective-permute-start(f32[256,128]{1,0:T(8,128)S(1)} %collective-permute-done.55.refs_14_), channel_id=1, source_target_pairs={{0,1},{1,0},{2,3},{3,2},{4,5},{5,4},{6,7},{7,6},{8,9},{9,8},{10,11... | collective-permute-start | bytes 393224 | tf_op jit(solution)/shard_map/ppermute | solution.py:99
  157.6 4.9 %collective-permute-start.58 = (f32[256,128]{1,0:T(8,128)S(1)}, f32[256,128]{1,0:T(8,128)S(1)}, u32[]{:S(2)}, u32[]{:S(2)}) collective-permute-start(f32[256,128]{1,0:T(8,128)S(1)} %collective-permute-done.54.refs_13_), channel_id=1, source_target_pairs={{0,1},{1,0},{2,3},{3,2},{4,5},{5,4},{6,7},{7,6},{8,9},{9,8},{10,11... | collective-permute-start | bytes 393224 | tf_op jit(solution)/shard_map/ppermute | solution.py:99
  158.1 5.5 %collective-permute-start.53 = (f32[8,128]{1,0:T(8,128)S(1)}, f32[8,128]{1,0:T(8,128)S(1)}, u32[]{:S(2)}, u32[]{:S(2)}) collective-permute-start(f32[8,128]{1,0:T(8,128)S(1)} %shard_map.65.refs_0_), channel_id=1, source_target_pairs={{0,24},{8,16},{16,8},{24,0},{1,25},{9,17},{17,9},{25,1},{2,26},{10... | collective-permute-start | bytes 12296 | tf_op jit(solution)/shard_map/ppermute | solution.py:96
  160.6 4.5 %collective-permute-start.52 = (f32[8,128]{1,0:T(8,128)S(1)}, f32[8,128]{1,0:T(8,128)S(1)}, u32[]{:S(2)}, u32[]{:S(2)}) collective-permute-start(f32[8,128]{1,0:T(8,128)S(1)} %shard_map.65.refs_0_), channel_id=1, source_target_pairs={{0,16},{8,24},{16,0},{24,8},{1,17},{9,25},{17,1},{25,9},{2,18},{10... | collective-permute-start | bytes 12296 | tf_op jit(solution)/shard_map/ppermute | solution.py:96
  160.6 4.5 %collective-permute-start.51 = (f32[8,128]{1,0:T(8,128)S(1)}, f32[8,128]{1,0:T(8,128)S(1)}, u32[]{:S(2)}, u32[]{:S(2)}) collective-permute-start(f32[8,128]{1,0:T(8,128)S(1)} %shard_map.65.refs_0_), channel_id=1, source_target_pairs={{0,8},{8,0},{16,24},{24,16},{1,9},{9,1},{17,25},{25,17},{2,10},{10... | collective-permute-start | bytes 12296 | tf_op jit(solution)/shard_map/ppermute | solution.py:96
  (3 other events, 5.6 us)

commit v2 on v1

v2 whole, which is shorter than its diff:
```python
import jax
import jax.numpy as jnp
from jax import lax
from jax.experimental import pallas as pl
from jax.experimental.pallas import tpu as pltpu
from jax.sharding import PartitionSpec as P

ITERS = 3
PAD = 16
F32 = jnp.float32
BF16 = jnp.bfloat16
ROW_WIRE = (F32, F32, BF16)
CORE_WIRE = (F32, F32, F32)
CHIP_WIRE = ((BF16, BF16), (BF16, BF16), (BF16, BF16))
LIMIT = 24 * 1024 * 1024


def tree_sum(terms):
    terms = list(terms)
    while len(terms) > 1:
        terms = [terms[i] + terms[i + 1] for i in range(0, len(terms), 2)]
    return terms[0]


def put_rows(ref, *values):
    rows = ref.shape[0] - PAD
    parts = []
    for value in values:
        high = value.astype(BF16).astype(F32)
        middle = (value - high).astype(BF16).astype(F32)
        parts += [high, middle, value - high - middle]
    shape = (PAD, ref.shape[1])
    index = lax.broadcasted_iota(jnp.int32, shape, 0)
    block = jnp.zeros(shape, F32)
    for place, part in enumerate(parts):
        block = jnp.where(index == place, jnp.broadcast_to(part, shape), block)
    ref[pl.ds(rows, PAD), :] = block.astype(ref.dtype)


def get_row(ref, which=0):
    rows = ref.shape[0] - PAD
    tail = ref[pl.ds(rows, PAD), :].astype(F32)
    at = 3 * which
    return tail[at : at + 1] + tail[at + 1 : at + 2] + tail[at + 2 : at + 3]


def body_of(ref):
    return ref[pl.ds(0, ref.shape[0] - PAD), :]


def column_sum(values):
    return jnp.sum(values, axis=0, keepdims=True)


def spread(ref, value):
    ref[...] = jnp.broadcast_to(value, ref.shape)


def call(kernel, outs, operands, scratch=()):
    vmem = pl.BlockSpec(memory_space=pltpu.VMEM)
    return pl.pallas_call(
        kernel,
        out_shape=[jax.ShapeDtypeStruct(shape, dtype) for shape, dtype in outs],
        in_specs=[vmem] * len(operands),
        out_specs=[vmem] * len(outs),
        scratch_shapes=scratch,
        compiler_params=pltpu.CompilerParams(vmem_limit_bytes=LIMIT),
    )(*operands)


def shards(states, targets, ridge):
    n_row = lax.axis_size("row")
    n_group = lax.axis_size("group")
    levels = (n_group // 2).bit_length() - 1
    tokens, feats = states.shape
    outs = targets.shape[1]
    feat_share = feats // n_row
    half = tokens // 2
    piece = half // levels
    block = 256
    ridge = ridge.reshape(1, outs)
    scalar = ((8, outs), F32)
    feature_rows = ((feat_share, outs), F32)
    token_rows = ((half, outs), F32)

    def over_row(step, value):
        return lax.ppermute(value, "row", [(i, i ^ step) for i in range(n_row)])

    def over_group(step, value):
        return lax.ppermute(value, "group", [(i, i ^ step) for i in range(n_group)])

    def row_place(step):
        return pl.multiple_of((lax.axis_index("row") ^ step) * feat_share, feat_share)

    def token_place(core_step):
        core = (lax.axis_index("group") % 2) ^ core_step
        return pl.multiple_of(core * half, half)

    def backward(wire, *blocks):
        first = len(blocks) == 1
        wide = 2 * outs if first else outs

        def kernel(a_ref, *refs):
            ins = refs[: len(blocks)]
            own_ref, delta_ref, *msg_refs, vec, prod = refs[len(blocks) :]
            if first:
                whole = ins[0][...]
                high = whole.astype(BF16)
                vec[:, 0:outs] = high
                vec[:, outs:wide] = (whole - high.astype(F32)).astype(BF16)
                delta = jnp.zeros((1, outs), F32)
            else:
                for core_step, ref in enumerate(ins):
                    vec[pl.ds(token_place(core_step), half), :] = body_of(ref)
                delta = get_row(ins[0]) + get_row(ins[1])
            spread(delta_ref, delta)
            turned = vec[...].T
            for start in range(0, feats, block):
                part = jnp.dot(turned, a_ref[:, start : start + block], preferred_element_type=F32)
                if first:
                    part = part[0:outs] + part[outs:wide]
                prod[start : start + block, :] = part.T
            own_ref[...] = prod[pl.ds(row_place(0), feat_share), :]
            for step, ref in enumerate(msg_refs, 1):
                ref[pl.ds(0, feat_share), :] = prod[pl.ds(row_place(step), feat_share), :].astype(wire)
                put_rows(ref, delta)

        msgs = [((feat_share + PAD, outs), wire)] * (n_row - 1)
        own, delta, *sends = call(
            kernel,
            [feature_rows, scalar] + msgs,
            (states,) + blocks,
            [pltpu.VMEM((tokens, wide), BF16), pltpu.VMEM((feats, outs), F32)],
        )
        return own, delta, [over_row(step, send) for step, send in enumerate(sends, 1)]

    def begin(own, got):
        def kernel(own_ref, *refs):
            ins, (grad_ref, msg_ref) = refs[: n_row - 1], refs[n_row - 1 :]
            grad = own_ref[...]
            for ref in ins:
                grad = grad + body_of(ref).astype(F32)
            grad_ref[...] = grad
            msg_ref[pl.ds(0, feat_share), :] = grad.astype(BF16)
            put_rows(msg_ref, column_sum(grad * grad), jnp.zeros((1, outs), F32))

        return call(kernel, [feature_rows, ((feat_share + PAD, outs), BF16)], [own] + got)

    def advance(own, delta, got, gamma, dir_sq, grad, direction, image, weights, residual):
        def kernel(own_ref, delta_ref, *refs):
            ins = refs[: n_row - 1]
            gamma_ref, sq_ref, grad_ref, dir_ref, image_ref, w_ref, r_ref, ridge_ref = refs[n_row - 1 : n_row + 7]
            w_out, r_out, grad_out, msg_ref = refs[n_row + 7 :]
            image_sq = tree_sum([delta_ref[0:1, :]] + [get_row(ref) for ref in ins])
            alpha = gamma_ref[0:1, :] / (image_sq + ridge_ref[...] * sq_ref[0:1, :])
            prod = own_ref[...]
            for ref in ins:
                prod = prod + body_of(ref).astype(F32)
            old_dir = dir_ref[...]
            new = grad_ref[...] - alpha * (prod + ridge_ref[...] * old_dir)
            msg_ref[pl.ds(0, feat_share), :] = new.astype(BF16)
            put_rows(msg_ref, column_sum(new * new), column_sum(new * old_dir))
            grad_out[...] = new
            w_out[...] = w_ref[...] + alpha * old_dir
            r_out[...] = r_ref[...] - alpha * image_ref[...]

        return call(
            kernel,
            [feature_rows, token_rows, feature_rows, ((feat_share + PAD, outs), BF16)],
            [own, delta, *got, gamma, dir_sq, grad, direction, image, weights, residual, ridge],
        )

    def forward(wire, msg):
        blocks = [msg] + [over_row(step, msg) for step in range(1, n_row)]

        def kernel(a_ref, *refs):
            ins = refs[:n_row]
            own_ref, gamma_ref, cross_ref, peer_ref, vec = refs[n_row:]
            for step, ref in enumerate(ins):
                vec[pl.ds(row_place(step), feat_share), :] = body_of(ref)
            gamma = tree_sum([get_row(ref, 0) for ref in ins])
            cross = tree_sum([get_row(ref, 1) for ref in ins])
            spread(gamma_ref, gamma)
            spread(cross_ref, cross)
            for core_step, ref in ((1, peer_ref), (0, own_ref)):
                for start in range(0, half, block):
                    part = jnp.dot(
                        a_ref[pl.ds(pl.multiple_of(token_place(core_step) + start, block), block), :],
                        vec[...],
                        preferred_element_type=F32,
                    )
                    ref[start : start + block, :] = part.astype(ref.dtype)
            put_rows(peer_ref, gamma, cross)

        own, gamma, cross, peer = call(
            kernel,
            [token_rows, scalar, scalar, ((half + PAD, outs), wire)],
            [states] + blocks,
            [pltpu.VMEM((feats, outs), BF16)],
        )
        return own, gamma, cross, over_group(1, peer)

    def pieces(wire):
        return [((piece + (0 if index else PAD), outs), wire) for index in range(levels)]

    def swapped(step, sends):
        return [
            over_group(2 << ((index + step) % levels), send) for index, send in enumerate(sends)
        ]

    def join_cores(wire, own, gamma, cross, got):
        def kernel(own_ref, gamma_ref, cross_ref, got_ref, *msg_refs):
            for index, ref in enumerate(msg_refs):
                place = pl.ds(index * piece, piece)
                both = own_ref[place, :] + got_ref[place, :].astype(F32)
                ref[pl.ds(0, piece), :] = both.astype(wire)
            put_rows(
                msg_refs[0],
                gamma_ref[0:1, :] + get_row(got_ref, 0),
                cross_ref[0:1, :] + get_row(got_ref, 1),
            )

        return call(kernel, pieces(wire), [own, gamma, cross, got])

    def join_chips(wire, sent, got):
        def kernel(*refs):
            mine, theirs, out_refs = refs[:levels], refs[levels : 2 * levels], refs[2 * levels :]
            for ref, own_ref, got_ref in zip(out_refs, mine, theirs):
                place = pl.ds(0, piece)
                both = own_ref[place, :].astype(F32) + got_ref[place, :].astype(F32)
                ref[place, :] = both.astype(wire)
            put_rows(out_refs[0], *[get_row(mine[0], k) + get_row(theirs[0], k) for k in range(2)])

        return call(kernel, pieces(wire), list(sent) + got)

    def image_of(wire, sent, got, grad, before):
        def kernel(*refs):
            mine, theirs = refs[:levels], refs[levels : 2 * levels]
            grad_ref, *rest = refs[2 * levels :]
            gamma_out, sq_out, dir_out, image_out, msg_ref, part_out = rest[-6:]
            gamma, cross = [get_row(mine[0], k) + get_row(theirs[0], k) for k in range(2)]
            spread(gamma_out, gamma)
            direction = grad_ref[...]
            dir_sq = gamma
            if before:
                old_gamma, old_sq, old_dir, old_image = rest[:4]
                beta = gamma / old_gamma[0:1, :]
                direction = direction + beta * old_dir[...]
                dir_sq = gamma + beta * (2.0 * cross + beta * old_sq[0:1, :])
            dir_out[...] = direction
            spread(sq_out, dir_sq)
            image_sq = jnp.zeros((1, outs), F32)
            for index, (own_ref, got_ref) in enumerate(zip(mine, theirs)):
                place = pl.ds(index * piece, piece)
                image = own_ref[pl.ds(0, piece), :].astype(F32) + got_ref[pl.ds(0, piece), :].astype(F32)
                if before:
                    image = image + beta * old_image[place, :]
                image_out[place, :] = image
                msg_ref[place, :] = image.astype(wire)
                image_sq = image_sq + column_sum(image * image)
            put_rows(msg_ref, image_sq)
            spread(part_out, image_sq)

        return call(
            kernel,
            [scalar, scalar, feature_rows, token_rows, ((half + PAD, outs), wire), scalar],
            list(sent) + got + [grad, *before],
        )

    core = lax.axis_index("group") % 2
    weights = jnp.zeros((feat_share, outs), F32)
    residual = lax.dynamic_slice_in_dim(targets, core * half, half, 0)
    own, _, got = backward(ROW_WIRE[0], targets)
    grad, msg = begin(own, got)
    before = ()
    for step in range(ITERS):
        own, gamma, cross, got = forward(CORE_WIRE[step], msg)
        sent = join_cores(CHIP_WIRE[step][0], own, gamma, cross, got)
        got = swapped(0, sent)
        for level in range(1, levels):
            sent = join_chips(CHIP_WIRE[step][1], sent, got)
            got = swapped(level, sent)
        last = step + 1 == ITERS
        gamma, dir_sq, direction, image, msg, part = image_of(
            F32 if last else BF16, sent, got, grad, before
        )
        if not last:
            own, delta, got = backward(ROW_WIRE[step + 1], msg, over_group(1, msg))
            weights, residual, grad, msg = advance(
                own, delta, got, gamma, dir_sq, grad, direction, image, weights, residual
            )
            before = (gamma, dir_sq, direction, image)

    def both_cores(own_ref, got_ref, out_ref):
        out_ref[...] = own_ref[...] + got_ref[...]

    (delta,) = call(both_cores, [scalar], [part, over_group(1, part)])
    other_image = over_group(1, image)
    other_residual = over_group(1, residual)
    deltas = [delta] + [over_row(step, delta) for step in range(1, n_row)]

    def finish(*refs):
        delta_refs, refs = refs[:n_row], refs[n_row:]
        gamma_ref, sq_ref, ridge_ref, image_ref, other_image_ref, r_ref, other_r_ref, dir_ref, w_ref, w_out, r_out = refs
        image_sq = tree_sum([ref[0:1, :] for ref in delta_refs])
        alpha = gamma_ref[0:1, :] / (image_sq + ridge_ref[...] * sq_ref[0:1, :])
        w_out[...] = w_ref[...] + alpha * dir_ref[...]
        r_out[pl.ds(token_place(0), half), :] = r_ref[...] - alpha * image_ref[...]
        r_out[pl.ds(token_place(1), half), :] = other_r_ref[...] - alpha * other_image_ref[...]

    weights, residual = call(
        finish,
        [feature_rows, ((tokens, outs), F32)],
        [*deltas, gamma, dir_sq, ridge, image, other_image, residual, other_residual, direction, weights],
    )
    return weights, residual


def solution(mesh):
    placed = (P("row", "group"), P("row", None), P())
    return jax.shard_map(
        shards,
        mesh=mesh,
        in_specs=placed,
        out_specs=(P(("group", "row"), None), P("row", None)),
        check_vma=False,
    )
```

time: 167 us -> 146 us (0.87)
  starting transfers between devices: 59 us -> 47.3 us
  waiting for transfers between devices: 90.2 us -> 79.6 us
  Pallas kernels: 9.78 us -> 12.3 us
    ppermute x40 -> x20, starting transfers between devices: 26.6 us -> 14.3 us  [over_group(): return lax.ppermute(value, 'group', [(i, i ^ step) for i in range(n_group)])]
    ppermute x40 -> x20, waiting for transfers between devices: 44.9 us -> 34.8 us  [over_group(): return lax.ppermute(value, 'group', [(i, i ^ step) for i in range(n_group)])]
    pallas_call x11 -> x20, Pallas kernels: 2.63 us -> 12.3 us  [call(): pl.pallas_call(kernel, out_shape=[jax.ShapeDtypeStruct(shape, dtype) for...]
    pallas_call x6 -> x0, Pallas kernels: 7.15 us -> none  [call_scratch(): pl.pallas_call(kernel, out_shape=[jax.ShapeDtypeStruct(shape, dtype) for...]
    unnamed x12 -> x14, local copies, waits for them, and re-layouts: 5.61 us -> 5.62 us
  transfers between devices with their start and end apart: 61 -> 41, of which waited for: 39 -> 24; matrix products, arithmetic and copies ran while one was open for 1% -> 0% of each run, Pallas kernels for 0% -> 1%
where the time goes in v2:
time: 146 us
  waiting for transfers between devices  79.6 us (55%)
  starting transfers between devices  47.3 us (32%)
  Pallas kernels  12.3 us (8%)
  local copies, waits for them, and re-layouts  5.66 us (4%)
    ppermute x21, waiting for transfers between devices, over_row(): return lax.ppermute(value, 'row', [(i, i ^ step) for i in range(n_row)])  44.8 us
    ppermute x20, waiting for transfers between devices, over_group(): return lax.ppermute(value, 'group', [(i, i ^ step) for i in range(n_group)])  34.8 us
    ppermute x21, starting transfers between devices, over_row(): return lax.ppermute(value, 'row', [(i, i ^ step) for i in range(n_row)])  33 us
    ppermute x20, starting transfers between devices, over_group(): return lax.ppermute(value, 'group', [(i, i ^ step) for i in range(n_group)])  14.3 us
    pallas_call x20, Pallas kernels, call(): pl.pallas_call(kernel, out_shape=[jax.ShapeDtypeStruct(shape, dtype) for...  12.3 us
    unnamed x14, local copies, waits for them, and re-layouts  5.62 us
  transfers between devices with their start and end apart: 41, of which 24 were waited for; matrix products, arithmetic and copies ran while one was open for 0% of the time, Pallas kernels for 1%

profile of v2, /device:TPU:0, one launch (start us, length us, event | category | flops | bytes accessed | tf_op | source)
XLA Modules:
  0.0 145.7 jit_solution(18347071666006556939)
XLA Ops:
  0.6 2.2 %copy-done = bf16[2048,1024]{1,0:T(8,128)(2,1)S(1)} copy-done((bf16[2048,1024]{1,0:T(8,128)(2,1)S(1)}, bf16[2048,1024]{1,0:T(8,128)(2,1)}, u32[]{:S(2)}) %copy-start) | copy-done | bytes 4194328
  2.8 1.2 copy-done.4
  4.0 1.9 %shard_map.50 = (f32[256,128]{1,0:T(8,128)S(1)}, f32[8,128]{1,0:T(8,128)}, f32[272,128]{1,0:T(8,128)S(1)}, f32[272,128]{1,0:T(8,128)S(1)}, f32[272,128]{1,0:T(8,128)S(1)}) custom-call(bf16[2048,1024]{1,0:T(8,128)(2,1)S(1)} %copy-done, f32[2048,128]{1,0:T(8,128)S(1)} %copy-done.4), custom_call_target="tpu_custom_call" | custom-call | tf_op jit(solution)/shard_map/pallas_call | solution.py:61
  6.0 3.0 %collective-permute-start = (f32[272,128]{1,0:T(8,128)S(1)}, f32[272,128]{1,0:T(8,128)S(1)}, u32[]{:S(2)}, u32[]{:S(2)}) collective-permute-start(f32[272,128]{1,0:T(8,128)S(1)} %get-tuple-element.66), channel_id=1, source_target_pairs={{0,8},{8,0},{16,24},{24,16},{1,9},{9,1},{17,25},{25,17},{2,10},{10... | collective-permute-start | bytes 417800 | tf_op jit(solution)/shard_map/ppermute | solution.py:87
  9.0 2.6 %collective-permute-start.1 = (f32[272,128]{1,0:T(8,128)S(1)}, f32[272,128]{1,0:T(8,128)S(1)}, u32[]{:S(2)}, u32[]{:S(2)}) collective-permute-start(f32[272,128]{1,0:T(8,128)S(1)} %get-tuple-element.67), channel_id=1, source_target_pairs={{0,16},{8,24},{16,0},{24,8},{1,17},{9,25},{17,1},{25,9},{2,18},{10... | collective-permute-start | bytes 417800 | tf_op jit(solution)/shard_map/ppermute | solution.py:87
  11.6 2.9 %collective-permute-done.refs_0_ = f32[272,128]{1,0:T(8,128)S(1)} collective-permute-done((f32[272,128]{1,0:T(8,128)S(1)}, f32[272,128]{1,0:T(8,128)S(1)}, u32[]{:S(2)}, u32[]{:S(2)}) %collective-permute-start) | collective-permute-done | bytes 139296 | tf_op jit(solution)/shard_map/ppermute | solution.py:87
  14.5 8.0 %collective-permute-done.1.refs_1_ = f32[272,128]{1,0:T(8,128)S(1)} collective-permute-done((f32[272,128]{1,0:T(8,128)S(1)}, f32[272,128]{1,0:T(8,128)S(1)}, u32[]{:S(2)}, u32[]{:S(2)}) %collective-permute-start.1) | collective-permute-done | bytes 139296 | tf_op jit(solution)/shard_map/ppermute | solution.py:87
  22.6 2.2 %collective-permute-start.3 = (bf16[272,128]{1,0:T(8,128)(2,1)S(1)}, bf16[272,128]{1,0:T(8,128)(2,1)S(1)}, u32[]{:S(2)}, u32[]{:S(2)}) collective-permute-start(bf16[272,128]{1,0:T(8,128)(2,1)S(1)} %get-tuple-element.69.refs_0_), channel_id=1, source_target_pairs={{0,8},{8,0},{16,24},{24,16},{1,9},{9,1},{17,25},{25,17},{2,10},{10... | collective-permute-start | bytes 208904 | tf_op jit(solution)/shard_map/ppermute | solution.py:87
  24.7 1.1 collective-permute-start.4
  25.8 1.4 collective-permute-start.5
  27.8 4.2 %collective-permute-done.4.refs_2_ = bf16[272,128]{1,0:T(8,128)(2,1)S(1)} collective-permute-done((bf16[272,128]{1,0:T(8,128)(2,1)S(1)}, bf16[272,128]{1,0:T(8,128)(2,1)S(1)}, u32[]{:S(2)}, u32[]{:S(2)}) %collective-permute-start.4) | collective-permute-done | bytes 69664 | tf_op jit(solution)/shard_map/ppermute | solution.py:87
  32.0 1.3 shard_map.52
  33.4 1.9 %collective-permute-done.6.got_ref = f32[1040,128]{1,0:T(8,128)S(1)} collective-permute-done((f32[1040,128]{1,0:T(8,128)S(1)}, f32[1040,128]{1,0:T(8,128)S(1)}, u32[]{:S(2)}, u32[]{:S(2)}) %collective-permute-start.6) | collective-permute-done | bytes 532512 | tf_op jit(solution)/shard_map/ppermute | solution.py:90
  35.4 1.5 %collective-permute-start.7 = (bf16[528,128]{1,0:T(8,128)(2,1)S(1)}, bf16[528,128]{1,0:T(8,128)(2,1)S(1)}, u32[]{:S(2)}, u32[]{:S(2)}) collective-permute-start(bf16[528,128]{1,0:T(8,128)(2,1)S(1)} %get-tuple-element.74.refs_0_), channel_id=1, source_target_pairs={{0,2},{1,3},{2,0},{3,1},{4,6},{5,7},{6,4},{7,5},{8,10},{9,11},{10,... | collective-permute-start | bytes 405512 | tf_op jit(solution)/shard_map/ppermute | solution.py:90
  37.0 1.5 %collective-permute-start.8 = (bf16[512,128]{1,0:T(8,128)(2,1)S(1)}, bf16[512,128]{1,0:T(8,128)(2,1)S(1)}, u32[]{:S(2)}, u32[]{:S(2)}) collective-permute-start(bf16[512,128]{1,0:T(8,128)(2,1)S(1)} %get-tuple-element.75.refs_1_), channel_id=1, source_target_pairs={{0,4},{1,5},{2,6},{3,7},{4,0},{5,1},{6,2},{7,3},{8,12},{9,13},{10,... | collective-permute-start | bytes 393224 | tf_op jit(solution)/shard_map/ppermute | solution.py:90
  38.5 3.7 %collective-permute-done.8.refs_3_ = bf16[512,128]{1,0:T(8,128)(2,1)S(1)} collective-permute-done((bf16[512,128]{1,0:T(8,128)(2,1)S(1)}, bf16[512,128]{1,0:T(8,128)(2,1)S(1)}, u32[]{:S(2)}, u32[]{:S(2)}) %collective-permute-start.8) | collective-permute-done | bytes 131104 | tf_op jit(solution)/shard_map/ppermute | solution.py:90
  42.3 1.6 %collective-permute-start.9 = (bf16[528,128]{1,0:T(8,128)(2,1)S(1)}, bf16[528,128]{1,0:T(8,128)(2,1)S(1)}, u32[]{:S(2)}, u32[]{:S(2)}) collective-permute-start(bf16[528,128]{1,0:T(8,128)(2,1)S(1)} %get-tuple-element.76.refs_0_), channel_id=1, source_target_pairs={{0,4},{1,5},{2,6},{3,7},{4,0},{5,1},{6,2},{7,3},{8,12},{9,13},{10,... | collective-permute-start | bytes 405512 | tf_op jit(solution)/shard_map/ppermute | solution.py:90
  44.4 4.4 %collective-permute-done.10.refs_3_ = bf16[512,128]{1,0:T(8,128)(2,1)S(1)} collective-permute-done((bf16[512,128]{1,0:T(8,128)(2,1)S(1)}, bf16[512,128]{1,0:T(8,128)(2,1)S(1)}, u32[]{:S(2)}, u32[]{:S(2)}) %collective-permute-start.10) | collective-permute-done | bytes 131104 | tf_op jit(solution)/shard_map/ppermute | solution.py:90
  48.9 0.8 shard_map.55
  49.6 1.5 %collective-permute-done.11.refs_1_ = bf16[1040,128]{1,0:T(8,128)(2,1)S(1)} collective-permute-done((bf16[1040,128]{1,0:T(8,128)(2,1)S(1)}, bf16[1040,128]{1,0:T(8,128)(2,1)S(1)}, u32[]{:S(2)}, u32[]{:S(2)}) %collective-permute-start.11) | collective-permute-done | bytes 266272 | tf_op jit(solution)/shard_map/ppermute | solution.py:90
  51.2 0.9 shard_map.56
  52.1 1.4 collective-permute-start.12
  53.5 1.6 %collective-permute-start.13 = (f32[272,128]{1,0:T(8,128)S(1)}, f32[272,128]{1,0:T(8,128)S(1)}, u32[]{:S(2)}, u32[]{:S(2)}) collective-permute-start(f32[272,128]{1,0:T(8,128)S(1)} %get-tuple-element.83), channel_id=1, source_target_pairs={{0,16},{8,24},{16,0},{24,8},{1,17},{9,25},{17,1},{25,9},{2,18},{10... | collective-permute-start | bytes 417800 | tf_op jit(solution)/shard_map/ppermute | solution.py:87
  55.1 1.5 %collective-permute-start.14 = (f32[272,128]{1,0:T(8,128)S(1)}, f32[272,128]{1,0:T(8,128)S(1)}, u32[]{:S(2)}, u32[]{:S(2)}) collective-permute-start(f32[272,128]{1,0:T(8,128)S(1)} %get-tuple-element.84), channel_id=1, source_target_pairs={{0,24},{8,16},{16,8},{24,0},{1,25},{9,17},{17,9},{25,1},{2,26},{10... | collective-permute-start | bytes 417800 | tf_op jit(solution)/shard_map/ppermute | solution.py:87
  56.6 3.5 %collective-permute-done.12.refs_0_ = f32[272,128]{1,0:T(8,128)S(1)} collective-permute-done((f32[272,128]{1,0:T(8,128)S(1)}, f32[272,128]{1,0:T(8,128)S(1)}, u32[]{:S(2)}, u32[]{:S(2)}) %collective-permute-start.12) | collective-permute-done | bytes 139296 | tf_op jit(solution)/shard_map/ppermute | solution.py:87
  60.1 6.8 %collective-permute-done.13.refs_1_ = f32[272,128]{1,0:T(8,128)S(1)} collective-permute-done((f32[272,128]{1,0:T(8,128)S(1)}, f32[272,128]{1,0:T(8,128)S(1)}, u32[]{:S(2)}, u32[]{:S(2)}) %collective-permute-start.13) | collective-permute-done | bytes 139296 | tf_op jit(solution)/shard_map/ppermute | solution.py:87
  67.1 2.5 %collective-permute-start.15 = (bf16[272,128]{1,0:T(8,128)(2,1)S(1)}, bf16[272,128]{1,0:T(8,128)(2,1)S(1)}, u32[]{:S(2)}, u32[]{:S(2)}) collective-permute-start(bf16[272,128]{1,0:T(8,128)(2,1)S(1)} %get-tuple-element.89.refs_0_), channel_id=1, source_target_pairs={{0,8},{8,0},{16,24},{24,16},{1,9},{9,1},{17,25},{25,17},{2,10},{10... | collective-permute-start | bytes 208904 | tf_op jit(solution)/shard_map/ppermute | solution.py:87
  69.7 0.9 collective-permute-start.16
  70.6 1.5 %collective-permute-start.17 = (bf16[272,128]{1,0:T(8,128)(2,1)S(1)}, bf16[272,128]{1,0:T(8,128)(2,1)S(1)}, u32[]{:S(2)}, u32[]{:S(2)}) collective-permute-start(bf16[272,128]{1,0:T(8,128)(2,1)S(1)} %get-tuple-element.89.refs_0_), channel_id=1, source_target_pairs={{0,24},{8,16},{16,8},{24,0},{1,25},{9,17},{17,9},{25,1},{2,26},{10... | collective-permute-start | bytes 208904 | tf_op jit(solution)/shard_map/ppermute | solution.py:87
  72.1 5.0 %collective-permute-done.16.refs_2_ = bf16[272,128]{1,0:T(8,128)(2,1)S(1)} collective-permute-done((bf16[272,128]{1,0:T(8,128)(2,1)S(1)}, bf16[272,128]{1,0:T(8,128)(2,1)S(1)}, u32[]{:S(2)}, u32[]{:S(2)}) %collective-permute-start.16) | collective-permute-done | bytes 69664 | tf_op jit(solution)/shard_map/ppermute | solution.py:87
  77.1 2.2 %copy-done.2 = bf16[2048,1024]{1,0:T(8,128)(2,1)S(1)} copy-done((bf16[2048,1024]{1,0:T(8,128)(2,1)S(1)}, bf16[2048,1024]{1,0:T(8,128)(2,1)}, u32[]{:S(2)}) %copy-start.2) | copy-done | bytes 4194328
  79.3 1.3 shard_map.58
  80.7 1.9 %collective-permute-done.18.got_ref = f32[1040,128]{1,0:T(8,128)S(1)} collective-permute-done((f32[1040,128]{1,0:T(8,128)S(1)}, f32[1040,128]{1,0:T(8,128)S(1)}, u32[]{:S(2)}, u32[]{:S(2)}) %collective-permute-start.18) | collective-permute-done | bytes 532512 | tf_op jit(solution)/shard_map/ppermute | solution.py:90
  82.7 0.6 collective-permute-start.19
  83.8 4.7 %collective-permute-done.20.refs_3_ = bf16[512,128]{1,0:T(8,128)(2,1)S(1)} collective-permute-done((bf16[512,128]{1,0:T(8,128)(2,1)S(1)}, bf16[512,128]{1,0:T(8,128)(2,1)S(1)}, u32[]{:S(2)}, u32[]{:S(2)}) %collective-permute-start.20) | collective-permute-done | bytes 131104 | tf_op jit(solution)/shard_map/ppermute | solution.py:90
  88.6 0.6 collective-permute-start.21
  89.2 1.5 %collective-permute-start.22 = (bf16[512,128]{1,0:T(8,128)(2,1)S(1)}, bf16[512,128]{1,0:T(8,128)(2,1)S(1)}, u32[]{:S(2)}, u32[]{:S(2)}) collective-permute-start(bf16[512,128]{1,0:T(8,128)(2,1)S(1)} %get-tuple-element.97.refs_1_), channel_id=1, source_target_pairs={{0,2},{1,3},{2,0},{3,1},{4,6},{5,7},{6,4},{7,5},{8,10},{9,11},{10,... | collective-permute-start | bytes 393224 | tf_op jit(solution)/shard_map/ppermute | solution.py:90
  90.7 3.5 %collective-permute-done.22.refs_3_ = bf16[512,128]{1,0:T(8,128)(2,1)S(1)} collective-permute-done((bf16[512,128]{1,0:T(8,128)(2,1)S(1)}, bf16[512,128]{1,0:T(8,128)(2,1)S(1)}, u32[]{:S(2)}, u32[]{:S(2)}) %collective-permute-start.22) | collective-permute-done | bytes 131104 | tf_op jit(solution)/shard_map/ppermute | solution.py:90
  94.2 0.8 shard_map.61
  95.0 1.5 %collective-permute-done.23.refs_1_ = bf16[1040,128]{1,0:T(8,128)(2,1)S(1)} collective-permute-done((bf16[1040,128]{1,0:T(8,128)(2,1)S(1)}, bf16[1040,128]{1,0:T(8,128)(2,1)S(1)}, u32[]{:S(2)}, u32[]{:S(2)}) %collective-permute-start.23) | collective-permute-done | bytes 266272 | tf_op jit(solution)/shard_map/ppermute | solution.py:90
  96.6 0.9 shard_map.62
  97.5 1.4 collective-permute-start.24
  98.9 1.4 collective-permute-start.25
  100.3 1.6 %collective-permute-start.26 = (bf16[272,128]{1,0:T(8,128)(2,1)S(1)}, bf16[272,128]{1,0:T(8,128)(2,1)S(1)}, u32[]{:S(2)}, u32[]{:S(2)}) collective-permute-start(bf16[272,128]{1,0:T(8,128)(2,1)S(1)} %get-tuple-element.104), channel_id=1, source_target_pairs={{0,24},{8,16},{16,8},{24,0},{1,25},{9,17},{17,9},{25,1},{2,26},{10... | collective-permute-start | bytes 208904 | tf_op jit(solution)/shard_map/ppermute | solution.py:87
  102.0 5.4 %collective-permute-done.25.refs_1_ = bf16[272,128]{1,0:T(8,128)(2,1)S(1)} collective-permute-done((bf16[272,128]{1,0:T(8,128)(2,1)S(1)}, bf16[272,128]{1,0:T(8,128)(2,1)S(1)}, u32[]{:S(2)}, u32[]{:S(2)}) %collective-permute-start.25) | collective-permute-done | bytes 69664 | tf_op jit(solution)/shard_map/ppermute | solution.py:87
  107.5 1.4 collective-permute-start.27
  109.0 1.4 collective-permute-start.28
  110.4 1.6 %collective-permute-start.29 = (bf16[272,128]{1,0:T(8,128)(2,1)S(1)}, bf16[272,128]{1,0:T(8,128)(2,1)S(1)}, u32[]{:S(2)}, u32[]{:S(2)}) collective-permute-start(bf16[272,128]{1,0:T(8,128)(2,1)S(1)} %get-tuple-element.111.refs_0_), channel_id=1, source_target_pairs={{0,24},{8,16},{16,8},{24,0},{1,25},{9,17},{17,9},{25,1},{2,26},{10... | collective-permute-start | bytes 208904 | tf_op jit(solution)/shard_map/ppermute | solution.py:87
  112.3 4.6 %collective-permute-done.28.refs_2_ = bf16[272,128]{1,0:T(8,128)(2,1)S(1)} collective-permute-done((bf16[272,128]{1,0:T(8,128)(2,1)S(1)}, bf16[272,128]{1,0:T(8,128)(2,1)S(1)}, u32[]{:S(2)}, u32[]{:S(2)}) %collective-permute-start.28) | collective-permute-done | bytes 69664 | tf_op jit(solution)/shard_map/ppermute | solution.py:87
  116.9 1.3 shard_map.64
  118.2 1.9 %collective-permute-done.30.got_ref = f32[1040,128]{1,0:T(8,128)S(1)} collective-permute-done((f32[1040,128]{1,0:T(8,128)S(1)}, f32[1040,128]{1,0:T(8,128)S(1)}, u32[]{:S(2)}, u32[]{:S(2)}) %collective-permute-start.30) | collective-permute-done | bytes 532512 | tf_op jit(solution)/shard_map/ppermute | solution.py:90
  120.2 1.5 %collective-permute-start.31 = (bf16[528,128]{1,0:T(8,128)(2,1)S(1)}, bf16[528,128]{1,0:T(8,128)(2,1)S(1)}, u32[]{:S(2)}, u32[]{:S(2)}) collective-permute-start(bf16[528,128]{1,0:T(8,128)(2,1)S(1)} %get-tuple-element.116.refs_0_), channel_id=1, source_target_pairs={{0,2},{1,3},{2,0},{3,1},{4,6},{5,7},{6,4},{7,5},{8,10},{9,11},{10,... | collective-permute-start | bytes 405512 | tf_op jit(solution)/shard_map/ppermute | solution.py:90
  121.7 1.6 %collective-permute-start.32 = (bf16[512,128]{1,0:T(8,128)(2,1)S(1)}, bf16[512,128]{1,0:T(8,128)(2,1)S(1)}, u32[]{:S(2)}, u32[]{:S(2)}) collective-permute-start(bf16[512,128]{1,0:T(8,128)(2,1)S(1)} %get-tuple-element.117.refs_1_), channel_id=1, source_target_pairs={{0,4},{1,5},{2,6},{3,7},{4,0},{5,1},{6,2},{7,3},{8,12},{9,13},{10,... | collective-permute-start | bytes 393224 | tf_op jit(solution)/shard_map/ppermute | solution.py:90
  123.3 3.7 %collective-permute-done.32.refs_3_ = bf16[512,128]{1,0:T(8,128)(2,1)S(1)} collective-permute-done((bf16[512,128]{1,0:T(8,128)(2,1)S(1)}, bf16[512,128]{1,0:T(8,128)(2,1)S(1)}, u32[]{:S(2)}, u32[]{:S(2)}) %collective-permute-start.32) | collective-permute-done | bytes 131104 | tf_op jit(solution)/shard_map/ppermute | solution.py:90
  127.1 1.6 %collective-permute-start.33 = (bf16[528,128]{1,0:T(8,128)(2,1)S(1)}, bf16[528,128]{1,0:T(8,128)(2,1)S(1)}, u32[]{:S(2)}, u32[]{:S(2)}) collective-permute-start(bf16[528,128]{1,0:T(8,128)(2,1)S(1)} %get-tuple-element.118.refs_0_), channel_id=1, source_target_pairs={{0,4},{1,5},{2,6},{3,7},{4,0},{5,1},{6,2},{7,3},{8,12},{9,13},{10,... | collective-permute-start | bytes 405512 | tf_op jit(solution)/shard_map/ppermute | solution.py:90
  129.2 4.5 %collective-permute-done.34.refs_3_ = bf16[512,128]{1,0:T(8,128)(2,1)S(1)} collective-permute-done((bf16[512,128]{1,0:T(8,128)(2,1)S(1)}, bf16[512,128]{1,0:T(8,128)(2,1)S(1)}, u32[]{:S(2)}, u32[]{:S(2)}) %collective-permute-start.34) | collective-permute-done | bytes 131104 | tf_op jit(solution)/shard_map/ppermute | solution.py:90
  133.7 1.0 shard_map.67
  135.2 1.4 collective-permute-done.35.got_ref
  136.6 1.3 collective-permute-start.36
  137.9 1.2 collective-permute-start.37
  139.1 1.9 %collective-permute-start.38 = (f32[8,128]{1,0:T(8,128)S(1)}, f32[8,128]{1,0:T(8,128)S(1)}, u32[]{:S(2)}, u32[]{:S(2)}) collective-permute-start(f32[8,128]{1,0:T(8,128)S(1)} %shard_map.68.refs_0_), channel_id=1, source_target_pairs={{0,24},{8,16},{16,8},{24,0},{1,25},{9,17},{17,9},{25,1},{2,26},{10... | collective-permute-start | bytes 12296 | tf_op jit(solution)/shard_map/ppermute | solution.py:87
  141.0 1.4 collective-permute-done.37.refs_2_
  142.4 2.1 %collective-permute-done.38.refs_3_ = f32[8,128]{1,0:T(8,128)S(1)} collective-permute-done((f32[8,128]{1,0:T(8,128)S(1)}, f32[8,128]{1,0:T(8,128)S(1)}, u32[]{:S(2)}, u32[]{:S(2)}) %collective-permute-start.38) | collective-permute-done | bytes 4128 | tf_op jit(solution)/shard_map/ppermute | solution.py:87
  144.5 1.2 shard_map.69
  (54 shorter events, 4.2 us)
Async XLA Ops:
  0.6 2.2 %copy-start = (bf16[2048,1024]{1,0:T(8,128)(2,1)S(1)}, bf16[2048,1024]{1,0:T(8,128)(2,1)}, u32[]{:S(2)}) copy-start(bf16[2048,1024]{1,0:T(8,128)(2,1)} %a_ref.11) | copy-start | bytes 12582916
  2.8 1.2 copy-start.4
  4.0 28.0 %copy-start.1 = (bf16[2048,1024]{1,0:T(8,128)(2,1)S(1)}, bf16[2048,1024]{1,0:T(8,128)(2,1)}, u32[]{:S(2)}) copy-start(bf16[2048,1024]{1,0:T(8,128)(2,1)} %a_ref.11) | copy-start | bytes 12582916
  6.0 8.5 %collective-permute-start = (f32[272,128]{1,0:T(8,128)S(1)}, f32[272,128]{1,0:T(8,128)S(1)}, u32[]{:S(2)}, u32[]{:S(2)}) collective-permute-start(f32[272,128]{1,0:T(8,128)S(1)} %get-tuple-element.66), channel_id=1, source_target_pairs={{0,8},{8,0},{16,24},{24,16},{1,9},{9,1},{17,25},{25,17},{2,10},{10... | collective-permute-start | bytes 417800 | tf_op jit(solution)/shard_map/ppermute | solution.py:87
  9.0 13.5 %collective-permute-start.1 = (f32[272,128]{1,0:T(8,128)S(1)}, f32[272,128]{1,0:T(8,128)S(1)}, u32[]{:S(2)}, u32[]{:S(2)}) collective-permute-start(f32[272,128]{1,0:T(8,128)S(1)} %get-tuple-element.67), channel_id=1, source_target_pairs={{0,16},{8,24},{16,0},{24,8},{1,17},{9,25},{17,1},{25,9},{2,18},{10... | collective-permute-start | bytes 417800 | tf_op jit(solution)/shard_map/ppermute | solution.py:87
  11.6 10.9 %collective-permute-start.2 = (f32[272,128]{1,0:T(8,128)S(1)}, f32[272,128]{1,0:T(8,128)S(1)}, u32[]{:S(2)}, u32[]{:S(2)}) collective-permute-start(f32[272,128]{1,0:T(8,128)S(1)} %get-tuple-element.68), channel_id=1, source_target_pairs={{0,24},{8,16},{16,8},{24,0},{1,25},{9,17},{17,9},{25,1},{2,26},{10... | collective-permute-start | bytes 417800 | tf_op jit(solution)/shard_map/ppermute | solution.py:87
  22.6 5.2 %collective-permute-start.3 = (bf16[272,128]{1,0:T(8,128)(2,1)S(1)}, bf16[272,128]{1,0:T(8,128)(2,1)S(1)}, u32[]{:S(2)}, u32[]{:S(2)}) collective-permute-start(bf16[272,128]{1,0:T(8,128)(2,1)S(1)} %get-tuple-element.69.refs_0_), channel_id=1, source_target_pairs={{0,8},{8,0},{16,24},{24,16},{1,9},{9,1},{17,25},{25,17},{2,10},{10... | collective-permute-start | bytes 208904 | tf_op jit(solution)/shard_map/ppermute | solution.py:87
  24.7 7.3 %collective-permute-start.4 = (bf16[272,128]{1,0:T(8,128)(2,1)S(1)}, bf16[272,128]{1,0:T(8,128)(2,1)S(1)}, u32[]{:S(2)}, u32[]{:S(2)}) collective-permute-start(bf16[272,128]{1,0:T(8,128)(2,1)S(1)} %get-tuple-element.69.refs_0_), channel_id=1, source_target_pairs={{0,16},{8,24},{16,0},{24,8},{1,17},{9,25},{17,1},{25,9},{2,18},{10... | collective-permute-start | bytes 208904 | tf_op jit(solution)/shard_map/ppermute | solution.py:87
  25.8 6.2 %collective-permute-start.5 = (bf16[272,128]{1,0:T(8,128)(2,1)S(1)}, bf16[272,128]{1,0:T(8,128)(2,1)S(1)}, u32[]{:S(2)}, u32[]{:S(2)}) collective-permute-start(bf16[272,128]{1,0:T(8,128)(2,1)S(1)} %get-tuple-element.69.refs_0_), channel_id=1, source_target_pairs={{0,24},{8,16},{16,8},{24,0},{1,25},{9,17},{17,9},{25,1},{2,26},{10... | collective-permute-start | bytes 208904 | tf_op jit(solution)/shard_map/ppermute | solution.py:87
  33.3 23.3 %copy-start.5 = (f32[2048,128]{1,0:T(8,128)S(1)}, f32[2048,128]{1,0:T(8,128)}, u32[]{:S(2)}) copy-start(f32[2048,128]{1,0:T(8,128)} %refs_0_.1) | copy-start | bytes 3145732
  33.3 33.6 %copy-start.6 = (f32[128]{0:T(128)S(1)}, f32[128]{0:T(128)}, u32[]{:S(2)}) copy-start(f32[128]{0:T(128)} %param.5) | copy-start | bytes 1540
  33.3 2.0 %collective-permute-start.6 = (f32[1040,128]{1,0:T(8,128)S(1)}, f32[1040,128]{1,0:T(8,128)S(1)}, u32[]{:S(2)}, u32[]{:S(2)}) collective-permute-start(f32[1040,128]{1,0:T(8,128)S(1)} %get-tuple-element.73), channel_id=1, source_target_pairs={{0,1},{1,0},{2,3},{3,2},{4,5},{5,4},{6,7},{7,6},{8,9},{9,8},{10,11... | collective-permute-start | bytes 1597448 | tf_op jit(solution)/shard_map/ppermute | solution.py:90
  35.4 6.8 %collective-permute-start.7 = (bf16[528,128]{1,0:T(8,128)(2,1)S(1)}, bf16[528,128]{1,0:T(8,128)(2,1)S(1)}, u32[]{:S(2)}, u32[]{:S(2)}) collective-permute-start(bf16[528,128]{1,0:T(8,128)(2,1)S(1)} %get-tuple-element.74.refs_0_), channel_id=1, source_target_pairs={{0,2},{1,3},{2,0},{3,1},{4,6},{5,7},{6,4},{7,5},{8,10},{9,11},{10,... | collective-permute-start | bytes 405512 | tf_op jit(solution)/shard_map/ppermute | solution.py:90
  37.0 5.3 %collective-permute-start.8 = (bf16[512,128]{1,0:T(8,128)(2,1)S(1)}, bf16[512,128]{1,0:T(8,128)(2,1)S(1)}, u32[]{:S(2)}, u32[]{:S(2)}) collective-permute-start(bf16[512,128]{1,0:T(8,128)(2,1)S(1)} %get-tuple-element.75.refs_1_), channel_id=1, source_target_pairs={{0,4},{1,5},{2,6},{3,7},{4,0},{5,1},{6,2},{7,3},{8,12},{9,13},{10,... | collective-permute-start | bytes 393224 | tf_op jit(solution)/shard_map/ppermute | solution.py:90
  42.3 6.6 %collective-permute-start.9 = (bf16[528,128]{1,0:T(8,128)(2,1)S(1)}, bf16[528,128]{1,0:T(8,128)(2,1)S(1)}, u32[]{:S(2)}, u32[]{:S(2)}) collective-permute-start(bf16[528,128]{1,0:T(8,128)(2,1)S(1)} %get-tuple-element.76.refs_0_), channel_id=1, source_target_pairs={{0,4},{1,5},{2,6},{3,7},{4,0},{5,1},{6,2},{7,3},{8,12},{9,13},{10,... | collective-permute-start | bytes 405512 | tf_op jit(solution)/shard_map/ppermute | solution.py:90
  43.9 5.0 %collective-permute-start.10 = (bf16[512,128]{1,0:T(8,128)(2,1)S(1)}, bf16[512,128]{1,0:T(8,128)(2,1)S(1)}, u32[]{:S(2)}, u32[]{:S(2)}) collective-permute-start(bf16[512,128]{1,0:T(8,128)(2,1)S(1)} %get-tuple-element.77.refs_1_), channel_id=1, source_target_pairs={{0,2},{1,3},{2,0},{3,1},{4,6},{5,7},{6,4},{7,5},{8,10},{9,11},{10,... | collective-permute-start | bytes 393224 | tf_op jit(solution)/shard_map/ppermute | solution.py:90
  49.6 1.5 %collective-permute-start.11 = (bf16[1040,128]{1,0:T(8,128)(2,1)S(1)}, bf16[1040,128]{1,0:T(8,128)(2,1)S(1)}, u32[]{:S(2)}, u32[]{:S(2)}) collective-permute-start(bf16[1040,128]{1,0:T(8,128)(2,1)S(1)} %get-tuple-element.79.refs_0_), channel_id=1, source_target_pairs={{0,1},{1,0},{2,3},{3,2},{4,5},{5,4},{6,7},{7,6},{8,9},{9,8},{10,11... | collective-permute-start | bytes 798728 | tf_op jit(solution)/shard_map/ppermute | solution.py:90
  52.1 8.0 %collective-permute-start.12 = (f32[272,128]{1,0:T(8,128)S(1)}, f32[272,128]{1,0:T(8,128)S(1)}, u32[]{:S(2)}, u32[]{:S(2)}) collective-permute-start(f32[272,128]{1,0:T(8,128)S(1)} %get-tuple-element.82), channel_id=1, source_target_pairs={{0,8},{8,0},{16,24},{24,16},{1,9},{9,1},{17,25},{25,17},{2,10},{10... | collective-permute-start | bytes 417800 | tf_op jit(solution)/shard_map/ppermute | solution.py:87
  53.5 13.4 %collective-permute-start.13 = (f32[272,128]{1,0:T(8,128)S(1)}, f32[272,128]{1,0:T(8,128)S(1)}, u32[]{:S(2)}, u32[]{:S(2)}) collective-permute-start(f32[272,128]{1,0:T(8,128)S(1)} %get-tuple-element.83), channel_id=1, source_target_pairs={{0,16},{8,24},{16,0},{24,8},{1,17},{9,25},{17,1},{25,9},{2,18},{10... | collective-permute-start | bytes 417800 | tf_op jit(solution)/shard_map/ppermute | solution.py:87
  55.1 11.8 %collective-permute-start.14 = (f32[272,128]{1,0:T(8,128)S(1)}, f32[272,128]{1,0:T(8,128)S(1)}, u32[]{:S(2)}, u32[]{:S(2)}) collective-permute-start(f32[272,128]{1,0:T(8,128)S(1)} %get-tuple-element.84), channel_id=1, source_target_pairs={{0,24},{8,16},{16,8},{24,0},{1,25},{9,17},{17,9},{25,1},{2,26},{10... | collective-permute-start | bytes 417800 | tf_op jit(solution)/shard_map/ppermute | solution.py:87
  67.1 5.0 %collective-permute-start.15 = (bf16[272,128]{1,0:T(8,128)(2,1)S(1)}, bf16[272,128]{1,0:T(8,128)(2,1)S(1)}, u32[]{:S(2)}, u32[]{:S(2)}) collective-permute-start(bf16[272,128]{1,0:T(8,128)(2,1)S(1)} %get-tuple-element.89.refs_0_), channel_id=1, source_target_pairs={{0,8},{8,0},{16,24},{24,16},{1,9},{9,1},{17,25},{25,17},{2,10},{10... | collective-permute-start | bytes 208904 | tf_op jit(solution)/shard_map/ppermute | solution.py:87
  69.7 7.5 %collective-permute-start.16 = (bf16[272,128]{1,0:T(8,128)(2,1)S(1)}, bf16[272,128]{1,0:T(8,128)(2,1)S(1)}, u32[]{:S(2)}, u32[]{:S(2)}) collective-permute-start(bf16[272,128]{1,0:T(8,128)(2,1)S(1)} %get-tuple-element.89.refs_0_), channel_id=1, source_target_pairs={{0,16},{8,24},{16,0},{24,8},{1,17},{9,25},{17,1},{25,9},{2,18},{10... | collective-permute-start | bytes 208904 | tf_op jit(solution)/shard_map/ppermute | solution.py:87
  70.6 6.5 %collective-permute-start.17 = (bf16[272,128]{1,0:T(8,128)(2,1)S(1)}, bf16[272,128]{1,0:T(8,128)(2,1)S(1)}, u32[]{:S(2)}, u32[]{:S(2)}) collective-permute-start(bf16[272,128]{1,0:T(8,128)(2,1)S(1)} %get-tuple-element.89.refs_0_), channel_id=1, source_target_pairs={{0,24},{8,16},{16,8},{24,0},{1,25},{9,17},{17,9},{25,1},{2,26},{10... | collective-permute-start | bytes 208904 | tf_op jit(solution)/shard_map/ppermute | solution.py:87
  77.1 2.2 %copy-start.2 = (bf16[2048,1024]{1,0:T(8,128)(2,1)S(1)}, bf16[2048,1024]{1,0:T(8,128)(2,1)}, u32[]{:S(2)}) copy-start(bf16[2048,1024]{1,0:T(8,128)(2,1)} %a_ref.11) | copy-start | bytes 12582916
  79.3 17.2 %copy-start.3 = (bf16[2048,1024]{1,0:T(8,128)(2,1)S(1)}, bf16[2048,1024]{1,0:T(8,128)(2,1)}, u32[]{:S(2)}) copy-start(bf16[2048,1024]{1,0:T(8,128)(2,1)} %a_ref.11) | copy-start | bytes 12582916
  80.6 2.0 %collective-permute-start.18 = (f32[1040,128]{1,0:T(8,128)S(1)}, f32[1040,128]{1,0:T(8,128)S(1)}, u32[]{:S(2)}, u32[]{:S(2)}) collective-permute-start(f32[1040,128]{1,0:T(8,128)S(1)} %get-tuple-element.93), channel_id=1, source_target_pairs={{0,1},{1,0},{2,3},{3,2},{4,5},{5,4},{6,7},{7,6},{8,9},{9,8},{10,11... | collective-permute-start | bytes 1597448 | tf_op jit(solution)/shard_map/ppermute | solution.py:90
  82.7 5.8 %collective-permute-start.19 = (bf16[528,128]{1,0:T(8,128)(2,1)S(1)}, bf16[528,128]{1,0:T(8,128)(2,1)S(1)}, u32[]{:S(2)}, u32[]{:S(2)}) collective-permute-start(bf16[528,128]{1,0:T(8,128)(2,1)S(1)} %get-tuple-element.94.refs_0_), channel_id=1, source_target_pairs={{0,2},{1,3},{2,0},{3,1},{4,6},{5,7},{6,4},{7,5},{8,10},{9,11},{10,... | collective-permute-start | bytes 405512 | tf_op jit(solution)/shard_map/ppermute | solution.py:90
  83.3 5.3 %collective-permute-start.20 = (bf16[512,128]{1,0:T(8,128)(2,1)S(1)}, bf16[512,128]{1,0:T(8,128)(2,1)S(1)}, u32[]{:S(2)}, u32[]{:S(2)}) collective-permute-start(bf16[512,128]{1,0:T(8,128)(2,1)S(1)} %get-tuple-element.95.refs_1_), channel_id=1, source_target_pairs={{0,4},{1,5},{2,6},{3,7},{4,0},{5,1},{6,2},{7,3},{8,12},{9,13},{10,... | collective-permute-start | bytes 393224 | tf_op jit(solution)/shard_map/ppermute | solution.py:90
  88.6 5.6 %collective-permute-start.21 = (bf16[528,128]{1,0:T(8,128)(2,1)S(1)}, bf16[528,128]{1,0:T(8,128)(2,1)S(1)}, u32[]{:S(2)}, u32[]{:S(2)}) collective-permute-start(bf16[528,128]{1,0:T(8,128)(2,1)S(1)} %get-tuple-element.96.refs_0_), channel_id=1, source_target_pairs={{0,4},{1,5},{2,6},{3,7},{4,0},{5,1},{6,2},{7,3},{8,12},{9,13},{10,... | collective-permute-start | bytes 405512 | tf_op jit(solution)/shard_map/ppermute | solution.py:90
  89.2 5.0 %collective-permute-start.22 = (bf16[512,128]{1,0:T(8,128)(2,1)S(1)}, bf16[512,128]{1,0:T(8,128)(2,1)S(1)}, u32[]{:S(2)}, u32[]{:S(2)}) collective-permute-start(bf16[512,128]{1,0:T(8,128)(2,1)S(1)} %get-tuple-element.97.refs_1_), channel_id=1, source_target_pairs={{0,2},{1,3},{2,0},{3,1},{4,6},{5,7},{6,4},{7,5},{8,10},{9,11},{10,... | collective-permute-start | bytes 393224 | tf_op jit(solution)/shard_map/ppermute | solution.py:90
  95.0 1.5 %collective-permute-start.23 = (bf16[1040,128]{1,0:T(8,128)(2,1)S(1)}, bf16[1040,128]{1,0:T(8,128)(2,1)S(1)}, u32[]{:S(2)}, u32[]{:S(2)}) collective-permute-start(bf16[1040,128]{1,0:T(8,128)(2,1)S(1)} %get-tuple-element.99.refs_0_), channel_id=1, source_target_pairs={{0,1},{1,0},{2,3},{3,2},{4,5},{5,4},{6,7},{7,6},{8,9},{9,8},{10,11... | collective-permute-start | bytes 798728 | tf_op jit(solution)/shard_map/ppermute | solution.py:90
  97.5 4.5 %collective-permute-start.24 = (bf16[272,128]{1,0:T(8,128)(2,1)S(1)}, bf16[272,128]{1,0:T(8,128)(2,1)S(1)}, u32[]{:S(2)}, u32[]{:S(2)}) collective-permute-start(bf16[272,128]{1,0:T(8,128)(2,1)S(1)} %get-tuple-element.102), channel_id=1, source_target_pairs={{0,8},{8,0},{16,24},{24,16},{1,9},{9,1},{17,25},{25,17},{2,10},{10... | collective-permute-start | bytes 208904 | tf_op jit(solution)/shard_map/ppermute | solution.py:87
  98.9 8.5 %collective-permute-start.25 = (bf16[272,128]{1,0:T(8,128)(2,1)S(1)}, bf16[272,128]{1,0:T(8,128)(2,1)S(1)}, u32[]{:S(2)}, u32[]{:S(2)}) collective-permute-start(bf16[272,128]{1,0:T(8,128)(2,1)S(1)} %get-tuple-element.103), channel_id=1, source_target_pairs={{0,16},{8,24},{16,0},{24,8},{1,17},{9,25},{17,1},{25,9},{2,18},{10... | collective-permute-start | bytes 208904 | tf_op jit(solution)/shard_map/ppermute | solution.py:87
  100.3 7.1 %collective-permute-start.26 = (bf16[272,128]{1,0:T(8,128)(2,1)S(1)}, bf16[272,128]{1,0:T(8,128)(2,1)S(1)}, u32[]{:S(2)}, u32[]{:S(2)}) collective-permute-start(bf16[272,128]{1,0:T(8,128)(2,1)S(1)} %get-tuple-element.104), channel_id=1, source_target_pairs={{0,24},{8,16},{16,8},{24,0},{1,25},{9,17},{17,9},{25,1},{2,26},{10... | collective-permute-start | bytes 208904 | tf_op jit(solution)/shard_map/ppermute | solution.py:87
  107.5 4.7 %collective-permute-start.27 = (bf16[272,128]{1,0:T(8,128)(2,1)S(1)}, bf16[272,128]{1,0:T(8,128)(2,1)S(1)}, u32[]{:S(2)}, u32[]{:S(2)}) collective-permute-start(bf16[272,128]{1,0:T(8,128)(2,1)S(1)} %get-tuple-element.111.refs_0_), channel_id=1, source_target_pairs={{0,8},{8,0},{16,24},{24,16},{1,9},{9,1},{17,25},{25,17},{2,10},{10... | collective-permute-start | bytes 208904 | tf_op jit(solution)/shard_map/ppermute | solution.py:87
  109.0 7.9 %collective-permute-start.28 = (bf16[272,128]{1,0:T(8,128)(2,1)S(1)}, bf16[272,128]{1,0:T(8,128)(2,1)S(1)}, u32[]{:S(2)}, u32[]{:S(2)}) collective-permute-start(bf16[272,128]{1,0:T(8,128)(2,1)S(1)} %get-tuple-element.111.refs_0_), channel_id=1, source_target_pairs={{0,16},{8,24},{16,0},{24,8},{1,17},{9,25},{17,1},{25,9},{2,18},{10... | collective-permute-start | bytes 208904 | tf_op jit(solution)/shard_map/ppermute | solution.py:87
  110.4 6.5 %collective-permute-start.29 = (bf16[272,128]{1,0:T(8,128)(2,1)S(1)}, bf16[272,128]{1,0:T(8,128)(2,1)S(1)}, u32[]{:S(2)}, u32[]{:S(2)}) collective-permute-start(bf16[272,128]{1,0:T(8,128)(2,1)S(1)} %get-tuple-element.111.refs_0_), channel_id=1, source_target_pairs={{0,24},{8,16},{16,8},{24,0},{1,25},{9,17},{17,9},{25,1},{2,26},{10... | collective-permute-start | bytes 208904 | tf_op jit(solution)/shard_map/ppermute | solution.py:87
  118.1 2.0 %collective-permute-start.30 = (f32[1040,128]{1,0:T(8,128)S(1)}, f32[1040,128]{1,0:T(8,128)S(1)}, u32[]{:S(2)}, u32[]{:S(2)}) collective-permute-start(f32[1040,128]{1,0:T(8,128)S(1)} %get-tuple-element.115), channel_id=1, source_target_pairs={{0,1},{1,0},{2,3},{3,2},{4,5},{5,4},{6,7},{7,6},{8,9},{9,8},{10,11... | collective-permute-start | bytes 1597448 | tf_op jit(solution)/shard_map/ppermute | solution.py:90
  120.2 6.8 %collective-permute-start.31 = (bf16[528,128]{1,0:T(8,128)(2,1)S(1)}, bf16[528,128]{1,0:T(8,128)(2,1)S(1)}, u32[]{:S(2)}, u32[]{:S(2)}) collective-permute-start(bf16[528,128]{1,0:T(8,128)(2,1)S(1)} %get-tuple-element.116.refs_0_), channel_id=1, source_target_pairs={{0,2},{1,3},{2,0},{3,1},{4,6},{5,7},{6,4},{7,5},{8,10},{9,11},{10,... | collective-permute-start | bytes 405512 | tf_op jit(solution)/shard_map/ppermute | solution.py:90
  121.7 5.3 %collective-permute-start.32 = (bf16[512,128]{1,0:T(8,128)(2,1)S(1)}, bf16[512,128]{1,0:T(8,128)(2,1)S(1)}, u32[]{:S(2)}, u32[]{:S(2)}) collective-permute-start(bf16[512,128]{1,0:T(8,128)(2,1)S(1)} %get-tuple-element.117.refs_1_), channel_id=1, source_target_pairs={{0,4},{1,5},{2,6},{3,7},{4,0},{5,1},{6,2},{7,3},{8,12},{9,13},{10,... | collective-permute-start | bytes 393224 | tf_op jit(solution)/shard_map/ppermute | solution.py:90
  127.1 6.6 %collective-permute-start.33 = (bf16[528,128]{1,0:T(8,128)(2,1)S(1)}, bf16[528,128]{1,0:T(8,128)(2,1)S(1)}, u32[]{:S(2)}, u32[]{:S(2)}) collective-permute-start(bf16[528,128]{1,0:T(8,128)(2,1)S(1)} %get-tuple-element.118.refs_0_), channel_id=1, source_target_pairs={{0,4},{1,5},{2,6},{3,7},{4,0},{5,1},{6,2},{7,3},{8,12},{9,13},{10,... | collective-permute-start | bytes 405512 | tf_op jit(solution)/shard_map/ppermute | solution.py:90
  128.7 5.0 %collective-permute-start.34 = (bf16[512,128]{1,0:T(8,128)(2,1)S(1)}, bf16[512,128]{1,0:T(8,128)(2,1)S(1)}, u32[]{:S(2)}, u32[]{:S(2)}) collective-permute-start(bf16[512,128]{1,0:T(8,128)(2,1)S(1)} %get-tuple-element.119.refs_1_), channel_id=1, source_target_pairs={{0,2},{1,3},{2,0},{3,1},{4,6},{5,7},{6,4},{7,5},{8,10},{9,11},{10,... | collective-permute-start | bytes 393224 | tf_op jit(solution)/shard_map/ppermute | solution.py:90
  129.2 11.7 %collective-permute-start.40 = (f32[1024,128]{1,0:T(8,128)S(1)}, f32[1024,128]{1,0:T(8,128)S(1)}, u32[]{:S(2)}, u32[]{:S(2)}) collective-permute-start(f32[1024,128]{1,0:T(8,128)S(1)} %get-tuple-element.125.refs_9_), channel_id=1, source_target_pairs={{0,1},{1,0},{2,3},{3,2},{4,5},{5,4},{6,7},{7,6},{8,9},{9,8},{10,11... | collective-permute-start | bytes 1572872 | tf_op jit(solution)/shard_map/ppermute | solution.py:90
  134.6 9.9 %collective-permute-start.39 = (f32[1024,128]{1,0:T(8,128)S(1)}, f32[1024,128]{1,0:T(8,128)S(1)}, u32[]{:S(2)}, u32[]{:S(2)}) collective-permute-start(f32[1024,128]{1,0:T(8,128)S(1)} %get-tuple-element.124.refs_7_), channel_id=1, source_target_pairs={{0,1},{1,0},{2,3},{3,2},{4,5},{5,4},{6,7},{7,6},{8,9},{9,8},{10,11... | collective-permute-start | bytes 1572872 | tf_op jit(solution)/shard_map/ppermute | solution.py:90
  134.6 1.9 %collective-permute-start.35 = (f32[8,128]{1,0:T(8,128)S(1)}, f32[8,128]{1,0:T(8,128)S(1)}, u32[]{:S(2)}, u32[]{:S(2)}) collective-permute-start(f32[8,128]{1,0:T(8,128)S(1)} %get-tuple-element.121.own_ref), channel_id=1, source_target_pairs={{0,1},{1,0},{2,3},{3,2},{4,5},{5,4},{6,7},{7,6},{8,9},{9,8},{10,11... | collective-permute-start | bytes 12296 | tf_op jit(solution)/shard_map/ppermute | solution.py:90
  136.6 4.4 %collective-permute-start.36 = (f32[8,128]{1,0:T(8,128)S(1)}, f32[8,128]{1,0:T(8,128)S(1)}, u32[]{:S(2)}, u32[]{:S(2)}) collective-permute-start(f32[8,128]{1,0:T(8,128)S(1)} %shard_map.68.refs_0_), channel_id=1, source_target_pairs={{0,8},{8,0},{16,24},{24,16},{1,9},{9,1},{17,25},{25,17},{2,10},{10... | collective-permute-start | bytes 12296 | tf_op jit(solution)/shard_map/ppermute | solution.py:87
  137.9 4.5 %collective-permute-start.37 = (f32[8,128]{1,0:T(8,128)S(1)}, f32[8,128]{1,0:T(8,128)S(1)}, u32[]{:S(2)}, u32[]{:S(2)}) collective-permute-start(f32[8,128]{1,0:T(8,128)S(1)} %shard_map.68.refs_0_), channel_id=1, source_target_pairs={{0,16},{8,24},{16,0},{24,8},{1,17},{9,25},{17,1},{25,9},{2,18},{10... | collective-permute-start | bytes 12296 | tf_op jit(solution)/shard_map/ppermute | solution.py:87
  139.1 5.4 %collective-permute-start.38 = (f32[8,128]{1,0:T(8,128)S(1)}, f32[8,128]{1,0:T(8,128)S(1)}, u32[]{:S(2)}, u32[]{:S(2)}) collective-permute-start(f32[8,128]{1,0:T(8,128)S(1)} %shard_map.68.refs_0_), channel_id=1, source_target_pairs={{0,24},{8,16},{16,8},{24,0},{1,25},{9,17},{17,9},{25,1},{2,26},{10... | collective-permute-start | bytes 12296 | tf_op jit(solution)/shard_map/ppermute | solution.py:87

commit v3 on v2

--- a/solution.py
+++ b/solution.py
@@ -9,7 +9,8 @@
 PAD = 16
 F32 = jnp.float32
 BF16 = jnp.bfloat16
-ROW_WIRE = (F32, F32, BF16)
+F16 = jnp.float16
+ROW_WIRE = (F16, F16, BF16)
 CORE_WIRE = (F32, F32, F32)
 CHIP_WIRE = ((BF16, BF16), (BF16, BF16), (BF16, BF16))
 LIMIT = 24 * 1024 * 1024
@@ -42,6 +43,32 @@
     tail = ref[pl.ds(rows, PAD), :].astype(F32)
     at = 3 * which
     return tail[at : at + 1] + tail[at + 1 : at + 2] + tail[at + 2 : at + 3]
+
+
+def exponent_of(value):
+    return jnp.clip(jnp.floor(jnp.log2(jnp.maximum(value, 1e-36))), -119.0, 119.0)
+
+
+def put_scaled(ref, exponent, value):
+    rows = ref.shape[0] - PAD
+    own = exponent_of(value)
+    scaled = value * jnp.exp2(-own)
+    high = scaled.astype(BF16).astype(F32)
+    middle = (scaled - high).astype(BF16).astype(F32)
+    parts = [exponent, own, high, 256.0 * middle, 65536.0 * (scaled - high - middle)]
+    shape = (PAD, ref.shape[1])
+    index = lax.broadcasted_iota(jnp.int32, shape, 0)
+    block = jnp.zeros(shape, F32)
+    for place, part in enumerate(parts):
+        block = jnp.where(index == place, jnp.broadcast_to(part, shape), block)
+    ref[pl.ds(rows, PAD), :] = block
+
+
+def get_scaled(ref):
+    rows = ref.shape[0] - PAD
+    tail = ref[pl.ds(rows, PAD), :]
+    value = tail[2:3] + tail[3:4] * (1.0 / 256.0) + tail[4:5] * (1.0 / 65536.0)
+    return jnp.exp2(tail[0:1]), value * jnp.exp2(tail[1:2])
 
 
 def body_of(ref):
@@ -121,41 +148,55 @@
                     part = part[0:outs] + part[outs:wide]
                 prod[start : start + block, :] = part.T
             own_ref[...] = prod[pl.ds(row_place(0), feat_share), :]
+            if scaled:
+                exponent = exponent_of(jnp.max(jnp.abs(prod[...]), axis=0, keepdims=True))
+                factor = jnp.exp2(-exponent)
             for step, ref in enumerate(msg_refs, 1):
-                ref[pl.ds(0, feat_share), :] = prod[pl.ds(row_place(step), feat_share), :].astype(wire)
-                put_rows(ref, delta)
-
-        msgs = [((feat_share + PAD, outs), wire)] * (n_row - 1)
+                part = prod[pl.ds(row_place(step), feat_share), :]
+                if scaled:
+                    ref[pl.ds(0, feat_share), :] = part * factor
+                    put_scaled(ref, exponent, delta)
+                else:
+                    ref[pl.ds(0, feat_share), :] = part.astype(wire)
+                    put_rows(ref, delta)
+
+        scaled = wire == F16
+        msgs = [((feat_share + PAD, outs), F32 if scaled else wire)] * (n_row - 1)
         own, delta, *sends = call(
             kernel,
             [feature_rows, scalar] + msgs,
             (states,) + blocks,
             [pltpu.VMEM((tokens, wide), BF16), pltpu.VMEM((feats, outs), F32)],
         )
-        return own, delta, [over_row(step, send) for step, send in enumerate(sends, 1)]
+        got = [over_row(step, send.astype(wire)) for step, send in enumerate(sends, 1)]
+        return own, delta, [send.astype(F32) if scaled else send for send in got]
 
     def begin(own, got):
         def kernel(own_ref, *refs):
             ins, (grad_ref, msg_ref) = refs[: n_row - 1], refs[n_row - 1 :]
             grad = own_ref[...]
             for ref in ins:
-                grad = grad + body_of(ref).astype(F32)
+                grad = grad + get_scaled(ref)[0] * body_of(ref)
             grad_ref[...] = grad
             msg_ref[pl.ds(0, feat_share), :] = grad.astype(BF16)
             put_rows(msg_ref, column_sum(grad * grad), jnp.zeros((1, outs), F32))
 
         return call(kernel, [feature_rows, ((feat_share + PAD, outs), BF16)], [own] + got)
 
-    def advance(own, delta, got, gamma, dir_sq, grad, direction, image, weights, residual):
+    def advance(wire, own, delta, got, gamma, dir_sq, grad, direction, image, weights, residual):
         def kernel(own_ref, delta_ref, *refs):
             ins = refs[: n_row - 1]
             gamma_ref, sq_ref, grad_ref, dir_ref, image_ref, w_ref, r_ref, ridge_ref = refs[n_row - 1 : n_row + 7]
             w_out, r_out, grad_out, msg_ref = refs[n_row + 7 :]
-            image_sq = tree_sum([delta_ref[0:1, :]] + [get_row(ref) for ref in ins])
+            if wire == F16:
+                tails = [get_scaled(ref) for ref in ins]
+            else:
+                tails = [(1.0, get_row(ref)) for ref in ins]
+            image_sq = tree_sum([delta_ref[0:1, :]] + [value for _, value in tails])
             alpha = gamma_ref[0:1, :] / (image_sq + ridge_ref[...] * sq_ref[0:1, :])
             prod = own_ref[...]
-            for ref in ins:
-                prod = prod + body_of(ref).astype(F32)
+            for ref, (scale, _) in zip(ins, tails):
+                prod = prod + scale * body_of(ref).astype(F32)
             old_dir = dir_ref[...]
             new = grad_ref[...] - alpha * (prod + ridge_ref[...] * old_dir)
             msg_ref[pl.ds(0, feat_share), :] = new.astype(BF16)
@@ -287,7 +328,7 @@
         if not last:
             own, delta, got = backward(ROW_WIRE[step + 1], msg, over_group(1, msg))
             weights, residual, grad, msg = advance(
-                own, delta, got, gamma, dir_sq, grad, direction, image, weights, residual
+                ROW_WIRE[step + 1], own, delta, got, gamma, dir_sq, grad, direction, image, weights, residual
             )
             before = (gamma, dir_sq, direction, image)
 

time: 146 us -> 134 us (0.918)
  waiting for transfers between devices: 79.6 us -> 68.2 us
    ppermute x21, waiting for transfers between devices: 44.8 us -> 33.4 us  [over_row(): return lax.ppermute(value, 'row', [(i, i ^ step) for i in range(n_row)])]
where the time goes in v3:
time: 134 us
  waiting for transfers between devices  68.2 us (51%)
  starting transfers between devices  46.8 us (35%)
  Pallas kernels  12.4 us (9%)
  local copies, waits for them, and re-layouts  5.66 us (4%)
    ppermute x20, waiting for transfers between devices, over_group(): return lax.ppermute(value, 'group', [(i, i ^ step) for i in range(n_group)])  34.8 us
    ppermute x21, waiting for transfers between devices, over_row(): return lax.ppermute(value, 'row', [(i, i ^ step) for i in range(n_row)])  33.4 us
    ppermute x21, starting transfers between devices, over_row(): return lax.ppermute(value, 'row', [(i, i ^ step) for i in range(n_row)])  32.6 us
    ppermute x20, starting transfers between devices, over_group(): return lax.ppermute(value, 'group', [(i, i ^ step) for i in range(n_group)])  14.3 us
    pallas_call x20, Pallas kernels, call(): pl.pallas_call(kernel, out_shape=[jax.ShapeDtypeStruct(shape, dtype) for...  12.4 us
    unnamed x14, local copies, waits for them, and re-layouts  5.61 us
  transfers between devices with their start and end apart: 41, of which 24 were waited for; matrix products, arithmetic and copies ran while one was open for 0% of the time, Pallas kernels for 1%

profile of v3, /device:TPU:0, one launch (start us, length us, event | category | flops | bytes accessed | tf_op | source)
XLA Modules:
  0.0 134.1 jit_solution(15887329490802814993)
XLA Ops:
  0.6 2.2 %copy-done = bf16[2048,1024]{1,0:T(8,128)(2,1)S(1)} copy-done((bf16[2048,1024]{1,0:T(8,128)(2,1)S(1)}, bf16[2048,1024]{1,0:T(8,128)(2,1)}, u32[]{:S(2)}) %copy-start) | copy-done | bytes 4194328
  2.8 1.2 copy-done.4
  4.0 1.9 %shard_map.50 = (f32[256,128]{1,0:T(8,128)S(1)}, f32[8,128]{1,0:T(8,128)}, f32[272,128]{1,0:T(8,128)S(1)}, f32[272,128]{1,0:T(8,128)S(1)}, f32[272,128]{1,0:T(8,128)S(1)}) custom-call(bf16[2048,1024]{1,0:T(8,128)(2,1)S(1)} %copy-done, f32[2048,128]{1,0:T(8,128)S(1)} %copy-done.4), custom_call_target="tpu_custom_call" | custom-call | tf_op jit(solution)/shard_map/pallas_call | solution.py:88
  6.0 3.1 %collective-permute-start = (f16[272,128]{1,0:T(8,128)(2,1)S(1)}, f16[272,128]{1,0:T(8,128)(2,1)S(1)}, u32[]{:S(2)}, u32[]{:S(2)}) collective-permute-start(f16[272,128]{1,0:T(8,128)(2,1)S(1)} %convert_element_type.36), channel_id=1, source_target_pairs={{0,8},{8,0},{16,24},{24,16},{1,9},{9,1},{17,25},{25,17},{2,10},{10... | collective-permute-start | bytes 208904 | tf_op jit(solution)/shard_map/ppermute | solution.py:114
  9.1 2.7 %collective-permute-start.1 = (f16[272,128]{1,0:T(8,128)(2,1)S(1)}, f16[272,128]{1,0:T(8,128)(2,1)S(1)}, u32[]{:S(2)}, u32[]{:S(2)}) collective-permute-start(f16[272,128]{1,0:T(8,128)(2,1)S(1)} %convert_element_type.38), channel_id=1, source_target_pairs={{0,16},{8,24},{16,0},{24,8},{1,17},{9,25},{17,1},{25,9},{2,18},{10... | collective-permute-start | bytes 208904 | tf_op jit(solution)/shard_map/ppermute | solution.py:114
  11.9 4.8 %collective-permute-done.1 = f16[272,128]{1,0:T(8,128)(2,1)S(1)} collective-permute-done((f16[272,128]{1,0:T(8,128)(2,1)S(1)}, f16[272,128]{1,0:T(8,128)(2,1)S(1)}, u32[]{:S(2)}, u32[]{:S(2)}) %collective-permute-start.1) | collective-permute-done | bytes 69664 | tf_op jit(solution)/shard_map/ppermute | solution.py:114
  16.7 1.3 %collective-permute-done.2 = f16[272,128]{1,0:T(8,128)(2,1)S(1)} collective-permute-done((f16[272,128]{1,0:T(8,128)(2,1)S(1)}, f16[272,128]{1,0:T(8,128)(2,1)S(1)}, u32[]{:S(2)}, u32[]{:S(2)}) %collective-permute-start.2) | collective-permute-done | bytes 69664 | tf_op jit(solution)/shard_map/ppermute | solution.py:114
  18.1 0.8 collective-permute-start.3
  18.9 1.8 %collective-permute-start.4 = (bf16[272,128]{1,0:T(8,128)(2,1)S(1)}, bf16[272,128]{1,0:T(8,128)(2,1)S(1)}, u32[]{:S(2)}, u32[]{:S(2)}) collective-permute-start(bf16[272,128]{1,0:T(8,128)(2,1)S(1)} %get-tuple-element.69.refs_0_), channel_id=1, source_target_pairs={{0,16},{8,24},{16,0},{24,8},{1,17},{9,25},{17,1},{25,9},{2,18},{10... | collective-permute-start | bytes 208904 | tf_op jit(solution)/shard_map/ppermute | solution.py:114
  20.7 1.9 %collective-permute-start.5 = (bf16[272,128]{1,0:T(8,128)(2,1)S(1)}, bf16[272,128]{1,0:T(8,128)(2,1)S(1)}, u32[]{:S(2)}, u32[]{:S(2)}) collective-permute-start(bf16[272,128]{1,0:T(8,128)(2,1)S(1)} %get-tuple-element.69.refs_0_), channel_id=1, source_target_pairs={{0,24},{8,16},{16,8},{24,0},{1,25},{9,17},{17,9},{25,1},{2,26},{10... | collective-permute-start | bytes 208904 | tf_op jit(solution)/shard_map/ppermute | solution.py:114
  22.6 2.6 %collective-permute-done.4.refs_2_ = bf16[272,128]{1,0:T(8,128)(2,1)S(1)} collective-permute-done((bf16[272,128]{1,0:T(8,128)(2,1)S(1)}, bf16[272,128]{1,0:T(8,128)(2,1)S(1)}, u32[]{:S(2)}, u32[]{:S(2)}) %collective-permute-start.4) | collective-permute-done | bytes 69664 | tf_op jit(solution)/shard_map/ppermute | solution.py:114
  25.2 1.6 %collective-permute-done.5.refs_3_ = bf16[272,128]{1,0:T(8,128)(2,1)S(1)} collective-permute-done((bf16[272,128]{1,0:T(8,128)(2,1)S(1)}, bf16[272,128]{1,0:T(8,128)(2,1)S(1)}, u32[]{:S(2)}, u32[]{:S(2)}) %collective-permute-start.5) | collective-permute-done | bytes 69664 | tf_op jit(solution)/shard_map/ppermute | solution.py:114
  26.8 1.3 shard_map.52
  28.2 1.9 %collective-permute-done.6.got_ref = f32[1040,128]{1,0:T(8,128)S(1)} collective-permute-done((f32[1040,128]{1,0:T(8,128)S(1)}, f32[1040,128]{1,0:T(8,128)S(1)}, u32[]{:S(2)}, u32[]{:S(2)}) %collective-permute-start.6) | collective-permute-done | bytes 532512 | tf_op jit(solution)/shard_map/ppermute | solution.py:117
  30.2 1.5 %collective-permute-start.7 = (bf16[528,128]{1,0:T(8,128)(2,1)S(1)}, bf16[528,128]{1,0:T(8,128)(2,1)S(1)}, u32[]{:S(2)}, u32[]{:S(2)}) collective-permute-start(bf16[528,128]{1,0:T(8,128)(2,1)S(1)} %get-tuple-element.74.refs_0_), channel_id=1, source_target_pairs={{0,2},{1,3},{2,0},{3,1},{4,6},{5,7},{6,4},{7,5},{8,10},{9,11},{10,... | collective-permute-start | bytes 405512 | tf_op jit(solution)/shard_map/ppermute | solution.py:117
  31.7 1.5 %collective-permute-start.8 = (bf16[512,128]{1,0:T(8,128)(2,1)S(1)}, bf16[512,128]{1,0:T(8,128)(2,1)S(1)}, u32[]{:S(2)}, u32[]{:S(2)}) collective-permute-start(bf16[512,128]{1,0:T(8,128)(2,1)S(1)} %get-tuple-element.75.refs_1_), channel_id=1, source_target_pairs={{0,4},{1,5},{2,6},{3,7},{4,0},{5,1},{6,2},{7,3},{8,12},{9,13},{10,... | collective-permute-start | bytes 393224 | tf_op jit(solution)/shard_map/ppermute | solution.py:117
  33.3 3.7 %collective-permute-done.8.refs_3_ = bf16[512,128]{1,0:T(8,128)(2,1)S(1)} collective-permute-done((bf16[512,128]{1,0:T(8,128)(2,1)S(1)}, bf16[512,128]{1,0:T(8,128)(2,1)S(1)}, u32[]{:S(2)}, u32[]{:S(2)}) %collective-permute-start.8) | collective-permute-done | bytes 131104 | tf_op jit(solution)/shard_map/ppermute | solution.py:117
  37.1 1.6 %collective-permute-start.9 = (bf16[528,128]{1,0:T(8,128)(2,1)S(1)}, bf16[528,128]{1,0:T(8,128)(2,1)S(1)}, u32[]{:S(2)}, u32[]{:S(2)}) collective-permute-start(bf16[528,128]{1,0:T(8,128)(2,1)S(1)} %get-tuple-element.76.refs_0_), channel_id=1, source_target_pairs={{0,4},{1,5},{2,6},{3,7},{4,0},{5,1},{6,2},{7,3},{8,12},{9,13},{10,... | collective-permute-start | bytes 405512 | tf_op jit(solution)/shard_map/ppermute | solution.py:117
  39.2 4.4 %collective-permute-done.10.refs_3_ = bf16[512,128]{1,0:T(8,128)(2,1)S(1)} collective-permute-done((bf16[512,128]{1,0:T(8,128)(2,1)S(1)}, bf16[512,128]{1,0:T(8,128)(2,1)S(1)}, u32[]{:S(2)}, u32[]{:S(2)}) %collective-permute-start.10) | collective-permute-done | bytes 131104 | tf_op jit(solution)/shard_map/ppermute | solution.py:117
  43.6 0.8 shard_map.55
  44.4 1.5 %collective-permute-done.11.refs_1_ = bf16[1040,128]{1,0:T(8,128)(2,1)S(1)} collective-permute-done((bf16[1040,128]{1,0:T(8,128)(2,1)S(1)}, bf16[1040,128]{1,0:T(8,128)(2,1)S(1)}, u32[]{:S(2)}, u32[]{:S(2)}) %collective-permute-start.11) | collective-permute-done | bytes 266272 | tf_op jit(solution)/shard_map/ppermute | solution.py:117
  45.9 2.2 %copy-done.2 = bf16[2048,1024]{1,0:T(8,128)(2,1)S(1)} copy-done((bf16[2048,1024]{1,0:T(8,128)(2,1)S(1)}, bf16[2048,1024]{1,0:T(8,128)(2,1)}, u32[]{:S(2)}) %copy-start.2) | copy-done | bytes 4194328
  48.1 1.0 shard_map.56
  49.2 2.7 %collective-permute-start.13 = (f16[272,128]{1,0:T(8,128)(2,1)S(1)}, f16[272,128]{1,0:T(8,128)(2,1)S(1)}, u32[]{:S(2)}, u32[]{:S(2)}) collective-permute-start(f16[272,128]{1,0:T(8,128)(2,1)S(1)} %convert_element_type.44), channel_id=1, source_target_pairs={{0,16},{8,24},{16,0},{24,8},{1,17},{9,25},{17,1},{25,9},{2,18},{10... | collective-permute-start | bytes 208904 | tf_op jit(solution)/shard_map/ppermute | solution.py:114
  51.9 1.8 %collective-permute-start.14 = (f16[272,128]{1,0:T(8,128)(2,1)S(1)}, f16[272,128]{1,0:T(8,128)(2,1)S(1)}, u32[]{:S(2)}, u32[]{:S(2)}) collective-permute-start(f16[272,128]{1,0:T(8,128)(2,1)S(1)} %convert_element_type.46), channel_id=1, source_target_pairs={{0,24},{8,16},{16,8},{24,0},{1,25},{9,17},{17,9},{25,1},{2,26},{10... | collective-permute-start | bytes 208904 | tf_op jit(solution)/shard_map/ppermute | solution.py:114
  53.8 0.9 collective-permute-done.12
  54.7 2.4 %collective-permute-done.13 = f16[272,128]{1,0:T(8,128)(2,1)S(1)} collective-permute-done((f16[272,128]{1,0:T(8,128)(2,1)S(1)}, f16[272,128]{1,0:T(8,128)(2,1)S(1)}, u32[]{:S(2)}, u32[]{:S(2)}) %collective-permute-start.13) | collective-permute-done | bytes 69664 | tf_op jit(solution)/shard_map/ppermute | solution.py:114
  57.1 1.1 collective-permute-done.14
  58.4 1.4 %collective-permute-start.15 = (bf16[272,128]{1,0:T(8,128)(2,1)S(1)}, bf16[272,128]{1,0:T(8,128)(2,1)S(1)}, u32[]{:S(2)}, u32[]{:S(2)}) collective-permute-start(bf16[272,128]{1,0:T(8,128)(2,1)S(1)} %get-tuple-element.89.refs_0_), channel_id=1, source_target_pairs={{0,8},{8,0},{16,24},{24,16},{1,9},{9,1},{17,25},{25,17},{2,10},{10... | collective-permute-start | bytes 208904 | tf_op jit(solution)/shard_map/ppermute | solution.py:114
  59.8 1.7 %collective-permute-start.16 = (bf16[272,128]{1,0:T(8,128)(2,1)S(1)}, bf16[272,128]{1,0:T(8,128)(2,1)S(1)}, u32[]{:S(2)}, u32[]{:S(2)}) collective-permute-start(bf16[272,128]{1,0:T(8,128)(2,1)S(1)} %get-tuple-element.89.refs_0_), channel_id=1, source_target_pairs={{0,16},{8,24},{16,0},{24,8},{1,17},{9,25},{17,1},{25,9},{2,18},{10... | collective-permute-start | bytes 208904 | tf_op jit(solution)/shard_map/ppermute | solution.py:114
  61.5 1.3 collective-permute-start.17
  62.9 4.9 %collective-permute-done.16.refs_2_ = bf16[272,128]{1,0:T(8,128)(2,1)S(1)} collective-permute-done((bf16[272,128]{1,0:T(8,128)(2,1)S(1)}, bf16[272,128]{1,0:T(8,128)(2,1)S(1)}, u32[]{:S(2)}, u32[]{:S(2)}) %collective-permute-start.16) | collective-permute-done | bytes 69664 | tf_op jit(solution)/shard_map/ppermute | solution.py:114
  67.8 1.3 shard_map.58
  69.2 1.9 %collective-permute-done.18.got_ref = f32[1040,128]{1,0:T(8,128)S(1)} collective-permute-done((f32[1040,128]{1,0:T(8,128)S(1)}, f32[1040,128]{1,0:T(8,128)S(1)}, u32[]{:S(2)}, u32[]{:S(2)}) %collective-permute-start.18) | collective-permute-done | bytes 532512 | tf_op jit(solution)/shard_map/ppermute | solution.py:117
  71.2 0.6 collective-permute-start.19
  72.3 4.7 %collective-permute-done.20.refs_3_ = bf16[512,128]{1,0:T(8,128)(2,1)S(1)} collective-permute-done((bf16[512,128]{1,0:T(8,128)(2,1)S(1)}, bf16[512,128]{1,0:T(8,128)(2,1)S(1)}, u32[]{:S(2)}, u32[]{:S(2)}) %collective-permute-start.20) | collective-permute-done | bytes 131104 | tf_op jit(solution)/shard_map/ppermute | solution.py:117
  77.7 1.5 %collective-permute-start.22 = (bf16[512,128]{1,0:T(8,128)(2,1)S(1)}, bf16[512,128]{1,0:T(8,128)(2,1)S(1)}, u32[]{:S(2)}, u32[]{:S(2)}) collective-permute-start(bf16[512,128]{1,0:T(8,128)(2,1)S(1)} %get-tuple-element.97.refs_1_), channel_id=1, source_target_pairs={{0,2},{1,3},{2,0},{3,1},{4,6},{5,7},{6,4},{7,5},{8,10},{9,11},{10,... | collective-permute-start | bytes 393224 | tf_op jit(solution)/shard_map/ppermute | solution.py:117
  79.2 3.5 %collective-permute-done.22.refs_3_ = bf16[512,128]{1,0:T(8,128)(2,1)S(1)} collective-permute-done((bf16[512,128]{1,0:T(8,128)(2,1)S(1)}, bf16[512,128]{1,0:T(8,128)(2,1)S(1)}, u32[]{:S(2)}, u32[]{:S(2)}) %collective-permute-start.22) | collective-permute-done | bytes 131104 | tf_op jit(solution)/shard_map/ppermute | solution.py:117
  82.7 0.8 shard_map.61
  83.5 1.5 %collective-permute-done.23.refs_1_ = bf16[1040,128]{1,0:T(8,128)(2,1)S(1)} collective-permute-done((bf16[1040,128]{1,0:T(8,128)(2,1)S(1)}, bf16[1040,128]{1,0:T(8,128)(2,1)S(1)}, u32[]{:S(2)}, u32[]{:S(2)}) %collective-permute-start.23) | collective-permute-done | bytes 266272 | tf_op jit(solution)/shard_map/ppermute | solution.py:117
  85.1 0.9 shard_map.62
  86.0 1.4 %collective-permute-start.24 = (bf16[272,128]{1,0:T(8,128)(2,1)S(1)}, bf16[272,128]{1,0:T(8,128)(2,1)S(1)}, u32[]{:S(2)}, u32[]{:S(2)}) collective-permute-start(bf16[272,128]{1,0:T(8,128)(2,1)S(1)} %get-tuple-element.102), channel_id=1, source_target_pairs={{0,8},{8,0},{16,24},{24,16},{1,9},{9,1},{17,25},{25,17},{2,10},{10... | collective-permute-start | bytes 208904 | tf_op jit(solution)/shard_map/ppermute | solution.py:114
  87.4 1.1 collective-permute-start.25
  88.5 1.9 %collective-permute-start.26 = (bf16[272,128]{1,0:T(8,128)(2,1)S(1)}, bf16[272,128]{1,0:T(8,128)(2,1)S(1)}, u32[]{:S(2)}, u32[]{:S(2)}) collective-permute-start(bf16[272,128]{1,0:T(8,128)(2,1)S(1)} %get-tuple-element.104), channel_id=1, source_target_pairs={{0,24},{8,16},{16,8},{24,0},{1,25},{9,17},{17,9},{25,1},{2,26},{10... | collective-permute-start | bytes 208904 | tf_op jit(solution)/shard_map/ppermute | solution.py:114
  90.5 5.4 %collective-permute-done.25.refs_1_ = bf16[272,128]{1,0:T(8,128)(2,1)S(1)} collective-permute-done((bf16[272,128]{1,0:T(8,128)(2,1)S(1)}, bf16[272,128]{1,0:T(8,128)(2,1)S(1)}, u32[]{:S(2)}, u32[]{:S(2)}) %collective-permute-start.25) | collective-permute-done | bytes 69664 | tf_op jit(solution)/shard_map/ppermute | solution.py:114
  96.0 1.5 %collective-permute-start.27 = (bf16[272,128]{1,0:T(8,128)(2,1)S(1)}, bf16[272,128]{1,0:T(8,128)(2,1)S(1)}, u32[]{:S(2)}, u32[]{:S(2)}) collective-permute-start(bf16[272,128]{1,0:T(8,128)(2,1)S(1)} %get-tuple-element.111.refs_0_), channel_id=1, source_target_pairs={{0,8},{8,0},{16,24},{24,16},{1,9},{9,1},{17,25},{25,17},{2,10},{10... | collective-permute-start | bytes 208904 | tf_op jit(solution)/shard_map/ppermute | solution.py:114
  97.5 1.0 collective-permute-start.28
  98.5 1.9 %collective-permute-start.29 = (bf16[272,128]{1,0:T(8,128)(2,1)S(1)}, bf16[272,128]{1,0:T(8,128)(2,1)S(1)}, u32[]{:S(2)}, u32[]{:S(2)}) collective-permute-start(bf16[272,128]{1,0:T(8,128)(2,1)S(1)} %get-tuple-element.111.refs_0_), channel_id=1, source_target_pairs={{0,24},{8,16},{16,8},{24,0},{1,25},{9,17},{17,9},{25,1},{2,26},{10... | collective-permute-start | bytes 208904 | tf_op jit(solution)/shard_map/ppermute | solution.py:114
  100.5 4.9 %collective-permute-done.28.refs_2_ = bf16[272,128]{1,0:T(8,128)(2,1)S(1)} collective-permute-done((bf16[272,128]{1,0:T(8,128)(2,1)S(1)}, bf16[272,128]{1,0:T(8,128)(2,1)S(1)}, u32[]{:S(2)}, u32[]{:S(2)}) %collective-permute-start.28) | collective-permute-done | bytes 69664 | tf_op jit(solution)/shard_map/ppermute | solution.py:114
  105.3 1.3 shard_map.64
  106.7 1.9 %collective-permute-done.30.got_ref = f32[1040,128]{1,0:T(8,128)S(1)} collective-permute-done((f32[1040,128]{1,0:T(8,128)S(1)}, f32[1040,128]{1,0:T(8,128)S(1)}, u32[]{:S(2)}, u32[]{:S(2)}) %collective-permute-start.30) | collective-permute-done | bytes 532512 | tf_op jit(solution)/shard_map/ppermute | solution.py:117
  108.7 1.6 %collective-permute-start.31 = (bf16[528,128]{1,0:T(8,128)(2,1)S(1)}, bf16[528,128]{1,0:T(8,128)(2,1)S(1)}, u32[]{:S(2)}, u32[]{:S(2)}) collective-permute-start(bf16[528,128]{1,0:T(8,128)(2,1)S(1)} %get-tuple-element.116.refs_0_), channel_id=1, source_target_pairs={{0,2},{1,3},{2,0},{3,1},{4,6},{5,7},{6,4},{7,5},{8,10},{9,11},{10,... | collective-permute-start | bytes 405512 | tf_op jit(solution)/shard_map/ppermute | solution.py:117
  110.3 1.5 %collective-permute-start.32 = (bf16[512,128]{1,0:T(8,128)(2,1)S(1)}, bf16[512,128]{1,0:T(8,128)(2,1)S(1)}, u32[]{:S(2)}, u32[]{:S(2)}) collective-permute-start(bf16[512,128]{1,0:T(8,128)(2,1)S(1)} %get-tuple-element.117.refs_1_), channel_id=1, source_target_pairs={{0,4},{1,5},{2,6},{3,7},{4,0},{5,1},{6,2},{7,3},{8,12},{9,13},{10,... | collective-permute-start | bytes 393224 | tf_op jit(solution)/shard_map/ppermute | solution.py:117
  111.8 3.7 %collective-permute-done.32.refs_3_ = bf16[512,128]{1,0:T(8,128)(2,1)S(1)} collective-permute-done((bf16[512,128]{1,0:T(8,128)(2,1)S(1)}, bf16[512,128]{1,0:T(8,128)(2,1)S(1)}, u32[]{:S(2)}, u32[]{:S(2)}) %collective-permute-start.32) | collective-permute-done | bytes 131104 | tf_op jit(solution)/shard_map/ppermute | solution.py:117
  115.6 1.6 %collective-permute-start.33 = (bf16[528,128]{1,0:T(8,128)(2,1)S(1)}, bf16[528,128]{1,0:T(8,128)(2,1)S(1)}, u32[]{:S(2)}, u32[]{:S(2)}) collective-permute-start(bf16[528,128]{1,0:T(8,128)(2,1)S(1)} %get-tuple-element.118.refs_0_), channel_id=1, source_target_pairs={{0,4},{1,5},{2,6},{3,7},{4,0},{5,1},{6,2},{7,3},{8,12},{9,13},{10,... | collective-permute-start | bytes 405512 | tf_op jit(solution)/shard_map/ppermute | solution.py:117
  117.7 4.5 %collective-permute-done.34.refs_3_ = bf16[512,128]{1,0:T(8,128)(2,1)S(1)} collective-permute-done((bf16[512,128]{1,0:T(8,128)(2,1)S(1)}, bf16[512,128]{1,0:T(8,128)(2,1)S(1)}, u32[]{:S(2)}, u32[]{:S(2)}) %collective-permute-start.34) | collective-permute-done | bytes 131104 | tf_op jit(solution)/shard_map/ppermute | solution.py:117
  122.2 1.0 shard_map.67
  123.6 1.4 %collective-permute-done.35.got_ref = f32[8,128]{1,0:T(8,128)S(1)} collective-permute-done((f32[8,128]{1,0:T(8,128)S(1)}, f32[8,128]{1,0:T(8,128)S(1)}, u32[]{:S(2)}, u32[]{:S(2)}) %collective-permute-start.35) | collective-permute-done | bytes 4128 | tf_op jit(solution)/shard_map/ppermute | solution.py:117
  125.0 1.3 collective-permute-start.36
  126.3 1.2 collective-permute-start.37
  127.5 1.9 %collective-permute-start.38 = (f32[8,128]{1,0:T(8,128)S(1)}, f32[8,128]{1,0:T(8,128)S(1)}, u32[]{:S(2)}, u32[]{:S(2)}) collective-permute-start(f32[8,128]{1,0:T(8,128)S(1)} %shard_map.68.refs_0_), channel_id=1, source_target_pairs={{0,24},{8,16},{16,8},{24,0},{1,25},{9,17},{17,9},{25,1},{2,26},{10... | collective-permute-start | bytes 12296 | tf_op jit(solution)/shard_map/ppermute | solution.py:114
  129.4 1.4 %collective-permute-done.37.refs_2_ = f32[8,128]{1,0:T(8,128)S(1)} collective-permute-done((f32[8,128]{1,0:T(8,128)S(1)}, f32[8,128]{1,0:T(8,128)S(1)}, u32[]{:S(2)}, u32[]{:S(2)}) %collective-permute-start.37) | collective-permute-done | bytes 4128 | tf_op jit(solution)/shard_map/ppermute | solution.py:114
  130.9 2.1 %collective-permute-done.38.refs_3_ = f32[8,128]{1,0:T(8,128)S(1)} collective-permute-done((f32[8,128]{1,0:T(8,128)S(1)}, f32[8,128]{1,0:T(8,128)S(1)}, u32[]{:S(2)}, u32[]{:S(2)}) %collective-permute-start.38) | collective-permute-done | bytes 4128 | tf_op jit(solution)/shard_map/ppermute | solution.py:114
  132.9 1.2 shard_map.69
  (66 shorter events, 4.2 us)
Async XLA Ops:
  0.6 2.2 %copy-start = (bf16[2048,1024]{1,0:T(8,128)(2,1)S(1)}, bf16[2048,1024]{1,0:T(8,128)(2,1)}, u32[]{:S(2)}) copy-start(bf16[2048,1024]{1,0:T(8,128)(2,1)} %a_ref.11) | copy-start | bytes 12582916
  2.8 1.2 copy-start.4
  4.0 22.7 %copy-start.1 = (bf16[2048,1024]{1,0:T(8,128)(2,1)S(1)}, bf16[2048,1024]{1,0:T(8,128)(2,1)}, u32[]{:S(2)}) copy-start(bf16[2048,1024]{1,0:T(8,128)(2,1)} %a_ref.11) | copy-start | bytes 12582916
  6.0 5.9 %collective-permute-start = (f16[272,128]{1,0:T(8,128)(2,1)S(1)}, f16[272,128]{1,0:T(8,128)(2,1)S(1)}, u32[]{:S(2)}, u32[]{:S(2)}) collective-permute-start(f16[272,128]{1,0:T(8,128)(2,1)S(1)} %convert_element_type.36), channel_id=1, source_target_pairs={{0,8},{8,0},{16,24},{24,16},{1,9},{9,1},{17,25},{25,17},{2,10},{10... | collective-permute-start | bytes 208904 | tf_op jit(solution)/shard_map/ppermute | solution.py:114
  9.1 7.6 %collective-permute-start.1 = (f16[272,128]{1,0:T(8,128)(2,1)S(1)}, f16[272,128]{1,0:T(8,128)(2,1)S(1)}, u32[]{:S(2)}, u32[]{:S(2)}) collective-permute-start(f16[272,128]{1,0:T(8,128)(2,1)S(1)} %convert_element_type.38), channel_id=1, source_target_pairs={{0,16},{8,24},{16,0},{24,8},{1,17},{9,25},{17,1},{25,9},{2,18},{10... | collective-permute-start | bytes 208904 | tf_op jit(solution)/shard_map/ppermute | solution.py:114
  11.8 6.3 %collective-permute-start.2 = (f16[272,128]{1,0:T(8,128)(2,1)S(1)}, f16[272,128]{1,0:T(8,128)(2,1)S(1)}, u32[]{:S(2)}, u32[]{:S(2)}) collective-permute-start(f16[272,128]{1,0:T(8,128)(2,1)S(1)} %convert_element_type.40), channel_id=1, source_target_pairs={{0,24},{8,16},{16,8},{24,0},{1,25},{9,17},{17,9},{25,1},{2,26},{10... | collective-permute-start | bytes 208904 | tf_op jit(solution)/shard_map/ppermute | solution.py:114
  18.1 4.5 %collective-permute-start.3 = (bf16[272,128]{1,0:T(8,128)(2,1)S(1)}, bf16[272,128]{1,0:T(8,128)(2,1)S(1)}, u32[]{:S(2)}, u32[]{:S(2)}) collective-permute-start(bf16[272,128]{1,0:T(8,128)(2,1)S(1)} %get-tuple-element.69.refs_0_), channel_id=1, source_target_pairs={{0,8},{8,0},{16,24},{24,16},{1,9},{9,1},{17,25},{25,17},{2,10},{10... | collective-permute-start | bytes 208904 | tf_op jit(solution)/shard_map/ppermute | solution.py:114
  18.9 6.3 %collective-permute-start.4 = (bf16[272,128]{1,0:T(8,128)(2,1)S(1)}, bf16[272,128]{1,0:T(8,128)(2,1)S(1)}, u32[]{:S(2)}, u32[]{:S(2)}) collective-permute-start(bf16[272,128]{1,0:T(8,128)(2,1)S(1)} %get-tuple-element.69.refs_0_), channel_id=1, source_target_pairs={{0,16},{8,24},{16,0},{24,8},{1,17},{9,25},{17,1},{25,9},{2,18},{10... | collective-permute-start | bytes 208904 | tf_op jit(solution)/shard_map/ppermute | solution.py:114
  20.7 6.1 %collective-permute-start.5 = (bf16[272,128]{1,0:T(8,128)(2,1)S(1)}, bf16[272,128]{1,0:T(8,128)(2,1)S(1)}, u32[]{:S(2)}, u32[]{:S(2)}) collective-permute-start(bf16[272,128]{1,0:T(8,128)(2,1)S(1)} %get-tuple-element.69.refs_0_), channel_id=1, source_target_pairs={{0,24},{8,16},{16,8},{24,0},{1,25},{9,17},{17,9},{25,1},{2,26},{10... | collective-permute-start | bytes 208904 | tf_op jit(solution)/shard_map/ppermute | solution.py:114
  28.1 25.7 %copy-start.5 = (f32[2048,128]{1,0:T(8,128)S(1)}, f32[2048,128]{1,0:T(8,128)}, u32[]{:S(2)}) copy-start(f32[2048,128]{1,0:T(8,128)} %refs_0_.1) | copy-start | bytes 3145732
  28.1 2.0 %collective-permute-start.6 = (f32[1040,128]{1,0:T(8,128)S(1)}, f32[1040,128]{1,0:T(8,128)S(1)}, u32[]{:S(2)}, u32[]{:S(2)}) collective-permute-start(f32[1040,128]{1,0:T(8,128)S(1)} %get-tuple-element.73), channel_id=1, source_target_pairs={{0,1},{1,0},{2,3},{3,2},{4,5},{5,4},{6,7},{7,6},{8,9},{9,8},{10,11... | collective-permute-start | bytes 1597448 | tf_op jit(solution)/shard_map/ppermute | solution.py:117
  30.2 6.8 %collective-permute-start.7 = (bf16[528,128]{1,0:T(8,128)(2,1)S(1)}, bf16[528,128]{1,0:T(8,128)(2,1)S(1)}, u32[]{:S(2)}, u32[]{:S(2)}) collective-permute-start(bf16[528,128]{1,0:T(8,128)(2,1)S(1)} %get-tuple-element.74.refs_0_), channel_id=1, source_target_pairs={{0,2},{1,3},{2,0},{3,1},{4,6},{5,7},{6,4},{7,5},{8,10},{9,11},{10,... | collective-permute-start | bytes 405512 | tf_op jit(solution)/shard_map/ppermute | solution.py:117
  31.7 26.5 %copy-start.6 = (f32[128]{0:T(128)S(1)}, f32[128]{0:T(128)}, u32[]{:S(2)}) copy-start(f32[128]{0:T(128)} %param.5) | copy-start | bytes 1540
  31.7 5.3 %collective-permute-start.8 = (bf16[512,128]{1,0:T(8,128)(2,1)S(1)}, bf16[512,128]{1,0:T(8,128)(2,1)S(1)}, u32[]{:S(2)}, u32[]{:S(2)}) collective-permute-start(bf16[512,128]{1,0:T(8,128)(2,1)S(1)} %get-tuple-element.75.refs_1_), channel_id=1, source_target_pairs={{0,4},{1,5},{2,6},{3,7},{4,0},{5,1},{6,2},{7,3},{8,12},{9,13},{10,... | collective-permute-start | bytes 393224 | tf_op jit(solution)/shard_map/ppermute | solution.py:117
  37.1 6.6 %collective-permute-start.9 = (bf16[528,128]{1,0:T(8,128)(2,1)S(1)}, bf16[528,128]{1,0:T(8,128)(2,1)S(1)}, u32[]{:S(2)}, u32[]{:S(2)}) collective-permute-start(bf16[528,128]{1,0:T(8,128)(2,1)S(1)} %get-tuple-element.76.refs_0_), channel_id=1, source_target_pairs={{0,4},{1,5},{2,6},{3,7},{4,0},{5,1},{6,2},{7,3},{8,12},{9,13},{10,... | collective-permute-start | bytes 405512 | tf_op jit(solution)/shard_map/ppermute | solution.py:117
  38.7 5.0 %collective-permute-start.10 = (bf16[512,128]{1,0:T(8,128)(2,1)S(1)}, bf16[512,128]{1,0:T(8,128)(2,1)S(1)}, u32[]{:S(2)}, u32[]{:S(2)}) collective-permute-start(bf16[512,128]{1,0:T(8,128)(2,1)S(1)} %get-tuple-element.77.refs_1_), channel_id=1, source_target_pairs={{0,2},{1,3},{2,0},{3,1},{4,6},{5,7},{6,4},{7,5},{8,10},{9,11},{10,... | collective-permute-start | bytes 393224 | tf_op jit(solution)/shard_map/ppermute | solution.py:117
  44.4 1.5 %collective-permute-start.11 = (bf16[1040,128]{1,0:T(8,128)(2,1)S(1)}, bf16[1040,128]{1,0:T(8,128)(2,1)S(1)}, u32[]{:S(2)}, u32[]{:S(2)}) collective-permute-start(bf16[1040,128]{1,0:T(8,128)(2,1)S(1)} %get-tuple-element.79.refs_0_), channel_id=1, source_target_pairs={{0,1},{1,0},{2,3},{3,2},{4,5},{5,4},{6,7},{7,6},{8,9},{9,8},{10,11... | collective-permute-start | bytes 798728 | tf_op jit(solution)/shard_map/ppermute | solution.py:117
  45.9 2.2 %copy-start.2 = (bf16[2048,1024]{1,0:T(8,128)(2,1)S(1)}, bf16[2048,1024]{1,0:T(8,128)(2,1)}, u32[]{:S(2)}) copy-start(bf16[2048,1024]{1,0:T(8,128)(2,1)} %a_ref.11) | copy-start | bytes 12582916
  48.1 19.7 %copy-start.3 = (bf16[2048,1024]{1,0:T(8,128)(2,1)S(1)}, bf16[2048,1024]{1,0:T(8,128)(2,1)}, u32[]{:S(2)}) copy-start(bf16[2048,1024]{1,0:T(8,128)(2,1)} %a_ref.11) | copy-start | bytes 12582916
  49.1 5.6 %collective-permute-start.12 = (f16[272,128]{1,0:T(8,128)(2,1)S(1)}, f16[272,128]{1,0:T(8,128)(2,1)S(1)}, u32[]{:S(2)}, u32[]{:S(2)}) collective-permute-start(f16[272,128]{1,0:T(8,128)(2,1)S(1)} %convert_element_type.42), channel_id=1, source_target_pairs={{0,8},{8,0},{16,24},{24,16},{1,9},{9,1},{17,25},{25,17},{2,10},{10... | collective-permute-start | bytes 208904 | tf_op jit(solution)/shard_map/ppermute | solution.py:114
  49.2 7.9 %collective-permute-start.13 = (f16[272,128]{1,0:T(8,128)(2,1)S(1)}, f16[272,128]{1,0:T(8,128)(2,1)S(1)}, u32[]{:S(2)}, u32[]{:S(2)}) collective-permute-start(f16[272,128]{1,0:T(8,128)(2,1)S(1)} %convert_element_type.44), channel_id=1, source_target_pairs={{0,16},{8,24},{16,0},{24,8},{1,17},{9,25},{17,1},{25,9},{2,18},{10... | collective-permute-start | bytes 208904 | tf_op jit(solution)/shard_map/ppermute | solution.py:114
  51.9 6.3 %collective-permute-start.14 = (f16[272,128]{1,0:T(8,128)(2,1)S(1)}, f16[272,128]{1,0:T(8,128)(2,1)S(1)}, u32[]{:S(2)}, u32[]{:S(2)}) collective-permute-start(f16[272,128]{1,0:T(8,128)(2,1)S(1)} %convert_element_type.46), channel_id=1, source_target_pairs={{0,24},{8,16},{16,8},{24,0},{1,25},{9,17},{17,9},{25,1},{2,26},{10... | collective-permute-start | bytes 208904 | tf_op jit(solution)/shard_map/ppermute | solution.py:114
  58.4 4.5 %collective-permute-start.15 = (bf16[272,128]{1,0:T(8,128)(2,1)S(1)}, bf16[272,128]{1,0:T(8,128)(2,1)S(1)}, u32[]{:S(2)}, u32[]{:S(2)}) collective-permute-start(bf16[272,128]{1,0:T(8,128)(2,1)S(1)} %get-tuple-element.89.refs_0_), channel_id=1, source_target_pairs={{0,8},{8,0},{16,24},{24,16},{1,9},{9,1},{17,25},{25,17},{2,10},{10... | collective-permute-start | bytes 208904 | tf_op jit(solution)/shard_map/ppermute | solution.py:114
  59.8 8.0 %collective-permute-start.16 = (bf16[272,128]{1,0:T(8,128)(2,1)S(1)}, bf16[272,128]{1,0:T(8,128)(2,1)S(1)}, u32[]{:S(2)}, u32[]{:S(2)}) collective-permute-start(bf16[272,128]{1,0:T(8,128)(2,1)S(1)} %get-tuple-element.89.refs_0_), channel_id=1, source_target_pairs={{0,16},{8,24},{16,0},{24,8},{1,17},{9,25},{17,1},{25,9},{2,18},{10... | collective-permute-start | bytes 208904 | tf_op jit(solution)/shard_map/ppermute | solution.py:114
  61.5 6.3 %collective-permute-start.17 = (bf16[272,128]{1,0:T(8,128)(2,1)S(1)}, bf16[272,128]{1,0:T(8,128)(2,1)S(1)}, u32[]{:S(2)}, u32[]{:S(2)}) collective-permute-start(bf16[272,128]{1,0:T(8,128)(2,1)S(1)} %get-tuple-element.89.refs_0_), channel_id=1, source_target_pairs={{0,24},{8,16},{16,8},{24,0},{1,25},{9,17},{17,9},{25,1},{2,26},{10... | collective-permute-start | bytes 208904 | tf_op jit(solution)/shard_map/ppermute | solution.py:114
  69.1 2.0 %collective-permute-start.18 = (f32[1040,128]{1,0:T(8,128)S(1)}, f32[1040,128]{1,0:T(8,128)S(1)}, u32[]{:S(2)}, u32[]{:S(2)}) collective-permute-start(f32[1040,128]{1,0:T(8,128)S(1)} %get-tuple-element.93), channel_id=1, source_target_pairs={{0,1},{1,0},{2,3},{3,2},{4,5},{5,4},{6,7},{7,6},{8,9},{9,8},{10,11... | collective-permute-start | bytes 1597448 | tf_op jit(solution)/shard_map/ppermute | solution.py:117
  71.2 5.9 %collective-permute-start.19 = (bf16[528,128]{1,0:T(8,128)(2,1)S(1)}, bf16[528,128]{1,0:T(8,128)(2,1)S(1)}, u32[]{:S(2)}, u32[]{:S(2)}) collective-permute-start(bf16[528,128]{1,0:T(8,128)(2,1)S(1)} %get-tuple-element.94.refs_0_), channel_id=1, source_target_pairs={{0,2},{1,3},{2,0},{3,1},{4,6},{5,7},{6,4},{7,5},{8,10},{9,11},{10,... | collective-permute-start | bytes 405512 | tf_op jit(solution)/shard_map/ppermute | solution.py:117
  71.8 5.3 %collective-permute-start.20 = (bf16[512,128]{1,0:T(8,128)(2,1)S(1)}, bf16[512,128]{1,0:T(8,128)(2,1)S(1)}, u32[]{:S(2)}, u32[]{:S(2)}) collective-permute-start(bf16[512,128]{1,0:T(8,128)(2,1)S(1)} %get-tuple-element.95.refs_1_), channel_id=1, source_target_pairs={{0,4},{1,5},{2,6},{3,7},{4,0},{5,1},{6,2},{7,3},{8,12},{9,13},{10,... | collective-permute-start | bytes 393224 | tf_op jit(solution)/shard_map/ppermute | solution.py:117
  77.1 5.6 %collective-permute-start.21 = (bf16[528,128]{1,0:T(8,128)(2,1)S(1)}, bf16[528,128]{1,0:T(8,128)(2,1)S(1)}, u32[]{:S(2)}, u32[]{:S(2)}) collective-permute-start(bf16[528,128]{1,0:T(8,128)(2,1)S(1)} %get-tuple-element.96.refs_0_), channel_id=1, source_target_pairs={{0,4},{1,5},{2,6},{3,7},{4,0},{5,1},{6,2},{7,3},{8,12},{9,13},{10,... | collective-permute-start | bytes 405512 | tf_op jit(solution)/shard_map/ppermute | solution.py:117
  77.7 5.0 %collective-permute-start.22 = (bf16[512,128]{1,0:T(8,128)(2,1)S(1)}, bf16[512,128]{1,0:T(8,128)(2,1)S(1)}, u32[]{:S(2)}, u32[]{:S(2)}) collective-permute-start(bf16[512,128]{1,0:T(8,128)(2,1)S(1)} %get-tuple-element.97.refs_1_), channel_id=1, source_target_pairs={{0,2},{1,3},{2,0},{3,1},{4,6},{5,7},{6,4},{7,5},{8,10},{9,11},{10,... | collective-permute-start | bytes 393224 | tf_op jit(solution)/shard_map/ppermute | solution.py:117
  83.5 1.5 %collective-permute-start.23 = (bf16[1040,128]{1,0:T(8,128)(2,1)S(1)}, bf16[1040,128]{1,0:T(8,128)(2,1)S(1)}, u32[]{:S(2)}, u32[]{:S(2)}) collective-permute-start(bf16[1040,128]{1,0:T(8,128)(2,1)S(1)} %get-tuple-element.99.refs_0_), channel_id=1, source_target_pairs={{0,1},{1,0},{2,3},{3,2},{4,5},{5,4},{6,7},{7,6},{8,9},{9,8},{10,11... | collective-permute-start | bytes 798728 | tf_op jit(solution)/shard_map/ppermute | solution.py:117
  86.0 4.5 %collective-permute-start.24 = (bf16[272,128]{1,0:T(8,128)(2,1)S(1)}, bf16[272,128]{1,0:T(8,128)(2,1)S(1)}, u32[]{:S(2)}, u32[]{:S(2)}) collective-permute-start(bf16[272,128]{1,0:T(8,128)(2,1)S(1)} %get-tuple-element.102), channel_id=1, source_target_pairs={{0,8},{8,0},{16,24},{24,16},{1,9},{9,1},{17,25},{25,17},{2,10},{10... | collective-permute-start | bytes 208904 | tf_op jit(solution)/shard_map/ppermute | solution.py:114
  87.4 8.5 %collective-permute-start.25 = (bf16[272,128]{1,0:T(8,128)(2,1)S(1)}, bf16[272,128]{1,0:T(8,128)(2,1)S(1)}, u32[]{:S(2)}, u32[]{:S(2)}) collective-permute-start(bf16[272,128]{1,0:T(8,128)(2,1)S(1)} %get-tuple-element.103), channel_id=1, source_target_pairs={{0,16},{8,24},{16,0},{24,8},{1,17},{9,25},{17,1},{25,9},{2,18},{10... | collective-permute-start | bytes 208904 | tf_op jit(solution)/shard_map/ppermute | solution.py:114
  88.5 7.3 %collective-permute-start.26 = (bf16[272,128]{1,0:T(8,128)(2,1)S(1)}, bf16[272,128]{1,0:T(8,128)(2,1)S(1)}, u32[]{:S(2)}, u32[]{:S(2)}) collective-permute-start(bf16[272,128]{1,0:T(8,128)(2,1)S(1)} %get-tuple-element.104), channel_id=1, source_target_pairs={{0,24},{8,16},{16,8},{24,0},{1,25},{9,17},{17,9},{25,1},{2,26},{10... | collective-permute-start | bytes 208904 | tf_op jit(solution)/shard_map/ppermute | solution.py:114
  96.0 4.5 %collective-permute-start.27 = (bf16[272,128]{1,0:T(8,128)(2,1)S(1)}, bf16[272,128]{1,0:T(8,128)(2,1)S(1)}, u32[]{:S(2)}, u32[]{:S(2)}) collective-permute-start(bf16[272,128]{1,0:T(8,128)(2,1)S(1)} %get-tuple-element.111.refs_0_), channel_id=1, source_target_pairs={{0,8},{8,0},{16,24},{24,16},{1,9},{9,1},{17,25},{25,17},{2,10},{10... | collective-permute-start | bytes 208904 | tf_op jit(solution)/shard_map/ppermute | solution.py:114
  97.5 7.9 %collective-permute-start.28 = (bf16[272,128]{1,0:T(8,128)(2,1)S(1)}, bf16[272,128]{1,0:T(8,128)(2,1)S(1)}, u32[]{:S(2)}, u32[]{:S(2)}) collective-permute-start(bf16[272,128]{1,0:T(8,128)(2,1)S(1)} %get-tuple-element.111.refs_0_), channel_id=1, source_target_pairs={{0,16},{8,24},{16,0},{24,8},{1,17},{9,25},{17,1},{25,9},{2,18},{10... | collective-permute-start | bytes 208904 | tf_op jit(solution)/shard_map/ppermute | solution.py:114
  98.5 6.8 %collective-permute-start.29 = (bf16[272,128]{1,0:T(8,128)(2,1)S(1)}, bf16[272,128]{1,0:T(8,128)(2,1)S(1)}, u32[]{:S(2)}, u32[]{:S(2)}) collective-permute-start(bf16[272,128]{1,0:T(8,128)(2,1)S(1)} %get-tuple-element.111.refs_0_), channel_id=1, source_target_pairs={{0,24},{8,16},{16,8},{24,0},{1,25},{9,17},{17,9},{25,1},{2,26},{10... | collective-permute-start | bytes 208904 | tf_op jit(solution)/shard_map/ppermute | solution.py:114
  106.6 2.0 %collective-permute-start.30 = (f32[1040,128]{1,0:T(8,128)S(1)}, f32[1040,128]{1,0:T(8,128)S(1)}, u32[]{:S(2)}, u32[]{:S(2)}) collective-permute-start(f32[1040,128]{1,0:T(8,128)S(1)} %get-tuple-element.115), channel_id=1, source_target_pairs={{0,1},{1,0},{2,3},{3,2},{4,5},{5,4},{6,7},{7,6},{8,9},{9,8},{10,11... | collective-permute-start | bytes 1597448 | tf_op jit(solution)/shard_map/ppermute | solution.py:117
  108.7 6.8 %collective-permute-start.31 = (bf16[528,128]{1,0:T(8,128)(2,1)S(1)}, bf16[528,128]{1,0:T(8,128)(2,1)S(1)}, u32[]{:S(2)}, u32[]{:S(2)}) collective-permute-start(bf16[528,128]{1,0:T(8,128)(2,1)S(1)} %get-tuple-element.116.refs_0_), channel_id=1, source_target_pairs={{0,2},{1,3},{2,0},{3,1},{4,6},{5,7},{6,4},{7,5},{8,10},{9,11},{10,... | collective-permute-start | bytes 405512 | tf_op jit(solution)/shard_map/ppermute | solution.py:117
  110.3 5.3 %collective-permute-start.32 = (bf16[512,128]{1,0:T(8,128)(2,1)S(1)}, bf16[512,128]{1,0:T(8,128)(2,1)S(1)}, u32[]{:S(2)}, u32[]{:S(2)}) collective-permute-start(bf16[512,128]{1,0:T(8,128)(2,1)S(1)} %get-tuple-element.117.refs_1_), channel_id=1, source_target_pairs={{0,4},{1,5},{2,6},{3,7},{4,0},{5,1},{6,2},{7,3},{8,12},{9,13},{10,... | collective-permute-start | bytes 393224 | tf_op jit(solution)/shard_map/ppermute | solution.py:117
  115.6 6.6 %collective-permute-start.33 = (bf16[528,128]{1,0:T(8,128)(2,1)S(1)}, bf16[528,128]{1,0:T(8,128)(2,1)S(1)}, u32[]{:S(2)}, u32[]{:S(2)}) collective-permute-start(bf16[528,128]{1,0:T(8,128)(2,1)S(1)} %get-tuple-element.118.refs_0_), channel_id=1, source_target_pairs={{0,4},{1,5},{2,6},{3,7},{4,0},{5,1},{6,2},{7,3},{8,12},{9,13},{10,... | collective-permute-start | bytes 405512 | tf_op jit(solution)/shard_map/ppermute | solution.py:117
  117.2 5.0 %collective-permute-start.34 = (bf16[512,128]{1,0:T(8,128)(2,1)S(1)}, bf16[512,128]{1,0:T(8,128)(2,1)S(1)}, u32[]{:S(2)}, u32[]{:S(2)}) collective-permute-start(bf16[512,128]{1,0:T(8,128)(2,1)S(1)} %get-tuple-element.119.refs_1_), channel_id=1, source_target_pairs={{0,2},{1,3},{2,0},{3,1},{4,6},{5,7},{6,4},{7,5},{8,10},{9,11},{10,... | collective-permute-start | bytes 393224 | tf_op jit(solution)/shard_map/ppermute | solution.py:117
  117.7 11.7 %collective-permute-start.40 = (f32[1024,128]{1,0:T(8,128)S(1)}, f32[1024,128]{1,0:T(8,128)S(1)}, u32[]{:S(2)}, u32[]{:S(2)}) collective-permute-start(f32[1024,128]{1,0:T(8,128)S(1)} %get-tuple-element.125.refs_9_), channel_id=1, source_target_pairs={{0,1},{1,0},{2,3},{3,2},{4,5},{5,4},{6,7},{7,6},{8,9},{9,8},{10,11... | collective-permute-start | bytes 1572872 | tf_op jit(solution)/shard_map/ppermute | solution.py:117
  123.1 9.8 %collective-permute-start.39 = (f32[1024,128]{1,0:T(8,128)S(1)}, f32[1024,128]{1,0:T(8,128)S(1)}, u32[]{:S(2)}, u32[]{:S(2)}) collective-permute-start(f32[1024,128]{1,0:T(8,128)S(1)} %get-tuple-element.124.refs_7_), channel_id=1, source_target_pairs={{0,1},{1,0},{2,3},{3,2},{4,5},{5,4},{6,7},{7,6},{8,9},{9,8},{10,11... | collective-permute-start | bytes 1572872 | tf_op jit(solution)/shard_map/ppermute | solution.py:117
  123.1 1.9 %collective-permute-start.35 = (f32[8,128]{1,0:T(8,128)S(1)}, f32[8,128]{1,0:T(8,128)S(1)}, u32[]{:S(2)}, u32[]{:S(2)}) collective-permute-start(f32[8,128]{1,0:T(8,128)S(1)} %get-tuple-element.121.own_ref), channel_id=1, source_target_pairs={{0,1},{1,0},{2,3},{3,2},{4,5},{5,4},{6,7},{7,6},{8,9},{9,8},{10,11... | collective-permute-start | bytes 12296 | tf_op jit(solution)/shard_map/ppermute | solution.py:117
  125.0 4.4 %collective-permute-start.36 = (f32[8,128]{1,0:T(8,128)S(1)}, f32[8,128]{1,0:T(8,128)S(1)}, u32[]{:S(2)}, u32[]{:S(2)}) collective-permute-start(f32[8,128]{1,0:T(8,128)S(1)} %shard_map.68.refs_0_), channel_id=1, source_target_pairs={{0,8},{8,0},{16,24},{24,16},{1,9},{9,1},{17,25},{25,17},{2,10},{10... | collective-permute-start | bytes 12296 | tf_op jit(solution)/shard_map/ppermute | solution.py:114
  126.3 4.5 %collective-permute-start.37 = (f32[8,128]{1,0:T(8,128)S(1)}, f32[8,128]{1,0:T(8,128)S(1)}, u32[]{:S(2)}, u32[]{:S(2)}) collective-permute-start(f32[8,128]{1,0:T(8,128)S(1)} %shard_map.68.refs_0_), channel_id=1, source_target_pairs={{0,16},{8,24},{16,0},{24,8},{1,17},{9,25},{17,1},{25,9},{2,18},{10... | collective-permute-start | bytes 12296 | tf_op jit(solution)/shard_map/ppermute | solution.py:114
  127.5 5.4 %collective-permute-start.38 = (f32[8,128]{1,0:T(8,128)S(1)}, f32[8,128]{1,0:T(8,128)S(1)}, u32[]{:S(2)}, u32[]{:S(2)}) collective-permute-start(f32[8,128]{1,0:T(8,128)S(1)} %shard_map.68.refs_0_), channel_id=1, source_target_pairs={{0,24},{8,16},{16,8},{24,0},{1,25},{9,17},{17,9},{25,1},{2,26},{10... | collective-permute-start | bytes 12296 | tf_op jit(solution)/shard_map/ppermute | solution.py:114

commit v4 on v3

--- a/solution.py
+++ b/solution.py
@@ -13,6 +13,8 @@
 ROW_WIRE = (F16, F16, BF16)
 CORE_WIRE = (F32, F32, F32)
 CHIP_WIRE = ((BF16, BF16), (BF16, BF16), (BF16, BF16))
+FIRST_PIECE = 9
+ROW_ORDER = 1
 LIMIT = 24 * 1024 * 1024
 
 
@@ -103,7 +105,11 @@
     outs = targets.shape[1]
     feat_share = feats // n_row
     half = tokens // 2
-    piece = half // levels
+    piece_rows = [half // levels] * levels
+    if levels == 2:
+        piece_rows = [half * FIRST_PIECE // 16, half - half * FIRST_PIECE // 16]
+    piece_starts = [sum(piece_rows[:index]) for index in range(levels)]
+    row_steps = list(range(1, n_row))[::ROW_ORDER]
     block = 256
     ridge = ridge.reshape(1, outs)
     scalar = ((8, outs), F32)
@@ -123,53 +129,84 @@
         core = (lax.axis_index("group") % 2) ^ core_step
         return pl.multiple_of(core * half, half)
 
-    def backward(wire, *blocks):
-        first = len(blocks) == 1
-        wide = 2 * outs if first else outs
-
-        def kernel(a_ref, *refs):
-            ins = refs[: len(blocks)]
-            own_ref, delta_ref, *msg_refs, vec, prod = refs[len(blocks) :]
-            if first:
-                whole = ins[0][...]
+    def cut(wire, prod, delta, own_ref, msg_refs):
+        own_ref[...] = prod[pl.ds(row_place(0), feat_share), :]
+        if wire == F16:
+            exponent = exponent_of(jnp.max(jnp.abs(prod[...]), axis=0, keepdims=True))
+            factor = jnp.exp2(-exponent)
+        for step, ref in zip(row_steps, msg_refs):
+            part = prod[pl.ds(row_place(step), feat_share), :]
+            if wire == F16:
+                ref[pl.ds(0, feat_share), :] = part * factor
+                put_scaled(ref, exponent, delta)
+            else:
+                ref[pl.ds(0, feat_share), :] = part.astype(wire)
+                put_rows(ref, delta)
+
+    def cut_shapes(wire):
+        return [((feat_share + PAD, outs), F32 if wire == F16 else wire)] * (n_row - 1)
+
+    def scattered(wire, sends):
+        got = {step: over_row(step, send.astype(wire)) for step, send in zip(row_steps, sends)}
+        got = [got[step] for step in range(1, n_row)]
+        return [send.astype(F32) if wire == F16 else send for send in got]
+
+    def backward_first(wire):
+        def split(t_ref, turned_ref, r_out):
+            for start in range(0, tokens, block):
+                whole = t_ref[start : start + block, :]
                 high = whole.astype(BF16)
-                vec[:, 0:outs] = high
-                vec[:, outs:wide] = (whole - high.astype(F32)).astype(BF16)
-                delta = jnp.zeros((1, outs), F32)
-            else:
-                for core_step, ref in enumerate(ins):
-                    vec[pl.ds(token_place(core_step), half), :] = body_of(ref)
-                delta = get_row(ins[0]) + get_row(ins[1])
+                turned_ref[0:outs, start : start + block] = high.T
+                turned_ref[outs : 2 * outs, start : start + block] = (whole - high.astype(F32)).astype(BF16).T
+            r_out[...] = t_ref[pl.ds(token_place(0), half), :]
+
+        def product(a_ref, turned_ref, own_ref, *refs):
+            *msg_refs, prod = refs
+            for start in range(0, feats, block):
+                cols = slice(start, start + block)
+                part = jnp.dot(turned_ref[...], a_ref[:, cols], preferred_element_type=F32)
+                prod[cols, :] = (part[0:outs] + part[outs : 2 * outs]).T
+            cut(wire, prod, jnp.zeros((1, outs), F32), own_ref, msg_refs)
+
+        turned, residual = call(split, [((2 * outs, tokens), BF16), token_rows], [targets])
+        own, *sends = call(
+            product,
+            [feature_rows] + cut_shapes(wire),
+            [states, turned],
+            [pltpu.VMEM((feats, outs), F32)],
+        )
+        return residual, own, scattered(wire, sends)
+
+    def backward(wire, mine, theirs):
+        def half_product(a_ref, ref, core_step, cols):
+            return jnp.dot(
+                body_of(ref).T,
+                a_ref[pl.ds(token_place(core_step), half), cols],
+                preferred_element_type=F32,
+            )
+
+        def first_half(a_ref, mine_ref, part_ref):
+            for start in range(0, feats, block):
+                cols = slice(start, start + block)
+                part_ref[:, cols] = half_product(a_ref, mine_ref, 0, cols)
+
+        def second_half(a_ref, mine_ref, theirs_ref, part_ref, own_ref, delta_ref, *refs):
+            *msg_refs, prod = refs
+            delta = get_row(mine_ref) + get_row(theirs_ref)
             spread(delta_ref, delta)
-            turned = vec[...].T
             for start in range(0, feats, block):
-                part = jnp.dot(turned, a_ref[:, start : start + block], preferred_element_type=F32)
-                if first:
-                    part = part[0:outs] + part[outs:wide]
-                prod[start : start + block, :] = part.T
-            own_ref[...] = prod[pl.ds(row_place(0), feat_share), :]
-            if scaled:
-                exponent = exponent_of(jnp.max(jnp.abs(prod[...]), axis=0, keepdims=True))
-                factor = jnp.exp2(-exponent)
-            for step, ref in enumerate(msg_refs, 1):
-                part = prod[pl.ds(row_place(step), feat_share), :]
-                if scaled:
-                    ref[pl.ds(0, feat_share), :] = part * factor
-                    put_scaled(ref, exponent, delta)
-                else:
-                    ref[pl.ds(0, feat_share), :] = part.astype(wire)
-                    put_rows(ref, delta)
-
-        scaled = wire == F16
-        msgs = [((feat_share + PAD, outs), F32 if scaled else wire)] * (n_row - 1)
+                cols = slice(start, start + block)
+                prod[cols, :] = (part_ref[:, cols] + half_product(a_ref, theirs_ref, 1, cols)).T
+            cut(wire, prod, delta, own_ref, msg_refs)
+
+        (part,) = call(first_half, [((outs, feats), F32)], [states, mine])
         own, delta, *sends = call(
-            kernel,
-            [feature_rows, scalar] + msgs,
-            (states,) + blocks,
-            [pltpu.VMEM((tokens, wide), BF16), pltpu.VMEM((feats, outs), F32)],
+            second_half,
+            [feature_rows, scalar] + cut_shapes(wire),
+            [states, mine, theirs, part],
+            [pltpu.VMEM((feats, outs), F32)],
         )
-        got = [over_row(step, send.astype(wire)) for step, send in enumerate(sends, 1)]
-        return own, delta, [send.astype(F32) if scaled else send for send in got]
+        return own, delta, scattered(wire, sends)
 
     def begin(own, got):
         def kernel(own_ref, *refs):
@@ -186,8 +223,8 @@
     def advance(wire, own, delta, got, gamma, dir_sq, grad, direction, image, weights, residual):
         def kernel(own_ref, delta_ref, *refs):
             ins = refs[: n_row - 1]
-            gamma_ref, sq_ref, grad_ref, dir_ref, image_ref, w_ref, r_ref, ridge_ref = refs[n_row - 1 : n_row + 7]
-            w_out, r_out, grad_out, msg_ref = refs[n_row + 7 :]
+            gamma_ref, sq_ref, grad_ref, dir_ref, image_ref, r_ref, ridge_ref = refs[n_row - 1 : n_row + 6]
+            *w_ref, w_out, r_out, grad_out, msg_ref = refs[n_row + 6 :]
             if wire == F16:
                 tails = [get_scaled(ref) for ref in ins]
             else:
@@ -202,47 +239,55 @@
             msg_ref[pl.ds(0, feat_share), :] = new.astype(BF16)
             put_rows(msg_ref, column_sum(new * new), column_sum(new * old_dir))
             grad_out[...] = new
-            w_out[...] = w_ref[...] + alpha * old_dir
+            step_taken = alpha * old_dir
+            w_out[...] = w_ref[0][...] + step_taken if w_ref else step_taken
             r_out[...] = r_ref[...] - alpha * image_ref[...]
 
         return call(
             kernel,
             [feature_rows, token_rows, feature_rows, ((feat_share + PAD, outs), BF16)],
-            [own, delta, *got, gamma, dir_sq, grad, direction, image, weights, residual, ridge],
+            [own, delta, *got, gamma, dir_sq, grad, direction, image, residual, ridge, *weights],
         )
 
     def forward(wire, msg):
-        blocks = [msg] + [over_row(step, msg) for step in range(1, n_row)]
-
-        def kernel(a_ref, *refs):
+        got = {step: over_row(step, msg) for step in row_steps}
+        blocks = [msg] + [got[step] for step in range(1, n_row)]
+
+        def half_product(a_ref, vec, core_step, ref):
+            for start in range(0, half, block):
+                part = jnp.dot(
+                    a_ref[pl.ds(pl.multiple_of(token_place(core_step) + start, block), block), :],
+                    vec[...],
+                    preferred_element_type=F32,
+                )
+                ref[start : start + block, :] = part.astype(ref.dtype)
+
+        def first_half(a_ref, *refs):
             ins = refs[:n_row]
-            own_ref, gamma_ref, cross_ref, peer_ref, vec = refs[n_row:]
+            peer_ref, gamma_ref, cross_ref, vec = refs[n_row:]
             for step, ref in enumerate(ins):
                 vec[pl.ds(row_place(step), feat_share), :] = body_of(ref)
             gamma = tree_sum([get_row(ref, 0) for ref in ins])
             cross = tree_sum([get_row(ref, 1) for ref in ins])
             spread(gamma_ref, gamma)
             spread(cross_ref, cross)
-            for core_step, ref in ((1, peer_ref), (0, own_ref)):
-                for start in range(0, half, block):
-                    part = jnp.dot(
-                        a_ref[pl.ds(pl.multiple_of(token_place(core_step) + start, block), block), :],
-                        vec[...],
-                        preferred_element_type=F32,
-                    )
-                    ref[start : start + block, :] = part.astype(ref.dtype)
+            half_product(a_ref, vec, 1, peer_ref)
             put_rows(peer_ref, gamma, cross)
 
-        own, gamma, cross, peer = call(
-            kernel,
-            [token_rows, scalar, scalar, ((half + PAD, outs), wire)],
+        def second_half(a_ref, vec, own_ref):
+            half_product(a_ref, vec, 0, own_ref)
+
+        peer, gamma, cross, vec = call(
+            first_half,
+            [((half + PAD, outs), wire), scalar, scalar, ((feats, outs), BF16)],
             [states] + blocks,
-            [pltpu.VMEM((feats, outs), BF16)],
         )
-        return own, gamma, cross, over_group(1, peer)
+        got = over_group(1, peer)
+        (own,) = call(second_half, [token_rows], [states, vec])
+        return own, gamma, cross, got
 
     def pieces(wire):
-        return [((piece + (0 if index else PAD), outs), wire) for index in range(levels)]
+        return [((rows + (0 if index else PAD), outs), wire) for index, rows in enumerate(piece_rows)]
 
     def swapped(step, sends):
         return [
@@ -252,9 +297,9 @@
     def join_cores(wire, own, gamma, cross, got):
         def kernel(own_ref, gamma_ref, cross_ref, got_ref, *msg_refs):
             for index, ref in enumerate(msg_refs):
-                place = pl.ds(index * piece, piece)
+                place = pl.ds(piece_starts[index], piece_rows[index])
                 both = own_ref[place, :] + got_ref[place, :].astype(F32)
-                ref[pl.ds(0, piece), :] = both.astype(wire)
+                ref[pl.ds(0, piece_rows[index]), :] = both.astype(wire)
             put_rows(
                 msg_refs[0],
                 gamma_ref[0:1, :] + get_row(got_ref, 0),
@@ -266,19 +311,19 @@
     def join_chips(wire, sent, got):
         def kernel(*refs):
             mine, theirs, out_refs = refs[:levels], refs[levels : 2 * levels], refs[2 * levels :]
-            for ref, own_ref, got_ref in zip(out_refs, mine, theirs):
-                place = pl.ds(0, piece)
+            for ref, own_ref, got_ref, rows in zip(out_refs, mine, theirs, piece_rows):
+                place = pl.ds(0, rows)
                 both = own_ref[place, :].astype(F32) + got_ref[place, :].astype(F32)
                 ref[place, :] = both.astype(wire)
             put_rows(out_refs[0], *[get_row(mine[0], k) + get_row(theirs[0], k) for k in range(2)])
 
         return call(kernel, pieces(wire), list(sent) + got)
 
-    def image_of(wire, sent, got, grad, before):
+    def image_of(last, sent, got, grad, before):
         def kernel(*refs):
             mine, theirs = refs[:levels], refs[levels : 2 * levels]
             grad_ref, *rest = refs[2 * levels :]
-            gamma_out, sq_out, dir_out, image_out, msg_ref, part_out = rest[-6:]
+            gamma_out, sq_out, dir_out, image_out, sum_out = rest[-5:]
             gamma, cross = [get_row(mine[0], k) + get_row(theirs[0], k) for k in range(2)]
             spread(gamma_out, gamma)
             direction = grad_ref[...]
@@ -292,26 +337,28 @@
             spread(sq_out, dir_sq)
             image_sq = jnp.zeros((1, outs), F32)
             for index, (own_ref, got_ref) in enumerate(zip(mine, theirs)):
-                place = pl.ds(index * piece, piece)
-                image = own_ref[pl.ds(0, piece), :].astype(F32) + got_ref[pl.ds(0, piece), :].astype(F32)
+                place = pl.ds(piece_starts[index], piece_rows[index])
+                there = pl.ds(0, piece_rows[index])
+                image = own_ref[there, :].astype(F32) + got_ref[there, :].astype(F32)
                 if before:
                     image = image + beta * old_image[place, :]
                 image_out[place, :] = image
-                msg_ref[place, :] = image.astype(wire)
+                if not last:
+                    sum_out[place, :] = image.astype(BF16)
                 image_sq = image_sq + column_sum(image * image)
-            put_rows(msg_ref, image_sq)
-            spread(part_out, image_sq)
+            if last:
+                spread(sum_out, image_sq)
+            else:
+                put_rows(sum_out, image_sq)
 
         return call(
             kernel,
-            [scalar, scalar, feature_rows, token_rows, ((half + PAD, outs), wire), scalar],
+            [scalar, scalar, feature_rows, token_rows, scalar if last else ((half + PAD, outs), BF16)],
             list(sent) + got + [grad, *before],
         )
 
-    core = lax.axis_index("group") % 2
-    weights = jnp.zeros((feat_share, outs), F32)
-    residual = lax.dynamic_slice_in_dim(targets, core * half, half, 0)
-    own, _, got = backward(ROW_WIRE[0], targets)
+    weights = ()
+    residual, own, got = backward_first(ROW_WIRE[0])
     grad, msg = begin(own, got)
     before = ()
     for step in range(ITERS):
@@ -322,23 +369,31 @@
             sent = join_chips(CHIP_WIRE[step][1], sent, got)
             got = swapped(level, sent)
         last = step + 1 == ITERS
-        gamma, dir_sq, direction, image, msg, part = image_of(
-            F32 if last else BF16, sent, got, grad, before
-        )
+        gamma, dir_sq, direction, image, msg = image_of(last, sent, got, grad, before)
         if not last:
             own, delta, got = backward(ROW_WIRE[step + 1], msg, over_group(1, msg))
-            weights, residual, grad, msg = advance(
+            new, residual, grad, msg = advance(
                 ROW_WIRE[step + 1], own, delta, got, gamma, dir_sq, grad, direction, image, weights, residual
             )
+            weights = (new,)
             before = (gamma, dir_sq, direction, image)
 
-    def both_cores(own_ref, got_ref, out_ref):
+    def both_cores(own_ref, got_ref, image_ref, out_ref, same_image_ref):
         out_ref[...] = own_ref[...] + got_ref[...]
 
-    (delta,) = call(both_cores, [scalar], [part, over_group(1, part)])
+    vmem, anywhere = pl.BlockSpec(memory_space=pltpu.VMEM), pl.BlockSpec(memory_space=pl.ANY)
+    delta, image = pl.pallas_call(
+        both_cores,
+        out_shape=[jax.ShapeDtypeStruct(*scalar), jax.ShapeDtypeStruct(*token_rows)],
+        in_specs=[vmem, vmem, anywhere],
+        out_specs=[vmem, anywhere],
+        input_output_aliases={2: 1},
+        compiler_params=pltpu.CompilerParams(vmem_limit_bytes=LIMIT),
+    )(msg, over_group(1, msg), image)
     other_image = over_group(1, image)
     other_residual = over_group(1, residual)
-    deltas = [delta] + [over_row(step, delta) for step in range(1, n_row)]
+    got = {step: over_row(step, delta) for step in row_steps}
+    deltas = [delta] + [got[step] for step in range(1, n_row)]
 
     def finish(*refs):
         delta_refs, refs = refs[:n_row], refs[n_row:]
@@ -352,7 +407,7 @@
     weights, residual = call(
         finish,
         [feature_rows, ((tokens, outs), F32)],
-        [*deltas, gamma, dir_sq, ridge, image, other_image, residual, other_residual, direction, weights],
+        [*deltas, gamma, dir_sq, ridge, image, other_image, residual, other_residual, direction, *weights],
     )
     return weights, residual
 

time: 134 us -> 126 us (0.940)
  waiting for transfers between devices: 68.2 us -> 62.1 us
  local copies, waits for them, and re-layouts: 5.66 us -> 3.41 us
  Pallas kernels: 12.4 us -> 10.9 us
    ppermute x20, waiting for transfers between devices: 34.8 us -> 28.7 us  [over_group(): return lax.ppermute(value, 'group', [(i, i ^ step) for i in range(n_group)])]
    unnamed x14 -> x8, local copies, waits for them, and re-layouts: 5.61 us -> 3.41 us
    pallas_call x20 -> x25, Pallas kernels: 12.4 us -> 10.9 us  [call(): pl.pallas_call(kernel, out_shape=[jax.ShapeDtypeStruct(shape, dtype) for...]
  transfers between devices with their start and end apart: 41 -> 41, of which waited for: 24 -> 24; matrix products, arithmetic and copies ran while one was open for 0% -> 0% of each run, Pallas kernels for 1% -> 2%
where the time goes in v4:
time: 126 us; the launch traced here: 125 us
  waiting for transfers between devices  62.1 us (49%)
  starting transfers between devices  47.9 us (38%)
  Pallas kernels  10.9 us (9%)
  local copies, waits for them, and re-layouts  3.41 us (3%)
    ppermute x21, waiting for transfers between devices, over_row(): return lax.ppermute(value, 'row', [(i, i ^ step) for i in range(n_row)])  33.4 us
    ppermute x21, starting transfers between devices, over_row(): return lax.ppermute(value, 'row', [(i, i ^ step) for i in range(n_row)])  32.6 us
    ppermute x20, waiting for transfers between devices, over_group(): return lax.ppermute(value, 'group', [(i, i ^ step) for i in range(n_group)])  28.7 us
    ppermute x20, starting transfers between devices, over_group(): return lax.ppermute(value, 'group', [(i, i ^ step) for i in range(n_group)])  15.3 us
    pallas_call x25, Pallas kernels, call(): pl.pallas_call(kernel, out_shape=[jax.ShapeDtypeStruct(shape, dtype) for...  10.9 us
    unnamed x8, local copies, waits for them, and re-layouts  3.41 us
  transfers between devices with their start and end apart: 41, of which 24 were waited for; matrix products, arithmetic and copies ran while one was open for 0% of the time, Pallas kernels for 2%

profile of v4, /device:TPU:0, one launch (start us, length us, event | category | flops | bytes accessed | tf_op | source)
XLA Modules:
  0.0 125.4 jit_solution(12773290826689822198)
XLA Ops:
  0.6 1.2 copy-done.2
  2.2 2.2 %copy-done = bf16[2048,1024]{1,0:T(8,128)(2,1)S(1)} copy-done((bf16[2048,1024]{1,0:T(8,128)(2,1)S(1)}, bf16[2048,1024]{1,0:T(8,128)(2,1)}, u32[]{:S(2)}) %copy-start) | copy-done | bytes 4194328
  4.4 1.4 %shard_map.51 = (f32[256,128]{1,0:T(8,128)S(1)}, f32[272,128]{1,0:T(8,128)S(1)}, f32[272,128]{1,0:T(8,128)S(1)}, f32[272,128]{1,0:T(8,128)S(1)}) custom-call(bf16[2048,1024]{1,0:T(8,128)(2,1)S(1)} %copy-done, bf16[256,2048]{1,0:T(8,128)(2,1)S(1)} %get-tuple-element.69.turned_ref), custom_call_target="tpu_custom_call" | custom-call | tf_op jit(solution)/shard_map/pallas_call | solution.py:90
  5.9 3.1 %collective-permute-start = (f16[272,128]{1,0:T(8,128)(2,1)S(1)}, f16[272,128]{1,0:T(8,128)(2,1)S(1)}, u32[]{:S(2)}, u32[]{:S(2)}) collective-permute-start(f16[272,128]{1,0:T(8,128)(2,1)S(1)} %convert_element_type.36), channel_id=1, source_target_pairs={{0,8},{8,0},{16,24},{24,16},{1,9},{9,1},{17,25},{25,17},{2,10},{10... | collective-permute-start | bytes 208904 | tf_op jit(solution)/shard_map/ppermute | solution.py:120
  9.0 2.7 %collective-permute-start.1 = (f16[272,128]{1,0:T(8,128)(2,1)S(1)}, f16[272,128]{1,0:T(8,128)(2,1)S(1)}, u32[]{:S(2)}, u32[]{:S(2)}) collective-permute-start(f16[272,128]{1,0:T(8,128)(2,1)S(1)} %convert_element_type.38), channel_id=1, source_target_pairs={{0,16},{8,24},{16,0},{24,8},{1,17},{9,25},{17,1},{25,9},{2,18},{10... | collective-permute-start | bytes 208904 | tf_op jit(solution)/shard_map/ppermute | solution.py:120
  11.8 4.8 %collective-permute-done.1 = f16[272,128]{1,0:T(8,128)(2,1)S(1)} collective-permute-done((f16[272,128]{1,0:T(8,128)(2,1)S(1)}, f16[272,128]{1,0:T(8,128)(2,1)S(1)}, u32[]{:S(2)}, u32[]{:S(2)}) %collective-permute-start.1) | collective-permute-done | bytes 69664 | tf_op jit(solution)/shard_map/ppermute | solution.py:120
  16.6 1.4 %collective-permute-done.2 = f16[272,128]{1,0:T(8,128)(2,1)S(1)} collective-permute-done((f16[272,128]{1,0:T(8,128)(2,1)S(1)}, f16[272,128]{1,0:T(8,128)(2,1)S(1)}, u32[]{:S(2)}, u32[]{:S(2)}) %collective-permute-start.2) | collective-permute-done | bytes 69664 | tf_op jit(solution)/shard_map/ppermute | solution.py:120
  18.0 0.8 collective-permute-start.3
  18.8 1.8 %collective-permute-start.4 = (bf16[272,128]{1,0:T(8,128)(2,1)S(1)}, bf16[272,128]{1,0:T(8,128)(2,1)S(1)}, u32[]{:S(2)}, u32[]{:S(2)}) collective-permute-start(bf16[272,128]{1,0:T(8,128)(2,1)S(1)} %get-tuple-element.74.refs_0_), channel_id=1, source_target_pairs={{0,16},{8,24},{16,0},{24,8},{1,17},{9,25},{17,1},{25,9},{2,18},{10... | collective-permute-start | bytes 208904 | tf_op jit(solution)/shard_map/ppermute | solution.py:120
  20.5 1.9 %collective-permute-start.5 = (bf16[272,128]{1,0:T(8,128)(2,1)S(1)}, bf16[272,128]{1,0:T(8,128)(2,1)S(1)}, u32[]{:S(2)}, u32[]{:S(2)}) collective-permute-start(bf16[272,128]{1,0:T(8,128)(2,1)S(1)} %get-tuple-element.74.refs_0_), channel_id=1, source_target_pairs={{0,24},{8,16},{16,8},{24,0},{1,25},{9,17},{17,9},{25,1},{2,26},{10... | collective-permute-start | bytes 208904 | tf_op jit(solution)/shard_map/ppermute | solution.py:120
  22.5 2.6 %collective-permute-done.4.refs_2_ = bf16[272,128]{1,0:T(8,128)(2,1)S(1)} collective-permute-done((bf16[272,128]{1,0:T(8,128)(2,1)S(1)}, bf16[272,128]{1,0:T(8,128)(2,1)S(1)}, u32[]{:S(2)}, u32[]{:S(2)}) %collective-permute-start.4) | collective-permute-done | bytes 69664 | tf_op jit(solution)/shard_map/ppermute | solution.py:120
  25.1 1.6 %collective-permute-done.5.refs_3_ = bf16[272,128]{1,0:T(8,128)(2,1)S(1)} collective-permute-done((bf16[272,128]{1,0:T(8,128)(2,1)S(1)}, bf16[272,128]{1,0:T(8,128)(2,1)S(1)}, u32[]{:S(2)}, u32[]{:S(2)}) %collective-permute-start.5) | collective-permute-done | bytes 69664 | tf_op jit(solution)/shard_map/ppermute | solution.py:120
  26.6 0.7 shard_map.53
  27.4 0.7 shard_map.54.own_ref
  28.2 1.2 collective-permute-done.6.got_ref
  29.5 1.5 %collective-permute-start.7 = (bf16[592,128]{1,0:T(8,128)(2,1)S(1)}, bf16[592,128]{1,0:T(8,128)(2,1)S(1)}, u32[]{:S(2)}, u32[]{:S(2)}) collective-permute-start(bf16[592,128]{1,0:T(8,128)(2,1)S(1)} %get-tuple-element.79.refs_0_), channel_id=1, source_target_pairs={{0,2},{1,3},{2,0},{3,1},{4,6},{5,7},{6,4},{7,5},{8,10},{9,11},{10,... | collective-permute-start | bytes 454664 | tf_op jit(solution)/shard_map/ppermute | solution.py:123
  31.0 1.5 %collective-permute-start.8 = (bf16[448,128]{1,0:T(8,128)(2,1)S(1)}, bf16[448,128]{1,0:T(8,128)(2,1)S(1)}, u32[]{:S(2)}, u32[]{:S(2)}) collective-permute-start(bf16[448,128]{1,0:T(8,128)(2,1)S(1)} %get-tuple-element.80.refs_1_), channel_id=1, source_target_pairs={{0,4},{1,5},{2,6},{3,7},{4,0},{5,1},{6,2},{7,3},{8,12},{9,13},{10,... | collective-permute-start | bytes 344072 | tf_op jit(solution)/shard_map/ppermute | solution.py:123
  32.5 3.4 %collective-permute-done.8.refs_3_ = bf16[448,128]{1,0:T(8,128)(2,1)S(1)} collective-permute-done((bf16[448,128]{1,0:T(8,128)(2,1)S(1)}, bf16[448,128]{1,0:T(8,128)(2,1)S(1)}, u32[]{:S(2)}, u32[]{:S(2)}) %collective-permute-start.8) | collective-permute-done | bytes 114720 | tf_op jit(solution)/shard_map/ppermute | solution.py:123
  36.0 1.6 %collective-permute-start.9 = (bf16[592,128]{1,0:T(8,128)(2,1)S(1)}, bf16[592,128]{1,0:T(8,128)(2,1)S(1)}, u32[]{:S(2)}, u32[]{:S(2)}) collective-permute-start(bf16[592,128]{1,0:T(8,128)(2,1)S(1)} %get-tuple-element.81.refs_0_), channel_id=1, source_target_pairs={{0,4},{1,5},{2,6},{3,7},{4,0},{5,1},{6,2},{7,3},{8,12},{9,13},{10,... | collective-permute-start | bytes 454664 | tf_op jit(solution)/shard_map/ppermute | solution.py:123
  37.6 1.1 collective-permute-start.10
  38.6 3.7 %collective-permute-done.10.refs_3_ = bf16[448,128]{1,0:T(8,128)(2,1)S(1)} collective-permute-done((bf16[448,128]{1,0:T(8,128)(2,1)S(1)}, bf16[448,128]{1,0:T(8,128)(2,1)S(1)}, u32[]{:S(2)}, u32[]{:S(2)}) %collective-permute-start.10) | collective-permute-done | bytes 114720 | tf_op jit(solution)/shard_map/ppermute | solution.py:123
  43.1 1.0 collective-permute-done.11.theirs_ref
  44.9 2.7 %collective-permute-start.13 = (f16[272,128]{1,0:T(8,128)(2,1)S(1)}, f16[272,128]{1,0:T(8,128)(2,1)S(1)}, u32[]{:S(2)}, u32[]{:S(2)}) collective-permute-start(f16[272,128]{1,0:T(8,128)(2,1)S(1)} %convert_element_type.44), channel_id=1, source_target_pairs={{0,16},{8,24},{16,0},{24,8},{1,17},{9,25},{17,1},{25,9},{2,18},{10... | collective-permute-start | bytes 208904 | tf_op jit(solution)/shard_map/ppermute | solution.py:120
  47.6 1.8 %collective-permute-start.14 = (f16[272,128]{1,0:T(8,128)(2,1)S(1)}, f16[272,128]{1,0:T(8,128)(2,1)S(1)}, u32[]{:S(2)}, u32[]{:S(2)}) collective-permute-start(f16[272,128]{1,0:T(8,128)(2,1)S(1)} %convert_element_type.46), channel_id=1, source_target_pairs={{0,24},{8,16},{16,8},{24,0},{1,25},{9,17},{17,9},{25,1},{2,26},{10... | collective-permute-start | bytes 208904 | tf_op jit(solution)/shard_map/ppermute | solution.py:120
  49.4 0.9 collective-permute-done.12
  50.4 2.4 %collective-permute-done.13 = f16[272,128]{1,0:T(8,128)(2,1)S(1)} collective-permute-done((f16[272,128]{1,0:T(8,128)(2,1)S(1)}, f16[272,128]{1,0:T(8,128)(2,1)S(1)}, u32[]{:S(2)}, u32[]{:S(2)}) %collective-permute-start.13) | collective-permute-done | bytes 69664 | tf_op jit(solution)/shard_map/ppermute | solution.py:120
  52.8 1.1 collective-permute-done.14
  54.0 1.4 %collective-permute-start.15 = (bf16[272,128]{1,0:T(8,128)(2,1)S(1)}, bf16[272,128]{1,0:T(8,128)(2,1)S(1)}, u32[]{:S(2)}, u32[]{:S(2)}) collective-permute-start(bf16[272,128]{1,0:T(8,128)(2,1)S(1)} %get-tuple-element.95.refs_0_), channel_id=1, source_target_pairs={{0,8},{8,0},{16,24},{24,16},{1,9},{9,1},{17,25},{25,17},{2,10},{10... | collective-permute-start | bytes 208904 | tf_op jit(solution)/shard_map/ppermute | solution.py:120
  55.4 1.7 %collective-permute-start.16 = (bf16[272,128]{1,0:T(8,128)(2,1)S(1)}, bf16[272,128]{1,0:T(8,128)(2,1)S(1)}, u32[]{:S(2)}, u32[]{:S(2)}) collective-permute-start(bf16[272,128]{1,0:T(8,128)(2,1)S(1)} %get-tuple-element.95.refs_0_), channel_id=1, source_target_pairs={{0,16},{8,24},{16,0},{24,8},{1,17},{9,25},{17,1},{25,9},{2,18},{10... | collective-permute-start | bytes 208904 | tf_op jit(solution)/shard_map/ppermute | solution.py:120
  57.1 1.3 %collective-permute-start.17 = (bf16[272,128]{1,0:T(8,128)(2,1)S(1)}, bf16[272,128]{1,0:T(8,128)(2,1)S(1)}, u32[]{:S(2)}, u32[]{:S(2)}) collective-permute-start(bf16[272,128]{1,0:T(8,128)(2,1)S(1)} %get-tuple-element.95.refs_0_), channel_id=1, source_target_pairs={{0,24},{8,16},{16,8},{24,0},{1,25},{9,17},{17,9},{25,1},{2,26},{10... | collective-permute-start | bytes 208904 | tf_op jit(solution)/shard_map/ppermute | solution.py:120
  58.5 4.9 %collective-permute-done.16.refs_2_ = bf16[272,128]{1,0:T(8,128)(2,1)S(1)} collective-permute-done((bf16[272,128]{1,0:T(8,128)(2,1)S(1)}, bf16[272,128]{1,0:T(8,128)(2,1)S(1)}, u32[]{:S(2)}, u32[]{:S(2)}) %collective-permute-start.16) | collective-permute-done | bytes 69664 | tf_op jit(solution)/shard_map/ppermute | solution.py:120
  63.4 0.7 shard_map.61
  64.2 0.7 shard_map.62.own_ref
  64.9 1.2 collective-permute-done.18.got_ref
  66.3 1.1 collective-permute-start.19
  67.9 4.4 %collective-permute-done.20.refs_3_ = bf16[448,128]{1,0:T(8,128)(2,1)S(1)} collective-permute-done((bf16[448,128]{1,0:T(8,128)(2,1)S(1)}, bf16[448,128]{1,0:T(8,128)(2,1)S(1)}, u32[]{:S(2)}, u32[]{:S(2)}) %collective-permute-start.20) | collective-permute-done | bytes 114720 | tf_op jit(solution)/shard_map/ppermute | solution.py:123
  72.9 1.1 collective-permute-start.22
  74.0 3.7 %collective-permute-done.22.refs_3_ = bf16[448,128]{1,0:T(8,128)(2,1)S(1)} collective-permute-done((bf16[448,128]{1,0:T(8,128)(2,1)S(1)}, bf16[448,128]{1,0:T(8,128)(2,1)S(1)}, u32[]{:S(2)}, u32[]{:S(2)}) %collective-permute-start.22) | collective-permute-done | bytes 114720 | tf_op jit(solution)/shard_map/ppermute | solution.py:123
  78.5 1.0 collective-permute-done.23.theirs_ref
  79.5 0.6 shard_map.67
  80.2 1.4 %collective-permute-start.24 = (bf16[272,128]{1,0:T(8,128)(2,1)S(1)}, bf16[272,128]{1,0:T(8,128)(2,1)S(1)}, u32[]{:S(2)}, u32[]{:S(2)}) collective-permute-start(bf16[272,128]{1,0:T(8,128)(2,1)S(1)} %get-tuple-element.108), channel_id=1, source_target_pairs={{0,8},{8,0},{16,24},{24,16},{1,9},{9,1},{17,25},{25,17},{2,10},{10... | collective-permute-start | bytes 208904 | tf_op jit(solution)/shard_map/ppermute | solution.py:120
  81.5 1.1 collective-permute-start.25
  82.7 2.0 %collective-permute-start.26 = (bf16[272,128]{1,0:T(8,128)(2,1)S(1)}, bf16[272,128]{1,0:T(8,128)(2,1)S(1)}, u32[]{:S(2)}, u32[]{:S(2)}) collective-permute-start(bf16[272,128]{1,0:T(8,128)(2,1)S(1)} %get-tuple-element.110), channel_id=1, source_target_pairs={{0,24},{8,16},{16,8},{24,0},{1,25},{9,17},{17,9},{25,1},{2,26},{10... | collective-permute-start | bytes 208904 | tf_op jit(solution)/shard_map/ppermute | solution.py:120
  84.6 5.4 %collective-permute-done.25.refs_1_ = bf16[272,128]{1,0:T(8,128)(2,1)S(1)} collective-permute-done((bf16[272,128]{1,0:T(8,128)(2,1)S(1)}, bf16[272,128]{1,0:T(8,128)(2,1)S(1)}, u32[]{:S(2)}, u32[]{:S(2)}) %collective-permute-start.25) | collective-permute-done | bytes 69664 | tf_op jit(solution)/shard_map/ppermute | solution.py:120
  90.2 1.5 %collective-permute-start.27 = (bf16[272,128]{1,0:T(8,128)(2,1)S(1)}, bf16[272,128]{1,0:T(8,128)(2,1)S(1)}, u32[]{:S(2)}, u32[]{:S(2)}) collective-permute-start(bf16[272,128]{1,0:T(8,128)(2,1)S(1)} %get-tuple-element.117.refs_0_), channel_id=1, source_target_pairs={{0,8},{8,0},{16,24},{24,16},{1,9},{9,1},{17,25},{25,17},{2,10},{10... | collective-permute-start | bytes 208904 | tf_op jit(solution)/shard_map/ppermute | solution.py:120
  91.6 1.0 collective-permute-start.28
  92.7 2.0 %collective-permute-start.29 = (bf16[272,128]{1,0:T(8,128)(2,1)S(1)}, bf16[272,128]{1,0:T(8,128)(2,1)S(1)}, u32[]{:S(2)}, u32[]{:S(2)}) collective-permute-start(bf16[272,128]{1,0:T(8,128)(2,1)S(1)} %get-tuple-element.117.refs_0_), channel_id=1, source_target_pairs={{0,24},{8,16},{16,8},{24,0},{1,25},{9,17},{17,9},{25,1},{2,26},{10... | collective-permute-start | bytes 208904 | tf_op jit(solution)/shard_map/ppermute | solution.py:120
  94.6 4.9 %collective-permute-done.28.refs_2_ = bf16[272,128]{1,0:T(8,128)(2,1)S(1)} collective-permute-done((bf16[272,128]{1,0:T(8,128)(2,1)S(1)}, bf16[272,128]{1,0:T(8,128)(2,1)S(1)}, u32[]{:S(2)}, u32[]{:S(2)}) %collective-permute-start.28) | collective-permute-done | bytes 69664 | tf_op jit(solution)/shard_map/ppermute | solution.py:120
  99.5 0.7 shard_map.69
  100.3 0.7 shard_map.70.own_ref
  101.0 1.2 collective-permute-done.30.got_ref
  102.3 1.1 collective-permute-start.31
  103.5 1.5 %collective-permute-start.32 = (bf16[448,128]{1,0:T(8,128)(2,1)S(1)}, bf16[448,128]{1,0:T(8,128)(2,1)S(1)}, u32[]{:S(2)}, u32[]{:S(2)}) collective-permute-start(bf16[448,128]{1,0:T(8,128)(2,1)S(1)} %get-tuple-element.123.refs_1_), channel_id=1, source_target_pairs={{0,4},{1,5},{2,6},{3,7},{4,0},{5,1},{6,2},{7,3},{8,12},{9,13},{10,... | collective-permute-start | bytes 344072 | tf_op jit(solution)/shard_map/ppermute | solution.py:123
  105.0 3.4 %collective-permute-done.32.refs_3_ = bf16[448,128]{1,0:T(8,128)(2,1)S(1)} collective-permute-done((bf16[448,128]{1,0:T(8,128)(2,1)S(1)}, bf16[448,128]{1,0:T(8,128)(2,1)S(1)}, u32[]{:S(2)}, u32[]{:S(2)}) %collective-permute-start.32) | collective-permute-done | bytes 114720 | tf_op jit(solution)/shard_map/ppermute | solution.py:123
  108.4 1.6 %collective-permute-start.33 = (bf16[592,128]{1,0:T(8,128)(2,1)S(1)}, bf16[592,128]{1,0:T(8,128)(2,1)S(1)}, u32[]{:S(2)}, u32[]{:S(2)}) collective-permute-start(bf16[592,128]{1,0:T(8,128)(2,1)S(1)} %get-tuple-element.124.refs_0_), channel_id=1, source_target_pairs={{0,4},{1,5},{2,6},{3,7},{4,0},{5,1},{6,2},{7,3},{8,12},{9,13},{10,... | collective-permute-start | bytes 454664 | tf_op jit(solution)/shard_map/ppermute | solution.py:123
  110.0 1.1 collective-permute-start.34
  111.1 3.7 %collective-permute-done.34.refs_3_ = bf16[448,128]{1,0:T(8,128)(2,1)S(1)} collective-permute-done((bf16[448,128]{1,0:T(8,128)(2,1)S(1)}, bf16[448,128]{1,0:T(8,128)(2,1)S(1)}, u32[]{:S(2)}, u32[]{:S(2)}) %collective-permute-start.34) | collective-permute-done | bytes 114720 | tf_op jit(solution)/shard_map/ppermute | solution.py:123
  115.6 0.7 collective-permute-done.35.got_ref
  116.4 1.3 %collective-permute-start.36 = (f32[8,128]{1,0:T(8,128)S(1)}, f32[8,128]{1,0:T(8,128)S(1)}, u32[]{:S(2)}, u32[]{:S(2)}) collective-permute-start(f32[8,128]{1,0:T(8,128)S(1)} %get-tuple-element.129.refs_0_), channel_id=1, source_target_pairs={{0,8},{8,0},{16,24},{24,16},{1,9},{9,1},{17,25},{25,17},{2,10},{10... | collective-permute-start | bytes 12296 | tf_op jit(solution)/shard_map/ppermute | solution.py:120
  117.7 1.2 collective-permute-start.37
  118.9 1.9 %collective-permute-start.38 = (f32[8,128]{1,0:T(8,128)S(1)}, f32[8,128]{1,0:T(8,128)S(1)}, u32[]{:S(2)}, u32[]{:S(2)}) collective-permute-start(f32[8,128]{1,0:T(8,128)S(1)} %get-tuple-element.129.refs_0_), channel_id=1, source_target_pairs={{0,24},{8,16},{16,8},{24,0},{1,25},{9,17},{17,9},{25,1},{2,26},{10... | collective-permute-start | bytes 12296 | tf_op jit(solution)/shard_map/ppermute | solution.py:120
  120.8 1.4 %collective-permute-done.37.refs_2_ = f32[8,128]{1,0:T(8,128)S(1)} collective-permute-done((f32[8,128]{1,0:T(8,128)S(1)}, f32[8,128]{1,0:T(8,128)S(1)}, u32[]{:S(2)}, u32[]{:S(2)}) %collective-permute-start.37) | collective-permute-done | bytes 4128 | tf_op jit(solution)/shard_map/ppermute | solution.py:120
  122.2 2.1 %collective-permute-done.38.refs_3_ = f32[8,128]{1,0:T(8,128)S(1)} collective-permute-done((f32[8,128]{1,0:T(8,128)S(1)}, f32[8,128]{1,0:T(8,128)S(1)}, u32[]{:S(2)}, u32[]{:S(2)}) %collective-permute-start.38) | collective-permute-done | bytes 4128 | tf_op jit(solution)/shard_map/ppermute | solution.py:120
  124.3 1.2 shard_map.75
  (64 shorter events, 5.9 us)
Async XLA Ops:
  0.6 1.2 copy-start.2
  2.2 2.2 %copy-start = (bf16[2048,1024]{1,0:T(8,128)(2,1)S(1)}, bf16[2048,1024]{1,0:T(8,128)(2,1)}, u32[]{:S(2)}) copy-start(bf16[2048,1024]{1,0:T(8,128)(2,1)} %a_ref.21) | copy-start | bytes 12582916
  4.4 22.3 %copy-start.1 = (bf16[2048,1024]{1,0:T(8,128)(2,1)S(1)}, bf16[2048,1024]{1,0:T(8,128)(2,1)}, u32[]{:S(2)}) copy-start(bf16[2048,1024]{1,0:T(8,128)(2,1)} %a_ref.21) | copy-start | bytes 12582916
  5.9 5.9 %collective-permute-start = (f16[272,128]{1,0:T(8,128)(2,1)S(1)}, f16[272,128]{1,0:T(8,128)(2,1)S(1)}, u32[]{:S(2)}, u32[]{:S(2)}) collective-permute-start(f16[272,128]{1,0:T(8,128)(2,1)S(1)} %convert_element_type.36), channel_id=1, source_target_pairs={{0,8},{8,0},{16,24},{24,16},{1,9},{9,1},{17,25},{25,17},{2,10},{10... | collective-permute-start | bytes 208904 | tf_op jit(solution)/shard_map/ppermute | solution.py:120
  9.0 7.6 %collective-permute-start.1 = (f16[272,128]{1,0:T(8,128)(2,1)S(1)}, f16[272,128]{1,0:T(8,128)(2,1)S(1)}, u32[]{:S(2)}, u32[]{:S(2)}) collective-permute-start(f16[272,128]{1,0:T(8,128)(2,1)S(1)} %convert_element_type.38), channel_id=1, source_target_pairs={{0,16},{8,24},{16,0},{24,8},{1,17},{9,25},{17,1},{25,9},{2,18},{10... | collective-permute-start | bytes 208904 | tf_op jit(solution)/shard_map/ppermute | solution.py:120
  11.6 6.3 %collective-permute-start.2 = (f16[272,128]{1,0:T(8,128)(2,1)S(1)}, f16[272,128]{1,0:T(8,128)(2,1)S(1)}, u32[]{:S(2)}, u32[]{:S(2)}) collective-permute-start(f16[272,128]{1,0:T(8,128)(2,1)S(1)} %convert_element_type.40), channel_id=1, source_target_pairs={{0,24},{8,16},{16,8},{24,0},{1,25},{9,17},{17,9},{25,1},{2,26},{10... | collective-permute-start | bytes 208904 | tf_op jit(solution)/shard_map/ppermute | solution.py:120
  18.0 4.5 %collective-permute-start.3 = (bf16[272,128]{1,0:T(8,128)(2,1)S(1)}, bf16[272,128]{1,0:T(8,128)(2,1)S(1)}, u32[]{:S(2)}, u32[]{:S(2)}) collective-permute-start(bf16[272,128]{1,0:T(8,128)(2,1)S(1)} %get-tuple-element.74.refs_0_), channel_id=1, source_target_pairs={{0,8},{8,0},{16,24},{24,16},{1,9},{9,1},{17,25},{25,17},{2,10},{10... | collective-permute-start | bytes 208904 | tf_op jit(solution)/shard_map/ppermute | solution.py:120
  18.8 6.3 %collective-permute-start.4 = (bf16[272,128]{1,0:T(8,128)(2,1)S(1)}, bf16[272,128]{1,0:T(8,128)(2,1)S(1)}, u32[]{:S(2)}, u32[]{:S(2)}) collective-permute-start(bf16[272,128]{1,0:T(8,128)(2,1)S(1)} %get-tuple-element.74.refs_0_), channel_id=1, source_target_pairs={{0,16},{8,24},{16,0},{24,8},{1,17},{9,25},{17,1},{25,9},{2,18},{10... | collective-permute-start | bytes 208904 | tf_op jit(solution)/shard_map/ppermute | solution.py:120
  20.5 6.1 %collective-permute-start.5 = (bf16[272,128]{1,0:T(8,128)(2,1)S(1)}, bf16[272,128]{1,0:T(8,128)(2,1)S(1)}, u32[]{:S(2)}, u32[]{:S(2)}) collective-permute-start(bf16[272,128]{1,0:T(8,128)(2,1)S(1)} %get-tuple-element.74.refs_0_), channel_id=1, source_target_pairs={{0,24},{8,16},{16,8},{24,0},{1,25},{9,17},{17,9},{25,1},{2,26},{10... | collective-permute-start | bytes 208904 | tf_op jit(solution)/shard_map/ppermute | solution.py:120
  27.4 2.0 %collective-permute-start.6 = (f32[1040,128]{1,0:T(8,128)S(1)}, f32[1040,128]{1,0:T(8,128)S(1)}, u32[]{:S(2)}, u32[]{:S(2)}) collective-permute-start(f32[1040,128]{1,0:T(8,128)S(1)} %get-tuple-element.78), channel_id=1, source_target_pairs={{0,1},{1,0},{2,3},{3,2},{4,5},{5,4},{6,7},{7,6},{8,9},{9,8},{10,11... | collective-permute-start | bytes 1597448 | tf_op jit(solution)/shard_map/ppermute | solution.py:123
  29.5 6.5 %collective-permute-start.7 = (bf16[592,128]{1,0:T(8,128)(2,1)S(1)}, bf16[592,128]{1,0:T(8,128)(2,1)S(1)}, u32[]{:S(2)}, u32[]{:S(2)}) collective-permute-start(bf16[592,128]{1,0:T(8,128)(2,1)S(1)} %get-tuple-element.79.refs_0_), channel_id=1, source_target_pairs={{0,2},{1,3},{2,0},{3,1},{4,6},{5,7},{6,4},{7,5},{8,10},{9,11},{10,... | collective-permute-start | bytes 454664 | tf_op jit(solution)/shard_map/ppermute | solution.py:123
  31.0 4.9 %collective-permute-start.8 = (bf16[448,128]{1,0:T(8,128)(2,1)S(1)}, bf16[448,128]{1,0:T(8,128)(2,1)S(1)}, u32[]{:S(2)}, u32[]{:S(2)}) collective-permute-start(bf16[448,128]{1,0:T(8,128)(2,1)S(1)} %get-tuple-element.80.refs_1_), channel_id=1, source_target_pairs={{0,4},{1,5},{2,6},{3,7},{4,0},{5,1},{6,2},{7,3},{8,12},{9,13},{10,... | collective-permute-start | bytes 344072 | tf_op jit(solution)/shard_map/ppermute | solution.py:123
  36.0 6.4 %collective-permute-start.9 = (bf16[592,128]{1,0:T(8,128)(2,1)S(1)}, bf16[592,128]{1,0:T(8,128)(2,1)S(1)}, u32[]{:S(2)}, u32[]{:S(2)}) collective-permute-start(bf16[592,128]{1,0:T(8,128)(2,1)S(1)} %get-tuple-element.81.refs_0_), channel_id=1, source_target_pairs={{0,4},{1,5},{2,6},{3,7},{4,0},{5,1},{6,2},{7,3},{8,12},{9,13},{10,... | collective-permute-start | bytes 454664 | tf_op jit(solution)/shard_map/ppermute | solution.py:123
  37.6 4.8 %collective-permute-start.10 = (bf16[448,128]{1,0:T(8,128)(2,1)S(1)}, bf16[448,128]{1,0:T(8,128)(2,1)S(1)}, u32[]{:S(2)}, u32[]{:S(2)}) collective-permute-start(bf16[448,128]{1,0:T(8,128)(2,1)S(1)} %get-tuple-element.82.refs_1_), channel_id=1, source_target_pairs={{0,2},{1,3},{2,0},{3,1},{4,6},{5,7},{6,4},{7,5},{8,10},{9,11},{10,... | collective-permute-start | bytes 344072 | tf_op jit(solution)/shard_map/ppermute | solution.py:123
  42.5 1.6 %collective-permute-start.11 = (bf16[1040,128]{1,0:T(8,128)(2,1)S(1)}, bf16[1040,128]{1,0:T(8,128)(2,1)S(1)}, u32[]{:S(2)}, u32[]{:S(2)}) collective-permute-start(bf16[1040,128]{1,0:T(8,128)(2,1)S(1)} %get-tuple-element.84.mine_ref), channel_id=1, source_target_pairs={{0,1},{1,0},{2,3},{3,2},{4,5},{5,4},{6,7},{7,6},{8,9},{9,8},{10,11... | collective-permute-start | bytes 798728 | tf_op jit(solution)/shard_map/ppermute | solution.py:123
  43.1 10.8 %copy-start.3 = (f32[128]{0:T(128)S(1)}, f32[128]{0:T(128)}, u32[]{:S(2)}) copy-start(f32[128]{0:T(128)} %param.5) | copy-start | bytes 1540
  44.8 5.6 %collective-permute-start.12 = (f16[272,128]{1,0:T(8,128)(2,1)S(1)}, f16[272,128]{1,0:T(8,128)(2,1)S(1)}, u32[]{:S(2)}, u32[]{:S(2)}) collective-permute-start(f16[272,128]{1,0:T(8,128)(2,1)S(1)} %convert_element_type.42), channel_id=1, source_target_pairs={{0,8},{8,0},{16,24},{24,16},{1,9},{9,1},{17,25},{25,17},{2,10},{10... | collective-permute-start | bytes 208904 | tf_op jit(solution)/shard_map/ppermute | solution.py:120
  44.9 7.9 %collective-permute-start.13 = (f16[272,128]{1,0:T(8,128)(2,1)S(1)}, f16[272,128]{1,0:T(8,128)(2,1)S(1)}, u32[]{:S(2)}, u32[]{:S(2)}) collective-permute-start(f16[272,128]{1,0:T(8,128)(2,1)S(1)} %convert_element_type.44), channel_id=1, source_target_pairs={{0,16},{8,24},{16,0},{24,8},{1,17},{9,25},{17,1},{25,9},{2,18},{10... | collective-permute-start | bytes 208904 | tf_op jit(solution)/shard_map/ppermute | solution.py:120
  47.6 6.3 %collective-permute-start.14 = (f16[272,128]{1,0:T(8,128)(2,1)S(1)}, f16[272,128]{1,0:T(8,128)(2,1)S(1)}, u32[]{:S(2)}, u32[]{:S(2)}) collective-permute-start(f16[272,128]{1,0:T(8,128)(2,1)S(1)} %convert_element_type.46), channel_id=1, source_target_pairs={{0,24},{8,16},{16,8},{24,0},{1,25},{9,17},{17,9},{25,1},{2,26},{10... | collective-permute-start | bytes 208904 | tf_op jit(solution)/shard_map/ppermute | solution.py:120
  54.0 4.5 %collective-permute-start.15 = (bf16[272,128]{1,0:T(8,128)(2,1)S(1)}, bf16[272,128]{1,0:T(8,128)(2,1)S(1)}, u32[]{:S(2)}, u32[]{:S(2)}) collective-permute-start(bf16[272,128]{1,0:T(8,128)(2,1)S(1)} %get-tuple-element.95.refs_0_), channel_id=1, source_target_pairs={{0,8},{8,0},{16,24},{24,16},{1,9},{9,1},{17,25},{25,17},{2,10},{10... | collective-permute-start | bytes 208904 | tf_op jit(solution)/shard_map/ppermute | solution.py:120
  55.4 8.0 %collective-permute-start.16 = (bf16[272,128]{1,0:T(8,128)(2,1)S(1)}, bf16[272,128]{1,0:T(8,128)(2,1)S(1)}, u32[]{:S(2)}, u32[]{:S(2)}) collective-permute-start(bf16[272,128]{1,0:T(8,128)(2,1)S(1)} %get-tuple-element.95.refs_0_), channel_id=1, source_target_pairs={{0,16},{8,24},{16,0},{24,8},{1,17},{9,25},{17,1},{25,9},{2,18},{10... | collective-permute-start | bytes 208904 | tf_op jit(solution)/shard_map/ppermute | solution.py:120
  57.1 6.3 %collective-permute-start.17 = (bf16[272,128]{1,0:T(8,128)(2,1)S(1)}, bf16[272,128]{1,0:T(8,128)(2,1)S(1)}, u32[]{:S(2)}, u32[]{:S(2)}) collective-permute-start(bf16[272,128]{1,0:T(8,128)(2,1)S(1)} %get-tuple-element.95.refs_0_), channel_id=1, source_target_pairs={{0,24},{8,16},{16,8},{24,0},{1,25},{9,17},{17,9},{25,1},{2,26},{10... | collective-permute-start | bytes 208904 | tf_op jit(solution)/shard_map/ppermute | solution.py:120
  64.2 2.0 %collective-permute-start.18 = (f32[1040,128]{1,0:T(8,128)S(1)}, f32[1040,128]{1,0:T(8,128)S(1)}, u32[]{:S(2)}, u32[]{:S(2)}) collective-permute-start(f32[1040,128]{1,0:T(8,128)S(1)} %get-tuple-element.99), channel_id=1, source_target_pairs={{0,1},{1,0},{2,3},{3,2},{4,5},{5,4},{6,7},{7,6},{8,9},{9,8},{10,11... | collective-permute-start | bytes 1597448 | tf_op jit(solution)/shard_map/ppermute | solution.py:123
  66.3 6.0 %collective-permute-start.19 = (bf16[592,128]{1,0:T(8,128)(2,1)S(1)}, bf16[592,128]{1,0:T(8,128)(2,1)S(1)}, u32[]{:S(2)}, u32[]{:S(2)}) collective-permute-start(bf16[592,128]{1,0:T(8,128)(2,1)S(1)} %get-tuple-element.100.refs_0_), channel_id=1, source_target_pairs={{0,2},{1,3},{2,0},{3,1},{4,6},{5,7},{6,4},{7,5},{8,10},{9,11},{10,... | collective-permute-start | bytes 454664 | tf_op jit(solution)/shard_map/ppermute | solution.py:123
  67.4 4.9 %collective-permute-start.20 = (bf16[448,128]{1,0:T(8,128)(2,1)S(1)}, bf16[448,128]{1,0:T(8,128)(2,1)S(1)}, u32[]{:S(2)}, u32[]{:S(2)}) collective-permute-start(bf16[448,128]{1,0:T(8,128)(2,1)S(1)} %get-tuple-element.101.refs_1_), channel_id=1, source_target_pairs={{0,4},{1,5},{2,6},{3,7},{4,0},{5,1},{6,2},{7,3},{8,12},{9,13},{10,... | collective-permute-start | bytes 344072 | tf_op jit(solution)/shard_map/ppermute | solution.py:123
  72.4 5.4 %collective-permute-start.21 = (bf16[592,128]{1,0:T(8,128)(2,1)S(1)}, bf16[592,128]{1,0:T(8,128)(2,1)S(1)}, u32[]{:S(2)}, u32[]{:S(2)}) collective-permute-start(bf16[592,128]{1,0:T(8,128)(2,1)S(1)} %get-tuple-element.102.refs_0_), channel_id=1, source_target_pairs={{0,4},{1,5},{2,6},{3,7},{4,0},{5,1},{6,2},{7,3},{8,12},{9,13},{10,... | collective-permute-start | bytes 454664 | tf_op jit(solution)/shard_map/ppermute | solution.py:123
  72.9 4.8 %collective-permute-start.22 = (bf16[448,128]{1,0:T(8,128)(2,1)S(1)}, bf16[448,128]{1,0:T(8,128)(2,1)S(1)}, u32[]{:S(2)}, u32[]{:S(2)}) collective-permute-start(bf16[448,128]{1,0:T(8,128)(2,1)S(1)} %get-tuple-element.103.refs_1_), channel_id=1, source_target_pairs={{0,2},{1,3},{2,0},{3,1},{4,6},{5,7},{6,4},{7,5},{8,10},{9,11},{10,... | collective-permute-start | bytes 344072 | tf_op jit(solution)/shard_map/ppermute | solution.py:123
  77.9 1.6 %collective-permute-start.23 = (bf16[1040,128]{1,0:T(8,128)(2,1)S(1)}, bf16[1040,128]{1,0:T(8,128)(2,1)S(1)}, u32[]{:S(2)}, u32[]{:S(2)}) collective-permute-start(bf16[1040,128]{1,0:T(8,128)(2,1)S(1)} %get-tuple-element.105.mine_ref), channel_id=1, source_target_pairs={{0,1},{1,0},{2,3},{3,2},{4,5},{5,4},{6,7},{7,6},{8,9},{9,8},{10,11... | collective-permute-start | bytes 798728 | tf_op jit(solution)/shard_map/ppermute | solution.py:123
  80.2 4.5 %collective-permute-start.24 = (bf16[272,128]{1,0:T(8,128)(2,1)S(1)}, bf16[272,128]{1,0:T(8,128)(2,1)S(1)}, u32[]{:S(2)}, u32[]{:S(2)}) collective-permute-start(bf16[272,128]{1,0:T(8,128)(2,1)S(1)} %get-tuple-element.108), channel_id=1, source_target_pairs={{0,8},{8,0},{16,24},{24,16},{1,9},{9,1},{17,25},{25,17},{2,10},{10... | collective-permute-start | bytes 208904 | tf_op jit(solution)/shard_map/ppermute | solution.py:120
  81.5 8.5 %collective-permute-start.25 = (bf16[272,128]{1,0:T(8,128)(2,1)S(1)}, bf16[272,128]{1,0:T(8,128)(2,1)S(1)}, u32[]{:S(2)}, u32[]{:S(2)}) collective-permute-start(bf16[272,128]{1,0:T(8,128)(2,1)S(1)} %get-tuple-element.109), channel_id=1, source_target_pairs={{0,16},{8,24},{16,0},{24,8},{1,17},{9,25},{17,1},{25,9},{2,18},{10... | collective-permute-start | bytes 208904 | tf_op jit(solution)/shard_map/ppermute | solution.py:120
  82.7 7.4 %collective-permute-start.26 = (bf16[272,128]{1,0:T(8,128)(2,1)S(1)}, bf16[272,128]{1,0:T(8,128)(2,1)S(1)}, u32[]{:S(2)}, u32[]{:S(2)}) collective-permute-start(bf16[272,128]{1,0:T(8,128)(2,1)S(1)} %get-tuple-element.110), channel_id=1, source_target_pairs={{0,24},{8,16},{16,8},{24,0},{1,25},{9,17},{17,9},{25,1},{2,26},{10... | collective-permute-start | bytes 208904 | tf_op jit(solution)/shard_map/ppermute | solution.py:120
  90.2 4.5 %collective-permute-start.27 = (bf16[272,128]{1,0:T(8,128)(2,1)S(1)}, bf16[272,128]{1,0:T(8,128)(2,1)S(1)}, u32[]{:S(2)}, u32[]{:S(2)}) collective-permute-start(bf16[272,128]{1,0:T(8,128)(2,1)S(1)} %get-tuple-element.117.refs_0_), channel_id=1, source_target_pairs={{0,8},{8,0},{16,24},{24,16},{1,9},{9,1},{17,25},{25,17},{2,10},{10... | collective-permute-start | bytes 208904 | tf_op jit(solution)/shard_map/ppermute | solution.py:120
  91.6 7.8 %collective-permute-start.28 = (bf16[272,128]{1,0:T(8,128)(2,1)S(1)}, bf16[272,128]{1,0:T(8,128)(2,1)S(1)}, u32[]{:S(2)}, u32[]{:S(2)}) collective-permute-start(bf16[272,128]{1,0:T(8,128)(2,1)S(1)} %get-tuple-element.117.refs_0_), channel_id=1, source_target_pairs={{0,16},{8,24},{16,0},{24,8},{1,17},{9,25},{17,1},{25,9},{2,18},{10... | collective-permute-start | bytes 208904 | tf_op jit(solution)/shard_map/ppermute | solution.py:120
  92.7 6.8 %collective-permute-start.29 = (bf16[272,128]{1,0:T(8,128)(2,1)S(1)}, bf16[272,128]{1,0:T(8,128)(2,1)S(1)}, u32[]{:S(2)}, u32[]{:S(2)}) collective-permute-start(bf16[272,128]{1,0:T(8,128)(2,1)S(1)} %get-tuple-element.117.refs_0_), channel_id=1, source_target_pairs={{0,24},{8,16},{16,8},{24,0},{1,25},{9,17},{17,9},{25,1},{2,26},{10... | collective-permute-start | bytes 208904 | tf_op jit(solution)/shard_map/ppermute | solution.py:120
  100.2 2.0 %collective-permute-start.30 = (f32[1040,128]{1,0:T(8,128)S(1)}, f32[1040,128]{1,0:T(8,128)S(1)}, u32[]{:S(2)}, u32[]{:S(2)}) collective-permute-start(f32[1040,128]{1,0:T(8,128)S(1)} %get-tuple-element.121), channel_id=1, source_target_pairs={{0,1},{1,0},{2,3},{3,2},{4,5},{5,4},{6,7},{7,6},{8,9},{9,8},{10,11... | collective-permute-start | bytes 1597448 | tf_op jit(solution)/shard_map/ppermute | solution.py:123
  102.3 6.0 %collective-permute-start.31 = (bf16[592,128]{1,0:T(8,128)(2,1)S(1)}, bf16[592,128]{1,0:T(8,128)(2,1)S(1)}, u32[]{:S(2)}, u32[]{:S(2)}) collective-permute-start(bf16[592,128]{1,0:T(8,128)(2,1)S(1)} %get-tuple-element.122.refs_0_), channel_id=1, source_target_pairs={{0,2},{1,3},{2,0},{3,1},{4,6},{5,7},{6,4},{7,5},{8,10},{9,11},{10,... | collective-permute-start | bytes 454664 | tf_op jit(solution)/shard_map/ppermute | solution.py:123
  103.5 4.9 %collective-permute-start.32 = (bf16[448,128]{1,0:T(8,128)(2,1)S(1)}, bf16[448,128]{1,0:T(8,128)(2,1)S(1)}, u32[]{:S(2)}, u32[]{:S(2)}) collective-permute-start(bf16[448,128]{1,0:T(8,128)(2,1)S(1)} %get-tuple-element.123.refs_1_), channel_id=1, source_target_pairs={{0,4},{1,5},{2,6},{3,7},{4,0},{5,1},{6,2},{7,3},{8,12},{9,13},{10,... | collective-permute-start | bytes 344072 | tf_op jit(solution)/shard_map/ppermute | solution.py:123
  108.4 6.4 %collective-permute-start.33 = (bf16[592,128]{1,0:T(8,128)(2,1)S(1)}, bf16[592,128]{1,0:T(8,128)(2,1)S(1)}, u32[]{:S(2)}, u32[]{:S(2)}) collective-permute-start(bf16[592,128]{1,0:T(8,128)(2,1)S(1)} %get-tuple-element.124.refs_0_), channel_id=1, source_target_pairs={{0,4},{1,5},{2,6},{3,7},{4,0},{5,1},{6,2},{7,3},{8,12},{9,13},{10,... | collective-permute-start | bytes 454664 | tf_op jit(solution)/shard_map/ppermute | solution.py:123
  110.0 4.8 %collective-permute-start.34 = (bf16[448,128]{1,0:T(8,128)(2,1)S(1)}, bf16[448,128]{1,0:T(8,128)(2,1)S(1)}, u32[]{:S(2)}, u32[]{:S(2)}) collective-permute-start(bf16[448,128]{1,0:T(8,128)(2,1)S(1)} %get-tuple-element.125.refs_1_), channel_id=1, source_target_pairs={{0,2},{1,3},{2,0},{3,1},{4,6},{5,7},{6,4},{7,5},{8,10},{9,11},{10,... | collective-permute-start | bytes 344072 | tf_op jit(solution)/shard_map/ppermute | solution.py:123
  115.0 1.2 collective-permute-start.35
  115.1 5.7 %collective-permute-start.40 = (f32[1024,128]{1,0:T(8,128)S(1)}, f32[1024,128]{1,0:T(8,128)S(1)}, u32[]{:S(2)}, u32[]{:S(2)}) collective-permute-start(f32[1024,128]{1,0:T(8,128)S(1)} %get-tuple-element.133.refs_9_), channel_id=1, source_target_pairs={{0,1},{1,0},{2,3},{3,2},{4,5},{5,4},{6,7},{7,6},{8,9},{9,8},{10,11... | collective-permute-start | bytes 1572872 | tf_op jit(solution)/shard_map/ppermute | solution.py:123
  116.2 8.0 %collective-permute-start.39 = (f32[1024,128]{1,0:T(8,128)S(1)}, f32[1024,128]{1,0:T(8,128)S(1)}, u32[]{:S(2)}, u32[]{:S(2)}) collective-permute-start(f32[1024,128]{1,0:T(8,128)S(1)} %get-tuple-element.132.refs_7_), channel_id=1, source_target_pairs={{0,1},{1,0},{2,3},{3,2},{4,5},{5,4},{6,7},{7,6},{8,9},{9,8},{10,11... | collective-permute-start | bytes 1572872 | tf_op jit(solution)/shard_map/ppermute | solution.py:123
  116.4 4.4 %collective-permute-start.36 = (f32[8,128]{1,0:T(8,128)S(1)}, f32[8,128]{1,0:T(8,128)S(1)}, u32[]{:S(2)}, u32[]{:S(2)}) collective-permute-start(f32[8,128]{1,0:T(8,128)S(1)} %get-tuple-element.129.refs_0_), channel_id=1, source_target_pairs={{0,8},{8,0},{16,24},{24,16},{1,9},{9,1},{17,25},{25,17},{2,10},{10... | collective-permute-start | bytes 12296 | tf_op jit(solution)/shard_map/ppermute | solution.py:120
  117.7 4.5 %collective-permute-start.37 = (f32[8,128]{1,0:T(8,128)S(1)}, f32[8,128]{1,0:T(8,128)S(1)}, u32[]{:S(2)}, u32[]{:S(2)}) collective-permute-start(f32[8,128]{1,0:T(8,128)S(1)} %get-tuple-element.129.refs_0_), channel_id=1, source_target_pairs={{0,16},{8,24},{16,0},{24,8},{1,17},{9,25},{17,1},{25,9},{2,18},{10... | collective-permute-start | bytes 12296 | tf_op jit(solution)/shard_map/ppermute | solution.py:120
  118.9 5.4 %collective-permute-start.38 = (f32[8,128]{1,0:T(8,128)S(1)}, f32[8,128]{1,0:T(8,128)S(1)}, u32[]{:S(2)}, u32[]{:S(2)}) collective-permute-start(f32[8,128]{1,0:T(8,128)S(1)} %get-tuple-element.129.refs_0_), channel_id=1, source_target_pairs={{0,24},{8,16},{16,8},{24,0},{1,25},{9,17},{17,9},{25,1},{2,26},{10... | collective-permute-start | bytes 12296 | tf_op jit(solution)/shard_map/ppermute | solution.py:120

commit v5 on v4

--- a/solution.py
+++ b/solution.py
@@ -1,3 +1,5 @@
+import functools
+
 import jax
 import jax.numpy as jnp
 from jax import lax
@@ -178,32 +180,35 @@
         return residual, own, scattered(wire, sends)
 
     def backward(wire, mine, theirs):
-        def half_product(a_ref, ref, core_step, cols):
-            return jnp.dot(
-                body_of(ref).T,
-                a_ref[pl.ds(token_place(core_step), half), cols],
-                preferred_element_type=F32,
-            )
-
-        def first_half(a_ref, mine_ref, part_ref):
+        def half_product(a_ref, refs, core_step, cols):
+            total = None
+            for ref, start, rows in zip(refs, piece_starts, piece_rows):
+                place = pl.ds(pl.multiple_of(token_place(core_step) + start, 64), rows)
+                part = jnp.dot(ref[pl.ds(0, rows), :].T, a_ref[place, cols], preferred_element_type=F32)
+                total = part if total is None else total + part
+            return total
+
+        def first_half(a_ref, *refs):
+            *mine_refs, part_ref = refs
             for start in range(0, feats, block):
                 cols = slice(start, start + block)
-                part_ref[:, cols] = half_product(a_ref, mine_ref, 0, cols)
-
-        def second_half(a_ref, mine_ref, theirs_ref, part_ref, own_ref, delta_ref, *refs):
-            *msg_refs, prod = refs
-            delta = get_row(mine_ref) + get_row(theirs_ref)
+                part_ref[:, cols] = half_product(a_ref, mine_refs, 0, cols)
+
+        def second_half(a_ref, *refs):
+            mine_ref, theirs_refs = refs[0], refs[1 : levels + 1]
+            part_ref, own_ref, delta_ref, *msg_refs, prod = refs[levels + 1 :]
+            delta = get_row(mine_ref) + get_row(theirs_refs[-1])
             spread(delta_ref, delta)
             for start in range(0, feats, block):
                 cols = slice(start, start + block)
-                prod[cols, :] = (part_ref[:, cols] + half_product(a_ref, theirs_ref, 1, cols)).T
+                prod[cols, :] = (part_ref[:, cols] + half_product(a_ref, theirs_refs, 1, cols)).T
             cut(wire, prod, delta, own_ref, msg_refs)
 
-        (part,) = call(first_half, [((outs, feats), F32)], [states, mine])
+        (part,) = call(first_half, [((outs, feats), F32)], [states, *mine])
         own, delta, *sends = call(
             second_half,
             [feature_rows, scalar] + cut_shapes(wire),
-            [states, mine, theirs, part],
+            [states, mine[-1], *theirs, part],
             [pltpu.VMEM((feats, outs), F32)],
         )
         return own, delta, scattered(wire, sends)
@@ -220,11 +225,12 @@
 
         return call(kernel, [feature_rows, ((feat_share + PAD, outs), BF16)], [own] + got)
 
-    def advance(wire, own, delta, got, gamma, dir_sq, grad, direction, image, weights, residual):
+    def advance(wire, own, delta, got, gamma, dir_sq, grad, direction, images, weights, residual):
         def kernel(own_ref, delta_ref, *refs):
             ins = refs[: n_row - 1]
-            gamma_ref, sq_ref, grad_ref, dir_ref, image_ref, r_ref, ridge_ref = refs[n_row - 1 : n_row + 6]
-            *w_ref, w_out, r_out, grad_out, msg_ref = refs[n_row + 6 :]
+            gamma_ref, sq_ref, grad_ref, dir_ref, r_ref, ridge_ref = refs[n_row - 1 : n_row + 5]
+            image_refs = refs[n_row + 5 : n_row + 5 + levels]
+            *w_ref, w_out, r_out, grad_out, msg_ref = refs[n_row + 5 + levels :]
             if wire == F16:
                 tails = [get_scaled(ref) for ref in ins]
             else:
@@ -241,28 +247,27 @@
             grad_out[...] = new
             step_taken = alpha * old_dir
             w_out[...] = w_ref[0][...] + step_taken if w_ref else step_taken
-            r_out[...] = r_ref[...] - alpha * image_ref[...]
+            for ref, start, rows in zip(image_refs, piece_starts, piece_rows):
+                place = pl.ds(start, rows)
+                r_out[place, :] = r_ref[place, :] - alpha * ref[...]
 
         return call(
             kernel,
             [feature_rows, token_rows, feature_rows, ((feat_share + PAD, outs), BF16)],
-            [own, delta, *got, gamma, dir_sq, grad, direction, image, residual, ridge, *weights],
+            [own, delta, *got, gamma, dir_sq, grad, direction, residual, ridge, *images, *weights],
         )
 
     def forward(wire, msg):
         got = {step: over_row(step, msg) for step in row_steps}
         blocks = [msg] + [got[step] for step in range(1, n_row)]
 
-        def half_product(a_ref, vec, core_step, ref):
-            for start in range(0, half, block):
-                part = jnp.dot(
-                    a_ref[pl.ds(pl.multiple_of(token_place(core_step) + start, block), block), :],
-                    vec[...],
-                    preferred_element_type=F32,
-                )
-                ref[start : start + block, :] = part.astype(ref.dtype)
-
-        def first_half(a_ref, *refs):
+        def product(a_ref, vec, core_step, index, ref):
+            start, rows = piece_starts[index], piece_rows[index]
+            place = pl.ds(pl.multiple_of(token_place(core_step) + start, 64), rows)
+            part = jnp.dot(a_ref[place, :], vec[...], preferred_element_type=F32)
+            ref[pl.ds(0, rows), :] = part.astype(ref.dtype)
+
+        def first_piece(a_ref, *refs):
             ins = refs[:n_row]
             peer_ref, gamma_ref, cross_ref, vec = refs[n_row:]
             for step, ref in enumerate(ins):
@@ -271,19 +276,26 @@
             cross = tree_sum([get_row(ref, 1) for ref in ins])
             spread(gamma_ref, gamma)
             spread(cross_ref, cross)
-            half_product(a_ref, vec, 1, peer_ref)
+            product(a_ref, vec, 1, 0, peer_ref)
             put_rows(peer_ref, gamma, cross)
 
-        def second_half(a_ref, vec, own_ref):
-            half_product(a_ref, vec, 0, own_ref)
+        def later_piece(index, a_ref, vec, peer_ref):
+            product(a_ref, vec, 1, index, peer_ref)
+
+        def own_pieces(a_ref, vec, *refs):
+            for index, ref in enumerate(refs):
+                product(a_ref, vec, 0, index, ref)
 
         peer, gamma, cross, vec = call(
-            first_half,
-            [((half + PAD, outs), wire), scalar, scalar, ((feats, outs), BF16)],
+            first_piece,
+            [pieces(wire)[0], scalar, scalar, ((feats, outs), BF16)],
             [states] + blocks,
         )
-        got = over_group(1, peer)
-        (own,) = call(second_half, [token_rows], [states, vec])
+        got = [over_group(1, peer)]
+        for index in range(1, levels):
+            (peer,) = call(functools.partial(later_piece, index), [pieces(wire)[index]], [states, vec])
+            got.append(over_group(1, peer))
+        own = call(own_pieces, [((rows, outs), F32) for rows in piece_rows], [states, vec])
         return own, gamma, cross, got
 
     def pieces(wire):
@@ -295,67 +307,96 @@
         ]
 
     def join_cores(wire, own, gamma, cross, got):
-        def kernel(own_ref, gamma_ref, cross_ref, got_ref, *msg_refs):
-            for index, ref in enumerate(msg_refs):
-                place = pl.ds(piece_starts[index], piece_rows[index])
-                both = own_ref[place, :] + got_ref[place, :].astype(F32)
-                ref[pl.ds(0, piece_rows[index]), :] = both.astype(wire)
-            put_rows(
-                msg_refs[0],
-                gamma_ref[0:1, :] + get_row(got_ref, 0),
-                cross_ref[0:1, :] + get_row(got_ref, 1),
-            )
-
-        return call(kernel, pieces(wire), [own, gamma, cross, got])
+        def kernel(own_ref, got_ref, *refs):
+            *scalars, out_ref = refs
+            place = pl.ds(0, own_ref.shape[0])
+            out_ref[place, :] = (own_ref[...] + got_ref[place, :].astype(F32)).astype(wire)
+            if scalars:
+                put_rows(out_ref, *[ref[0:1, :] + get_row(got_ref, k) for k, ref in enumerate(scalars)])
+
+        return [
+            call(kernel, [shape], [own[index], got[index]] + ([] if index else [gamma, cross]))[0]
+            for index, shape in enumerate(pieces(wire))
+        ]
 
     def join_chips(wire, sent, got):
-        def kernel(*refs):
-            mine, theirs, out_refs = refs[:levels], refs[levels : 2 * levels], refs[2 * levels :]
-            for ref, own_ref, got_ref, rows in zip(out_refs, mine, theirs, piece_rows):
-                place = pl.ds(0, rows)
-                both = own_ref[place, :].astype(F32) + got_ref[place, :].astype(F32)
-                ref[place, :] = both.astype(wire)
-            put_rows(out_refs[0], *[get_row(mine[0], k) + get_row(theirs[0], k) for k in range(2)])
-
-        return call(kernel, pieces(wire), list(sent) + got)
+        def kernel(has_scalars, rows, own_ref, got_ref, out_ref):
+            place = pl.ds(0, rows)
+            both = own_ref[place, :].astype(F32) + got_ref[place, :].astype(F32)
+            out_ref[place, :] = both.astype(wire)
+            if has_scalars:
+                put_rows(out_ref, *[get_row(own_ref, k) + get_row(got_ref, k) for k in range(2)])
+
+        return [
+            call(functools.partial(kernel, index == 0, piece_rows[index]), [shape], [sent[index], got[index]])[0]
+            for index, shape in enumerate(pieces(wire))
+        ]
 
     def image_of(last, sent, got, grad, before):
-        def kernel(*refs):
-            mine, theirs = refs[:levels], refs[levels : 2 * levels]
-            grad_ref, *rest = refs[2 * levels :]
-            gamma_out, sq_out, dir_out, image_out, sum_out = rest[-5:]
-            gamma, cross = [get_row(mine[0], k) + get_row(theirs[0], k) for k in range(2)]
+        def first_piece(own_ref, got_ref, grad_ref, *refs):
+            old, (gamma_out, beta_out, sq_out, dir_out, *outputs) = refs[:-6 - more], refs[-6 - more :]
+            gamma, cross = [get_row(own_ref, k) + get_row(got_ref, k) for k in range(2)]
             spread(gamma_out, gamma)
             direction = grad_ref[...]
             dir_sq = gamma
+            beta = None
             if before:
-                old_gamma, old_sq, old_dir, old_image = rest[:4]
+                old_gamma, old_sq, old_dir = old[:3]
                 beta = gamma / old_gamma[0:1, :]
                 direction = direction + beta * old_dir[...]
                 dir_sq = gamma + beta * (2.0 * cross + beta * old_sq[0:1, :])
+                spread(beta_out, beta)
+            else:
+                spread(beta_out, gamma)
             dir_out[...] = direction
             spread(sq_out, dir_sq)
-            image_sq = jnp.zeros((1, outs), F32)
-            for index, (own_ref, got_ref) in enumerate(zip(mine, theirs)):
-                place = pl.ds(piece_starts[index], piece_rows[index])
-                there = pl.ds(0, piece_rows[index])
-                image = own_ref[there, :].astype(F32) + got_ref[there, :].astype(F32)
-                if before:
-                    image = image + beta * old_image[place, :]
-                image_out[place, :] = image
-                if not last:
-                    sum_out[place, :] = image.astype(BF16)
-                image_sq = image_sq + column_sum(image * image)
-            if last:
-                spread(sum_out, image_sq)
+            part = piece_image(0, own_ref, got_ref, beta, old[3:], outputs)
+            spread(outputs[-1], part)
+
+        def later_piece(index, own_ref, got_ref, part_ref, beta_ref, *refs):
+            count = len(shapes(index))
+            old, outputs = refs[:-count], refs[-count:]
+            part = part_ref[0:1, :] + piece_image(index, own_ref, got_ref, beta_ref[0:1, :], old, outputs)
+            if not last and index + 1 == levels:
+                put_rows(outputs[1], part)
             else:
-                put_rows(sum_out, image_sq)
-
-        return call(
-            kernel,
-            [scalar, scalar, feature_rows, token_rows, scalar if last else ((half + PAD, outs), BF16)],
-            list(sent) + got + [grad, *before],
+                spread(outputs[-1], part)
+
+        def piece_image(index, own_ref, got_ref, beta, old, outputs):
+            place = pl.ds(0, piece_rows[index])
+            image = own_ref[place, :].astype(F32) + got_ref[place, :].astype(F32)
+            if before:
+                image = image + beta * old[0][...]
+            outputs[0][...] = image
+            if not last:
+                outputs[1][place, :] = image.astype(BF16)
+            return column_sum(image * image)
+
+        more = 0 if last else 1
+
+        def shapes(index):
+            rows = piece_rows[index]
+            tail = PAD if index + 1 == levels else 0
+            shape = [((rows, outs), F32)] + [((rows + tail, outs), BF16)] * more
+            return shape + [scalar] if last or index + 1 < levels else shape
+
+        gamma, beta, dir_sq, direction, image, *msg, part = call(
+            first_piece,
+            [scalar, scalar, scalar, feature_rows] + shapes(0),
+            [sent[0], got[0], grad] + list(before[:3]) + list(before[3][:1] if before else ()),
         )
+        images, msgs = [image], msg
+        for index in range(1, levels):
+            image, *msg = call(
+                functools.partial(later_piece, index),
+                shapes(index),
+                [sent[index], got[index], part, beta] + list(before[3][index : index + 1] if before else ()),
+            )
+            if last or index + 1 < levels:
+                *msg, part = msg
+            images.append(image)
+            msgs += msg
+        return gamma, dir_sq, direction, images, msgs, part
 
     weights = ()
     residual, own, got = backward_first(ROW_WIRE[0])
@@ -369,45 +410,52 @@
             sent = join_chips(CHIP_WIRE[step][1], sent, got)
             got = swapped(level, sent)
         last = step + 1 == ITERS
-        gamma, dir_sq, direction, image, msg = image_of(last, sent, got, grad, before)
+        gamma, dir_sq, direction, images, msgs, part = image_of(last, sent, got, grad, before)
         if not last:
-            own, delta, got = backward(ROW_WIRE[step + 1], msg, over_group(1, msg))
+            own, delta, got = backward(
+                ROW_WIRE[step + 1], msgs, [over_group(1, msg) for msg in msgs]
+            )
             new, residual, grad, msg = advance(
-                ROW_WIRE[step + 1], own, delta, got, gamma, dir_sq, grad, direction, image, weights, residual
+                ROW_WIRE[step + 1], own, delta, got, gamma, dir_sq, grad, direction, images, weights, residual
             )
             weights = (new,)
-            before = (gamma, dir_sq, direction, image)
-
-    def both_cores(own_ref, got_ref, image_ref, out_ref, same_image_ref):
+            before = (gamma, dir_sq, direction, images)
+
+    def both_cores(own_ref, got_ref, *refs):
+        out_ref = refs[levels]
         out_ref[...] = own_ref[...] + got_ref[...]
 
     vmem, anywhere = pl.BlockSpec(memory_space=pltpu.VMEM), pl.BlockSpec(memory_space=pl.ANY)
-    delta, image = pl.pallas_call(
+    delta, *images = pl.pallas_call(
         both_cores,
-        out_shape=[jax.ShapeDtypeStruct(*scalar), jax.ShapeDtypeStruct(*token_rows)],
-        in_specs=[vmem, vmem, anywhere],
-        out_specs=[vmem, anywhere],
-        input_output_aliases={2: 1},
+        out_shape=[jax.ShapeDtypeStruct(*scalar)] + [jax.ShapeDtypeStruct((rows, outs), F32) for rows in piece_rows],
+        in_specs=[vmem, vmem] + [anywhere] * levels,
+        out_specs=[vmem] + [anywhere] * levels,
+        input_output_aliases={2 + index: 1 + index for index in range(levels)},
         compiler_params=pltpu.CompilerParams(vmem_limit_bytes=LIMIT),
-    )(msg, over_group(1, msg), image)
-    other_image = over_group(1, image)
+    )(part, over_group(1, part), *images)
+    other_images = [over_group(1, image) for image in images]
     other_residual = over_group(1, residual)
     got = {step: over_row(step, delta) for step in row_steps}
     deltas = [delta] + [got[step] for step in range(1, n_row)]
 
     def finish(*refs):
         delta_refs, refs = refs[:n_row], refs[n_row:]
-        gamma_ref, sq_ref, ridge_ref, image_ref, other_image_ref, r_ref, other_r_ref, dir_ref, w_ref, w_out, r_out = refs
+        image_refs, refs = refs[:levels], refs[levels:]
+        other_image_refs, refs = refs[:levels], refs[levels:]
+        gamma_ref, sq_ref, ridge_ref, r_ref, other_r_ref, dir_ref, w_ref, w_out, r_out = refs
         image_sq = tree_sum([ref[0:1, :] for ref in delta_refs])
         alpha = gamma_ref[0:1, :] / (image_sq + ridge_ref[...] * sq_ref[0:1, :])
         w_out[...] = w_ref[...] + alpha * dir_ref[...]
-        r_out[pl.ds(token_place(0), half), :] = r_ref[...] - alpha * image_ref[...]
-        r_out[pl.ds(token_place(1), half), :] = other_r_ref[...] - alpha * other_image_ref[...]
+        for core_step, old_ref, refs in ((0, r_ref, image_refs), (1, other_r_ref, other_image_refs)):
+            for ref, start, rows in zip(refs, piece_starts, piece_rows):
+                place = pl.ds(pl.multiple_of(token_place(core_step) + start, 64), rows)
+                r_out[place, :] = old_ref[pl.ds(start, rows), :] - alpha * ref[...]
 
     weights, residual = call(
         finish,
         [feature_rows, ((tokens, outs), F32)],
-        [*deltas, gamma, dir_sq, ridge, image, other_image, residual, other_residual, direction, *weights],
+        [*deltas, *images, *other_images, gamma, dir_sq, ridge, residual, other_residual, direction, *weights],
     )
     return weights, residual
 

time: 126 us -> 119 us (0.944)
  waiting for transfers between devices: 62.1 us -> 50.6 us
  starting transfers between devices: 47.9 us -> 52.3 us
    ppermute x20 -> x26, waiting for transfers between devices: 28.7 us -> 21.2 us  [over_group(): return lax.ppermute(value, 'group', [(i, i ^ step) for i in range(n_group)])]
    ppermute x20 -> x26, starting transfers between devices: 15.3 us -> 19.8 us  [over_group(): return lax.ppermute(value, 'group', [(i, i ^ step) for i in range(n_group)])]
    ppermute x21, waiting for transfers between devices: 33.4 us -> 29.4 us  [over_row(): return lax.ppermute(value, 'row', [(i, i ^ step) for i in range(n_row)])]
    pallas_call x25 -> x37, Pallas kernels: 10.9 us -> 11.7 us  [call(): pl.pallas_call(kernel, out_shape=[jax.ShapeDtypeStruct(shape, dtype) for...]
  transfers between devices with their start and end apart: 41 -> 47, of which waited for: 24 -> 26; matrix products, arithmetic and copies ran while one was open for 0% -> 0% of each run, Pallas kernels for 2% -> 5%
where the time goes in v5:
time: 119 us
  starting transfers between devices  52.3 us (44%)
  waiting for transfers between devices  50.6 us (43%)
  Pallas kernels  11.7 us (10%)
  local copies, waits for them, and re-layouts  3.41 us (3%)
    ppermute x21, starting transfers between devices, over_row(): return lax.ppermute(value, 'row', [(i, i ^ step) for i in range(n_row)])  32.5 us
    ppermute x21, waiting for transfers between devices, over_row(): return lax.ppermute(value, 'row', [(i, i ^ step) for i in range(n_row)])  29.4 us
    ppermute x26, waiting for transfers between devices, over_group(): return lax.ppermute(value, 'group', [(i, i ^ step) for i in range(n_group)])  21.2 us
    ppermute x26, starting transfers between devices, over_group(): return lax.ppermute(value, 'group', [(i, i ^ step) for i in range(n_group)])  19.8 us
    pallas_call x37, Pallas kernels, call(): pl.pallas_call(kernel, out_shape=[jax.ShapeDtypeStruct(shape, dtype) for...  11.7 us
    unnamed x8, local copies, waits for them, and re-layouts  3.41 us
  transfers between devices with their start and end apart: 47, of which 26 were waited for; matrix products, arithmetic and copies ran while one was open for 0% of the time, Pallas kernels for 5%

profile of v5, /device:TPU:0, one launch (start us, length us, event | category | flops | bytes accessed | tf_op | source)
XLA Modules:
  0.0 119.2 jit_solution(2702096733301345152)
XLA Ops:
  0.6 1.2 %copy-done.2 = f32[2048,128]{1,0:T(8,128)S(1)} copy-done((f32[2048,128]{1,0:T(8,128)S(1)}, f32[2048,128]{1,0:T(8,128)}, u32[]{:S(2)}) %copy-start.2) | copy-done | bytes 1048600
  2.2 2.2 %copy-done = bf16[2048,1024]{1,0:T(8,128)(2,1)S(1)} copy-done((bf16[2048,1024]{1,0:T(8,128)(2,1)S(1)}, bf16[2048,1024]{1,0:T(8,128)(2,1)}, u32[]{:S(2)}) %copy-start) | copy-done | bytes 4194328
  4.4 1.4 %shard_map.51 = (f32[256,128]{1,0:T(8,128)S(1)}, f32[272,128]{1,0:T(8,128)S(1)}, f32[272,128]{1,0:T(8,128)S(1)}, f32[272,128]{1,0:T(8,128)S(1)}) custom-call(bf16[2048,1024]{1,0:T(8,128)(2,1)S(1)} %copy-done, bf16[256,2048]{1,0:T(8,128)(2,1)S(1)} %get-tuple-element.75.turned_ref), custom_call_target="tpu_custom_call" | custom-call | tf_op jit(solution)/shard_map/pallas_call | solution.py:92
  5.9 5.1 %collective-permute-start.2 = (f16[272,128]{1,0:T(8,128)(2,1)S(1)}, f16[272,128]{1,0:T(8,128)(2,1)S(1)}, u32[]{:S(2)}, u32[]{:S(2)}) collective-permute-start(f16[272,128]{1,0:T(8,128)(2,1)S(1)} %convert_element_type.40), channel_id=1, source_target_pairs={{0,24},{8,16},{16,8},{24,0},{1,25},{9,17},{17,9},{25,1},{2,26},{10... | collective-permute-start | bytes 208904 | tf_op jit(solution)/shard_map/ppermute | solution.py:122
  11.1 0.6 collective-permute-start
  11.7 1.8 %collective-permute-done.2 = f16[272,128]{1,0:T(8,128)(2,1)S(1)} collective-permute-done((f16[272,128]{1,0:T(8,128)(2,1)S(1)}, f16[272,128]{1,0:T(8,128)(2,1)S(1)}, u32[]{:S(2)}, u32[]{:S(2)}) %collective-permute-start.2) | collective-permute-done | bytes 69664 | tf_op jit(solution)/shard_map/ppermute | solution.py:122
  13.6 3.3 %collective-permute-done.1 = f16[272,128]{1,0:T(8,128)(2,1)S(1)} collective-permute-done((f16[272,128]{1,0:T(8,128)(2,1)S(1)}, f16[272,128]{1,0:T(8,128)(2,1)S(1)}, u32[]{:S(2)}, u32[]{:S(2)}) %collective-permute-start.1) | collective-permute-done | bytes 69664 | tf_op jit(solution)/shard_map/ppermute | solution.py:122
  17.0 2.8 %collective-permute-start.5 = (bf16[272,128]{1,0:T(8,128)(2,1)S(1)}, bf16[272,128]{1,0:T(8,128)(2,1)S(1)}, u32[]{:S(2)}, u32[]{:S(2)}) collective-permute-start(bf16[272,128]{1,0:T(8,128)(2,1)S(1)} %get-tuple-element.80.refs_0_), channel_id=1, source_target_pairs={{0,24},{8,16},{16,8},{24,0},{1,25},{9,17},{17,9},{25,1},{2,26},{10... | collective-permute-start | bytes 208904 | tf_op jit(solution)/shard_map/ppermute | solution.py:122
  19.8 1.6 %collective-permute-start.3 = (bf16[272,128]{1,0:T(8,128)(2,1)S(1)}, bf16[272,128]{1,0:T(8,128)(2,1)S(1)}, u32[]{:S(2)}, u32[]{:S(2)}) collective-permute-start(bf16[272,128]{1,0:T(8,128)(2,1)S(1)} %get-tuple-element.80.refs_0_), channel_id=1, source_target_pairs={{0,8},{8,0},{16,24},{24,16},{1,9},{9,1},{17,25},{25,17},{2,10},{10... | collective-permute-start | bytes 208904 | tf_op jit(solution)/shard_map/ppermute | solution.py:122
  21.5 2.4 %collective-permute-done.5.refs_3_ = bf16[272,128]{1,0:T(8,128)(2,1)S(1)} collective-permute-done((bf16[272,128]{1,0:T(8,128)(2,1)S(1)}, bf16[272,128]{1,0:T(8,128)(2,1)S(1)}, u32[]{:S(2)}, u32[]{:S(2)}) %collective-permute-start.5) | collective-permute-done | bytes 69664 | tf_op jit(solution)/shard_map/ppermute | solution.py:122
  23.8 2.4 %collective-permute-done.4.refs_2_ = bf16[272,128]{1,0:T(8,128)(2,1)S(1)} collective-permute-done((bf16[272,128]{1,0:T(8,128)(2,1)S(1)}, bf16[272,128]{1,0:T(8,128)(2,1)S(1)}, u32[]{:S(2)}, u32[]{:S(2)}) %collective-permute-start.4) | collective-permute-done | bytes 69664 | tf_op jit(solution)/shard_map/ppermute | solution.py:122
  27.2 0.6 collective-permute-start.6
  27.8 0.7 shard_map.54
  28.6 1.6 %collective-permute-start.10 = (bf16[592,128]{1,0:T(8,128)(2,1)S(1)}, bf16[592,128]{1,0:T(8,128)(2,1)S(1)}, u32[]{:S(2)}, u32[]{:S(2)}) collective-permute-start(bf16[592,128]{1,0:T(8,128)(2,1)S(1)} %shard_map.58.own_ref), channel_id=1, source_target_pairs={{0,2},{1,3},{2,0},{3,1},{4,6},{5,7},{6,4},{7,5},{8,10},{9,11},{10,... | collective-permute-start | bytes 454664 | tf_op jit(solution)/shard_map/ppermute | solution.py:125
  30.2 1.6 %collective-permute-start.7 = (bf16[448,128]{1,0:T(8,128)(2,1)S(1)}, bf16[448,128]{1,0:T(8,128)(2,1)S(1)}, u32[]{:S(2)}, u32[]{:S(2)}) collective-permute-start(bf16[448,128]{1,0:T(8,128)(2,1)S(1)} %shard_map.56.own_ref), channel_id=1, source_target_pairs={{0,4},{1,5},{2,6},{3,7},{4,0},{5,1},{6,2},{7,3},{8,12},{9,13},{10,... | collective-permute-start | bytes 344072 | tf_op jit(solution)/shard_map/ppermute | solution.py:125
  31.8 2.7 %collective-permute-done.10.got_ref = bf16[592,128]{1,0:T(8,128)(2,1)S(1)} collective-permute-done((bf16[592,128]{1,0:T(8,128)(2,1)S(1)}, bf16[592,128]{1,0:T(8,128)(2,1)S(1)}, u32[]{:S(2)}, u32[]{:S(2)}) %collective-permute-start.10) | collective-permute-done | bytes 151584 | tf_op jit(solution)/shard_map/ppermute | solution.py:125
  34.6 1.6 %collective-permute-start.11 = (bf16[592,128]{1,0:T(8,128)(2,1)S(1)}, bf16[592,128]{1,0:T(8,128)(2,1)S(1)}, u32[]{:S(2)}, u32[]{:S(2)}) collective-permute-start(bf16[592,128]{1,0:T(8,128)(2,1)S(1)} %shard_map.59.own_ref), channel_id=1, source_target_pairs={{0,4},{1,5},{2,6},{3,7},{4,0},{5,1},{6,2},{7,3},{8,12},{9,13},{10,... | collective-permute-start | bytes 454664 | tf_op jit(solution)/shard_map/ppermute | solution.py:125
  36.2 1.6 %collective-permute-start.8 = (bf16[448,128]{1,0:T(8,128)(2,1)S(1)}, bf16[448,128]{1,0:T(8,128)(2,1)S(1)}, u32[]{:S(2)}, u32[]{:S(2)}) collective-permute-start(bf16[448,128]{1,0:T(8,128)(2,1)S(1)} %shard_map.57.own_ref), channel_id=1, source_target_pairs={{0,2},{1,3},{2,0},{3,1},{4,6},{5,7},{6,4},{7,5},{8,10},{9,11},{10,... | collective-permute-start | bytes 344072 | tf_op jit(solution)/shard_map/ppermute | solution.py:125
  37.8 2.0 %collective-permute-done.11.got_ref = bf16[592,128]{1,0:T(8,128)(2,1)S(1)} collective-permute-done((bf16[592,128]{1,0:T(8,128)(2,1)S(1)}, bf16[592,128]{1,0:T(8,128)(2,1)S(1)}, u32[]{:S(2)}, u32[]{:S(2)}) %collective-permute-start.11) | collective-permute-done | bytes 151584 | tf_op jit(solution)/shard_map/ppermute | solution.py:125
  40.0 1.1 collective-permute-done.8.got_ref
  41.8 0.7 collective-permute-done.13.refs_2_
  42.6 0.7 shard_map.63
  43.3 1.8 %collective-permute-start.16 = (f16[272,128]{1,0:T(8,128)(2,1)S(1)}, f16[272,128]{1,0:T(8,128)(2,1)S(1)}, u32[]{:S(2)}, u32[]{:S(2)}) collective-permute-start(f16[272,128]{1,0:T(8,128)(2,1)S(1)} %convert_element_type.46), channel_id=1, source_target_pairs={{0,24},{8,16},{16,8},{24,0},{1,25},{9,17},{17,9},{25,1},{2,26},{10... | collective-permute-start | bytes 208904 | tf_op jit(solution)/shard_map/ppermute | solution.py:122
  45.1 2.7 %collective-permute-start.14 = (f16[272,128]{1,0:T(8,128)(2,1)S(1)}, f16[272,128]{1,0:T(8,128)(2,1)S(1)}, u32[]{:S(2)}, u32[]{:S(2)}) collective-permute-start(f16[272,128]{1,0:T(8,128)(2,1)S(1)} %convert_element_type.42), channel_id=1, source_target_pairs={{0,8},{8,0},{16,24},{24,16},{1,9},{9,1},{17,25},{25,17},{2,10},{10... | collective-permute-start | bytes 208904 | tf_op jit(solution)/shard_map/ppermute | solution.py:122
  47.9 2.4 %collective-permute-done.16 = f16[272,128]{1,0:T(8,128)(2,1)S(1)} collective-permute-done((f16[272,128]{1,0:T(8,128)(2,1)S(1)}, f16[272,128]{1,0:T(8,128)(2,1)S(1)}, u32[]{:S(2)}, u32[]{:S(2)}) %collective-permute-start.16) | collective-permute-done | bytes 69664 | tf_op jit(solution)/shard_map/ppermute | solution.py:122
  50.3 2.1 %collective-permute-done.15 = f16[272,128]{1,0:T(8,128)(2,1)S(1)} collective-permute-done((f16[272,128]{1,0:T(8,128)(2,1)S(1)}, f16[272,128]{1,0:T(8,128)(2,1)S(1)}, u32[]{:S(2)}, u32[]{:S(2)}) %collective-permute-start.15) | collective-permute-done | bytes 69664 | tf_op jit(solution)/shard_map/ppermute | solution.py:122
  52.6 1.8 %collective-permute-start.19 = (bf16[272,128]{1,0:T(8,128)(2,1)S(1)}, bf16[272,128]{1,0:T(8,128)(2,1)S(1)}, u32[]{:S(2)}, u32[]{:S(2)}) collective-permute-start(bf16[272,128]{1,0:T(8,128)(2,1)S(1)} %get-tuple-element.103.refs_0_), channel_id=1, source_target_pairs={{0,24},{8,16},{16,8},{24,0},{1,25},{9,17},{17,9},{25,1},{2,26},{10... | collective-permute-start | bytes 208904 | tf_op jit(solution)/shard_map/ppermute | solution.py:122
  54.4 2.7 %collective-permute-start.17 = (bf16[272,128]{1,0:T(8,128)(2,1)S(1)}, bf16[272,128]{1,0:T(8,128)(2,1)S(1)}, u32[]{:S(2)}, u32[]{:S(2)}) collective-permute-start(bf16[272,128]{1,0:T(8,128)(2,1)S(1)} %get-tuple-element.103.refs_0_), channel_id=1, source_target_pairs={{0,8},{8,0},{16,24},{24,16},{1,9},{9,1},{17,25},{25,17},{2,10},{10... | collective-permute-start | bytes 208904 | tf_op jit(solution)/shard_map/ppermute | solution.py:122
  57.1 2.5 %collective-permute-done.19.refs_3_ = bf16[272,128]{1,0:T(8,128)(2,1)S(1)} collective-permute-done((bf16[272,128]{1,0:T(8,128)(2,1)S(1)}, bf16[272,128]{1,0:T(8,128)(2,1)S(1)}, u32[]{:S(2)}, u32[]{:S(2)}) %collective-permute-start.19) | collective-permute-done | bytes 69664 | tf_op jit(solution)/shard_map/ppermute | solution.py:122
  59.6 2.0 %collective-permute-done.18.refs_2_ = bf16[272,128]{1,0:T(8,128)(2,1)S(1)} collective-permute-done((bf16[272,128]{1,0:T(8,128)(2,1)S(1)}, bf16[272,128]{1,0:T(8,128)(2,1)S(1)}, u32[]{:S(2)}, u32[]{:S(2)}) %collective-permute-start.18) | collective-permute-done | bytes 69664 | tf_op jit(solution)/shard_map/ppermute | solution.py:122
  62.6 0.6 collective-permute-start.20
  63.1 0.7 shard_map.66
  63.9 1.6 %collective-permute-start.24 = (bf16[592,128]{1,0:T(8,128)(2,1)S(1)}, bf16[592,128]{1,0:T(8,128)(2,1)S(1)}, u32[]{:S(2)}, u32[]{:S(2)}) collective-permute-start(bf16[592,128]{1,0:T(8,128)(2,1)S(1)} %shard_map.70.own_ref), channel_id=1, source_target_pairs={{0,2},{1,3},{2,0},{3,1},{4,6},{5,7},{6,4},{7,5},{8,10},{9,11},{10,... | collective-permute-start | bytes 454664 | tf_op jit(solution)/shard_map/ppermute | solution.py:125
  65.5 0.9 collective-permute-start.21
  66.4 3.5 %collective-permute-done.24.got_ref = bf16[592,128]{1,0:T(8,128)(2,1)S(1)} collective-permute-done((bf16[592,128]{1,0:T(8,128)(2,1)S(1)}, bf16[592,128]{1,0:T(8,128)(2,1)S(1)}, u32[]{:S(2)}, u32[]{:S(2)}) %collective-permute-start.24) | collective-permute-done | bytes 151584 | tf_op jit(solution)/shard_map/ppermute | solution.py:125
  69.9 0.9 collective-permute-start.25
  70.8 1.6 %collective-permute-start.22 = (bf16[448,128]{1,0:T(8,128)(2,1)S(1)}, bf16[448,128]{1,0:T(8,128)(2,1)S(1)}, u32[]{:S(2)}, u32[]{:S(2)}) collective-permute-start(bf16[448,128]{1,0:T(8,128)(2,1)S(1)} %shard_map.69.own_ref), channel_id=1, source_target_pairs={{0,2},{1,3},{2,0},{3,1},{4,6},{5,7},{6,4},{7,5},{8,10},{9,11},{10,... | collective-permute-start | bytes 344072 | tf_op jit(solution)/shard_map/ppermute | solution.py:125
  72.4 2.8 %collective-permute-done.25.got_ref = bf16[592,128]{1,0:T(8,128)(2,1)S(1)} collective-permute-done((bf16[592,128]{1,0:T(8,128)(2,1)S(1)}, bf16[592,128]{1,0:T(8,128)(2,1)S(1)}, u32[]{:S(2)}, u32[]{:S(2)}) %collective-permute-start.25) | collective-permute-done | bytes 151584 | tf_op jit(solution)/shard_map/ppermute | solution.py:125
  76.5 0.6 collective-permute-done.27.refs_2_
  77.2 0.7 shard_map.75
  78.0 2.3 %collective-permute-start.29 = (bf16[272,128]{1,0:T(8,128)(2,1)S(1)}, bf16[272,128]{1,0:T(8,128)(2,1)S(1)}, u32[]{:S(2)}, u32[]{:S(2)}) collective-permute-start(bf16[272,128]{1,0:T(8,128)(2,1)S(1)} %get-tuple-element.118), channel_id=1, source_target_pairs={{0,16},{8,24},{16,0},{24,8},{1,17},{9,25},{17,1},{25,9},{2,18},{10... | collective-permute-start | bytes 208904 | tf_op jit(solution)/shard_map/ppermute | solution.py:122
  80.2 2.1 %collective-permute-start.30 = (bf16[272,128]{1,0:T(8,128)(2,1)S(1)}, bf16[272,128]{1,0:T(8,128)(2,1)S(1)}, u32[]{:S(2)}, u32[]{:S(2)}) collective-permute-start(bf16[272,128]{1,0:T(8,128)(2,1)S(1)} %get-tuple-element.119), channel_id=1, source_target_pairs={{0,24},{8,16},{16,8},{24,0},{1,25},{9,17},{17,9},{25,1},{2,26},{10... | collective-permute-start | bytes 208904 | tf_op jit(solution)/shard_map/ppermute | solution.py:122
  82.3 0.9 collective-permute-done.28.refs_0_
  83.2 3.7 %collective-permute-done.29.refs_1_ = bf16[272,128]{1,0:T(8,128)(2,1)S(1)} collective-permute-done((bf16[272,128]{1,0:T(8,128)(2,1)S(1)}, bf16[272,128]{1,0:T(8,128)(2,1)S(1)}, u32[]{:S(2)}, u32[]{:S(2)}) %collective-permute-start.29) | collective-permute-done | bytes 69664 | tf_op jit(solution)/shard_map/ppermute | solution.py:122
  87.1 2.0 %collective-permute-start.33 = (bf16[272,128]{1,0:T(8,128)(2,1)S(1)}, bf16[272,128]{1,0:T(8,128)(2,1)S(1)}, u32[]{:S(2)}, u32[]{:S(2)}) collective-permute-start(bf16[272,128]{1,0:T(8,128)(2,1)S(1)} %get-tuple-element.127.refs_0_), channel_id=1, source_target_pairs={{0,24},{8,16},{16,8},{24,0},{1,25},{9,17},{17,9},{25,1},{2,26},{10... | collective-permute-start | bytes 208904 | tf_op jit(solution)/shard_map/ppermute | solution.py:122
  89.0 0.9 collective-permute-start.32
  89.9 1.6 %collective-permute-start.31 = (bf16[272,128]{1,0:T(8,128)(2,1)S(1)}, bf16[272,128]{1,0:T(8,128)(2,1)S(1)}, u32[]{:S(2)}, u32[]{:S(2)}) collective-permute-start(bf16[272,128]{1,0:T(8,128)(2,1)S(1)} %get-tuple-element.127.refs_0_), channel_id=1, source_target_pairs={{0,8},{8,0},{16,24},{24,16},{1,9},{9,1},{17,25},{25,17},{2,10},{10... | collective-permute-start | bytes 208904 | tf_op jit(solution)/shard_map/ppermute | solution.py:122
  91.5 1.9 %collective-permute-done.33.refs_3_ = bf16[272,128]{1,0:T(8,128)(2,1)S(1)} collective-permute-done((bf16[272,128]{1,0:T(8,128)(2,1)S(1)}, bf16[272,128]{1,0:T(8,128)(2,1)S(1)}, u32[]{:S(2)}, u32[]{:S(2)}) %collective-permute-start.33) | collective-permute-done | bytes 69664 | tf_op jit(solution)/shard_map/ppermute | solution.py:122
  93.4 2.1 %collective-permute-done.32.refs_2_ = bf16[272,128]{1,0:T(8,128)(2,1)S(1)} collective-permute-done((bf16[272,128]{1,0:T(8,128)(2,1)S(1)}, bf16[272,128]{1,0:T(8,128)(2,1)S(1)}, u32[]{:S(2)}, u32[]{:S(2)}) %collective-permute-start.32) | collective-permute-done | bytes 69664 | tf_op jit(solution)/shard_map/ppermute | solution.py:122
  96.5 0.6 collective-permute-start.34
  97.0 0.7 shard_map.78
  97.8 1.6 %collective-permute-start.38 = (bf16[592,128]{1,0:T(8,128)(2,1)S(1)}, bf16[592,128]{1,0:T(8,128)(2,1)S(1)}, u32[]{:S(2)}, u32[]{:S(2)}) collective-permute-start(bf16[592,128]{1,0:T(8,128)(2,1)S(1)} %shard_map.82.own_ref), channel_id=1, source_target_pairs={{0,2},{1,3},{2,0},{3,1},{4,6},{5,7},{6,4},{7,5},{8,10},{9,11},{10,... | collective-permute-start | bytes 454664 | tf_op jit(solution)/shard_map/ppermute | solution.py:125
  99.4 1.2 %collective-permute-start.35 = (bf16[448,128]{1,0:T(8,128)(2,1)S(1)}, bf16[448,128]{1,0:T(8,128)(2,1)S(1)}, u32[]{:S(2)}, u32[]{:S(2)}) collective-permute-start(bf16[448,128]{1,0:T(8,128)(2,1)S(1)} %shard_map.80.own_ref), channel_id=1, source_target_pairs={{0,4},{1,5},{2,6},{3,7},{4,0},{5,1},{6,2},{7,3},{8,12},{9,13},{10,... | collective-permute-start | bytes 344072 | tf_op jit(solution)/shard_map/ppermute | solution.py:125
  100.7 3.1 %collective-permute-done.38.got_ref = bf16[592,128]{1,0:T(8,128)(2,1)S(1)} collective-permute-done((bf16[592,128]{1,0:T(8,128)(2,1)S(1)}, bf16[592,128]{1,0:T(8,128)(2,1)S(1)}, u32[]{:S(2)}, u32[]{:S(2)}) %collective-permute-start.38) | collective-permute-done | bytes 151584 | tf_op jit(solution)/shard_map/ppermute | solution.py:125
  103.8 1.2 %collective-permute-start.39 = (bf16[592,128]{1,0:T(8,128)(2,1)S(1)}, bf16[592,128]{1,0:T(8,128)(2,1)S(1)}, u32[]{:S(2)}, u32[]{:S(2)}) collective-permute-start(bf16[592,128]{1,0:T(8,128)(2,1)S(1)} %shard_map.83.own_ref), channel_id=1, source_target_pairs={{0,4},{1,5},{2,6},{3,7},{4,0},{5,1},{6,2},{7,3},{8,12},{9,13},{10,... | collective-permute-start | bytes 454664 | tf_op jit(solution)/shard_map/ppermute | solution.py:125
  105.1 1.6 %collective-permute-start.36 = (bf16[448,128]{1,0:T(8,128)(2,1)S(1)}, bf16[448,128]{1,0:T(8,128)(2,1)S(1)}, u32[]{:S(2)}, u32[]{:S(2)}) collective-permute-start(bf16[448,128]{1,0:T(8,128)(2,1)S(1)} %shard_map.81.own_ref), channel_id=1, source_target_pairs={{0,2},{1,3},{2,0},{3,1},{4,6},{5,7},{6,4},{7,5},{8,10},{9,11},{10,... | collective-permute-start | bytes 344072 | tf_op jit(solution)/shard_map/ppermute | solution.py:125
  106.6 2.4 %collective-permute-done.39.got_ref = bf16[592,128]{1,0:T(8,128)(2,1)S(1)} collective-permute-done((bf16[592,128]{1,0:T(8,128)(2,1)S(1)}, bf16[592,128]{1,0:T(8,128)(2,1)S(1)}, u32[]{:S(2)}, u32[]{:S(2)}) %collective-permute-start.39) | collective-permute-done | bytes 151584 | tf_op jit(solution)/shard_map/ppermute | solution.py:125
  109.2 0.8 collective-permute-done.36.got_ref
  110.1 1.2 collective-permute-done.40.got_ref
  111.8 1.8 %collective-permute-start.43 = (f32[8,128]{1,0:T(8,128)S(1)}, f32[8,128]{1,0:T(8,128)S(1)}, u32[]{:S(2)}, u32[]{:S(2)}) collective-permute-start(f32[8,128]{1,0:T(8,128)S(1)} %get-tuple-element.140.refs_0_), channel_id=1, source_target_pairs={{0,24},{8,16},{16,8},{24,0},{1,25},{9,17},{17,9},{25,1},{2,26},{10... | collective-permute-start | bytes 12296 | tf_op jit(solution)/shard_map/ppermute | solution.py:122
  113.6 2.6 %collective-permute-start.41 = (f32[8,128]{1,0:T(8,128)S(1)}, f32[8,128]{1,0:T(8,128)S(1)}, u32[]{:S(2)}, u32[]{:S(2)}) collective-permute-start(f32[8,128]{1,0:T(8,128)S(1)} %get-tuple-element.140.refs_0_), channel_id=1, source_target_pairs={{0,8},{8,0},{16,24},{24,16},{1,9},{9,1},{17,25},{25,17},{2,10},{10... | collective-permute-start | bytes 12296 | tf_op jit(solution)/shard_map/ppermute | solution.py:122
  116.1 1.0 collective-permute-done.43.refs_3_
  117.2 0.9 collective-permute-done.42.refs_2_
  118.1 1.1 shard_map.87
  (88 shorter events, 7.6 us)
Async XLA Ops:
  0.6 1.2 %copy-start.2 = (f32[2048,128]{1,0:T(8,128)S(1)}, f32[2048,128]{1,0:T(8,128)}, u32[]{:S(2)}) copy-start(f32[2048,128]{1,0:T(8,128)} %t_ref.1) | copy-start | bytes 3145732
  2.2 2.2 %copy-start = (bf16[2048,1024]{1,0:T(8,128)(2,1)S(1)}, bf16[2048,1024]{1,0:T(8,128)(2,1)}, u32[]{:S(2)}) copy-start(bf16[2048,1024]{1,0:T(8,128)(2,1)} %a_ref.27) | copy-start | bytes 12582916
  4.4 21.9 %copy-start.1 = (bf16[2048,1024]{1,0:T(8,128)(2,1)S(1)}, bf16[2048,1024]{1,0:T(8,128)(2,1)}, u32[]{:S(2)}) copy-start(bf16[2048,1024]{1,0:T(8,128)(2,1)} %a_ref.27) | copy-start | bytes 12582916
  5.9 7.7 %collective-permute-start.2 = (f16[272,128]{1,0:T(8,128)(2,1)S(1)}, f16[272,128]{1,0:T(8,128)(2,1)S(1)}, u32[]{:S(2)}, u32[]{:S(2)}) collective-permute-start(f16[272,128]{1,0:T(8,128)(2,1)S(1)} %convert_element_type.40), channel_id=1, source_target_pairs={{0,24},{8,16},{16,8},{24,0},{1,25},{9,17},{17,9},{25,1},{2,26},{10... | collective-permute-start | bytes 208904 | tf_op jit(solution)/shard_map/ppermute | solution.py:122
  11.0 5.9 %collective-permute-start.1 = (f16[272,128]{1,0:T(8,128)(2,1)S(1)}, f16[272,128]{1,0:T(8,128)(2,1)S(1)}, u32[]{:S(2)}, u32[]{:S(2)}) collective-permute-start(f16[272,128]{1,0:T(8,128)(2,1)S(1)} %convert_element_type.38), channel_id=1, source_target_pairs={{0,16},{8,24},{16,0},{24,8},{1,17},{9,25},{17,1},{25,9},{2,18},{10... | collective-permute-start | bytes 208904 | tf_op jit(solution)/shard_map/ppermute | solution.py:122
  11.1 5.8 %collective-permute-start = (f16[272,128]{1,0:T(8,128)(2,1)S(1)}, f16[272,128]{1,0:T(8,128)(2,1)S(1)}, u32[]{:S(2)}, u32[]{:S(2)}) collective-permute-start(f16[272,128]{1,0:T(8,128)(2,1)S(1)} %convert_element_type.36), channel_id=1, source_target_pairs={{0,8},{8,0},{16,24},{24,16},{1,9},{9,1},{17,25},{25,17},{2,10},{10... | collective-permute-start | bytes 208904 | tf_op jit(solution)/shard_map/ppermute | solution.py:122
  17.0 6.8 %collective-permute-start.5 = (bf16[272,128]{1,0:T(8,128)(2,1)S(1)}, bf16[272,128]{1,0:T(8,128)(2,1)S(1)}, u32[]{:S(2)}, u32[]{:S(2)}) collective-permute-start(bf16[272,128]{1,0:T(8,128)(2,1)S(1)} %get-tuple-element.80.refs_0_), channel_id=1, source_target_pairs={{0,24},{8,16},{16,8},{24,0},{1,25},{9,17},{17,9},{25,1},{2,26},{10... | collective-permute-start | bytes 208904 | tf_op jit(solution)/shard_map/ppermute | solution.py:122
  19.8 6.4 %collective-permute-start.4 = (bf16[272,128]{1,0:T(8,128)(2,1)S(1)}, bf16[272,128]{1,0:T(8,128)(2,1)S(1)}, u32[]{:S(2)}, u32[]{:S(2)}) collective-permute-start(bf16[272,128]{1,0:T(8,128)(2,1)S(1)} %get-tuple-element.80.refs_0_), channel_id=1, source_target_pairs={{0,16},{8,24},{16,0},{24,8},{1,17},{9,25},{17,1},{25,9},{2,18},{10... | collective-permute-start | bytes 208904 | tf_op jit(solution)/shard_map/ppermute | solution.py:122
  19.8 6.4 %collective-permute-start.3 = (bf16[272,128]{1,0:T(8,128)(2,1)S(1)}, bf16[272,128]{1,0:T(8,128)(2,1)S(1)}, u32[]{:S(2)}, u32[]{:S(2)}) collective-permute-start(bf16[272,128]{1,0:T(8,128)(2,1)S(1)} %get-tuple-element.80.refs_0_), channel_id=1, source_target_pairs={{0,8},{8,0},{16,24},{24,16},{1,9},{9,1},{17,25},{25,17},{2,10},{10... | collective-permute-start | bytes 208904 | tf_op jit(solution)/shard_map/ppermute | solution.py:122
  26.8 1.8 %collective-permute-start.9 = (f32[592,128]{1,0:T(8,128)S(1)}, f32[592,128]{1,0:T(8,128)S(1)}, u32[]{:S(2)}, u32[]{:S(2)}) collective-permute-start(f32[592,128]{1,0:T(8,128)S(1)} %get-tuple-element.84), channel_id=1, source_target_pairs={{0,1},{1,0},{2,3},{3,2},{4,5},{5,4},{6,7},{7,6},{8,9},{9,8},{10,11... | collective-permute-start | bytes 909320 | tf_op jit(solution)/shard_map/ppermute | solution.py:125
  27.2 3.0 %collective-permute-start.6 = (f32[448,128]{1,0:T(8,128)S(1)}, f32[448,128]{1,0:T(8,128)S(1)}, u32[]{:S(2)}, u32[]{:S(2)}) collective-permute-start(f32[448,128]{1,0:T(8,128)S(1)} %shard_map.55), channel_id=1, source_target_pairs={{0,1},{1,0},{2,3},{3,2},{4,5},{5,4},{6,7},{7,6},{8,9},{9,8},{10,11... | collective-permute-start | bytes 688136 | tf_op jit(solution)/shard_map/ppermute | solution.py:125
  28.6 5.9 %collective-permute-start.10 = (bf16[592,128]{1,0:T(8,128)(2,1)S(1)}, bf16[592,128]{1,0:T(8,128)(2,1)S(1)}, u32[]{:S(2)}, u32[]{:S(2)}) collective-permute-start(bf16[592,128]{1,0:T(8,128)(2,1)S(1)} %shard_map.58.own_ref), channel_id=1, source_target_pairs={{0,2},{1,3},{2,0},{3,1},{4,6},{5,7},{6,4},{7,5},{8,10},{9,11},{10,... | collective-permute-start | bytes 454664 | tf_op jit(solution)/shard_map/ppermute | solution.py:125
  30.2 6.0 %collective-permute-start.7 = (bf16[448,128]{1,0:T(8,128)(2,1)S(1)}, bf16[448,128]{1,0:T(8,128)(2,1)S(1)}, u32[]{:S(2)}, u32[]{:S(2)}) collective-permute-start(bf16[448,128]{1,0:T(8,128)(2,1)S(1)} %shard_map.56.own_ref), channel_id=1, source_target_pairs={{0,4},{1,5},{2,6},{3,7},{4,0},{5,1},{6,2},{7,3},{8,12},{9,13},{10,... | collective-permute-start | bytes 344072 | tf_op jit(solution)/shard_map/ppermute | solution.py:125
  34.6 5.3 %collective-permute-start.11 = (bf16[592,128]{1,0:T(8,128)(2,1)S(1)}, bf16[592,128]{1,0:T(8,128)(2,1)S(1)}, u32[]{:S(2)}, u32[]{:S(2)}) collective-permute-start(bf16[592,128]{1,0:T(8,128)(2,1)S(1)} %shard_map.59.own_ref), channel_id=1, source_target_pairs={{0,4},{1,5},{2,6},{3,7},{4,0},{5,1},{6,2},{7,3},{8,12},{9,13},{10,... | collective-permute-start | bytes 454664 | tf_op jit(solution)/shard_map/ppermute | solution.py:125
  36.2 4.9 %collective-permute-start.8 = (bf16[448,128]{1,0:T(8,128)(2,1)S(1)}, bf16[448,128]{1,0:T(8,128)(2,1)S(1)}, u32[]{:S(2)}, u32[]{:S(2)}) collective-permute-start(bf16[448,128]{1,0:T(8,128)(2,1)S(1)} %shard_map.57.own_ref), channel_id=1, source_target_pairs={{0,2},{1,3},{2,0},{3,1},{4,6},{5,7},{6,4},{7,5},{8,10},{9,11},{10,... | collective-permute-start | bytes 344072 | tf_op jit(solution)/shard_map/ppermute | solution.py:125
  39.9 2.7 %collective-permute-start.12 = (bf16[576,128]{1,0:T(8,128)(2,1)S(1)}, bf16[576,128]{1,0:T(8,128)(2,1)S(1)}, u32[]{:S(2)}, u32[]{:S(2)}) collective-permute-start(bf16[576,128]{1,0:T(8,128)(2,1)S(1)} %get-tuple-element.91.refs_0_), channel_id=1, source_target_pairs={{0,1},{1,0},{2,3},{3,2},{4,5},{5,4},{6,7},{7,6},{8,9},{9,8},{10,11... | collective-permute-start | bytes 442376 | tf_op jit(solution)/shard_map/ppermute | solution.py:125
  41.2 1.4 %collective-permute-start.13 = (bf16[464,128]{1,0:T(8,128)(2,1)S(1)}, bf16[464,128]{1,0:T(8,128)(2,1)S(1)}, u32[]{:S(2)}, u32[]{:S(2)}) collective-permute-start(bf16[464,128]{1,0:T(8,128)(2,1)S(1)} %get-tuple-element.90.refs_1_.refs_0_), channel_id=1, source_target_pairs={{0,1},{1,0},{2,3},{3,2},{4,5},{5,4},{6,7},{7,6},{8,9},{9,8},{10,11... | collective-permute-start | bytes 356360 | tf_op jit(solution)/shard_map/ppermute | solution.py:125
  41.8 10.6 %copy-start.3 = (f32[128]{0:T(128)S(1)}, f32[128]{0:T(128)}, u32[]{:S(2)}) copy-start(f32[128]{0:T(128)} %param.5) | copy-start | bytes 1540
  43.3 6.9 %collective-permute-start.16 = (f16[272,128]{1,0:T(8,128)(2,1)S(1)}, f16[272,128]{1,0:T(8,128)(2,1)S(1)}, u32[]{:S(2)}, u32[]{:S(2)}) collective-permute-start(f16[272,128]{1,0:T(8,128)(2,1)S(1)} %convert_element_type.46), channel_id=1, source_target_pairs={{0,24},{8,16},{16,8},{24,0},{1,25},{9,17},{17,9},{25,1},{2,26},{10... | collective-permute-start | bytes 208904 | tf_op jit(solution)/shard_map/ppermute | solution.py:122
  45.1 7.3 %collective-permute-start.15 = (f16[272,128]{1,0:T(8,128)(2,1)S(1)}, f16[272,128]{1,0:T(8,128)(2,1)S(1)}, u32[]{:S(2)}, u32[]{:S(2)}) collective-permute-start(f16[272,128]{1,0:T(8,128)(2,1)S(1)} %convert_element_type.44), channel_id=1, source_target_pairs={{0,16},{8,24},{16,0},{24,8},{1,17},{9,25},{17,1},{25,9},{2,18},{10... | collective-permute-start | bytes 208904 | tf_op jit(solution)/shard_map/ppermute | solution.py:122
  45.1 7.3 %collective-permute-start.14 = (f16[272,128]{1,0:T(8,128)(2,1)S(1)}, f16[272,128]{1,0:T(8,128)(2,1)S(1)}, u32[]{:S(2)}, u32[]{:S(2)}) collective-permute-start(f16[272,128]{1,0:T(8,128)(2,1)S(1)} %convert_element_type.42), channel_id=1, source_target_pairs={{0,8},{8,0},{16,24},{24,16},{1,9},{9,1},{17,25},{25,17},{2,10},{10... | collective-permute-start | bytes 208904 | tf_op jit(solution)/shard_map/ppermute | solution.py:122
  52.6 6.9 %collective-permute-start.19 = (bf16[272,128]{1,0:T(8,128)(2,1)S(1)}, bf16[272,128]{1,0:T(8,128)(2,1)S(1)}, u32[]{:S(2)}, u32[]{:S(2)}) collective-permute-start(bf16[272,128]{1,0:T(8,128)(2,1)S(1)} %get-tuple-element.103.refs_0_), channel_id=1, source_target_pairs={{0,24},{8,16},{16,8},{24,0},{1,25},{9,17},{17,9},{25,1},{2,26},{10... | collective-permute-start | bytes 208904 | tf_op jit(solution)/shard_map/ppermute | solution.py:122
  54.4 7.2 %collective-permute-start.18 = (bf16[272,128]{1,0:T(8,128)(2,1)S(1)}, bf16[272,128]{1,0:T(8,128)(2,1)S(1)}, u32[]{:S(2)}, u32[]{:S(2)}) collective-permute-start(bf16[272,128]{1,0:T(8,128)(2,1)S(1)} %get-tuple-element.103.refs_0_), channel_id=1, source_target_pairs={{0,16},{8,24},{16,0},{24,8},{1,17},{9,25},{17,1},{25,9},{2,18},{10... | collective-permute-start | bytes 208904 | tf_op jit(solution)/shard_map/ppermute | solution.py:122
  54.4 7.2 %collective-permute-start.17 = (bf16[272,128]{1,0:T(8,128)(2,1)S(1)}, bf16[272,128]{1,0:T(8,128)(2,1)S(1)}, u32[]{:S(2)}, u32[]{:S(2)}) collective-permute-start(bf16[272,128]{1,0:T(8,128)(2,1)S(1)} %get-tuple-element.103.refs_0_), channel_id=1, source_target_pairs={{0,8},{8,0},{16,24},{24,16},{1,9},{9,1},{17,25},{25,17},{2,10},{10... | collective-permute-start | bytes 208904 | tf_op jit(solution)/shard_map/ppermute | solution.py:122
  62.1 1.8 %collective-permute-start.23 = (f32[592,128]{1,0:T(8,128)S(1)}, f32[592,128]{1,0:T(8,128)S(1)}, u32[]{:S(2)}, u32[]{:S(2)}) collective-permute-start(f32[592,128]{1,0:T(8,128)S(1)} %get-tuple-element.107), channel_id=1, source_target_pairs={{0,1},{1,0},{2,3},{3,2},{4,5},{5,4},{6,7},{7,6},{8,9},{9,8},{10,11... | collective-permute-start | bytes 909320 | tf_op jit(solution)/shard_map/ppermute | solution.py:125
  62.6 2.9 %collective-permute-start.20 = (f32[448,128]{1,0:T(8,128)S(1)}, f32[448,128]{1,0:T(8,128)S(1)}, u32[]{:S(2)}, u32[]{:S(2)}) collective-permute-start(f32[448,128]{1,0:T(8,128)S(1)} %shard_map.67), channel_id=1, source_target_pairs={{0,1},{1,0},{2,3},{3,2},{4,5},{5,4},{6,7},{7,6},{8,9},{9,8},{10,11... | collective-permute-start | bytes 688136 | tf_op jit(solution)/shard_map/ppermute | solution.py:125
  63.9 5.9 %collective-permute-start.24 = (bf16[592,128]{1,0:T(8,128)(2,1)S(1)}, bf16[592,128]{1,0:T(8,128)(2,1)S(1)}, u32[]{:S(2)}, u32[]{:S(2)}) collective-permute-start(bf16[592,128]{1,0:T(8,128)(2,1)S(1)} %shard_map.70.own_ref), channel_id=1, source_target_pairs={{0,2},{1,3},{2,0},{3,1},{4,6},{5,7},{6,4},{7,5},{8,10},{9,11},{10,... | collective-permute-start | bytes 454664 | tf_op jit(solution)/shard_map/ppermute | solution.py:125
  65.5 5.3 %collective-permute-start.21 = (bf16[448,128]{1,0:T(8,128)(2,1)S(1)}, bf16[448,128]{1,0:T(8,128)(2,1)S(1)}, u32[]{:S(2)}, u32[]{:S(2)}) collective-permute-start(bf16[448,128]{1,0:T(8,128)(2,1)S(1)} %shard_map.68.own_ref), channel_id=1, source_target_pairs={{0,4},{1,5},{2,6},{3,7},{4,0},{5,1},{6,2},{7,3},{8,12},{9,13},{10,... | collective-permute-start | bytes 344072 | tf_op jit(solution)/shard_map/ppermute | solution.py:125
  69.9 5.3 %collective-permute-start.25 = (bf16[592,128]{1,0:T(8,128)(2,1)S(1)}, bf16[592,128]{1,0:T(8,128)(2,1)S(1)}, u32[]{:S(2)}, u32[]{:S(2)}) collective-permute-start(bf16[592,128]{1,0:T(8,128)(2,1)S(1)} %shard_map.71.own_ref), channel_id=1, source_target_pairs={{0,4},{1,5},{2,6},{3,7},{4,0},{5,1},{6,2},{7,3},{8,12},{9,13},{10,... | collective-permute-start | bytes 454664 | tf_op jit(solution)/shard_map/ppermute | solution.py:125
  70.8 4.9 %collective-permute-start.22 = (bf16[448,128]{1,0:T(8,128)(2,1)S(1)}, bf16[448,128]{1,0:T(8,128)(2,1)S(1)}, u32[]{:S(2)}, u32[]{:S(2)}) collective-permute-start(bf16[448,128]{1,0:T(8,128)(2,1)S(1)} %shard_map.69.own_ref), channel_id=1, source_target_pairs={{0,2},{1,3},{2,0},{3,1},{4,6},{5,7},{6,4},{7,5},{8,10},{9,11},{10,... | collective-permute-start | bytes 344072 | tf_op jit(solution)/shard_map/ppermute | solution.py:125
  75.3 1.9 %collective-permute-start.26 = (bf16[576,128]{1,0:T(8,128)(2,1)S(1)}, bf16[576,128]{1,0:T(8,128)(2,1)S(1)}, u32[]{:S(2)}, u32[]{:S(2)}) collective-permute-start(bf16[576,128]{1,0:T(8,128)(2,1)S(1)} %get-tuple-element.114.refs_0_), channel_id=1, source_target_pairs={{0,1},{1,0},{2,3},{3,2},{4,5},{5,4},{6,7},{7,6},{8,9},{9,8},{10,11... | collective-permute-start | bytes 442376 | tf_op jit(solution)/shard_map/ppermute | solution.py:125
  75.8 1.4 %collective-permute-start.27 = (bf16[464,128]{1,0:T(8,128)(2,1)S(1)}, bf16[464,128]{1,0:T(8,128)(2,1)S(1)}, u32[]{:S(2)}, u32[]{:S(2)}) collective-permute-start(bf16[464,128]{1,0:T(8,128)(2,1)S(1)} %get-tuple-element.113.refs_1_.refs_0_), channel_id=1, source_target_pairs={{0,1},{1,0},{2,3},{3,2},{4,5},{5,4},{6,7},{7,6},{8,9},{9,8},{10,11... | collective-permute-start | bytes 356360 | tf_op jit(solution)/shard_map/ppermute | solution.py:125
  77.9 5.3 %collective-permute-start.28 = (bf16[272,128]{1,0:T(8,128)(2,1)S(1)}, bf16[272,128]{1,0:T(8,128)(2,1)S(1)}, u32[]{:S(2)}, u32[]{:S(2)}) collective-permute-start(bf16[272,128]{1,0:T(8,128)(2,1)S(1)} %get-tuple-element.117), channel_id=1, source_target_pairs={{0,8},{8,0},{16,24},{24,16},{1,9},{9,1},{17,25},{25,17},{2,10},{10... | collective-permute-start | bytes 208904 | tf_op jit(solution)/shard_map/ppermute | solution.py:122
  78.0 8.9 %collective-permute-start.29 = (bf16[272,128]{1,0:T(8,128)(2,1)S(1)}, bf16[272,128]{1,0:T(8,128)(2,1)S(1)}, u32[]{:S(2)}, u32[]{:S(2)}) collective-permute-start(bf16[272,128]{1,0:T(8,128)(2,1)S(1)} %get-tuple-element.118), channel_id=1, source_target_pairs={{0,16},{8,24},{16,0},{24,8},{1,17},{9,25},{17,1},{25,9},{2,18},{10... | collective-permute-start | bytes 208904 | tf_op jit(solution)/shard_map/ppermute | solution.py:122
  80.2 6.7 %collective-permute-start.30 = (bf16[272,128]{1,0:T(8,128)(2,1)S(1)}, bf16[272,128]{1,0:T(8,128)(2,1)S(1)}, u32[]{:S(2)}, u32[]{:S(2)}) collective-permute-start(bf16[272,128]{1,0:T(8,128)(2,1)S(1)} %get-tuple-element.119), channel_id=1, source_target_pairs={{0,24},{8,16},{16,8},{24,0},{1,25},{9,17},{17,9},{25,1},{2,26},{10... | collective-permute-start | bytes 208904 | tf_op jit(solution)/shard_map/ppermute | solution.py:122
  87.1 6.3 %collective-permute-start.33 = (bf16[272,128]{1,0:T(8,128)(2,1)S(1)}, bf16[272,128]{1,0:T(8,128)(2,1)S(1)}, u32[]{:S(2)}, u32[]{:S(2)}) collective-permute-start(bf16[272,128]{1,0:T(8,128)(2,1)S(1)} %get-tuple-element.127.refs_0_), channel_id=1, source_target_pairs={{0,24},{8,16},{16,8},{24,0},{1,25},{9,17},{17,9},{25,1},{2,26},{10... | collective-permute-start | bytes 208904 | tf_op jit(solution)/shard_map/ppermute | solution.py:122
  89.0 6.4 %collective-permute-start.32 = (bf16[272,128]{1,0:T(8,128)(2,1)S(1)}, bf16[272,128]{1,0:T(8,128)(2,1)S(1)}, u32[]{:S(2)}, u32[]{:S(2)}) collective-permute-start(bf16[272,128]{1,0:T(8,128)(2,1)S(1)} %get-tuple-element.127.refs_0_), channel_id=1, source_target_pairs={{0,16},{8,24},{16,0},{24,8},{1,17},{9,25},{17,1},{25,9},{2,18},{10... | collective-permute-start | bytes 208904 | tf_op jit(solution)/shard_map/ppermute | solution.py:122
  89.9 5.6 %collective-permute-start.31 = (bf16[272,128]{1,0:T(8,128)(2,1)S(1)}, bf16[272,128]{1,0:T(8,128)(2,1)S(1)}, u32[]{:S(2)}, u32[]{:S(2)}) collective-permute-start(bf16[272,128]{1,0:T(8,128)(2,1)S(1)} %get-tuple-element.127.refs_0_), channel_id=1, source_target_pairs={{0,8},{8,0},{16,24},{24,16},{1,9},{9,1},{17,25},{25,17},{2,10},{10... | collective-permute-start | bytes 208904 | tf_op jit(solution)/shard_map/ppermute | solution.py:122
  96.0 1.8 %collective-permute-start.37 = (f32[592,128]{1,0:T(8,128)S(1)}, f32[592,128]{1,0:T(8,128)S(1)}, u32[]{:S(2)}, u32[]{:S(2)}) collective-permute-start(f32[592,128]{1,0:T(8,128)S(1)} %get-tuple-element.131), channel_id=1, source_target_pairs={{0,1},{1,0},{2,3},{3,2},{4,5},{5,4},{6,7},{7,6},{8,9},{9,8},{10,11... | collective-permute-start | bytes 909320 | tf_op jit(solution)/shard_map/ppermute | solution.py:125
  96.5 2.9 %collective-permute-start.34 = (f32[448,128]{1,0:T(8,128)S(1)}, f32[448,128]{1,0:T(8,128)S(1)}, u32[]{:S(2)}, u32[]{:S(2)}) collective-permute-start(f32[448,128]{1,0:T(8,128)S(1)} %shard_map.79), channel_id=1, source_target_pairs={{0,1},{1,0},{2,3},{3,2},{4,5},{5,4},{6,7},{7,6},{8,9},{9,8},{10,11... | collective-permute-start | bytes 688136 | tf_op jit(solution)/shard_map/ppermute | solution.py:125
  97.8 5.9 %collective-permute-start.38 = (bf16[592,128]{1,0:T(8,128)(2,1)S(1)}, bf16[592,128]{1,0:T(8,128)(2,1)S(1)}, u32[]{:S(2)}, u32[]{:S(2)}) collective-permute-start(bf16[592,128]{1,0:T(8,128)(2,1)S(1)} %shard_map.82.own_ref), channel_id=1, source_target_pairs={{0,2},{1,3},{2,0},{3,1},{4,6},{5,7},{6,4},{7,5},{8,10},{9,11},{10,... | collective-permute-start | bytes 454664 | tf_op jit(solution)/shard_map/ppermute | solution.py:125
  99.4 5.6 %collective-permute-start.35 = (bf16[448,128]{1,0:T(8,128)(2,1)S(1)}, bf16[448,128]{1,0:T(8,128)(2,1)S(1)}, u32[]{:S(2)}, u32[]{:S(2)}) collective-permute-start(bf16[448,128]{1,0:T(8,128)(2,1)S(1)} %shard_map.80.own_ref), channel_id=1, source_target_pairs={{0,4},{1,5},{2,6},{3,7},{4,0},{5,1},{6,2},{7,3},{8,12},{9,13},{10,... | collective-permute-start | bytes 344072 | tf_op jit(solution)/shard_map/ppermute | solution.py:125
  100.7 12.9 %collective-permute-start.46 = (f32[1024,128]{1,0:T(8,128)S(1)}, f32[1024,128]{1,0:T(8,128)S(1)}, u32[]{:S(2)}, u32[]{:S(2)}) collective-permute-start(f32[1024,128]{1,0:T(8,128)S(1)} %get-tuple-element.145.refs_11_), channel_id=1, source_target_pairs={{0,1},{1,0},{2,3},{3,2},{4,5},{5,4},{6,7},{7,6},{8,9},{9,8},{10,11... | collective-permute-start | bytes 1572872 | tf_op jit(solution)/shard_map/ppermute | solution.py:125
  103.8 5.3 %collective-permute-start.39 = (bf16[592,128]{1,0:T(8,128)(2,1)S(1)}, bf16[592,128]{1,0:T(8,128)(2,1)S(1)}, u32[]{:S(2)}, u32[]{:S(2)}) collective-permute-start(bf16[592,128]{1,0:T(8,128)(2,1)S(1)} %shard_map.83.own_ref), channel_id=1, source_target_pairs={{0,4},{1,5},{2,6},{3,7},{4,0},{5,1},{6,2},{7,3},{8,12},{9,13},{10,... | collective-permute-start | bytes 454664 | tf_op jit(solution)/shard_map/ppermute | solution.py:125
  105.1 4.9 %collective-permute-start.36 = (bf16[448,128]{1,0:T(8,128)(2,1)S(1)}, bf16[448,128]{1,0:T(8,128)(2,1)S(1)}, u32[]{:S(2)}, u32[]{:S(2)}) collective-permute-start(bf16[448,128]{1,0:T(8,128)(2,1)S(1)} %shard_map.81.own_ref), channel_id=1, source_target_pairs={{0,2},{1,3},{2,0},{3,1},{4,6},{5,7},{6,4},{7,5},{8,10},{9,11},{10,... | collective-permute-start | bytes 344072 | tf_op jit(solution)/shard_map/ppermute | solution.py:125
  110.0 1.2 %collective-permute-start.40 = (f32[8,128]{1,0:T(8,128)S(1)}, f32[8,128]{1,0:T(8,128)S(1)}, u32[]{:S(2)}, u32[]{:S(2)}) collective-permute-start(f32[8,128]{1,0:T(8,128)S(1)} %get-tuple-element.137.own_ref), channel_id=1, source_target_pairs={{0,1},{1,0},{2,3},{3,2},{4,5},{5,4},{6,7},{7,6},{8,9},{9,8},{10,11... | collective-permute-start | bytes 12296 | tf_op jit(solution)/shard_map/ppermute | solution.py:125
  111.2 6.8 %collective-permute-start.44 = (f32[576,128]{1,0:T(8,128)S(1)}, f32[576,128]{1,0:T(8,128)S(1)}, u32[]{:S(2)}, u32[]{:S(2)}) collective-permute-start(f32[576,128]{1,0:T(8,128)S(1)} %get-tuple-element.141.refs_4_), channel_id=1, source_target_pairs={{0,1},{1,0},{2,3},{3,2},{4,5},{5,4},{6,7},{7,6},{8,9},{9,8},{10,11... | collective-permute-start | bytes 884744 | tf_op jit(solution)/shard_map/ppermute | solution.py:125
  111.4 6.7 %collective-permute-start.45 = (f32[448,128]{1,0:T(8,128)S(1)}, f32[448,128]{1,0:T(8,128)S(1)}, u32[]{:S(2)}, u32[]{:S(2)}) collective-permute-start(f32[448,128]{1,0:T(8,128)S(1)} %get-tuple-element.142.refs_5_), channel_id=1, source_target_pairs={{0,1},{1,0},{2,3},{3,2},{4,5},{5,4},{6,7},{7,6},{8,9},{9,8},{10,11... | collective-permute-start | bytes 688136 | tf_op jit(solution)/shard_map/ppermute | solution.py:125
  111.8 5.4 %collective-permute-start.43 = (f32[8,128]{1,0:T(8,128)S(1)}, f32[8,128]{1,0:T(8,128)S(1)}, u32[]{:S(2)}, u32[]{:S(2)}) collective-permute-start(f32[8,128]{1,0:T(8,128)S(1)} %get-tuple-element.140.refs_0_), channel_id=1, source_target_pairs={{0,24},{8,16},{16,8},{24,0},{1,25},{9,17},{17,9},{25,1},{2,26},{10... | collective-permute-start | bytes 12296 | tf_op jit(solution)/shard_map/ppermute | solution.py:122
  113.6 4.5 %collective-permute-start.42 = (f32[8,128]{1,0:T(8,128)S(1)}, f32[8,128]{1,0:T(8,128)S(1)}, u32[]{:S(2)}, u32[]{:S(2)}) collective-permute-start(f32[8,128]{1,0:T(8,128)S(1)} %get-tuple-element.140.refs_0_), channel_id=1, source_target_pairs={{0,16},{8,24},{16,0},{24,8},{1,17},{9,25},{17,1},{25,9},{2,18},{10... | collective-permute-start | bytes 12296 | tf_op jit(solution)/shard_map/ppermute | solution.py:122
  113.6 4.5 %collective-permute-start.41 = (f32[8,128]{1,0:T(8,128)S(1)}, f32[8,128]{1,0:T(8,128)S(1)}, u32[]{:S(2)}, u32[]{:S(2)}) collective-permute-start(f32[8,128]{1,0:T(8,128)S(1)} %get-tuple-element.140.refs_0_), channel_id=1, source_target_pairs={{0,8},{8,0},{16,24},{24,16},{1,9},{9,1},{17,25},{25,17},{2,10},{10... | collective-permute-start | bytes 12296 | tf_op jit(solution)/shard_map/ppermute | solution.py:122

commit v6 on v5

--- a/solution.py
+++ b/solution.py
@@ -145,6 +145,20 @@
                 ref[pl.ds(0, feat_share), :] = part.astype(wire)
                 put_rows(ref, delta)
 
+    def put_block(wire, ref, part, delta):
+        if wire == F16:
+            exponent = exponent_of(jnp.max(jnp.abs(part), axis=0, keepdims=True))
+            ref[pl.ds(0, feat_share), :] = part * jnp.exp2(-exponent)
+            put_scaled(ref, exponent, delta)
+        else:
+            ref[pl.ds(0, feat_share), :] = part.astype(wire)
+            put_rows(ref, delta)
+
+    by_block = feat_share % 128 == 0
+
+    def columns(step):
+        return pl.ds(row_place(step), feat_share)
+
     def cut_shapes(wire):
         return [((feat_share + PAD, outs), F32 if wire == F16 else wire)] * (n_row - 1)
 
@@ -170,7 +184,22 @@
                 prod[cols, :] = (part[0:outs] + part[outs : 2 * outs]).T
             cut(wire, prod, jnp.zeros((1, outs), F32), own_ref, msg_refs)
 
+        def block_product(a_ref, turned_ref, step):
+            part = jnp.dot(turned_ref[...], a_ref[:, columns(step)], preferred_element_type=F32)
+            return (part[0:outs] + part[outs : 2 * outs]).T
+
+        def messages(a_ref, turned_ref, *msg_refs):
+            for step, ref in zip(row_steps, msg_refs):
+                put_block(wire, ref, block_product(a_ref, turned_ref, step), jnp.zeros((1, outs), F32))
+
+        def own_block(a_ref, turned_ref, own_ref):
+            own_ref[...] = block_product(a_ref, turned_ref, 0)
+
         turned, residual = call(split, [((2 * outs, tokens), BF16), token_rows], [targets])
+        if by_block:
+            got = scattered(wire, call(messages, cut_shapes(wire), [states, turned]))
+            (own,) = call(own_block, [feature_rows], [states, turned])
+            return residual, own, got
         own, *sends = call(
             product,
             [feature_rows] + cut_shapes(wire),
@@ -204,7 +233,29 @@
                 prod[cols, :] = (part_ref[:, cols] + half_product(a_ref, theirs_refs, 1, cols)).T
             cut(wire, prod, delta, own_ref, msg_refs)
 
+        def block_product(a_ref, part_ref, refs, step):
+            return (part_ref[:, columns(step)] + half_product(a_ref, refs, 1, columns(step))).T
+
+        def messages(a_ref, *refs):
+            mine_ref, theirs_refs, part_ref = refs[0], refs[1 : levels + 1], refs[levels + 1]
+            delta_ref, *msg_refs = refs[levels + 2 :]
+            delta = get_row(mine_ref) + get_row(theirs_refs[-1])
+            spread(delta_ref, delta)
+            for step, ref in zip(row_steps, msg_refs):
+                put_block(wire, ref, block_product(a_ref, part_ref, theirs_refs, step), delta)
+
+        def own_block(a_ref, *refs):
+            *theirs_refs, part_ref, own_ref = refs
+            own_ref[...] = block_product(a_ref, part_ref, theirs_refs, 0)
+
         (part,) = call(first_half, [((outs, feats), F32)], [states, *mine])
+        if by_block:
+            delta, *sends = call(
+                messages, [scalar] + cut_shapes(wire), [states, mine[-1], *theirs, part]
+            )
+            got = scattered(wire, sends)
+            (own,) = call(own_block, [feature_rows], [states, *theirs, part])
+            return own, delta, got
         own, delta, *sends = call(
             second_half,
             [feature_rows, scalar] + cut_shapes(wire),
@@ -422,18 +473,19 @@
             before = (gamma, dir_sq, direction, images)
 
     def both_cores(own_ref, got_ref, *refs):
-        out_ref = refs[levels]
+        out_ref = refs[levels - 1]
         out_ref[...] = own_ref[...] + got_ref[...]
 
     vmem, anywhere = pl.BlockSpec(memory_space=pltpu.VMEM), pl.BlockSpec(memory_space=pl.ANY)
-    delta, *images = pl.pallas_call(
+    delta, *later = pl.pallas_call(
         both_cores,
-        out_shape=[jax.ShapeDtypeStruct(*scalar)] + [jax.ShapeDtypeStruct((rows, outs), F32) for rows in piece_rows],
-        in_specs=[vmem, vmem] + [anywhere] * levels,
-        out_specs=[vmem] + [anywhere] * levels,
-        input_output_aliases={2 + index: 1 + index for index in range(levels)},
+        out_shape=[jax.ShapeDtypeStruct(*scalar)] + [jax.ShapeDtypeStruct((rows, outs), F32) for rows in piece_rows[1:]],
+        in_specs=[vmem, vmem] + [anywhere] * (levels - 1),
+        out_specs=[vmem] + [anywhere] * (levels - 1),
+        input_output_aliases={2 + index: 1 + index for index in range(levels - 1)},
         compiler_params=pltpu.CompilerParams(vmem_limit_bytes=LIMIT),
-    )(part, over_group(1, part), *images)
+    )(part, over_group(1, part), *images[1:])
+    images = [images[0], *later]
     other_images = [over_group(1, image) for image in images]
     other_residual = over_group(1, residual)
     got = {step: over_row(step, delta) for step in row_steps}

time: 119 us -> 119 us (level)
  waiting for transfers between devices: 50.6 us -> 49.3 us
    ppermute x21, waiting for transfers between devices: 29.4 us -> 28.2 us  [over_row(): return lax.ppermute(value, 'row', [(i, i ^ step) for i in range(n_row)])]
    pallas_call x37 -> x40, Pallas kernels: 11.7 us -> 12.4 us  [call(): pl.pallas_call(kernel, out_shape=[jax.ShapeDtypeStruct(shape, dtype) for...]
  transfers between devices with their start and end apart: 47 -> 47, of which waited for: 26 -> 26; matrix products, arithmetic and copies ran while one was open for 0% -> 0% of each run, Pallas kernels for 5% -> 6%
where the time goes in v6:
time: 119 us; the launch traced here: 118 us
  starting transfers between devices  52 us (44%)
  waiting for transfers between devices  49.3 us (41%)
  Pallas kernels  12.4 us (10%)
  local copies, waits for them, and re-layouts  3.41 us (3%)
    ppermute x21, starting transfers between devices, over_row(): return lax.ppermute(value, 'row', [(i, i ^ step) for i in range(n_row)])  32.5 us
    ppermute x21, waiting for transfers between devices, over_row(): return lax.ppermute(value, 'row', [(i, i ^ step) for i in range(n_row)])  28.2 us
    ppermute x26, waiting for transfers between devices, over_group(): return lax.ppermute(value, 'group', [(i, i ^ step) for i in range(n_group)])  21.1 us
    ppermute x26, starting transfers between devices, over_group(): return lax.ppermute(value, 'group', [(i, i ^ step) for i in range(n_group)])  19.4 us
    pallas_call x40, Pallas kernels, call(): pl.pallas_call(kernel, out_shape=[jax.ShapeDtypeStruct(shape, dtype) for...  12.4 us
    unnamed x8, local copies, waits for them, and re-layouts  3.41 us
  transfers between devices with their start and end apart: 47, of which 26 were waited for; matrix products, arithmetic and copies ran while one was open for 0% of the time, Pallas kernels for 6%

profile of v6, /device:TPU:0, one launch (start us, length us, event | category | flops | bytes accessed | tf_op | source)
XLA Modules:
  0.0 118.3 jit_solution(16100681955499689232)
XLA Ops:
  0.6 1.2 %copy-done.2 = f32[2048,128]{1,0:T(8,128)S(1)} copy-done((f32[2048,128]{1,0:T(8,128)S(1)}, f32[2048,128]{1,0:T(8,128)}, u32[]{:S(2)}) %copy-start.2) | copy-done | bytes 1048600
  2.2 2.2 %copy-done = bf16[2048,1024]{1,0:T(8,128)(2,1)S(1)} copy-done((bf16[2048,1024]{1,0:T(8,128)(2,1)S(1)}, bf16[2048,1024]{1,0:T(8,128)(2,1)}, u32[]{:S(2)}) %copy-start) | copy-done | bytes 4194328
  4.4 1.2 shard_map.52
  5.6 5.1 %collective-permute-start.2 = (f16[272,128]{1,0:T(8,128)(2,1)S(1)}, f16[272,128]{1,0:T(8,128)(2,1)S(1)}, u32[]{:S(2)}, u32[]{:S(2)}) collective-permute-start(f16[272,128]{1,0:T(8,128)(2,1)S(1)} %convert_element_type.40), channel_id=1, source_target_pairs={{0,24},{8,16},{16,8},{24,0},{1,25},{9,17},{17,9},{25,1},{2,26},{10... | collective-permute-start | bytes 208904 | tf_op jit(solution)/shard_map/ppermute | solution.py:122
  10.8 0.6 collective-permute-start
  12.0 1.3 %collective-permute-done.2 = f16[272,128]{1,0:T(8,128)(2,1)S(1)} collective-permute-done((f16[272,128]{1,0:T(8,128)(2,1)S(1)}, f16[272,128]{1,0:T(8,128)(2,1)S(1)}, u32[]{:S(2)}, u32[]{:S(2)}) %collective-permute-start.2) | collective-permute-done | bytes 69664 | tf_op jit(solution)/shard_map/ppermute | solution.py:122
  13.3 3.3 %collective-permute-done.1 = f16[272,128]{1,0:T(8,128)(2,1)S(1)} collective-permute-done((f16[272,128]{1,0:T(8,128)(2,1)S(1)}, f16[272,128]{1,0:T(8,128)(2,1)S(1)}, u32[]{:S(2)}, u32[]{:S(2)}) %collective-permute-start.1) | collective-permute-done | bytes 69664 | tf_op jit(solution)/shard_map/ppermute | solution.py:122
  16.7 2.8 %collective-permute-start.5 = (bf16[272,128]{1,0:T(8,128)(2,1)S(1)}, bf16[272,128]{1,0:T(8,128)(2,1)S(1)}, u32[]{:S(2)}, u32[]{:S(2)}) collective-permute-start(bf16[272,128]{1,0:T(8,128)(2,1)S(1)} %get-tuple-element.75.refs_0_), channel_id=1, source_target_pairs={{0,24},{8,16},{16,8},{24,0},{1,25},{9,17},{17,9},{25,1},{2,26},{10... | collective-permute-start | bytes 208904 | tf_op jit(solution)/shard_map/ppermute | solution.py:122
  19.5 1.6 %collective-permute-start.3 = (bf16[272,128]{1,0:T(8,128)(2,1)S(1)}, bf16[272,128]{1,0:T(8,128)(2,1)S(1)}, u32[]{:S(2)}, u32[]{:S(2)}) collective-permute-start(bf16[272,128]{1,0:T(8,128)(2,1)S(1)} %get-tuple-element.75.refs_0_), channel_id=1, source_target_pairs={{0,8},{8,0},{16,24},{24,16},{1,9},{9,1},{17,25},{25,17},{2,10},{10... | collective-permute-start | bytes 208904 | tf_op jit(solution)/shard_map/ppermute | solution.py:122
  21.2 2.4 %collective-permute-done.5.refs_3_ = bf16[272,128]{1,0:T(8,128)(2,1)S(1)} collective-permute-done((bf16[272,128]{1,0:T(8,128)(2,1)S(1)}, bf16[272,128]{1,0:T(8,128)(2,1)S(1)}, u32[]{:S(2)}, u32[]{:S(2)}) %collective-permute-start.5) | collective-permute-done | bytes 69664 | tf_op jit(solution)/shard_map/ppermute | solution.py:122
  23.6 2.4 %collective-permute-done.4.refs_2_ = bf16[272,128]{1,0:T(8,128)(2,1)S(1)} collective-permute-done((bf16[272,128]{1,0:T(8,128)(2,1)S(1)}, bf16[272,128]{1,0:T(8,128)(2,1)S(1)}, u32[]{:S(2)}, u32[]{:S(2)}) %collective-permute-start.4) | collective-permute-done | bytes 69664 | tf_op jit(solution)/shard_map/ppermute | solution.py:122
  27.0 0.6 collective-permute-start.10
  27.5 0.7 shard_map.55
  28.3 1.6 %collective-permute-start.7 = (bf16[592,128]{1,0:T(8,128)(2,1)S(1)}, bf16[592,128]{1,0:T(8,128)(2,1)S(1)}, u32[]{:S(2)}, u32[]{:S(2)}) collective-permute-start(bf16[592,128]{1,0:T(8,128)(2,1)S(1)} %shard_map.56.own_ref), channel_id=1, source_target_pairs={{0,2},{1,3},{2,0},{3,1},{4,6},{5,7},{6,4},{7,5},{8,10},{9,11},{10,... | collective-permute-start | bytes 454664 | tf_op jit(solution)/shard_map/ppermute | solution.py:125
  30.0 1.6 %collective-permute-start.11 = (bf16[448,128]{1,0:T(8,128)(2,1)S(1)}, bf16[448,128]{1,0:T(8,128)(2,1)S(1)}, u32[]{:S(2)}, u32[]{:S(2)}) collective-permute-start(bf16[448,128]{1,0:T(8,128)(2,1)S(1)} %shard_map.60.own_ref), channel_id=1, source_target_pairs={{0,4},{1,5},{2,6},{3,7},{4,0},{5,1},{6,2},{7,3},{8,12},{9,13},{10,... | collective-permute-start | bytes 344072 | tf_op jit(solution)/shard_map/ppermute | solution.py:125
  31.5 2.7 %collective-permute-done.7.got_ref = bf16[592,128]{1,0:T(8,128)(2,1)S(1)} collective-permute-done((bf16[592,128]{1,0:T(8,128)(2,1)S(1)}, bf16[592,128]{1,0:T(8,128)(2,1)S(1)}, u32[]{:S(2)}, u32[]{:S(2)}) %collective-permute-start.7) | collective-permute-done | bytes 151584 | tf_op jit(solution)/shard_map/ppermute | solution.py:125
  34.3 1.6 %collective-permute-start.8 = (bf16[592,128]{1,0:T(8,128)(2,1)S(1)}, bf16[592,128]{1,0:T(8,128)(2,1)S(1)}, u32[]{:S(2)}, u32[]{:S(2)}) collective-permute-start(bf16[592,128]{1,0:T(8,128)(2,1)S(1)} %shard_map.57.own_ref), channel_id=1, source_target_pairs={{0,4},{1,5},{2,6},{3,7},{4,0},{5,1},{6,2},{7,3},{8,12},{9,13},{10,... | collective-permute-start | bytes 454664 | tf_op jit(solution)/shard_map/ppermute | solution.py:125
  36.0 1.5 %collective-permute-start.12 = (bf16[448,128]{1,0:T(8,128)(2,1)S(1)}, bf16[448,128]{1,0:T(8,128)(2,1)S(1)}, u32[]{:S(2)}, u32[]{:S(2)}) collective-permute-start(bf16[448,128]{1,0:T(8,128)(2,1)S(1)} %shard_map.61.own_ref), channel_id=1, source_target_pairs={{0,2},{1,3},{2,0},{3,1},{4,6},{5,7},{6,4},{7,5},{8,10},{9,11},{10,... | collective-permute-start | bytes 344072 | tf_op jit(solution)/shard_map/ppermute | solution.py:125
  37.5 2.0 %collective-permute-done.8.got_ref = bf16[592,128]{1,0:T(8,128)(2,1)S(1)} collective-permute-done((bf16[592,128]{1,0:T(8,128)(2,1)S(1)}, bf16[592,128]{1,0:T(8,128)(2,1)S(1)}, u32[]{:S(2)}, u32[]{:S(2)}) %collective-permute-start.8) | collective-permute-done | bytes 151584 | tf_op jit(solution)/shard_map/ppermute | solution.py:125
  39.7 1.1 collective-permute-done.12.got_ref
  41.0 0.6 shard_map.63.refs_2_.refs_3_
  41.5 0.8 collective-permute-done.13.refs_1_.refs_2_
  42.3 0.6 shard_map.65
  42.9 1.8 %collective-permute-start.16 = (f16[272,128]{1,0:T(8,128)(2,1)S(1)}, f16[272,128]{1,0:T(8,128)(2,1)S(1)}, u32[]{:S(2)}, u32[]{:S(2)}) collective-permute-start(f16[272,128]{1,0:T(8,128)(2,1)S(1)} %convert_element_type.46), channel_id=1, source_target_pairs={{0,24},{8,16},{16,8},{24,0},{1,25},{9,17},{17,9},{25,1},{2,26},{10... | collective-permute-start | bytes 208904 | tf_op jit(solution)/shard_map/ppermute | solution.py:122
  44.7 2.8 %collective-permute-start.14 = (f16[272,128]{1,0:T(8,128)(2,1)S(1)}, f16[272,128]{1,0:T(8,128)(2,1)S(1)}, u32[]{:S(2)}, u32[]{:S(2)}) collective-permute-start(f16[272,128]{1,0:T(8,128)(2,1)S(1)} %convert_element_type.42), channel_id=1, source_target_pairs={{0,8},{8,0},{16,24},{24,16},{1,9},{9,1},{17,25},{25,17},{2,10},{10... | collective-permute-start | bytes 208904 | tf_op jit(solution)/shard_map/ppermute | solution.py:122
  47.8 2.1 %collective-permute-done.16 = f16[272,128]{1,0:T(8,128)(2,1)S(1)} collective-permute-done((f16[272,128]{1,0:T(8,128)(2,1)S(1)}, f16[272,128]{1,0:T(8,128)(2,1)S(1)}, u32[]{:S(2)}, u32[]{:S(2)}) %collective-permute-start.16) | collective-permute-done | bytes 69664 | tf_op jit(solution)/shard_map/ppermute | solution.py:122
  49.9 2.1 %collective-permute-done.15 = f16[272,128]{1,0:T(8,128)(2,1)S(1)} collective-permute-done((f16[272,128]{1,0:T(8,128)(2,1)S(1)}, f16[272,128]{1,0:T(8,128)(2,1)S(1)}, u32[]{:S(2)}, u32[]{:S(2)}) %collective-permute-start.15) | collective-permute-done | bytes 69664 | tf_op jit(solution)/shard_map/ppermute | solution.py:122
  52.2 1.8 %collective-permute-start.19 = (bf16[272,128]{1,0:T(8,128)(2,1)S(1)}, bf16[272,128]{1,0:T(8,128)(2,1)S(1)}, u32[]{:S(2)}, u32[]{:S(2)}) collective-permute-start(bf16[272,128]{1,0:T(8,128)(2,1)S(1)} %get-tuple-element.97.refs_0_), channel_id=1, source_target_pairs={{0,24},{8,16},{16,8},{24,0},{1,25},{9,17},{17,9},{25,1},{2,26},{10... | collective-permute-start | bytes 208904 | tf_op jit(solution)/shard_map/ppermute | solution.py:122
  54.0 2.7 %collective-permute-start.17 = (bf16[272,128]{1,0:T(8,128)(2,1)S(1)}, bf16[272,128]{1,0:T(8,128)(2,1)S(1)}, u32[]{:S(2)}, u32[]{:S(2)}) collective-permute-start(bf16[272,128]{1,0:T(8,128)(2,1)S(1)} %get-tuple-element.97.refs_0_), channel_id=1, source_target_pairs={{0,8},{8,0},{16,24},{24,16},{1,9},{9,1},{17,25},{25,17},{2,10},{10... | collective-permute-start | bytes 208904 | tf_op jit(solution)/shard_map/ppermute | solution.py:122
  56.7 2.5 %collective-permute-done.19.refs_3_ = bf16[272,128]{1,0:T(8,128)(2,1)S(1)} collective-permute-done((bf16[272,128]{1,0:T(8,128)(2,1)S(1)}, bf16[272,128]{1,0:T(8,128)(2,1)S(1)}, u32[]{:S(2)}, u32[]{:S(2)}) %collective-permute-start.19) | collective-permute-done | bytes 69664 | tf_op jit(solution)/shard_map/ppermute | solution.py:122
  59.2 2.0 %collective-permute-done.18.refs_2_ = bf16[272,128]{1,0:T(8,128)(2,1)S(1)} collective-permute-done((bf16[272,128]{1,0:T(8,128)(2,1)S(1)}, bf16[272,128]{1,0:T(8,128)(2,1)S(1)}, u32[]{:S(2)}, u32[]{:S(2)}) %collective-permute-start.18) | collective-permute-done | bytes 69664 | tf_op jit(solution)/shard_map/ppermute | solution.py:122
  62.2 0.6 collective-permute-start.24
  62.7 0.7 shard_map.68
  63.5 1.6 %collective-permute-start.21 = (bf16[592,128]{1,0:T(8,128)(2,1)S(1)}, bf16[592,128]{1,0:T(8,128)(2,1)S(1)}, u32[]{:S(2)}, u32[]{:S(2)}) collective-permute-start(bf16[592,128]{1,0:T(8,128)(2,1)S(1)} %shard_map.69.own_ref), channel_id=1, source_target_pairs={{0,2},{1,3},{2,0},{3,1},{4,6},{5,7},{6,4},{7,5},{8,10},{9,11},{10,... | collective-permute-start | bytes 454664 | tf_op jit(solution)/shard_map/ppermute | solution.py:125
  65.1 0.9 collective-permute-start.25
  66.0 3.4 %collective-permute-done.21.got_ref = bf16[592,128]{1,0:T(8,128)(2,1)S(1)} collective-permute-done((bf16[592,128]{1,0:T(8,128)(2,1)S(1)}, bf16[592,128]{1,0:T(8,128)(2,1)S(1)}, u32[]{:S(2)}, u32[]{:S(2)}) %collective-permute-start.21) | collective-permute-done | bytes 151584 | tf_op jit(solution)/shard_map/ppermute | solution.py:125
  69.5 0.9 collective-permute-start.22
  70.4 1.6 %collective-permute-start.26 = (bf16[448,128]{1,0:T(8,128)(2,1)S(1)}, bf16[448,128]{1,0:T(8,128)(2,1)S(1)}, u32[]{:S(2)}, u32[]{:S(2)}) collective-permute-start(bf16[448,128]{1,0:T(8,128)(2,1)S(1)} %shard_map.74.own_ref), channel_id=1, source_target_pairs={{0,2},{1,3},{2,0},{3,1},{4,6},{5,7},{6,4},{7,5},{8,10},{9,11},{10,... | collective-permute-start | bytes 344072 | tf_op jit(solution)/shard_map/ppermute | solution.py:125
  72.0 2.8 %collective-permute-done.22.got_ref = bf16[592,128]{1,0:T(8,128)(2,1)S(1)} collective-permute-done((bf16[592,128]{1,0:T(8,128)(2,1)S(1)}, bf16[592,128]{1,0:T(8,128)(2,1)S(1)}, u32[]{:S(2)}, u32[]{:S(2)}) %collective-permute-start.22) | collective-permute-done | bytes 151584 | tf_op jit(solution)/shard_map/ppermute | solution.py:125
  75.6 0.6 shard_map.76.refs_2_.refs_3_
  76.1 0.6 collective-permute-done.27.refs_1_.refs_2_
  77.4 2.3 %collective-permute-start.29 = (bf16[272,128]{1,0:T(8,128)(2,1)S(1)}, bf16[272,128]{1,0:T(8,128)(2,1)S(1)}, u32[]{:S(2)}, u32[]{:S(2)}) collective-permute-start(bf16[272,128]{1,0:T(8,128)(2,1)S(1)} %get-tuple-element.111), channel_id=1, source_target_pairs={{0,16},{8,24},{16,0},{24,8},{1,17},{9,25},{17,1},{25,9},{2,18},{10... | collective-permute-start | bytes 208904 | tf_op jit(solution)/shard_map/ppermute | solution.py:122
  79.6 2.1 %collective-permute-start.30 = (bf16[272,128]{1,0:T(8,128)(2,1)S(1)}, bf16[272,128]{1,0:T(8,128)(2,1)S(1)}, u32[]{:S(2)}, u32[]{:S(2)}) collective-permute-start(bf16[272,128]{1,0:T(8,128)(2,1)S(1)} %get-tuple-element.112), channel_id=1, source_target_pairs={{0,24},{8,16},{16,8},{24,0},{1,25},{9,17},{17,9},{25,1},{2,26},{10... | collective-permute-start | bytes 208904 | tf_op jit(solution)/shard_map/ppermute | solution.py:122
  82.6 3.7 %collective-permute-done.29.refs_1_ = bf16[272,128]{1,0:T(8,128)(2,1)S(1)} collective-permute-done((bf16[272,128]{1,0:T(8,128)(2,1)S(1)}, bf16[272,128]{1,0:T(8,128)(2,1)S(1)}, u32[]{:S(2)}, u32[]{:S(2)}) %collective-permute-start.29) | collective-permute-done | bytes 69664 | tf_op jit(solution)/shard_map/ppermute | solution.py:122
  86.5 2.0 %collective-permute-start.33 = (bf16[272,128]{1,0:T(8,128)(2,1)S(1)}, bf16[272,128]{1,0:T(8,128)(2,1)S(1)}, u32[]{:S(2)}, u32[]{:S(2)}) collective-permute-start(bf16[272,128]{1,0:T(8,128)(2,1)S(1)} %get-tuple-element.120.refs_0_), channel_id=1, source_target_pairs={{0,24},{8,16},{16,8},{24,0},{1,25},{9,17},{17,9},{25,1},{2,26},{10... | collective-permute-start | bytes 208904 | tf_op jit(solution)/shard_map/ppermute | solution.py:122
  88.4 0.9 collective-permute-start.32
  89.3 1.6 %collective-permute-start.31 = (bf16[272,128]{1,0:T(8,128)(2,1)S(1)}, bf16[272,128]{1,0:T(8,128)(2,1)S(1)}, u32[]{:S(2)}, u32[]{:S(2)}) collective-permute-start(bf16[272,128]{1,0:T(8,128)(2,1)S(1)} %get-tuple-element.120.refs_0_), channel_id=1, source_target_pairs={{0,8},{8,0},{16,24},{24,16},{1,9},{9,1},{17,25},{25,17},{2,10},{10... | collective-permute-start | bytes 208904 | tf_op jit(solution)/shard_map/ppermute | solution.py:122
  90.9 1.9 %collective-permute-done.33.refs_3_ = bf16[272,128]{1,0:T(8,128)(2,1)S(1)} collective-permute-done((bf16[272,128]{1,0:T(8,128)(2,1)S(1)}, bf16[272,128]{1,0:T(8,128)(2,1)S(1)}, u32[]{:S(2)}, u32[]{:S(2)}) %collective-permute-start.33) | collective-permute-done | bytes 69664 | tf_op jit(solution)/shard_map/ppermute | solution.py:122
  92.8 2.1 %collective-permute-done.32.refs_2_ = bf16[272,128]{1,0:T(8,128)(2,1)S(1)} collective-permute-done((bf16[272,128]{1,0:T(8,128)(2,1)S(1)}, bf16[272,128]{1,0:T(8,128)(2,1)S(1)}, u32[]{:S(2)}, u32[]{:S(2)}) %collective-permute-start.32) | collective-permute-done | bytes 69664 | tf_op jit(solution)/shard_map/ppermute | solution.py:122
  95.9 0.6 collective-permute-start.34
  96.5 0.7 shard_map.81
  97.2 1.5 %collective-permute-start.38 = (bf16[592,128]{1,0:T(8,128)(2,1)S(1)}, bf16[592,128]{1,0:T(8,128)(2,1)S(1)}, u32[]{:S(2)}, u32[]{:S(2)}) collective-permute-start(bf16[592,128]{1,0:T(8,128)(2,1)S(1)} %shard_map.85.own_ref), channel_id=1, source_target_pairs={{0,2},{1,3},{2,0},{3,1},{4,6},{5,7},{6,4},{7,5},{8,10},{9,11},{10,... | collective-permute-start | bytes 454664 | tf_op jit(solution)/shard_map/ppermute | solution.py:125
  98.8 1.2 %collective-permute-start.35 = (bf16[448,128]{1,0:T(8,128)(2,1)S(1)}, bf16[448,128]{1,0:T(8,128)(2,1)S(1)}, u32[]{:S(2)}, u32[]{:S(2)}) collective-permute-start(bf16[448,128]{1,0:T(8,128)(2,1)S(1)} %shard_map.83.own_ref), channel_id=1, source_target_pairs={{0,4},{1,5},{2,6},{3,7},{4,0},{5,1},{6,2},{7,3},{8,12},{9,13},{10,... | collective-permute-start | bytes 344072 | tf_op jit(solution)/shard_map/ppermute | solution.py:125
  100.1 3.1 %collective-permute-done.38.got_ref = bf16[592,128]{1,0:T(8,128)(2,1)S(1)} collective-permute-done((bf16[592,128]{1,0:T(8,128)(2,1)S(1)}, bf16[592,128]{1,0:T(8,128)(2,1)S(1)}, u32[]{:S(2)}, u32[]{:S(2)}) %collective-permute-start.38) | collective-permute-done | bytes 151584 | tf_op jit(solution)/shard_map/ppermute | solution.py:125
  103.2 1.2 %collective-permute-start.39 = (bf16[592,128]{1,0:T(8,128)(2,1)S(1)}, bf16[592,128]{1,0:T(8,128)(2,1)S(1)}, u32[]{:S(2)}, u32[]{:S(2)}) collective-permute-start(bf16[592,128]{1,0:T(8,128)(2,1)S(1)} %shard_map.86.own_ref), channel_id=1, source_target_pairs={{0,4},{1,5},{2,6},{3,7},{4,0},{5,1},{6,2},{7,3},{8,12},{9,13},{10,... | collective-permute-start | bytes 454664 | tf_op jit(solution)/shard_map/ppermute | solution.py:125
  104.5 1.5 %collective-permute-start.36 = (bf16[448,128]{1,0:T(8,128)(2,1)S(1)}, bf16[448,128]{1,0:T(8,128)(2,1)S(1)}, u32[]{:S(2)}, u32[]{:S(2)}) collective-permute-start(bf16[448,128]{1,0:T(8,128)(2,1)S(1)} %shard_map.84.own_ref), channel_id=1, source_target_pairs={{0,2},{1,3},{2,0},{3,1},{4,6},{5,7},{6,4},{7,5},{8,10},{9,11},{10,... | collective-permute-start | bytes 344072 | tf_op jit(solution)/shard_map/ppermute | solution.py:125
  106.0 2.4 %collective-permute-done.39.got_ref = bf16[592,128]{1,0:T(8,128)(2,1)S(1)} collective-permute-done((bf16[592,128]{1,0:T(8,128)(2,1)S(1)}, bf16[592,128]{1,0:T(8,128)(2,1)S(1)}, u32[]{:S(2)}, u32[]{:S(2)}) %collective-permute-start.39) | collective-permute-done | bytes 151584 | tf_op jit(solution)/shard_map/ppermute | solution.py:125
  108.7 0.7 collective-permute-done.36.got_ref
  109.5 1.2 collective-permute-done.40.got_ref
  110.8 1.8 %collective-permute-start.43 = (f32[8,128]{1,0:T(8,128)S(1)}, f32[8,128]{1,0:T(8,128)S(1)}, u32[]{:S(2)}, u32[]{:S(2)}) collective-permute-start(f32[8,128]{1,0:T(8,128)S(1)} %get-tuple-element.132.refs_0_), channel_id=1, source_target_pairs={{0,24},{8,16},{16,8},{24,0},{1,25},{9,17},{17,9},{25,1},{2,26},{10... | collective-permute-start | bytes 12296 | tf_op jit(solution)/shard_map/ppermute | solution.py:122
  112.7 2.6 %collective-permute-start.41 = (f32[8,128]{1,0:T(8,128)S(1)}, f32[8,128]{1,0:T(8,128)S(1)}, u32[]{:S(2)}, u32[]{:S(2)}) collective-permute-start(f32[8,128]{1,0:T(8,128)S(1)} %get-tuple-element.132.refs_0_), channel_id=1, source_target_pairs={{0,8},{8,0},{16,24},{24,16},{1,9},{9,1},{17,25},{25,17},{2,10},{10... | collective-permute-start | bytes 12296 | tf_op jit(solution)/shard_map/ppermute | solution.py:122
  115.2 1.0 collective-permute-done.43.refs_3_
  116.2 0.9 collective-permute-done.42.refs_2_
  117.2 1.2 shard_map.90
  (91 shorter events, 8.5 us)
Async XLA Ops:
  0.6 1.2 %copy-start.2 = (f32[2048,128]{1,0:T(8,128)S(1)}, f32[2048,128]{1,0:T(8,128)}, u32[]{:S(2)}) copy-start(f32[2048,128]{1,0:T(8,128)} %t_ref.1) | copy-start | bytes 3145732
  2.2 2.2 %copy-start = (bf16[2048,1024]{1,0:T(8,128)(2,1)S(1)}, bf16[2048,1024]{1,0:T(8,128)(2,1)}, u32[]{:S(2)}) copy-start(bf16[2048,1024]{1,0:T(8,128)(2,1)} %a_ref.33) | copy-start | bytes 12582916
  5.5 20.4 %copy-start.1 = (bf16[2048,1024]{1,0:T(8,128)(2,1)S(1)}, bf16[2048,1024]{1,0:T(8,128)(2,1)}, u32[]{:S(2)}) copy-start(bf16[2048,1024]{1,0:T(8,128)(2,1)} %a_ref.33) | copy-start | bytes 12582916
  5.6 7.7 %collective-permute-start.2 = (f16[272,128]{1,0:T(8,128)(2,1)S(1)}, f16[272,128]{1,0:T(8,128)(2,1)S(1)}, u32[]{:S(2)}, u32[]{:S(2)}) collective-permute-start(f16[272,128]{1,0:T(8,128)(2,1)S(1)} %convert_element_type.40), channel_id=1, source_target_pairs={{0,24},{8,16},{16,8},{24,0},{1,25},{9,17},{17,9},{25,1},{2,26},{10... | collective-permute-start | bytes 208904 | tf_op jit(solution)/shard_map/ppermute | solution.py:122
  10.7 5.9 %collective-permute-start.1 = (f16[272,128]{1,0:T(8,128)(2,1)S(1)}, f16[272,128]{1,0:T(8,128)(2,1)S(1)}, u32[]{:S(2)}, u32[]{:S(2)}) collective-permute-start(f16[272,128]{1,0:T(8,128)(2,1)S(1)} %convert_element_type.38), channel_id=1, source_target_pairs={{0,16},{8,24},{16,0},{24,8},{1,17},{9,25},{17,1},{25,9},{2,18},{10... | collective-permute-start | bytes 208904 | tf_op jit(solution)/shard_map/ppermute | solution.py:122
  10.8 5.8 %collective-permute-start = (f16[272,128]{1,0:T(8,128)(2,1)S(1)}, f16[272,128]{1,0:T(8,128)(2,1)S(1)}, u32[]{:S(2)}, u32[]{:S(2)}) collective-permute-start(f16[272,128]{1,0:T(8,128)(2,1)S(1)} %convert_element_type.36), channel_id=1, source_target_pairs={{0,8},{8,0},{16,24},{24,16},{1,9},{9,1},{17,25},{25,17},{2,10},{10... | collective-permute-start | bytes 208904 | tf_op jit(solution)/shard_map/ppermute | solution.py:122
  16.7 6.8 %collective-permute-start.5 = (bf16[272,128]{1,0:T(8,128)(2,1)S(1)}, bf16[272,128]{1,0:T(8,128)(2,1)S(1)}, u32[]{:S(2)}, u32[]{:S(2)}) collective-permute-start(bf16[272,128]{1,0:T(8,128)(2,1)S(1)} %get-tuple-element.75.refs_0_), channel_id=1, source_target_pairs={{0,24},{8,16},{16,8},{24,0},{1,25},{9,17},{17,9},{25,1},{2,26},{10... | collective-permute-start | bytes 208904 | tf_op jit(solution)/shard_map/ppermute | solution.py:122
  19.5 6.4 %collective-permute-start.4 = (bf16[272,128]{1,0:T(8,128)(2,1)S(1)}, bf16[272,128]{1,0:T(8,128)(2,1)S(1)}, u32[]{:S(2)}, u32[]{:S(2)}) collective-permute-start(bf16[272,128]{1,0:T(8,128)(2,1)S(1)} %get-tuple-element.75.refs_0_), channel_id=1, source_target_pairs={{0,16},{8,24},{16,0},{24,8},{1,17},{9,25},{17,1},{25,9},{2,18},{10... | collective-permute-start | bytes 208904 | tf_op jit(solution)/shard_map/ppermute | solution.py:122
  19.5 6.4 %collective-permute-start.3 = (bf16[272,128]{1,0:T(8,128)(2,1)S(1)}, bf16[272,128]{1,0:T(8,128)(2,1)S(1)}, u32[]{:S(2)}, u32[]{:S(2)}) collective-permute-start(bf16[272,128]{1,0:T(8,128)(2,1)S(1)} %get-tuple-element.75.refs_0_), channel_id=1, source_target_pairs={{0,8},{8,0},{16,24},{24,16},{1,9},{9,1},{17,25},{25,17},{2,10},{10... | collective-permute-start | bytes 208904 | tf_op jit(solution)/shard_map/ppermute | solution.py:122
  26.5 1.8 %collective-permute-start.6 = (f32[592,128]{1,0:T(8,128)S(1)}, f32[592,128]{1,0:T(8,128)S(1)}, u32[]{:S(2)}, u32[]{:S(2)}) collective-permute-start(f32[592,128]{1,0:T(8,128)S(1)} %get-tuple-element.78), channel_id=1, source_target_pairs={{0,1},{1,0},{2,3},{3,2},{4,5},{5,4},{6,7},{7,6},{8,9},{9,8},{10,11... | collective-permute-start | bytes 909320 | tf_op jit(solution)/shard_map/ppermute | solution.py:125
  27.0 2.9 %collective-permute-start.10 = (f32[448,128]{1,0:T(8,128)S(1)}, f32[448,128]{1,0:T(8,128)S(1)}, u32[]{:S(2)}, u32[]{:S(2)}) collective-permute-start(f32[448,128]{1,0:T(8,128)S(1)} %shard_map.59), channel_id=1, source_target_pairs={{0,1},{1,0},{2,3},{3,2},{4,5},{5,4},{6,7},{7,6},{8,9},{9,8},{10,11... | collective-permute-start | bytes 688136 | tf_op jit(solution)/shard_map/ppermute | solution.py:125
  28.3 5.9 %collective-permute-start.7 = (bf16[592,128]{1,0:T(8,128)(2,1)S(1)}, bf16[592,128]{1,0:T(8,128)(2,1)S(1)}, u32[]{:S(2)}, u32[]{:S(2)}) collective-permute-start(bf16[592,128]{1,0:T(8,128)(2,1)S(1)} %shard_map.56.own_ref), channel_id=1, source_target_pairs={{0,2},{1,3},{2,0},{3,1},{4,6},{5,7},{6,4},{7,5},{8,10},{9,11},{10,... | collective-permute-start | bytes 454664 | tf_op jit(solution)/shard_map/ppermute | solution.py:125
  30.0 6.0 %collective-permute-start.11 = (bf16[448,128]{1,0:T(8,128)(2,1)S(1)}, bf16[448,128]{1,0:T(8,128)(2,1)S(1)}, u32[]{:S(2)}, u32[]{:S(2)}) collective-permute-start(bf16[448,128]{1,0:T(8,128)(2,1)S(1)} %shard_map.60.own_ref), channel_id=1, source_target_pairs={{0,4},{1,5},{2,6},{3,7},{4,0},{5,1},{6,2},{7,3},{8,12},{9,13},{10,... | collective-permute-start | bytes 344072 | tf_op jit(solution)/shard_map/ppermute | solution.py:125
  34.3 5.3 %collective-permute-start.8 = (bf16[592,128]{1,0:T(8,128)(2,1)S(1)}, bf16[592,128]{1,0:T(8,128)(2,1)S(1)}, u32[]{:S(2)}, u32[]{:S(2)}) collective-permute-start(bf16[592,128]{1,0:T(8,128)(2,1)S(1)} %shard_map.57.own_ref), channel_id=1, source_target_pairs={{0,4},{1,5},{2,6},{3,7},{4,0},{5,1},{6,2},{7,3},{8,12},{9,13},{10,... | collective-permute-start | bytes 454664 | tf_op jit(solution)/shard_map/ppermute | solution.py:125
  36.0 4.9 %collective-permute-start.12 = (bf16[448,128]{1,0:T(8,128)(2,1)S(1)}, bf16[448,128]{1,0:T(8,128)(2,1)S(1)}, u32[]{:S(2)}, u32[]{:S(2)}) collective-permute-start(bf16[448,128]{1,0:T(8,128)(2,1)S(1)} %shard_map.61.own_ref), channel_id=1, source_target_pairs={{0,2},{1,3},{2,0},{3,1},{4,6},{5,7},{6,4},{7,5},{8,10},{9,11},{10,... | collective-permute-start | bytes 344072 | tf_op jit(solution)/shard_map/ppermute | solution.py:125
  39.6 2.7 %collective-permute-start.9 = (bf16[576,128]{1,0:T(8,128)(2,1)S(1)}, bf16[576,128]{1,0:T(8,128)(2,1)S(1)}, u32[]{:S(2)}, u32[]{:S(2)}) collective-permute-start(bf16[576,128]{1,0:T(8,128)(2,1)S(1)} %get-tuple-element.82.refs_0_), channel_id=1, source_target_pairs={{0,1},{1,0},{2,3},{3,2},{4,5},{5,4},{6,7},{7,6},{8,9},{9,8},{10,11... | collective-permute-start | bytes 442376 | tf_op jit(solution)/shard_map/ppermute | solution.py:125
  40.9 1.4 %collective-permute-start.13 = (bf16[464,128]{1,0:T(8,128)(2,1)S(1)}, bf16[464,128]{1,0:T(8,128)(2,1)S(1)}, u32[]{:S(2)}, u32[]{:S(2)}) collective-permute-start(bf16[464,128]{1,0:T(8,128)(2,1)S(1)} %get-tuple-element.86.refs_1_.refs_0_), channel_id=1, source_target_pairs={{0,1},{1,0},{2,3},{3,2},{4,5},{5,4},{6,7},{7,6},{8,9},{9,8},{10,11... | collective-permute-start | bytes 356360 | tf_op jit(solution)/shard_map/ppermute | solution.py:125
  42.9 9.2 %copy-start.3 = (f32[128]{0:T(128)S(1)}, f32[128]{0:T(128)}, u32[]{:S(2)}) copy-start(f32[128]{0:T(128)} %param.5) | copy-start | bytes 1540
  42.9 6.9 %collective-permute-start.16 = (f16[272,128]{1,0:T(8,128)(2,1)S(1)}, f16[272,128]{1,0:T(8,128)(2,1)S(1)}, u32[]{:S(2)}, u32[]{:S(2)}) collective-permute-start(f16[272,128]{1,0:T(8,128)(2,1)S(1)} %convert_element_type.46), channel_id=1, source_target_pairs={{0,24},{8,16},{16,8},{24,0},{1,25},{9,17},{17,9},{25,1},{2,26},{10... | collective-permute-start | bytes 208904 | tf_op jit(solution)/shard_map/ppermute | solution.py:122
  44.7 7.3 %collective-permute-start.15 = (f16[272,128]{1,0:T(8,128)(2,1)S(1)}, f16[272,128]{1,0:T(8,128)(2,1)S(1)}, u32[]{:S(2)}, u32[]{:S(2)}) collective-permute-start(f16[272,128]{1,0:T(8,128)(2,1)S(1)} %convert_element_type.44), channel_id=1, source_target_pairs={{0,16},{8,24},{16,0},{24,8},{1,17},{9,25},{17,1},{25,9},{2,18},{10... | collective-permute-start | bytes 208904 | tf_op jit(solution)/shard_map/ppermute | solution.py:122
  44.7 7.3 %collective-permute-start.14 = (f16[272,128]{1,0:T(8,128)(2,1)S(1)}, f16[272,128]{1,0:T(8,128)(2,1)S(1)}, u32[]{:S(2)}, u32[]{:S(2)}) collective-permute-start(f16[272,128]{1,0:T(8,128)(2,1)S(1)} %convert_element_type.42), channel_id=1, source_target_pairs={{0,8},{8,0},{16,24},{24,16},{1,9},{9,1},{17,25},{25,17},{2,10},{10... | collective-permute-start | bytes 208904 | tf_op jit(solution)/shard_map/ppermute | solution.py:122
  52.2 6.9 %collective-permute-start.19 = (bf16[272,128]{1,0:T(8,128)(2,1)S(1)}, bf16[272,128]{1,0:T(8,128)(2,1)S(1)}, u32[]{:S(2)}, u32[]{:S(2)}) collective-permute-start(bf16[272,128]{1,0:T(8,128)(2,1)S(1)} %get-tuple-element.97.refs_0_), channel_id=1, source_target_pairs={{0,24},{8,16},{16,8},{24,0},{1,25},{9,17},{17,9},{25,1},{2,26},{10... | collective-permute-start | bytes 208904 | tf_op jit(solution)/shard_map/ppermute | solution.py:122
  54.0 7.2 %collective-permute-start.18 = (bf16[272,128]{1,0:T(8,128)(2,1)S(1)}, bf16[272,128]{1,0:T(8,128)(2,1)S(1)}, u32[]{:S(2)}, u32[]{:S(2)}) collective-permute-start(bf16[272,128]{1,0:T(8,128)(2,1)S(1)} %get-tuple-element.97.refs_0_), channel_id=1, source_target_pairs={{0,16},{8,24},{16,0},{24,8},{1,17},{9,25},{17,1},{25,9},{2,18},{10... | collective-permute-start | bytes 208904 | tf_op jit(solution)/shard_map/ppermute | solution.py:122
  54.0 7.2 %collective-permute-start.17 = (bf16[272,128]{1,0:T(8,128)(2,1)S(1)}, bf16[272,128]{1,0:T(8,128)(2,1)S(1)}, u32[]{:S(2)}, u32[]{:S(2)}) collective-permute-start(bf16[272,128]{1,0:T(8,128)(2,1)S(1)} %get-tuple-element.97.refs_0_), channel_id=1, source_target_pairs={{0,8},{8,0},{16,24},{24,16},{1,9},{9,1},{17,25},{25,17},{2,10},{10... | collective-permute-start | bytes 208904 | tf_op jit(solution)/shard_map/ppermute | solution.py:122
  61.7 1.8 %collective-permute-start.20 = (f32[592,128]{1,0:T(8,128)S(1)}, f32[592,128]{1,0:T(8,128)S(1)}, u32[]{:S(2)}, u32[]{:S(2)}) collective-permute-start(f32[592,128]{1,0:T(8,128)S(1)} %get-tuple-element.100), channel_id=1, source_target_pairs={{0,1},{1,0},{2,3},{3,2},{4,5},{5,4},{6,7},{7,6},{8,9},{9,8},{10,11... | collective-permute-start | bytes 909320 | tf_op jit(solution)/shard_map/ppermute | solution.py:125
  62.2 2.9 %collective-permute-start.24 = (f32[448,128]{1,0:T(8,128)S(1)}, f32[448,128]{1,0:T(8,128)S(1)}, u32[]{:S(2)}, u32[]{:S(2)}) collective-permute-start(f32[448,128]{1,0:T(8,128)S(1)} %shard_map.72), channel_id=1, source_target_pairs={{0,1},{1,0},{2,3},{3,2},{4,5},{5,4},{6,7},{7,6},{8,9},{9,8},{10,11... | collective-permute-start | bytes 688136 | tf_op jit(solution)/shard_map/ppermute | solution.py:125
  63.5 5.9 %collective-permute-start.21 = (bf16[592,128]{1,0:T(8,128)(2,1)S(1)}, bf16[592,128]{1,0:T(8,128)(2,1)S(1)}, u32[]{:S(2)}, u32[]{:S(2)}) collective-permute-start(bf16[592,128]{1,0:T(8,128)(2,1)S(1)} %shard_map.69.own_ref), channel_id=1, source_target_pairs={{0,2},{1,3},{2,0},{3,1},{4,6},{5,7},{6,4},{7,5},{8,10},{9,11},{10,... | collective-permute-start | bytes 454664 | tf_op jit(solution)/shard_map/ppermute | solution.py:125
  65.1 5.3 %collective-permute-start.25 = (bf16[448,128]{1,0:T(8,128)(2,1)S(1)}, bf16[448,128]{1,0:T(8,128)(2,1)S(1)}, u32[]{:S(2)}, u32[]{:S(2)}) collective-permute-start(bf16[448,128]{1,0:T(8,128)(2,1)S(1)} %shard_map.73.own_ref), channel_id=1, source_target_pairs={{0,4},{1,5},{2,6},{3,7},{4,0},{5,1},{6,2},{7,3},{8,12},{9,13},{10,... | collective-permute-start | bytes 344072 | tf_op jit(solution)/shard_map/ppermute | solution.py:125
  69.5 5.3 %collective-permute-start.22 = (bf16[592,128]{1,0:T(8,128)(2,1)S(1)}, bf16[592,128]{1,0:T(8,128)(2,1)S(1)}, u32[]{:S(2)}, u32[]{:S(2)}) collective-permute-start(bf16[592,128]{1,0:T(8,128)(2,1)S(1)} %shard_map.70.own_ref), channel_id=1, source_target_pairs={{0,4},{1,5},{2,6},{3,7},{4,0},{5,1},{6,2},{7,3},{8,12},{9,13},{10,... | collective-permute-start | bytes 454664 | tf_op jit(solution)/shard_map/ppermute | solution.py:125
  70.4 4.9 %collective-permute-start.26 = (bf16[448,128]{1,0:T(8,128)(2,1)S(1)}, bf16[448,128]{1,0:T(8,128)(2,1)S(1)}, u32[]{:S(2)}, u32[]{:S(2)}) collective-permute-start(bf16[448,128]{1,0:T(8,128)(2,1)S(1)} %shard_map.74.own_ref), channel_id=1, source_target_pairs={{0,2},{1,3},{2,0},{3,1},{4,6},{5,7},{6,4},{7,5},{8,10},{9,11},{10,... | collective-permute-start | bytes 344072 | tf_op jit(solution)/shard_map/ppermute | solution.py:125
  74.9 1.9 %collective-permute-start.23 = (bf16[576,128]{1,0:T(8,128)(2,1)S(1)}, bf16[576,128]{1,0:T(8,128)(2,1)S(1)}, u32[]{:S(2)}, u32[]{:S(2)}) collective-permute-start(bf16[576,128]{1,0:T(8,128)(2,1)S(1)} %get-tuple-element.104.refs_0_), channel_id=1, source_target_pairs={{0,1},{1,0},{2,3},{3,2},{4,5},{5,4},{6,7},{7,6},{8,9},{9,8},{10,11... | collective-permute-start | bytes 442376 | tf_op jit(solution)/shard_map/ppermute | solution.py:125
  75.4 1.4 %collective-permute-start.27 = (bf16[464,128]{1,0:T(8,128)(2,1)S(1)}, bf16[464,128]{1,0:T(8,128)(2,1)S(1)}, u32[]{:S(2)}, u32[]{:S(2)}) collective-permute-start(bf16[464,128]{1,0:T(8,128)(2,1)S(1)} %get-tuple-element.108.refs_1_.refs_0_), channel_id=1, source_target_pairs={{0,1},{1,0},{2,3},{3,2},{4,5},{5,4},{6,7},{7,6},{8,9},{9,8},{10,11... | collective-permute-start | bytes 356360 | tf_op jit(solution)/shard_map/ppermute | solution.py:125
  77.3 5.3 %collective-permute-start.28 = (bf16[272,128]{1,0:T(8,128)(2,1)S(1)}, bf16[272,128]{1,0:T(8,128)(2,1)S(1)}, u32[]{:S(2)}, u32[]{:S(2)}) collective-permute-start(bf16[272,128]{1,0:T(8,128)(2,1)S(1)} %get-tuple-element.110), channel_id=1, source_target_pairs={{0,8},{8,0},{16,24},{24,16},{1,9},{9,1},{17,25},{25,17},{2,10},{10... | collective-permute-start | bytes 208904 | tf_op jit(solution)/shard_map/ppermute | solution.py:122
  77.4 8.9 %collective-permute-start.29 = (bf16[272,128]{1,0:T(8,128)(2,1)S(1)}, bf16[272,128]{1,0:T(8,128)(2,1)S(1)}, u32[]{:S(2)}, u32[]{:S(2)}) collective-permute-start(bf16[272,128]{1,0:T(8,128)(2,1)S(1)} %get-tuple-element.111), channel_id=1, source_target_pairs={{0,16},{8,24},{16,0},{24,8},{1,17},{9,25},{17,1},{25,9},{2,18},{10... | collective-permute-start | bytes 208904 | tf_op jit(solution)/shard_map/ppermute | solution.py:122
  79.6 6.7 %collective-permute-start.30 = (bf16[272,128]{1,0:T(8,128)(2,1)S(1)}, bf16[272,128]{1,0:T(8,128)(2,1)S(1)}, u32[]{:S(2)}, u32[]{:S(2)}) collective-permute-start(bf16[272,128]{1,0:T(8,128)(2,1)S(1)} %get-tuple-element.112), channel_id=1, source_target_pairs={{0,24},{8,16},{16,8},{24,0},{1,25},{9,17},{17,9},{25,1},{2,26},{10... | collective-permute-start | bytes 208904 | tf_op jit(solution)/shard_map/ppermute | solution.py:122
  86.5 6.3 %collective-permute-start.33 = (bf16[272,128]{1,0:T(8,128)(2,1)S(1)}, bf16[272,128]{1,0:T(8,128)(2,1)S(1)}, u32[]{:S(2)}, u32[]{:S(2)}) collective-permute-start(bf16[272,128]{1,0:T(8,128)(2,1)S(1)} %get-tuple-element.120.refs_0_), channel_id=1, source_target_pairs={{0,24},{8,16},{16,8},{24,0},{1,25},{9,17},{17,9},{25,1},{2,26},{10... | collective-permute-start | bytes 208904 | tf_op jit(solution)/shard_map/ppermute | solution.py:122
  88.4 6.4 %collective-permute-start.32 = (bf16[272,128]{1,0:T(8,128)(2,1)S(1)}, bf16[272,128]{1,0:T(8,128)(2,1)S(1)}, u32[]{:S(2)}, u32[]{:S(2)}) collective-permute-start(bf16[272,128]{1,0:T(8,128)(2,1)S(1)} %get-tuple-element.120.refs_0_), channel_id=1, source_target_pairs={{0,16},{8,24},{16,0},{24,8},{1,17},{9,25},{17,1},{25,9},{2,18},{10... | collective-permute-start | bytes 208904 | tf_op jit(solution)/shard_map/ppermute | solution.py:122
  89.3 5.6 %collective-permute-start.31 = (bf16[272,128]{1,0:T(8,128)(2,1)S(1)}, bf16[272,128]{1,0:T(8,128)(2,1)S(1)}, u32[]{:S(2)}, u32[]{:S(2)}) collective-permute-start(bf16[272,128]{1,0:T(8,128)(2,1)S(1)} %get-tuple-element.120.refs_0_), channel_id=1, source_target_pairs={{0,8},{8,0},{16,24},{24,16},{1,9},{9,1},{17,25},{25,17},{2,10},{10... | collective-permute-start | bytes 208904 | tf_op jit(solution)/shard_map/ppermute | solution.py:122
  95.4 1.8 %collective-permute-start.37 = (f32[592,128]{1,0:T(8,128)S(1)}, f32[592,128]{1,0:T(8,128)S(1)}, u32[]{:S(2)}, u32[]{:S(2)}) collective-permute-start(f32[592,128]{1,0:T(8,128)S(1)} %get-tuple-element.124), channel_id=1, source_target_pairs={{0,1},{1,0},{2,3},{3,2},{4,5},{5,4},{6,7},{7,6},{8,9},{9,8},{10,11... | collective-permute-start | bytes 909320 | tf_op jit(solution)/shard_map/ppermute | solution.py:125
  95.9 2.9 %collective-permute-start.34 = (f32[448,128]{1,0:T(8,128)S(1)}, f32[448,128]{1,0:T(8,128)S(1)}, u32[]{:S(2)}, u32[]{:S(2)}) collective-permute-start(f32[448,128]{1,0:T(8,128)S(1)} %shard_map.82), channel_id=1, source_target_pairs={{0,1},{1,0},{2,3},{3,2},{4,5},{5,4},{6,7},{7,6},{8,9},{9,8},{10,11... | collective-permute-start | bytes 688136 | tf_op jit(solution)/shard_map/ppermute | solution.py:125
  97.2 5.9 %collective-permute-start.38 = (bf16[592,128]{1,0:T(8,128)(2,1)S(1)}, bf16[592,128]{1,0:T(8,128)(2,1)S(1)}, u32[]{:S(2)}, u32[]{:S(2)}) collective-permute-start(bf16[592,128]{1,0:T(8,128)(2,1)S(1)} %shard_map.85.own_ref), channel_id=1, source_target_pairs={{0,2},{1,3},{2,0},{3,1},{4,6},{5,7},{6,4},{7,5},{8,10},{9,11},{10,... | collective-permute-start | bytes 454664 | tf_op jit(solution)/shard_map/ppermute | solution.py:125
  98.8 13.9 %collective-permute-start.46 = (f32[1024,128]{1,0:T(8,128)S(1)}, f32[1024,128]{1,0:T(8,128)S(1)}, u32[]{:S(2)}, u32[]{:S(2)}) collective-permute-start(f32[1024,128]{1,0:T(8,128)S(1)} %get-tuple-element.137.refs_11_), channel_id=1, source_target_pairs={{0,1},{1,0},{2,3},{3,2},{4,5},{5,4},{6,7},{7,6},{8,9},{9,8},{10,11... | collective-permute-start | bytes 1572872 | tf_op jit(solution)/shard_map/ppermute | solution.py:125
  98.8 5.6 %collective-permute-start.35 = (bf16[448,128]{1,0:T(8,128)(2,1)S(1)}, bf16[448,128]{1,0:T(8,128)(2,1)S(1)}, u32[]{:S(2)}, u32[]{:S(2)}) collective-permute-start(bf16[448,128]{1,0:T(8,128)(2,1)S(1)} %shard_map.83.own_ref), channel_id=1, source_target_pairs={{0,4},{1,5},{2,6},{3,7},{4,0},{5,1},{6,2},{7,3},{8,12},{9,13},{10,... | collective-permute-start | bytes 344072 | tf_op jit(solution)/shard_map/ppermute | solution.py:125
  103.2 5.3 %collective-permute-start.39 = (bf16[592,128]{1,0:T(8,128)(2,1)S(1)}, bf16[592,128]{1,0:T(8,128)(2,1)S(1)}, u32[]{:S(2)}, u32[]{:S(2)}) collective-permute-start(bf16[592,128]{1,0:T(8,128)(2,1)S(1)} %shard_map.86.own_ref), channel_id=1, source_target_pairs={{0,4},{1,5},{2,6},{3,7},{4,0},{5,1},{6,2},{7,3},{8,12},{9,13},{10,... | collective-permute-start | bytes 454664 | tf_op jit(solution)/shard_map/ppermute | solution.py:125
  104.5 4.9 %collective-permute-start.36 = (bf16[448,128]{1,0:T(8,128)(2,1)S(1)}, bf16[448,128]{1,0:T(8,128)(2,1)S(1)}, u32[]{:S(2)}, u32[]{:S(2)}) collective-permute-start(bf16[448,128]{1,0:T(8,128)(2,1)S(1)} %shard_map.84.own_ref), channel_id=1, source_target_pairs={{0,2},{1,3},{2,0},{3,1},{4,6},{5,7},{6,4},{7,5},{8,10},{9,11},{10,... | collective-permute-start | bytes 344072 | tf_op jit(solution)/shard_map/ppermute | solution.py:125
  108.6 8.6 %collective-permute-start.44 = (f32[576,128]{1,0:T(8,128)S(1)}, f32[576,128]{1,0:T(8,128)S(1)}, u32[]{:S(2)}, u32[]{:S(2)}) collective-permute-start(f32[576,128]{1,0:T(8,128)S(1)} %get-tuple-element.133.refs_4_), channel_id=1, source_target_pairs={{0,1},{1,0},{2,3},{3,2},{4,5},{5,4},{6,7},{7,6},{8,9},{9,8},{10,11... | collective-permute-start | bytes 884744 | tf_op jit(solution)/shard_map/ppermute | solution.py:125
  109.4 1.2 %collective-permute-start.40 = (f32[8,128]{1,0:T(8,128)S(1)}, f32[8,128]{1,0:T(8,128)S(1)}, u32[]{:S(2)}, u32[]{:S(2)}) collective-permute-start(f32[8,128]{1,0:T(8,128)S(1)} %get-tuple-element.130.own_ref), channel_id=1, source_target_pairs={{0,1},{1,0},{2,3},{3,2},{4,5},{5,4},{6,7},{7,6},{8,9},{9,8},{10,11... | collective-permute-start | bytes 12296 | tf_op jit(solution)/shard_map/ppermute | solution.py:125
  110.7 6.5 %collective-permute-start.45 = (f32[448,128]{1,0:T(8,128)S(1)}, f32[448,128]{1,0:T(8,128)S(1)}, u32[]{:S(2)}, u32[]{:S(2)}) collective-permute-start(f32[448,128]{1,0:T(8,128)S(1)} %get-tuple-element.134.refs_5_), channel_id=1, source_target_pairs={{0,1},{1,0},{2,3},{3,2},{4,5},{5,4},{6,7},{7,6},{8,9},{9,8},{10,11... | collective-permute-start | bytes 688136 | tf_op jit(solution)/shard_map/ppermute | solution.py:125
  110.8 5.4 %collective-permute-start.43 = (f32[8,128]{1,0:T(8,128)S(1)}, f32[8,128]{1,0:T(8,128)S(1)}, u32[]{:S(2)}, u32[]{:S(2)}) collective-permute-start(f32[8,128]{1,0:T(8,128)S(1)} %get-tuple-element.132.refs_0_), channel_id=1, source_target_pairs={{0,24},{8,16},{16,8},{24,0},{1,25},{9,17},{17,9},{25,1},{2,26},{10... | collective-permute-start | bytes 12296 | tf_op jit(solution)/shard_map/ppermute | solution.py:122
  112.7 4.5 %collective-permute-start.42 = (f32[8,128]{1,0:T(8,128)S(1)}, f32[8,128]{1,0:T(8,128)S(1)}, u32[]{:S(2)}, u32[]{:S(2)}) collective-permute-start(f32[8,128]{1,0:T(8,128)S(1)} %get-tuple-element.132.refs_0_), channel_id=1, source_target_pairs={{0,16},{8,24},{16,0},{24,8},{1,17},{9,25},{17,1},{25,9},{2,18},{10... | collective-permute-start | bytes 12296 | tf_op jit(solution)/shard_map/ppermute | solution.py:122
  112.7 4.5 %collective-permute-start.41 = (f32[8,128]{1,0:T(8,128)S(1)}, f32[8,128]{1,0:T(8,128)S(1)}, u32[]{:S(2)}, u32[]{:S(2)}) collective-permute-start(f32[8,128]{1,0:T(8,128)S(1)} %get-tuple-element.132.refs_0_), channel_id=1, source_target_pairs={{0,8},{8,0},{16,24},{24,16},{1,9},{9,1},{17,25},{25,17},{2,10},{10... | collective-permute-start | bytes 12296 | tf_op jit(solution)/shard_map/ppermute | solution.py:122

commit v7 on v6

--- a/solution.py
+++ b/solution.py
@@ -9,6 +9,7 @@
 
 ITERS = 3
 PAD = 16
+TWO_PARTS = (1,)
 F32 = jnp.float32
 BF16 = jnp.bfloat16
 F16 = jnp.float16
@@ -308,7 +309,7 @@
             [own, delta, *got, gamma, dir_sq, grad, direction, residual, ridge, *images, *weights],
         )
 
-    def forward(wire, msg):
+    def forward(wire, in_two, msg):
         got = {step: over_row(step, msg) for step in row_steps}
         blocks = [msg] + [got[step] for step in range(1, n_row)]
 
@@ -337,6 +338,8 @@
             for index, ref in enumerate(refs):
                 product(a_ref, vec, 0, index, ref)
 
+        if in_two and by_block:
+            return forward_in_two(wire, blocks)
         peer, gamma, cross, vec = call(
             first_piece,
             [pieces(wire)[0], scalar, scalar, ((feats, outs), BF16)],
@@ -347,6 +350,64 @@
             (peer,) = call(functools.partial(later_piece, index), [pieces(wire)[index]], [states, vec])
             got.append(over_group(1, peer))
         own = call(own_pieces, [((rows, outs), F32) for rows in piece_rows], [states, vec])
+        return own, gamma, cross, got
+
+    def forward_in_two(wire, blocks):
+        early, late = [0, n_row - 1], list(range(1, n_row - 1))
+
+        def product(a_ref, core_step, index, step, block_ref):
+            start, rows = piece_starts[index], piece_rows[index]
+            place = pl.ds(pl.multiple_of(token_place(core_step) + start, 64), rows)
+            return jnp.dot(
+                a_ref[place, pl.ds(row_place(step), feat_share)],
+                body_of(block_ref),
+                preferred_element_type=F32,
+            )
+
+        def summed(a_ref, core_step, index, steps, block_refs, total=None):
+            for step, ref in zip(steps, block_refs):
+                part = product(a_ref, core_step, index, step, ref)
+                total = part if total is None else total + part
+            return total
+
+        def early_part(a_ref, *refs):
+            ins, parts = refs[: len(early)], refs[len(early) :]
+            for core_step in (1, 0):
+                for index in range(levels):
+                    parts[(1 - core_step) * levels + index][...] = summed(a_ref, core_step, index, early, ins)
+
+        def first_piece(a_ref, part_ref, *refs):
+            ins, (peer_ref, gamma_ref, cross_ref) = refs[:n_row], refs[n_row:]
+            gamma = tree_sum([get_row(ref, 0) for ref in ins])
+            cross = tree_sum([get_row(ref, 1) for ref in ins])
+            spread(gamma_ref, gamma)
+            spread(cross_ref, cross)
+            total = summed(a_ref, 1, 0, late, [ins[step] for step in late], part_ref[...])
+            peer_ref[pl.ds(0, piece_rows[0]), :] = total.astype(wire)
+            put_rows(peer_ref, gamma, cross)
+
+        def later_piece(index, a_ref, part_ref, *refs):
+            *block_refs, peer_ref = refs
+            peer_ref[...] = summed(a_ref, 1, index, late, block_refs, part_ref[...]).astype(wire)
+
+        def own_pieces(a_ref, *refs):
+            block_refs, refs = refs[: len(late)], refs[len(late) :]
+            for index in range(levels):
+                refs[levels + index][...] = summed(a_ref, 0, index, late, block_refs, refs[index][...])
+
+        own_shapes = [((rows, outs), F32) for rows in piece_rows]
+        late_blocks = [blocks[step] for step in late]
+        parts = call(early_part, own_shapes * 2, [states] + [blocks[step] for step in early])
+        peer, gamma, cross = call(
+            first_piece, [pieces(wire)[0], scalar, scalar], [states, parts[0]] + blocks
+        )
+        got = [over_group(1, peer)]
+        for index in range(1, levels):
+            (peer,) = call(
+                functools.partial(later_piece, index), [pieces(wire)[index]], [states, parts[index], *late_blocks]
+            )
+            got.append(over_group(1, peer))
+        own = call(own_pieces, own_shapes, [states, *late_blocks] + list(parts[levels:]))
         return own, gamma, cross, got
 
     def pieces(wire):
@@ -454,7 +515,7 @@
     grad, msg = begin(own, got)
     before = ()
     for step in range(ITERS):
-        own, gamma, cross, got = forward(CORE_WIRE[step], msg)
+        own, gamma, cross, got = forward(CORE_WIRE[step], step in TWO_PARTS, msg)
         sent = join_cores(CHIP_WIRE[step][0], own, gamma, cross, got)
         got = swapped(0, sent)
         for level in range(1, levels):

time: 119 us -> 118 us (level)
    pallas_call x40 -> x41, Pallas kernels: 12.4 us -> 12.5 us  [call(): pl.pallas_call(kernel, out_shape=[jax.ShapeDtypeStruct(shape, dtype) for...]
  transfers between devices with their start and end apart: 47 -> 47, of which waited for: 26 -> 27; matrix products, arithmetic and copies ran while one was open for 0% -> 0% of each run, Pallas kernels for 6% -> 6%
where the time goes in v7:
time: 118 us
  starting transfers between devices  52 us (44%)
  waiting for transfers between devices  49 us (42%)
  Pallas kernels  12.5 us (11%)
  local copies, waits for them, and re-layouts  3.41 us (3%)
    ppermute x21, starting transfers between devices, over_row(): return lax.ppermute(value, 'row', [(i, i ^ step) for i in range(n_row)])  32.5 us
    ppermute x21, waiting for transfers between devices, over_row(): return lax.ppermute(value, 'row', [(i, i ^ step) for i in range(n_row)])  27.5 us
    ppermute x26, waiting for transfers between devices, over_group(): return lax.ppermute(value, 'group', [(i, i ^ step) for i in range(n_group)])  21.5 us
    ppermute x26, starting transfers between devices, over_group(): return lax.ppermute(value, 'group', [(i, i ^ step) for i in range(n_group)])  19.5 us
    pallas_call x41, Pallas kernels, call(): pl.pallas_call(kernel, out_shape=[jax.ShapeDtypeStruct(shape, dtype) for...  12.5 us
    unnamed x8, local copies, waits for them, and re-layouts  3.41 us
  transfers between devices with their start and end apart: 47, of which 27 were waited for; matrix products, arithmetic and copies ran while one was open for 0% of the time, Pallas kernels for 6%

profile of v7, /device:TPU:0, one launch (start us, length us, event | category | flops | bytes accessed | tf_op | source)
XLA Modules:
  0.0 118.1 jit_solution(585702024178175890)
XLA Ops:
  0.6 1.2 %copy-done.2 = f32[2048,128]{1,0:T(8,128)S(1)} copy-done((f32[2048,128]{1,0:T(8,128)S(1)}, f32[2048,128]{1,0:T(8,128)}, u32[]{:S(2)}) %copy-start.2) | copy-done | bytes 1048600
  2.2 2.2 %copy-done = bf16[2048,1024]{1,0:T(8,128)(2,1)S(1)} copy-done((bf16[2048,1024]{1,0:T(8,128)(2,1)S(1)}, bf16[2048,1024]{1,0:T(8,128)(2,1)}, u32[]{:S(2)}) %copy-start) | copy-done | bytes 4194328
  4.4 1.2 shard_map.52
  5.6 5.1 %collective-permute-start.2 = (f16[272,128]{1,0:T(8,128)(2,1)S(1)}, f16[272,128]{1,0:T(8,128)(2,1)S(1)}, u32[]{:S(2)}, u32[]{:S(2)}) collective-permute-start(f16[272,128]{1,0:T(8,128)(2,1)S(1)} %convert_element_type.40), channel_id=1, source_target_pairs={{0,24},{8,16},{16,8},{24,0},{1,25},{9,17},{17,9},{25,1},{2,26},{10... | collective-permute-start | bytes 208904 | tf_op jit(solution)/shard_map/ppermute | solution.py:123
  10.8 0.6 collective-permute-start
  12.0 1.3 %collective-permute-done.2 = f16[272,128]{1,0:T(8,128)(2,1)S(1)} collective-permute-done((f16[272,128]{1,0:T(8,128)(2,1)S(1)}, f16[272,128]{1,0:T(8,128)(2,1)S(1)}, u32[]{:S(2)}, u32[]{:S(2)}) %collective-permute-start.2) | collective-permute-done | bytes 69664 | tf_op jit(solution)/shard_map/ppermute | solution.py:123
  13.3 3.3 %collective-permute-done.1 = f16[272,128]{1,0:T(8,128)(2,1)S(1)} collective-permute-done((f16[272,128]{1,0:T(8,128)(2,1)S(1)}, f16[272,128]{1,0:T(8,128)(2,1)S(1)}, u32[]{:S(2)}, u32[]{:S(2)}) %collective-permute-start.1) | collective-permute-done | bytes 69664 | tf_op jit(solution)/shard_map/ppermute | solution.py:123
  16.7 2.8 %collective-permute-start.5 = (bf16[272,128]{1,0:T(8,128)(2,1)S(1)}, bf16[272,128]{1,0:T(8,128)(2,1)S(1)}, u32[]{:S(2)}, u32[]{:S(2)}) collective-permute-start(bf16[272,128]{1,0:T(8,128)(2,1)S(1)} %get-tuple-element.78.refs_0_), channel_id=1, source_target_pairs={{0,24},{8,16},{16,8},{24,0},{1,25},{9,17},{17,9},{25,1},{2,26},{10... | collective-permute-start | bytes 208904 | tf_op jit(solution)/shard_map/ppermute | solution.py:123
  19.5 1.6 %collective-permute-start.3 = (bf16[272,128]{1,0:T(8,128)(2,1)S(1)}, bf16[272,128]{1,0:T(8,128)(2,1)S(1)}, u32[]{:S(2)}, u32[]{:S(2)}) collective-permute-start(bf16[272,128]{1,0:T(8,128)(2,1)S(1)} %get-tuple-element.78.refs_0_), channel_id=1, source_target_pairs={{0,8},{8,0},{16,24},{24,16},{1,9},{9,1},{17,25},{25,17},{2,10},{10... | collective-permute-start | bytes 208904 | tf_op jit(solution)/shard_map/ppermute | solution.py:123
  21.2 2.4 %collective-permute-done.5.refs_3_ = bf16[272,128]{1,0:T(8,128)(2,1)S(1)} collective-permute-done((bf16[272,128]{1,0:T(8,128)(2,1)S(1)}, bf16[272,128]{1,0:T(8,128)(2,1)S(1)}, u32[]{:S(2)}, u32[]{:S(2)}) %collective-permute-start.5) | collective-permute-done | bytes 69664 | tf_op jit(solution)/shard_map/ppermute | solution.py:123
  23.6 2.4 %collective-permute-done.4.refs_2_ = bf16[272,128]{1,0:T(8,128)(2,1)S(1)} collective-permute-done((bf16[272,128]{1,0:T(8,128)(2,1)S(1)}, bf16[272,128]{1,0:T(8,128)(2,1)S(1)}, u32[]{:S(2)}, u32[]{:S(2)}) %collective-permute-start.4) | collective-permute-done | bytes 69664 | tf_op jit(solution)/shard_map/ppermute | solution.py:123
  27.0 0.6 collective-permute-start.10
  27.5 0.7 shard_map.55
  28.3 1.6 %collective-permute-start.7 = (bf16[592,128]{1,0:T(8,128)(2,1)S(1)}, bf16[592,128]{1,0:T(8,128)(2,1)S(1)}, u32[]{:S(2)}, u32[]{:S(2)}) collective-permute-start(bf16[592,128]{1,0:T(8,128)(2,1)S(1)} %shard_map.56.own_ref), channel_id=1, source_target_pairs={{0,2},{1,3},{2,0},{3,1},{4,6},{5,7},{6,4},{7,5},{8,10},{9,11},{10,... | collective-permute-start | bytes 454664 | tf_op jit(solution)/shard_map/ppermute | solution.py:126
  30.0 1.6 %collective-permute-start.11 = (bf16[448,128]{1,0:T(8,128)(2,1)S(1)}, bf16[448,128]{1,0:T(8,128)(2,1)S(1)}, u32[]{:S(2)}, u32[]{:S(2)}) collective-permute-start(bf16[448,128]{1,0:T(8,128)(2,1)S(1)} %shard_map.60.own_ref), channel_id=1, source_target_pairs={{0,4},{1,5},{2,6},{3,7},{4,0},{5,1},{6,2},{7,3},{8,12},{9,13},{10,... | collective-permute-start | bytes 344072 | tf_op jit(solution)/shard_map/ppermute | solution.py:126
  31.5 2.7 %collective-permute-done.7.got_ref = bf16[592,128]{1,0:T(8,128)(2,1)S(1)} collective-permute-done((bf16[592,128]{1,0:T(8,128)(2,1)S(1)}, bf16[592,128]{1,0:T(8,128)(2,1)S(1)}, u32[]{:S(2)}, u32[]{:S(2)}) %collective-permute-start.7) | collective-permute-done | bytes 151584 | tf_op jit(solution)/shard_map/ppermute | solution.py:126
  34.3 1.6 %collective-permute-start.8 = (bf16[592,128]{1,0:T(8,128)(2,1)S(1)}, bf16[592,128]{1,0:T(8,128)(2,1)S(1)}, u32[]{:S(2)}, u32[]{:S(2)}) collective-permute-start(bf16[592,128]{1,0:T(8,128)(2,1)S(1)} %shard_map.57.own_ref), channel_id=1, source_target_pairs={{0,4},{1,5},{2,6},{3,7},{4,0},{5,1},{6,2},{7,3},{8,12},{9,13},{10,... | collective-permute-start | bytes 454664 | tf_op jit(solution)/shard_map/ppermute | solution.py:126
  36.0 1.5 %collective-permute-start.12 = (bf16[448,128]{1,0:T(8,128)(2,1)S(1)}, bf16[448,128]{1,0:T(8,128)(2,1)S(1)}, u32[]{:S(2)}, u32[]{:S(2)}) collective-permute-start(bf16[448,128]{1,0:T(8,128)(2,1)S(1)} %shard_map.61.own_ref), channel_id=1, source_target_pairs={{0,2},{1,3},{2,0},{3,1},{4,6},{5,7},{6,4},{7,5},{8,10},{9,11},{10,... | collective-permute-start | bytes 344072 | tf_op jit(solution)/shard_map/ppermute | solution.py:126
  37.5 2.0 %collective-permute-done.8.got_ref = bf16[592,128]{1,0:T(8,128)(2,1)S(1)} collective-permute-done((bf16[592,128]{1,0:T(8,128)(2,1)S(1)}, bf16[592,128]{1,0:T(8,128)(2,1)S(1)}, u32[]{:S(2)}, u32[]{:S(2)}) %collective-permute-start.8) | collective-permute-done | bytes 151584 | tf_op jit(solution)/shard_map/ppermute | solution.py:126
  39.7 1.1 collective-permute-done.12.got_ref
  41.0 0.6 shard_map.63.refs_2_.refs_3_
  41.5 0.8 collective-permute-done.13.refs_1_.refs_2_
  42.3 0.6 shard_map.65
  42.9 1.8 %collective-permute-start.16 = (f16[272,128]{1,0:T(8,128)(2,1)S(1)}, f16[272,128]{1,0:T(8,128)(2,1)S(1)}, u32[]{:S(2)}, u32[]{:S(2)}) collective-permute-start(f16[272,128]{1,0:T(8,128)(2,1)S(1)} %convert_element_type.46), channel_id=1, source_target_pairs={{0,24},{8,16},{16,8},{24,0},{1,25},{9,17},{17,9},{25,1},{2,26},{10... | collective-permute-start | bytes 208904 | tf_op jit(solution)/shard_map/ppermute | solution.py:123
  44.7 2.8 %collective-permute-start.14 = (f16[272,128]{1,0:T(8,128)(2,1)S(1)}, f16[272,128]{1,0:T(8,128)(2,1)S(1)}, u32[]{:S(2)}, u32[]{:S(2)}) collective-permute-start(f16[272,128]{1,0:T(8,128)(2,1)S(1)} %convert_element_type.42), channel_id=1, source_target_pairs={{0,8},{8,0},{16,24},{24,16},{1,9},{9,1},{17,25},{25,17},{2,10},{10... | collective-permute-start | bytes 208904 | tf_op jit(solution)/shard_map/ppermute | solution.py:123
  47.8 2.1 %collective-permute-done.16 = f16[272,128]{1,0:T(8,128)(2,1)S(1)} collective-permute-done((f16[272,128]{1,0:T(8,128)(2,1)S(1)}, f16[272,128]{1,0:T(8,128)(2,1)S(1)}, u32[]{:S(2)}, u32[]{:S(2)}) %collective-permute-start.16) | collective-permute-done | bytes 69664 | tf_op jit(solution)/shard_map/ppermute | solution.py:123
  49.9 2.1 %collective-permute-done.15 = f16[272,128]{1,0:T(8,128)(2,1)S(1)} collective-permute-done((f16[272,128]{1,0:T(8,128)(2,1)S(1)}, f16[272,128]{1,0:T(8,128)(2,1)S(1)}, u32[]{:S(2)}, u32[]{:S(2)}) %collective-permute-start.15) | collective-permute-done | bytes 69664 | tf_op jit(solution)/shard_map/ppermute | solution.py:123
  52.2 1.8 %collective-permute-start.19 = (bf16[272,128]{1,0:T(8,128)(2,1)S(1)}, bf16[272,128]{1,0:T(8,128)(2,1)S(1)}, u32[]{:S(2)}, u32[]{:S(2)}) collective-permute-start(bf16[272,128]{1,0:T(8,128)(2,1)S(1)} %get-tuple-element.100.refs_0_), channel_id=1, source_target_pairs={{0,24},{8,16},{16,8},{24,0},{1,25},{9,17},{17,9},{25,1},{2,26},{10... | collective-permute-start | bytes 208904 | tf_op jit(solution)/shard_map/ppermute | solution.py:123
  54.0 2.7 %collective-permute-start.17 = (bf16[272,128]{1,0:T(8,128)(2,1)S(1)}, bf16[272,128]{1,0:T(8,128)(2,1)S(1)}, u32[]{:S(2)}, u32[]{:S(2)}) collective-permute-start(bf16[272,128]{1,0:T(8,128)(2,1)S(1)} %get-tuple-element.100.refs_0_), channel_id=1, source_target_pairs={{0,8},{8,0},{16,24},{24,16},{1,9},{9,1},{17,25},{25,17},{2,10},{10... | collective-permute-start | bytes 208904 | tf_op jit(solution)/shard_map/ppermute | solution.py:123
  56.7 2.5 %collective-permute-done.19.refs_1_.refs_3_ = bf16[272,128]{1,0:T(8,128)(2,1)S(1)} collective-permute-done((bf16[272,128]{1,0:T(8,128)(2,1)S(1)}, bf16[272,128]{1,0:T(8,128)(2,1)S(1)}, u32[]{:S(2)}, u32[]{:S(2)}) %collective-permute-start.19) | collective-permute-done | bytes 69664 | tf_op jit(solution)/shard_map/ppermute | solution.py:123
  59.2 0.7 shard_map.67
  59.9 1.3 %collective-permute-done.18.refs_1_.refs_2_ = bf16[272,128]{1,0:T(8,128)(2,1)S(1)} collective-permute-done((bf16[272,128]{1,0:T(8,128)(2,1)S(1)}, bf16[272,128]{1,0:T(8,128)(2,1)S(1)}, u32[]{:S(2)}, u32[]{:S(2)}) %collective-permute-start.18) | collective-permute-done | bytes 69664 | tf_op jit(solution)/shard_map/ppermute | solution.py:123
  61.9 0.6 collective-permute-start.24
  63.2 1.5 %collective-permute-start.21 = (bf16[592,128]{1,0:T(8,128)(2,1)S(1)}, bf16[592,128]{1,0:T(8,128)(2,1)S(1)}, u32[]{:S(2)}, u32[]{:S(2)}) collective-permute-start(bf16[592,128]{1,0:T(8,128)(2,1)S(1)} %shard_map.70.own_ref), channel_id=1, source_target_pairs={{0,2},{1,3},{2,0},{3,1},{4,6},{5,7},{6,4},{7,5},{8,10},{9,11},{10,... | collective-permute-start | bytes 454664 | tf_op jit(solution)/shard_map/ppermute | solution.py:126
  64.8 0.9 collective-permute-start.25
  65.7 3.6 %collective-permute-done.21.got_ref = bf16[592,128]{1,0:T(8,128)(2,1)S(1)} collective-permute-done((bf16[592,128]{1,0:T(8,128)(2,1)S(1)}, bf16[592,128]{1,0:T(8,128)(2,1)S(1)}, u32[]{:S(2)}, u32[]{:S(2)}) %collective-permute-start.21) | collective-permute-done | bytes 151584 | tf_op jit(solution)/shard_map/ppermute | solution.py:126
  69.3 0.9 collective-permute-start.22
  70.2 1.6 %collective-permute-start.26 = (bf16[448,128]{1,0:T(8,128)(2,1)S(1)}, bf16[448,128]{1,0:T(8,128)(2,1)S(1)}, u32[]{:S(2)}, u32[]{:S(2)}) collective-permute-start(bf16[448,128]{1,0:T(8,128)(2,1)S(1)} %shard_map.75.own_ref), channel_id=1, source_target_pairs={{0,2},{1,3},{2,0},{3,1},{4,6},{5,7},{6,4},{7,5},{8,10},{9,11},{10,... | collective-permute-start | bytes 344072 | tf_op jit(solution)/shard_map/ppermute | solution.py:126
  71.8 2.8 %collective-permute-done.22.got_ref = bf16[592,128]{1,0:T(8,128)(2,1)S(1)} collective-permute-done((bf16[592,128]{1,0:T(8,128)(2,1)S(1)}, bf16[592,128]{1,0:T(8,128)(2,1)S(1)}, u32[]{:S(2)}, u32[]{:S(2)}) %collective-permute-start.22) | collective-permute-done | bytes 151584 | tf_op jit(solution)/shard_map/ppermute | solution.py:126
  75.4 0.6 shard_map.77.refs_2_.refs_3_
  76.0 0.6 collective-permute-done.27.refs_1_.refs_2_
  77.2 2.3 %collective-permute-start.29 = (bf16[272,128]{1,0:T(8,128)(2,1)S(1)}, bf16[272,128]{1,0:T(8,128)(2,1)S(1)}, u32[]{:S(2)}, u32[]{:S(2)}) collective-permute-start(bf16[272,128]{1,0:T(8,128)(2,1)S(1)} %get-tuple-element.117), channel_id=1, source_target_pairs={{0,16},{8,24},{16,0},{24,8},{1,17},{9,25},{17,1},{25,9},{2,18},{10... | collective-permute-start | bytes 208904 | tf_op jit(solution)/shard_map/ppermute | solution.py:123
  79.4 2.1 %collective-permute-start.30 = (bf16[272,128]{1,0:T(8,128)(2,1)S(1)}, bf16[272,128]{1,0:T(8,128)(2,1)S(1)}, u32[]{:S(2)}, u32[]{:S(2)}) collective-permute-start(bf16[272,128]{1,0:T(8,128)(2,1)S(1)} %get-tuple-element.118), channel_id=1, source_target_pairs={{0,24},{8,16},{16,8},{24,0},{1,25},{9,17},{17,9},{25,1},{2,26},{10... | collective-permute-start | bytes 208904 | tf_op jit(solution)/shard_map/ppermute | solution.py:123
  82.4 3.7 %collective-permute-done.29.refs_1_ = bf16[272,128]{1,0:T(8,128)(2,1)S(1)} collective-permute-done((bf16[272,128]{1,0:T(8,128)(2,1)S(1)}, bf16[272,128]{1,0:T(8,128)(2,1)S(1)}, u32[]{:S(2)}, u32[]{:S(2)}) %collective-permute-start.29) | collective-permute-done | bytes 69664 | tf_op jit(solution)/shard_map/ppermute | solution.py:123
  86.3 2.0 %collective-permute-start.33 = (bf16[272,128]{1,0:T(8,128)(2,1)S(1)}, bf16[272,128]{1,0:T(8,128)(2,1)S(1)}, u32[]{:S(2)}, u32[]{:S(2)}) collective-permute-start(bf16[272,128]{1,0:T(8,128)(2,1)S(1)} %get-tuple-element.126.refs_0_), channel_id=1, source_target_pairs={{0,24},{8,16},{16,8},{24,0},{1,25},{9,17},{17,9},{25,1},{2,26},{10... | collective-permute-start | bytes 208904 | tf_op jit(solution)/shard_map/ppermute | solution.py:123
  88.2 0.9 collective-permute-start.32
  89.1 1.6 %collective-permute-start.31 = (bf16[272,128]{1,0:T(8,128)(2,1)S(1)}, bf16[272,128]{1,0:T(8,128)(2,1)S(1)}, u32[]{:S(2)}, u32[]{:S(2)}) collective-permute-start(bf16[272,128]{1,0:T(8,128)(2,1)S(1)} %get-tuple-element.126.refs_0_), channel_id=1, source_target_pairs={{0,8},{8,0},{16,24},{24,16},{1,9},{9,1},{17,25},{25,17},{2,10},{10... | collective-permute-start | bytes 208904 | tf_op jit(solution)/shard_map/ppermute | solution.py:123
  90.7 1.9 %collective-permute-done.33.refs_3_ = bf16[272,128]{1,0:T(8,128)(2,1)S(1)} collective-permute-done((bf16[272,128]{1,0:T(8,128)(2,1)S(1)}, bf16[272,128]{1,0:T(8,128)(2,1)S(1)}, u32[]{:S(2)}, u32[]{:S(2)}) %collective-permute-start.33) | collective-permute-done | bytes 69664 | tf_op jit(solution)/shard_map/ppermute | solution.py:123
  92.6 2.1 %collective-permute-done.32.refs_2_ = bf16[272,128]{1,0:T(8,128)(2,1)S(1)} collective-permute-done((bf16[272,128]{1,0:T(8,128)(2,1)S(1)}, bf16[272,128]{1,0:T(8,128)(2,1)S(1)}, u32[]{:S(2)}, u32[]{:S(2)}) %collective-permute-start.32) | collective-permute-done | bytes 69664 | tf_op jit(solution)/shard_map/ppermute | solution.py:123
  95.7 0.6 collective-permute-start.34
  96.2 0.7 shard_map.82
  97.0 1.6 %collective-permute-start.38 = (bf16[592,128]{1,0:T(8,128)(2,1)S(1)}, bf16[592,128]{1,0:T(8,128)(2,1)S(1)}, u32[]{:S(2)}, u32[]{:S(2)}) collective-permute-start(bf16[592,128]{1,0:T(8,128)(2,1)S(1)} %shard_map.86.own_ref), channel_id=1, source_target_pairs={{0,2},{1,3},{2,0},{3,1},{4,6},{5,7},{6,4},{7,5},{8,10},{9,11},{10,... | collective-permute-start | bytes 454664 | tf_op jit(solution)/shard_map/ppermute | solution.py:126
  98.6 1.2 %collective-permute-start.35 = (bf16[448,128]{1,0:T(8,128)(2,1)S(1)}, bf16[448,128]{1,0:T(8,128)(2,1)S(1)}, u32[]{:S(2)}, u32[]{:S(2)}) collective-permute-start(bf16[448,128]{1,0:T(8,128)(2,1)S(1)} %shard_map.84.own_ref), channel_id=1, source_target_pairs={{0,4},{1,5},{2,6},{3,7},{4,0},{5,1},{6,2},{7,3},{8,12},{9,13},{10,... | collective-permute-start | bytes 344072 | tf_op jit(solution)/shard_map/ppermute | solution.py:126
  99.9 3.1 %collective-permute-done.38.got_ref = bf16[592,128]{1,0:T(8,128)(2,1)S(1)} collective-permute-done((bf16[592,128]{1,0:T(8,128)(2,1)S(1)}, bf16[592,128]{1,0:T(8,128)(2,1)S(1)}, u32[]{:S(2)}, u32[]{:S(2)}) %collective-permute-start.38) | collective-permute-done | bytes 151584 | tf_op jit(solution)/shard_map/ppermute | solution.py:126
  103.0 1.2 %collective-permute-start.39 = (bf16[592,128]{1,0:T(8,128)(2,1)S(1)}, bf16[592,128]{1,0:T(8,128)(2,1)S(1)}, u32[]{:S(2)}, u32[]{:S(2)}) collective-permute-start(bf16[592,128]{1,0:T(8,128)(2,1)S(1)} %shard_map.87.own_ref), channel_id=1, source_target_pairs={{0,4},{1,5},{2,6},{3,7},{4,0},{5,1},{6,2},{7,3},{8,12},{9,13},{10,... | collective-permute-start | bytes 454664 | tf_op jit(solution)/shard_map/ppermute | solution.py:126
  104.3 1.6 %collective-permute-start.36 = (bf16[448,128]{1,0:T(8,128)(2,1)S(1)}, bf16[448,128]{1,0:T(8,128)(2,1)S(1)}, u32[]{:S(2)}, u32[]{:S(2)}) collective-permute-start(bf16[448,128]{1,0:T(8,128)(2,1)S(1)} %shard_map.85.own_ref), channel_id=1, source_target_pairs={{0,2},{1,3},{2,0},{3,1},{4,6},{5,7},{6,4},{7,5},{8,10},{9,11},{10,... | collective-permute-start | bytes 344072 | tf_op jit(solution)/shard_map/ppermute | solution.py:126
  105.8 2.4 %collective-permute-done.39.got_ref = bf16[592,128]{1,0:T(8,128)(2,1)S(1)} collective-permute-done((bf16[592,128]{1,0:T(8,128)(2,1)S(1)}, bf16[592,128]{1,0:T(8,128)(2,1)S(1)}, u32[]{:S(2)}, u32[]{:S(2)}) %collective-permute-start.39) | collective-permute-done | bytes 151584 | tf_op jit(solution)/shard_map/ppermute | solution.py:126
  108.5 0.7 collective-permute-done.36.got_ref
  109.3 1.2 collective-permute-done.40.got_ref
  110.6 1.8 %collective-permute-start.43 = (f32[8,128]{1,0:T(8,128)S(1)}, f32[8,128]{1,0:T(8,128)S(1)}, u32[]{:S(2)}, u32[]{:S(2)}) collective-permute-start(f32[8,128]{1,0:T(8,128)S(1)} %get-tuple-element.138.refs_0_), channel_id=1, source_target_pairs={{0,24},{8,16},{16,8},{24,0},{1,25},{9,17},{17,9},{25,1},{2,26},{10... | collective-permute-start | bytes 12296 | tf_op jit(solution)/shard_map/ppermute | solution.py:123
  112.5 2.6 %collective-permute-start.41 = (f32[8,128]{1,0:T(8,128)S(1)}, f32[8,128]{1,0:T(8,128)S(1)}, u32[]{:S(2)}, u32[]{:S(2)}) collective-permute-start(f32[8,128]{1,0:T(8,128)S(1)} %get-tuple-element.138.refs_0_), channel_id=1, source_target_pairs={{0,8},{8,0},{16,24},{24,16},{1,9},{9,1},{17,25},{25,17},{2,10},{10... | collective-permute-start | bytes 12296 | tf_op jit(solution)/shard_map/ppermute | solution.py:123
  115.0 1.0 collective-permute-done.43.refs_3_
  116.0 0.9 collective-permute-done.42.refs_2_
  117.0 1.2 shard_map.91
  (92 shorter events, 8.9 us)
Async XLA Ops:
  0.6 1.2 %copy-start.2 = (f32[2048,128]{1,0:T(8,128)S(1)}, f32[2048,128]{1,0:T(8,128)}, u32[]{:S(2)}) copy-start(f32[2048,128]{1,0:T(8,128)} %t_ref.1) | copy-start | bytes 3145732
  2.2 2.2 %copy-start = (bf16[2048,1024]{1,0:T(8,128)(2,1)S(1)}, bf16[2048,1024]{1,0:T(8,128)(2,1)}, u32[]{:S(2)}) copy-start(bf16[2048,1024]{1,0:T(8,128)(2,1)} %a_ref.35) | copy-start | bytes 12582916
  5.5 20.4 %copy-start.1 = (bf16[2048,1024]{1,0:T(8,128)(2,1)S(1)}, bf16[2048,1024]{1,0:T(8,128)(2,1)}, u32[]{:S(2)}) copy-start(bf16[2048,1024]{1,0:T(8,128)(2,1)} %a_ref.35) | copy-start | bytes 12582916
  5.6 7.7 %collective-permute-start.2 = (f16[272,128]{1,0:T(8,128)(2,1)S(1)}, f16[272,128]{1,0:T(8,128)(2,1)S(1)}, u32[]{:S(2)}, u32[]{:S(2)}) collective-permute-start(f16[272,128]{1,0:T(8,128)(2,1)S(1)} %convert_element_type.40), channel_id=1, source_target_pairs={{0,24},{8,16},{16,8},{24,0},{1,25},{9,17},{17,9},{25,1},{2,26},{10... | collective-permute-start | bytes 208904 | tf_op jit(solution)/shard_map/ppermute | solution.py:123
  10.7 5.9 %collective-permute-start.1 = (f16[272,128]{1,0:T(8,128)(2,1)S(1)}, f16[272,128]{1,0:T(8,128)(2,1)S(1)}, u32[]{:S(2)}, u32[]{:S(2)}) collective-permute-start(f16[272,128]{1,0:T(8,128)(2,1)S(1)} %convert_element_type.38), channel_id=1, source_target_pairs={{0,16},{8,24},{16,0},{24,8},{1,17},{9,25},{17,1},{25,9},{2,18},{10... | collective-permute-start | bytes 208904 | tf_op jit(solution)/shard_map/ppermute | solution.py:123
  10.8 5.8 %collective-permute-start = (f16[272,128]{1,0:T(8,128)(2,1)S(1)}, f16[272,128]{1,0:T(8,128)(2,1)S(1)}, u32[]{:S(2)}, u32[]{:S(2)}) collective-permute-start(f16[272,128]{1,0:T(8,128)(2,1)S(1)} %convert_element_type.36), channel_id=1, source_target_pairs={{0,8},{8,0},{16,24},{24,16},{1,9},{9,1},{17,25},{25,17},{2,10},{10... | collective-permute-start | bytes 208904 | tf_op jit(solution)/shard_map/ppermute | solution.py:123
  16.7 6.8 %collective-permute-start.5 = (bf16[272,128]{1,0:T(8,128)(2,1)S(1)}, bf16[272,128]{1,0:T(8,128)(2,1)S(1)}, u32[]{:S(2)}, u32[]{:S(2)}) collective-permute-start(bf16[272,128]{1,0:T(8,128)(2,1)S(1)} %get-tuple-element.78.refs_0_), channel_id=1, source_target_pairs={{0,24},{8,16},{16,8},{24,0},{1,25},{9,17},{17,9},{25,1},{2,26},{10... | collective-permute-start | bytes 208904 | tf_op jit(solution)/shard_map/ppermute | solution.py:123
  19.5 6.4 %collective-permute-start.4 = (bf16[272,128]{1,0:T(8,128)(2,1)S(1)}, bf16[272,128]{1,0:T(8,128)(2,1)S(1)}, u32[]{:S(2)}, u32[]{:S(2)}) collective-permute-start(bf16[272,128]{1,0:T(8,128)(2,1)S(1)} %get-tuple-element.78.refs_0_), channel_id=1, source_target_pairs={{0,16},{8,24},{16,0},{24,8},{1,17},{9,25},{17,1},{25,9},{2,18},{10... | collective-permute-start | bytes 208904 | tf_op jit(solution)/shard_map/ppermute | solution.py:123
  19.5 6.4 %collective-permute-start.3 = (bf16[272,128]{1,0:T(8,128)(2,1)S(1)}, bf16[272,128]{1,0:T(8,128)(2,1)S(1)}, u32[]{:S(2)}, u32[]{:S(2)}) collective-permute-start(bf16[272,128]{1,0:T(8,128)(2,1)S(1)} %get-tuple-element.78.refs_0_), channel_id=1, source_target_pairs={{0,8},{8,0},{16,24},{24,16},{1,9},{9,1},{17,25},{25,17},{2,10},{10... | collective-permute-start | bytes 208904 | tf_op jit(solution)/shard_map/ppermute | solution.py:123
  26.5 1.8 %collective-permute-start.6 = (f32[592,128]{1,0:T(8,128)S(1)}, f32[592,128]{1,0:T(8,128)S(1)}, u32[]{:S(2)}, u32[]{:S(2)}) collective-permute-start(f32[592,128]{1,0:T(8,128)S(1)} %get-tuple-element.81), channel_id=1, source_target_pairs={{0,1},{1,0},{2,3},{3,2},{4,5},{5,4},{6,7},{7,6},{8,9},{9,8},{10,11... | collective-permute-start | bytes 909320 | tf_op jit(solution)/shard_map/ppermute | solution.py:126
  27.0 2.9 %collective-permute-start.10 = (f32[448,128]{1,0:T(8,128)S(1)}, f32[448,128]{1,0:T(8,128)S(1)}, u32[]{:S(2)}, u32[]{:S(2)}) collective-permute-start(f32[448,128]{1,0:T(8,128)S(1)} %shard_map.59), channel_id=1, source_target_pairs={{0,1},{1,0},{2,3},{3,2},{4,5},{5,4},{6,7},{7,6},{8,9},{9,8},{10,11... | collective-permute-start | bytes 688136 | tf_op jit(solution)/shard_map/ppermute | solution.py:126
  28.3 5.9 %collective-permute-start.7 = (bf16[592,128]{1,0:T(8,128)(2,1)S(1)}, bf16[592,128]{1,0:T(8,128)(2,1)S(1)}, u32[]{:S(2)}, u32[]{:S(2)}) collective-permute-start(bf16[592,128]{1,0:T(8,128)(2,1)S(1)} %shard_map.56.own_ref), channel_id=1, source_target_pairs={{0,2},{1,3},{2,0},{3,1},{4,6},{5,7},{6,4},{7,5},{8,10},{9,11},{10,... | collective-permute-start | bytes 454664 | tf_op jit(solution)/shard_map/ppermute | solution.py:126
  30.0 6.0 %collective-permute-start.11 = (bf16[448,128]{1,0:T(8,128)(2,1)S(1)}, bf16[448,128]{1,0:T(8,128)(2,1)S(1)}, u32[]{:S(2)}, u32[]{:S(2)}) collective-permute-start(bf16[448,128]{1,0:T(8,128)(2,1)S(1)} %shard_map.60.own_ref), channel_id=1, source_target_pairs={{0,4},{1,5},{2,6},{3,7},{4,0},{5,1},{6,2},{7,3},{8,12},{9,13},{10,... | collective-permute-start | bytes 344072 | tf_op jit(solution)/shard_map/ppermute | solution.py:126
  34.3 5.3 %collective-permute-start.8 = (bf16[592,128]{1,0:T(8,128)(2,1)S(1)}, bf16[592,128]{1,0:T(8,128)(2,1)S(1)}, u32[]{:S(2)}, u32[]{:S(2)}) collective-permute-start(bf16[592,128]{1,0:T(8,128)(2,1)S(1)} %shard_map.57.own_ref), channel_id=1, source_target_pairs={{0,4},{1,5},{2,6},{3,7},{4,0},{5,1},{6,2},{7,3},{8,12},{9,13},{10,... | collective-permute-start | bytes 454664 | tf_op jit(solution)/shard_map/ppermute | solution.py:126
  36.0 4.9 %collective-permute-start.12 = (bf16[448,128]{1,0:T(8,128)(2,1)S(1)}, bf16[448,128]{1,0:T(8,128)(2,1)S(1)}, u32[]{:S(2)}, u32[]{:S(2)}) collective-permute-start(bf16[448,128]{1,0:T(8,128)(2,1)S(1)} %shard_map.61.own_ref), channel_id=1, source_target_pairs={{0,2},{1,3},{2,0},{3,1},{4,6},{5,7},{6,4},{7,5},{8,10},{9,11},{10,... | collective-permute-start | bytes 344072 | tf_op jit(solution)/shard_map/ppermute | solution.py:126
  39.6 2.7 %collective-permute-start.9 = (bf16[576,128]{1,0:T(8,128)(2,1)S(1)}, bf16[576,128]{1,0:T(8,128)(2,1)S(1)}, u32[]{:S(2)}, u32[]{:S(2)}) collective-permute-start(bf16[576,128]{1,0:T(8,128)(2,1)S(1)} %get-tuple-element.85.refs_0_), channel_id=1, source_target_pairs={{0,1},{1,0},{2,3},{3,2},{4,5},{5,4},{6,7},{7,6},{8,9},{9,8},{10,11... | collective-permute-start | bytes 442376 | tf_op jit(solution)/shard_map/ppermute | solution.py:126
  40.9 1.4 %collective-permute-start.13 = (bf16[464,128]{1,0:T(8,128)(2,1)S(1)}, bf16[464,128]{1,0:T(8,128)(2,1)S(1)}, u32[]{:S(2)}, u32[]{:S(2)}) collective-permute-start(bf16[464,128]{1,0:T(8,128)(2,1)S(1)} %get-tuple-element.89.refs_1_.refs_0_), channel_id=1, source_target_pairs={{0,1},{1,0},{2,3},{3,2},{4,5},{5,4},{6,7},{7,6},{8,9},{9,8},{10,11... | collective-permute-start | bytes 356360 | tf_op jit(solution)/shard_map/ppermute | solution.py:126
  42.9 9.2 %copy-start.3 = (f32[128]{0:T(128)S(1)}, f32[128]{0:T(128)}, u32[]{:S(2)}) copy-start(f32[128]{0:T(128)} %param.5) | copy-start | bytes 1540
  42.9 6.9 %collective-permute-start.16 = (f16[272,128]{1,0:T(8,128)(2,1)S(1)}, f16[272,128]{1,0:T(8,128)(2,1)S(1)}, u32[]{:S(2)}, u32[]{:S(2)}) collective-permute-start(f16[272,128]{1,0:T(8,128)(2,1)S(1)} %convert_element_type.46), channel_id=1, source_target_pairs={{0,24},{8,16},{16,8},{24,0},{1,25},{9,17},{17,9},{25,1},{2,26},{10... | collective-permute-start | bytes 208904 | tf_op jit(solution)/shard_map/ppermute | solution.py:123
  44.7 7.3 %collective-permute-start.15 = (f16[272,128]{1,0:T(8,128)(2,1)S(1)}, f16[272,128]{1,0:T(8,128)(2,1)S(1)}, u32[]{:S(2)}, u32[]{:S(2)}) collective-permute-start(f16[272,128]{1,0:T(8,128)(2,1)S(1)} %convert_element_type.44), channel_id=1, source_target_pairs={{0,16},{8,24},{16,0},{24,8},{1,17},{9,25},{17,1},{25,9},{2,18},{10... | collective-permute-start | bytes 208904 | tf_op jit(solution)/shard_map/ppermute | solution.py:123
  44.7 7.3 %collective-permute-start.14 = (f16[272,128]{1,0:T(8,128)(2,1)S(1)}, f16[272,128]{1,0:T(8,128)(2,1)S(1)}, u32[]{:S(2)}, u32[]{:S(2)}) collective-permute-start(f16[272,128]{1,0:T(8,128)(2,1)S(1)} %convert_element_type.42), channel_id=1, source_target_pairs={{0,8},{8,0},{16,24},{24,16},{1,9},{9,1},{17,25},{25,17},{2,10},{10... | collective-permute-start | bytes 208904 | tf_op jit(solution)/shard_map/ppermute | solution.py:123
  52.2 6.9 %collective-permute-start.19 = (bf16[272,128]{1,0:T(8,128)(2,1)S(1)}, bf16[272,128]{1,0:T(8,128)(2,1)S(1)}, u32[]{:S(2)}, u32[]{:S(2)}) collective-permute-start(bf16[272,128]{1,0:T(8,128)(2,1)S(1)} %get-tuple-element.100.refs_0_), channel_id=1, source_target_pairs={{0,24},{8,16},{16,8},{24,0},{1,25},{9,17},{17,9},{25,1},{2,26},{10... | collective-permute-start | bytes 208904 | tf_op jit(solution)/shard_map/ppermute | solution.py:123
  54.0 7.2 %collective-permute-start.18 = (bf16[272,128]{1,0:T(8,128)(2,1)S(1)}, bf16[272,128]{1,0:T(8,128)(2,1)S(1)}, u32[]{:S(2)}, u32[]{:S(2)}) collective-permute-start(bf16[272,128]{1,0:T(8,128)(2,1)S(1)} %get-tuple-element.100.refs_0_), channel_id=1, source_target_pairs={{0,16},{8,24},{16,0},{24,8},{1,17},{9,25},{17,1},{25,9},{2,18},{10... | collective-permute-start | bytes 208904 | tf_op jit(solution)/shard_map/ppermute | solution.py:123
  54.0 7.2 %collective-permute-start.17 = (bf16[272,128]{1,0:T(8,128)(2,1)S(1)}, bf16[272,128]{1,0:T(8,128)(2,1)S(1)}, u32[]{:S(2)}, u32[]{:S(2)}) collective-permute-start(bf16[272,128]{1,0:T(8,128)(2,1)S(1)} %get-tuple-element.100.refs_0_), channel_id=1, source_target_pairs={{0,8},{8,0},{16,24},{24,16},{1,9},{9,1},{17,25},{25,17},{2,10},{10... | collective-permute-start | bytes 208904 | tf_op jit(solution)/shard_map/ppermute | solution.py:123
  61.5 1.7 %collective-permute-start.20 = (f32[592,128]{1,0:T(8,128)S(1)}, f32[592,128]{1,0:T(8,128)S(1)}, u32[]{:S(2)}, u32[]{:S(2)}) collective-permute-start(f32[592,128]{1,0:T(8,128)S(1)} %get-tuple-element.105), channel_id=1, source_target_pairs={{0,1},{1,0},{2,3},{3,2},{4,5},{5,4},{6,7},{7,6},{8,9},{9,8},{10,11... | collective-permute-start | bytes 909320 | tf_op jit(solution)/shard_map/ppermute | solution.py:126
  61.9 2.9 %collective-permute-start.24 = (f32[448,128]{1,0:T(8,128)S(1)}, f32[448,128]{1,0:T(8,128)S(1)}, u32[]{:S(2)}, u32[]{:S(2)}) collective-permute-start(f32[448,128]{1,0:T(8,128)S(1)} %shard_map.73), channel_id=1, source_target_pairs={{0,1},{1,0},{2,3},{3,2},{4,5},{5,4},{6,7},{7,6},{8,9},{9,8},{10,11... | collective-permute-start | bytes 688136 | tf_op jit(solution)/shard_map/ppermute | solution.py:126
  63.2 6.0 %collective-permute-start.21 = (bf16[592,128]{1,0:T(8,128)(2,1)S(1)}, bf16[592,128]{1,0:T(8,128)(2,1)S(1)}, u32[]{:S(2)}, u32[]{:S(2)}) collective-permute-start(bf16[592,128]{1,0:T(8,128)(2,1)S(1)} %shard_map.70.own_ref), channel_id=1, source_target_pairs={{0,2},{1,3},{2,0},{3,1},{4,6},{5,7},{6,4},{7,5},{8,10},{9,11},{10,... | collective-permute-start | bytes 454664 | tf_op jit(solution)/shard_map/ppermute | solution.py:126
  64.8 5.4 %collective-permute-start.25 = (bf16[448,128]{1,0:T(8,128)(2,1)S(1)}, bf16[448,128]{1,0:T(8,128)(2,1)S(1)}, u32[]{:S(2)}, u32[]{:S(2)}) collective-permute-start(bf16[448,128]{1,0:T(8,128)(2,1)S(1)} %shard_map.74.own_ref), channel_id=1, source_target_pairs={{0,4},{1,5},{2,6},{3,7},{4,0},{5,1},{6,2},{7,3},{8,12},{9,13},{10,... | collective-permute-start | bytes 344072 | tf_op jit(solution)/shard_map/ppermute | solution.py:126
  69.3 5.3 %collective-permute-start.22 = (bf16[592,128]{1,0:T(8,128)(2,1)S(1)}, bf16[592,128]{1,0:T(8,128)(2,1)S(1)}, u32[]{:S(2)}, u32[]{:S(2)}) collective-permute-start(bf16[592,128]{1,0:T(8,128)(2,1)S(1)} %shard_map.71.own_ref), channel_id=1, source_target_pairs={{0,4},{1,5},{2,6},{3,7},{4,0},{5,1},{6,2},{7,3},{8,12},{9,13},{10,... | collective-permute-start | bytes 454664 | tf_op jit(solution)/shard_map/ppermute | solution.py:126
  70.2 4.9 %collective-permute-start.26 = (bf16[448,128]{1,0:T(8,128)(2,1)S(1)}, bf16[448,128]{1,0:T(8,128)(2,1)S(1)}, u32[]{:S(2)}, u32[]{:S(2)}) collective-permute-start(bf16[448,128]{1,0:T(8,128)(2,1)S(1)} %shard_map.75.own_ref), channel_id=1, source_target_pairs={{0,2},{1,3},{2,0},{3,1},{4,6},{5,7},{6,4},{7,5},{8,10},{9,11},{10,... | collective-permute-start | bytes 344072 | tf_op jit(solution)/shard_map/ppermute | solution.py:126
  74.7 1.9 %collective-permute-start.23 = (bf16[576,128]{1,0:T(8,128)(2,1)S(1)}, bf16[576,128]{1,0:T(8,128)(2,1)S(1)}, u32[]{:S(2)}, u32[]{:S(2)}) collective-permute-start(bf16[576,128]{1,0:T(8,128)(2,1)S(1)} %get-tuple-element.109.refs_0_), channel_id=1, source_target_pairs={{0,1},{1,0},{2,3},{3,2},{4,5},{5,4},{6,7},{7,6},{8,9},{9,8},{10,11... | collective-permute-start | bytes 442376 | tf_op jit(solution)/shard_map/ppermute | solution.py:126
  75.2 1.4 %collective-permute-start.27 = (bf16[464,128]{1,0:T(8,128)(2,1)S(1)}, bf16[464,128]{1,0:T(8,128)(2,1)S(1)}, u32[]{:S(2)}, u32[]{:S(2)}) collective-permute-start(bf16[464,128]{1,0:T(8,128)(2,1)S(1)} %get-tuple-element.114.refs_1_.refs_0_), channel_id=1, source_target_pairs={{0,1},{1,0},{2,3},{3,2},{4,5},{5,4},{6,7},{7,6},{8,9},{9,8},{10,11... | collective-permute-start | bytes 356360 | tf_op jit(solution)/shard_map/ppermute | solution.py:126
  77.1 5.3 %collective-permute-start.28 = (bf16[272,128]{1,0:T(8,128)(2,1)S(1)}, bf16[272,128]{1,0:T(8,128)(2,1)S(1)}, u32[]{:S(2)}, u32[]{:S(2)}) collective-permute-start(bf16[272,128]{1,0:T(8,128)(2,1)S(1)} %get-tuple-element.116), channel_id=1, source_target_pairs={{0,8},{8,0},{16,24},{24,16},{1,9},{9,1},{17,25},{25,17},{2,10},{10... | collective-permute-start | bytes 208904 | tf_op jit(solution)/shard_map/ppermute | solution.py:123
  77.2 8.9 %collective-permute-start.29 = (bf16[272,128]{1,0:T(8,128)(2,1)S(1)}, bf16[272,128]{1,0:T(8,128)(2,1)S(1)}, u32[]{:S(2)}, u32[]{:S(2)}) collective-permute-start(bf16[272,128]{1,0:T(8,128)(2,1)S(1)} %get-tuple-element.117), channel_id=1, source_target_pairs={{0,16},{8,24},{16,0},{24,8},{1,17},{9,25},{17,1},{25,9},{2,18},{10... | collective-permute-start | bytes 208904 | tf_op jit(solution)/shard_map/ppermute | solution.py:123
  79.4 6.7 %collective-permute-start.30 = (bf16[272,128]{1,0:T(8,128)(2,1)S(1)}, bf16[272,128]{1,0:T(8,128)(2,1)S(1)}, u32[]{:S(2)}, u32[]{:S(2)}) collective-permute-start(bf16[272,128]{1,0:T(8,128)(2,1)S(1)} %get-tuple-element.118), channel_id=1, source_target_pairs={{0,24},{8,16},{16,8},{24,0},{1,25},{9,17},{17,9},{25,1},{2,26},{10... | collective-permute-start | bytes 208904 | tf_op jit(solution)/shard_map/ppermute | solution.py:123
  86.3 6.3 %collective-permute-start.33 = (bf16[272,128]{1,0:T(8,128)(2,1)S(1)}, bf16[272,128]{1,0:T(8,128)(2,1)S(1)}, u32[]{:S(2)}, u32[]{:S(2)}) collective-permute-start(bf16[272,128]{1,0:T(8,128)(2,1)S(1)} %get-tuple-element.126.refs_0_), channel_id=1, source_target_pairs={{0,24},{8,16},{16,8},{24,0},{1,25},{9,17},{17,9},{25,1},{2,26},{10... | collective-permute-start | bytes 208904 | tf_op jit(solution)/shard_map/ppermute | solution.py:123
  88.2 6.4 %collective-permute-start.32 = (bf16[272,128]{1,0:T(8,128)(2,1)S(1)}, bf16[272,128]{1,0:T(8,128)(2,1)S(1)}, u32[]{:S(2)}, u32[]{:S(2)}) collective-permute-start(bf16[272,128]{1,0:T(8,128)(2,1)S(1)} %get-tuple-element.126.refs_0_), channel_id=1, source_target_pairs={{0,16},{8,24},{16,0},{24,8},{1,17},{9,25},{17,1},{25,9},{2,18},{10... | collective-permute-start | bytes 208904 | tf_op jit(solution)/shard_map/ppermute | solution.py:123
  89.1 5.6 %collective-permute-start.31 = (bf16[272,128]{1,0:T(8,128)(2,1)S(1)}, bf16[272,128]{1,0:T(8,128)(2,1)S(1)}, u32[]{:S(2)}, u32[]{:S(2)}) collective-permute-start(bf16[272,128]{1,0:T(8,128)(2,1)S(1)} %get-tuple-element.126.refs_0_), channel_id=1, source_target_pairs={{0,8},{8,0},{16,24},{24,16},{1,9},{9,1},{17,25},{25,17},{2,10},{10... | collective-permute-start | bytes 208904 | tf_op jit(solution)/shard_map/ppermute | solution.py:123
  95.2 1.8 %collective-permute-start.37 = (f32[592,128]{1,0:T(8,128)S(1)}, f32[592,128]{1,0:T(8,128)S(1)}, u32[]{:S(2)}, u32[]{:S(2)}) collective-permute-start(f32[592,128]{1,0:T(8,128)S(1)} %get-tuple-element.130), channel_id=1, source_target_pairs={{0,1},{1,0},{2,3},{3,2},{4,5},{5,4},{6,7},{7,6},{8,9},{9,8},{10,11... | collective-permute-start | bytes 909320 | tf_op jit(solution)/shard_map/ppermute | solution.py:126
  95.7 2.9 %collective-permute-start.34 = (f32[448,128]{1,0:T(8,128)S(1)}, f32[448,128]{1,0:T(8,128)S(1)}, u32[]{:S(2)}, u32[]{:S(2)}) collective-permute-start(f32[448,128]{1,0:T(8,128)S(1)} %shard_map.83), channel_id=1, source_target_pairs={{0,1},{1,0},{2,3},{3,2},{4,5},{5,4},{6,7},{7,6},{8,9},{9,8},{10,11... | collective-permute-start | bytes 688136 | tf_op jit(solution)/shard_map/ppermute | solution.py:126
  97.0 5.9 %collective-permute-start.38 = (bf16[592,128]{1,0:T(8,128)(2,1)S(1)}, bf16[592,128]{1,0:T(8,128)(2,1)S(1)}, u32[]{:S(2)}, u32[]{:S(2)}) collective-permute-start(bf16[592,128]{1,0:T(8,128)(2,1)S(1)} %shard_map.86.own_ref), channel_id=1, source_target_pairs={{0,2},{1,3},{2,0},{3,1},{4,6},{5,7},{6,4},{7,5},{8,10},{9,11},{10,... | collective-permute-start | bytes 454664 | tf_op jit(solution)/shard_map/ppermute | solution.py:126
  98.6 13.9 %collective-permute-start.46 = (f32[1024,128]{1,0:T(8,128)S(1)}, f32[1024,128]{1,0:T(8,128)S(1)}, u32[]{:S(2)}, u32[]{:S(2)}) collective-permute-start(f32[1024,128]{1,0:T(8,128)S(1)} %get-tuple-element.143.refs_11_), channel_id=1, source_target_pairs={{0,1},{1,0},{2,3},{3,2},{4,5},{5,4},{6,7},{7,6},{8,9},{9,8},{10,11... | collective-permute-start | bytes 1572872 | tf_op jit(solution)/shard_map/ppermute | solution.py:126
  98.6 5.6 %collective-permute-start.35 = (bf16[448,128]{1,0:T(8,128)(2,1)S(1)}, bf16[448,128]{1,0:T(8,128)(2,1)S(1)}, u32[]{:S(2)}, u32[]{:S(2)}) collective-permute-start(bf16[448,128]{1,0:T(8,128)(2,1)S(1)} %shard_map.84.own_ref), channel_id=1, source_target_pairs={{0,4},{1,5},{2,6},{3,7},{4,0},{5,1},{6,2},{7,3},{8,12},{9,13},{10,... | collective-permute-start | bytes 344072 | tf_op jit(solution)/shard_map/ppermute | solution.py:126
  103.0 5.3 %collective-permute-start.39 = (bf16[592,128]{1,0:T(8,128)(2,1)S(1)}, bf16[592,128]{1,0:T(8,128)(2,1)S(1)}, u32[]{:S(2)}, u32[]{:S(2)}) collective-permute-start(bf16[592,128]{1,0:T(8,128)(2,1)S(1)} %shard_map.87.own_ref), channel_id=1, source_target_pairs={{0,4},{1,5},{2,6},{3,7},{4,0},{5,1},{6,2},{7,3},{8,12},{9,13},{10,... | collective-permute-start | bytes 454664 | tf_op jit(solution)/shard_map/ppermute | solution.py:126
  104.3 4.9 %collective-permute-start.36 = (bf16[448,128]{1,0:T(8,128)(2,1)S(1)}, bf16[448,128]{1,0:T(8,128)(2,1)S(1)}, u32[]{:S(2)}, u32[]{:S(2)}) collective-permute-start(bf16[448,128]{1,0:T(8,128)(2,1)S(1)} %shard_map.85.own_ref), channel_id=1, source_target_pairs={{0,2},{1,3},{2,0},{3,1},{4,6},{5,7},{6,4},{7,5},{8,10},{9,11},{10,... | collective-permute-start | bytes 344072 | tf_op jit(solution)/shard_map/ppermute | solution.py:126
  108.4 8.6 %collective-permute-start.44 = (f32[576,128]{1,0:T(8,128)S(1)}, f32[576,128]{1,0:T(8,128)S(1)}, u32[]{:S(2)}, u32[]{:S(2)}) collective-permute-start(f32[576,128]{1,0:T(8,128)S(1)} %get-tuple-element.139.refs_4_), channel_id=1, source_target_pairs={{0,1},{1,0},{2,3},{3,2},{4,5},{5,4},{6,7},{7,6},{8,9},{9,8},{10,11... | collective-permute-start | bytes 884744 | tf_op jit(solution)/shard_map/ppermute | solution.py:126
  109.2 1.2 %collective-permute-start.40 = (f32[8,128]{1,0:T(8,128)S(1)}, f32[8,128]{1,0:T(8,128)S(1)}, u32[]{:S(2)}, u32[]{:S(2)}) collective-permute-start(f32[8,128]{1,0:T(8,128)S(1)} %get-tuple-element.136.own_ref), channel_id=1, source_target_pairs={{0,1},{1,0},{2,3},{3,2},{4,5},{5,4},{6,7},{7,6},{8,9},{9,8},{10,11... | collective-permute-start | bytes 12296 | tf_op jit(solution)/shard_map/ppermute | solution.py:126
  110.5 6.5 %collective-permute-start.45 = (f32[448,128]{1,0:T(8,128)S(1)}, f32[448,128]{1,0:T(8,128)S(1)}, u32[]{:S(2)}, u32[]{:S(2)}) collective-permute-start(f32[448,128]{1,0:T(8,128)S(1)} %get-tuple-element.140.refs_5_), channel_id=1, source_target_pairs={{0,1},{1,0},{2,3},{3,2},{4,5},{5,4},{6,7},{7,6},{8,9},{9,8},{10,11... | collective-permute-start | bytes 688136 | tf_op jit(solution)/shard_map/ppermute | solution.py:126
  110.6 5.4 %collective-permute-start.43 = (f32[8,128]{1,0:T(8,128)S(1)}, f32[8,128]{1,0:T(8,128)S(1)}, u32[]{:S(2)}, u32[]{:S(2)}) collective-permute-start(f32[8,128]{1,0:T(8,128)S(1)} %get-tuple-element.138.refs_0_), channel_id=1, source_target_pairs={{0,24},{8,16},{16,8},{24,0},{1,25},{9,17},{17,9},{25,1},{2,26},{10... | collective-permute-start | bytes 12296 | tf_op jit(solution)/shard_map/ppermute | solution.py:123
  112.5 4.5 %collective-permute-start.42 = (f32[8,128]{1,0:T(8,128)S(1)}, f32[8,128]{1,0:T(8,128)S(1)}, u32[]{:S(2)}, u32[]{:S(2)}) collective-permute-start(f32[8,128]{1,0:T(8,128)S(1)} %get-tuple-element.138.refs_0_), channel_id=1, source_target_pairs={{0,16},{8,24},{16,0},{24,8},{1,17},{9,25},{17,1},{25,9},{2,18},{10... | collective-permute-start | bytes 12296 | tf_op jit(solution)/shard_map/ppermute | solution.py:123
  112.5 4.5 %collective-permute-start.41 = (f32[8,128]{1,0:T(8,128)S(1)}, f32[8,128]{1,0:T(8,128)S(1)}, u32[]{:S(2)}, u32[]{:S(2)}) collective-permute-start(f32[8,128]{1,0:T(8,128)S(1)} %get-tuple-element.138.refs_0_), channel_id=1, source_target_pairs={{0,8},{8,0},{16,24},{24,16},{1,9},{9,1},{17,25},{25,17},{2,10},{10... | collective-permute-start | bytes 12296 | tf_op jit(solution)/shard_map/ppermute | solution.py:123

commit v8 on v7

--- a/solution.py
+++ b/solution.py
@@ -278,17 +278,16 @@
         return call(kernel, [feature_rows, ((feat_share + PAD, outs), BF16)], [own] + got)
 
     def advance(wire, own, delta, got, gamma, dir_sq, grad, direction, images, weights, residual):
-        def kernel(own_ref, delta_ref, *refs):
+        def critical(own_ref, delta_ref, *refs):
             ins = refs[: n_row - 1]
-            gamma_ref, sq_ref, grad_ref, dir_ref, r_ref, ridge_ref = refs[n_row - 1 : n_row + 5]
-            image_refs = refs[n_row + 5 : n_row + 5 + levels]
-            *w_ref, w_out, r_out, grad_out, msg_ref = refs[n_row + 5 + levels :]
+            gamma_ref, sq_ref, grad_ref, dir_ref, ridge_ref, grad_out, msg_ref, alpha_ref = refs[n_row - 1 :]
             if wire == F16:
                 tails = [get_scaled(ref) for ref in ins]
             else:
                 tails = [(1.0, get_row(ref)) for ref in ins]
             image_sq = tree_sum([delta_ref[0:1, :]] + [value for _, value in tails])
             alpha = gamma_ref[0:1, :] / (image_sq + ridge_ref[...] * sq_ref[0:1, :])
+            spread(alpha_ref, alpha)
             prod = own_ref[...]
             for ref, (scale, _) in zip(ins, tails):
                 prod = prod + scale * body_of(ref).astype(F32)
@@ -297,17 +296,26 @@
             msg_ref[pl.ds(0, feat_share), :] = new.astype(BF16)
             put_rows(msg_ref, column_sum(new * new), column_sum(new * old_dir))
             grad_out[...] = new
-            step_taken = alpha * old_dir
+
+        def updates(alpha_ref, dir_ref, r_ref, *refs):
+            image_refs = refs[:levels]
+            *w_ref, w_out, r_out = refs[levels:]
+            alpha = alpha_ref[0:1, :]
+            step_taken = alpha * dir_ref[...]
             w_out[...] = w_ref[0][...] + step_taken if w_ref else step_taken
             for ref, start, rows in zip(image_refs, piece_starts, piece_rows):
                 place = pl.ds(start, rows)
                 r_out[place, :] = r_ref[place, :] - alpha * ref[...]
 
-        return call(
-            kernel,
-            [feature_rows, token_rows, feature_rows, ((feat_share + PAD, outs), BF16)],
-            [own, delta, *got, gamma, dir_sq, grad, direction, residual, ridge, *images, *weights],
-        )
+        grad, msg, alpha = call(
+            critical,
+            [feature_rows, ((feat_share + PAD, outs), BF16), scalar],
+            [own, delta, *got, gamma, dir_sq, grad, direction, ridge],
+        )
+        new_weights, new_residual = call(
+            updates, [feature_rows, token_rows], [alpha, direction, residual, *images, *weights]
+        )
+        return new_weights, new_residual, grad, msg
 
     def forward(wire, in_two, msg):
         got = {step: over_row(step, msg) for step in row_steps}

time: 118 us -> 118 us (level)
    pallas_call x41 -> x43, Pallas kernels: 12.5 us -> 12.6 us  [call(): pl.pallas_call(kernel, out_shape=[jax.ShapeDtypeStruct(shape, dtype) for...]
  transfers between devices with their start and end apart: 47 -> 47, of which waited for: 27 -> 28; matrix products, arithmetic and copies ran while one was open for 0% -> 0% of each run, Pallas kernels for 6% -> 6%
where the time goes in v8:
time: 118 us
  starting transfers between devices  51.8 us (44%)
  waiting for transfers between devices  49.2 us (42%)
  Pallas kernels  12.6 us (11%)
  local copies, waits for them, and re-layouts  3.41 us (3%)
    ppermute x21, starting transfers between devices, over_row(): return lax.ppermute(value, 'row', [(i, i ^ step) for i in range(n_row)])  32.5 us
    ppermute x21, waiting for transfers between devices, over_row(): return lax.ppermute(value, 'row', [(i, i ^ step) for i in range(n_row)])  27.5 us
    ppermute x26, waiting for transfers between devices, over_group(): return lax.ppermute(value, 'group', [(i, i ^ step) for i in range(n_group)])  21.8 us
    ppermute x26, starting transfers between devices, over_group(): return lax.ppermute(value, 'group', [(i, i ^ step) for i in range(n_group)])  19.3 us
    pallas_call x43, Pallas kernels, call(): pl.pallas_call(kernel, out_shape=[jax.ShapeDtypeStruct(shape, dtype) for...  12.6 us
    unnamed x8, local copies, waits for them, and re-layouts  3.41 us
  transfers between devices with their start and end apart: 47, of which 28 were waited for; matrix products, arithmetic and copies ran while one was open for 0% of the time, Pallas kernels for 6%

profile of v8, /device:TPU:0, one launch (start us, length us, event | category | flops | bytes accessed | tf_op | source)
XLA Modules:
  0.0 118.3 jit_solution(11332077650315329319)
XLA Ops:
  0.6 1.2 %copy-done.2 = f32[2048,128]{1,0:T(8,128)S(1)} copy-done((f32[2048,128]{1,0:T(8,128)S(1)}, f32[2048,128]{1,0:T(8,128)}, u32[]{:S(2)}) %copy-start.2) | copy-done | bytes 1048600
  2.2 2.2 %copy-done = bf16[2048,1024]{1,0:T(8,128)(2,1)S(1)} copy-done((bf16[2048,1024]{1,0:T(8,128)(2,1)S(1)}, bf16[2048,1024]{1,0:T(8,128)(2,1)}, u32[]{:S(2)}) %copy-start) | copy-done | bytes 4194328
  4.4 1.2 shard_map.52
  5.6 5.1 %collective-permute-start.2 = (f16[272,128]{1,0:T(8,128)(2,1)S(1)}, f16[272,128]{1,0:T(8,128)(2,1)S(1)}, u32[]{:S(2)}, u32[]{:S(2)}) collective-permute-start(f16[272,128]{1,0:T(8,128)(2,1)S(1)} %convert_element_type.40), channel_id=1, source_target_pairs={{0,24},{8,16},{16,8},{24,0},{1,25},{9,17},{17,9},{25,1},{2,26},{10... | collective-permute-start | bytes 208904 | tf_op jit(solution)/shard_map/ppermute | solution.py:123
  10.8 0.6 collective-permute-start
  12.0 1.3 %collective-permute-done.2 = f16[272,128]{1,0:T(8,128)(2,1)S(1)} collective-permute-done((f16[272,128]{1,0:T(8,128)(2,1)S(1)}, f16[272,128]{1,0:T(8,128)(2,1)S(1)}, u32[]{:S(2)}, u32[]{:S(2)}) %collective-permute-start.2) | collective-permute-done | bytes 69664 | tf_op jit(solution)/shard_map/ppermute | solution.py:123
  13.3 3.3 %collective-permute-done.1 = f16[272,128]{1,0:T(8,128)(2,1)S(1)} collective-permute-done((f16[272,128]{1,0:T(8,128)(2,1)S(1)}, f16[272,128]{1,0:T(8,128)(2,1)S(1)}, u32[]{:S(2)}, u32[]{:S(2)}) %collective-permute-start.1) | collective-permute-done | bytes 69664 | tf_op jit(solution)/shard_map/ppermute | solution.py:123
  16.7 2.8 %collective-permute-start.5 = (bf16[272,128]{1,0:T(8,128)(2,1)S(1)}, bf16[272,128]{1,0:T(8,128)(2,1)S(1)}, u32[]{:S(2)}, u32[]{:S(2)}) collective-permute-start(bf16[272,128]{1,0:T(8,128)(2,1)S(1)} %get-tuple-element.80.refs_0_), channel_id=1, source_target_pairs={{0,24},{8,16},{16,8},{24,0},{1,25},{9,17},{17,9},{25,1},{2,26},{10... | collective-permute-start | bytes 208904 | tf_op jit(solution)/shard_map/ppermute | solution.py:123
  19.5 1.6 %collective-permute-start.3 = (bf16[272,128]{1,0:T(8,128)(2,1)S(1)}, bf16[272,128]{1,0:T(8,128)(2,1)S(1)}, u32[]{:S(2)}, u32[]{:S(2)}) collective-permute-start(bf16[272,128]{1,0:T(8,128)(2,1)S(1)} %get-tuple-element.80.refs_0_), channel_id=1, source_target_pairs={{0,8},{8,0},{16,24},{24,16},{1,9},{9,1},{17,25},{25,17},{2,10},{10... | collective-permute-start | bytes 208904 | tf_op jit(solution)/shard_map/ppermute | solution.py:123
  21.2 2.4 %collective-permute-done.5.refs_3_ = bf16[272,128]{1,0:T(8,128)(2,1)S(1)} collective-permute-done((bf16[272,128]{1,0:T(8,128)(2,1)S(1)}, bf16[272,128]{1,0:T(8,128)(2,1)S(1)}, u32[]{:S(2)}, u32[]{:S(2)}) %collective-permute-start.5) | collective-permute-done | bytes 69664 | tf_op jit(solution)/shard_map/ppermute | solution.py:123
  23.6 2.4 %collective-permute-done.4.refs_2_ = bf16[272,128]{1,0:T(8,128)(2,1)S(1)} collective-permute-done((bf16[272,128]{1,0:T(8,128)(2,1)S(1)}, bf16[272,128]{1,0:T(8,128)(2,1)S(1)}, u32[]{:S(2)}, u32[]{:S(2)}) %collective-permute-start.4) | collective-permute-done | bytes 69664 | tf_op jit(solution)/shard_map/ppermute | solution.py:123
  27.0 0.6 collective-permute-start.10
  27.5 0.7 shard_map.55
  28.3 1.6 %collective-permute-start.7 = (bf16[592,128]{1,0:T(8,128)(2,1)S(1)}, bf16[592,128]{1,0:T(8,128)(2,1)S(1)}, u32[]{:S(2)}, u32[]{:S(2)}) collective-permute-start(bf16[592,128]{1,0:T(8,128)(2,1)S(1)} %shard_map.56.own_ref), channel_id=1, source_target_pairs={{0,2},{1,3},{2,0},{3,1},{4,6},{5,7},{6,4},{7,5},{8,10},{9,11},{10,... | collective-permute-start | bytes 454664 | tf_op jit(solution)/shard_map/ppermute | solution.py:126
  30.0 1.6 %collective-permute-start.11 = (bf16[448,128]{1,0:T(8,128)(2,1)S(1)}, bf16[448,128]{1,0:T(8,128)(2,1)S(1)}, u32[]{:S(2)}, u32[]{:S(2)}) collective-permute-start(bf16[448,128]{1,0:T(8,128)(2,1)S(1)} %shard_map.60.own_ref), channel_id=1, source_target_pairs={{0,4},{1,5},{2,6},{3,7},{4,0},{5,1},{6,2},{7,3},{8,12},{9,13},{10,... | collective-permute-start | bytes 344072 | tf_op jit(solution)/shard_map/ppermute | solution.py:126
  31.5 2.7 %collective-permute-done.7.got_ref = bf16[592,128]{1,0:T(8,128)(2,1)S(1)} collective-permute-done((bf16[592,128]{1,0:T(8,128)(2,1)S(1)}, bf16[592,128]{1,0:T(8,128)(2,1)S(1)}, u32[]{:S(2)}, u32[]{:S(2)}) %collective-permute-start.7) | collective-permute-done | bytes 151584 | tf_op jit(solution)/shard_map/ppermute | solution.py:126
  34.3 1.6 %collective-permute-start.8 = (bf16[592,128]{1,0:T(8,128)(2,1)S(1)}, bf16[592,128]{1,0:T(8,128)(2,1)S(1)}, u32[]{:S(2)}, u32[]{:S(2)}) collective-permute-start(bf16[592,128]{1,0:T(8,128)(2,1)S(1)} %shard_map.57.own_ref), channel_id=1, source_target_pairs={{0,4},{1,5},{2,6},{3,7},{4,0},{5,1},{6,2},{7,3},{8,12},{9,13},{10,... | collective-permute-start | bytes 454664 | tf_op jit(solution)/shard_map/ppermute | solution.py:126
  36.0 1.5 %collective-permute-start.12 = (bf16[448,128]{1,0:T(8,128)(2,1)S(1)}, bf16[448,128]{1,0:T(8,128)(2,1)S(1)}, u32[]{:S(2)}, u32[]{:S(2)}) collective-permute-start(bf16[448,128]{1,0:T(8,128)(2,1)S(1)} %shard_map.61.own_ref), channel_id=1, source_target_pairs={{0,2},{1,3},{2,0},{3,1},{4,6},{5,7},{6,4},{7,5},{8,10},{9,11},{10,... | collective-permute-start | bytes 344072 | tf_op jit(solution)/shard_map/ppermute | solution.py:126
  37.5 2.0 %collective-permute-done.8.got_ref = bf16[592,128]{1,0:T(8,128)(2,1)S(1)} collective-permute-done((bf16[592,128]{1,0:T(8,128)(2,1)S(1)}, bf16[592,128]{1,0:T(8,128)(2,1)S(1)}, u32[]{:S(2)}, u32[]{:S(2)}) %collective-permute-start.8) | collective-permute-done | bytes 151584 | tf_op jit(solution)/shard_map/ppermute | solution.py:126
  39.7 1.1 collective-permute-done.12.got_ref
  41.0 0.5 shard_map.63.refs_2_.refs_3_
  41.5 0.8 collective-permute-done.13.refs_1_.refs_2_
  42.3 0.6 shard_map.65
  42.9 1.8 %collective-permute-start.16 = (f16[272,128]{1,0:T(8,128)(2,1)S(1)}, f16[272,128]{1,0:T(8,128)(2,1)S(1)}, u32[]{:S(2)}, u32[]{:S(2)}) collective-permute-start(f16[272,128]{1,0:T(8,128)(2,1)S(1)} %convert_element_type.46), channel_id=1, source_target_pairs={{0,24},{8,16},{16,8},{24,0},{1,25},{9,17},{17,9},{25,1},{2,26},{10... | collective-permute-start | bytes 208904 | tf_op jit(solution)/shard_map/ppermute | solution.py:123
  44.7 2.8 %collective-permute-start.14 = (f16[272,128]{1,0:T(8,128)(2,1)S(1)}, f16[272,128]{1,0:T(8,128)(2,1)S(1)}, u32[]{:S(2)}, u32[]{:S(2)}) collective-permute-start(f16[272,128]{1,0:T(8,128)(2,1)S(1)} %convert_element_type.42), channel_id=1, source_target_pairs={{0,8},{8,0},{16,24},{24,16},{1,9},{9,1},{17,25},{25,17},{2,10},{10... | collective-permute-start | bytes 208904 | tf_op jit(solution)/shard_map/ppermute | solution.py:123
  47.8 2.1 %collective-permute-done.16 = f16[272,128]{1,0:T(8,128)(2,1)S(1)} collective-permute-done((f16[272,128]{1,0:T(8,128)(2,1)S(1)}, f16[272,128]{1,0:T(8,128)(2,1)S(1)}, u32[]{:S(2)}, u32[]{:S(2)}) %collective-permute-start.16) | collective-permute-done | bytes 69664 | tf_op jit(solution)/shard_map/ppermute | solution.py:123
  49.9 2.1 %collective-permute-done.15 = f16[272,128]{1,0:T(8,128)(2,1)S(1)} collective-permute-done((f16[272,128]{1,0:T(8,128)(2,1)S(1)}, f16[272,128]{1,0:T(8,128)(2,1)S(1)}, u32[]{:S(2)}, u32[]{:S(2)}) %collective-permute-start.15) | collective-permute-done | bytes 69664 | tf_op jit(solution)/shard_map/ppermute | solution.py:123
  52.2 1.8 %collective-permute-start.19 = (bf16[272,128]{1,0:T(8,128)(2,1)S(1)}, bf16[272,128]{1,0:T(8,128)(2,1)S(1)}, u32[]{:S(2)}, u32[]{:S(2)}) collective-permute-start(bf16[272,128]{1,0:T(8,128)(2,1)S(1)} %get-tuple-element.99.refs_0_), channel_id=1, source_target_pairs={{0,24},{8,16},{16,8},{24,0},{1,25},{9,17},{17,9},{25,1},{2,26},{10... | collective-permute-start | bytes 208904 | tf_op jit(solution)/shard_map/ppermute | solution.py:123
  53.9 2.7 %collective-permute-start.17 = (bf16[272,128]{1,0:T(8,128)(2,1)S(1)}, bf16[272,128]{1,0:T(8,128)(2,1)S(1)}, u32[]{:S(2)}, u32[]{:S(2)}) collective-permute-start(bf16[272,128]{1,0:T(8,128)(2,1)S(1)} %get-tuple-element.99.refs_0_), channel_id=1, source_target_pairs={{0,8},{8,0},{16,24},{24,16},{1,9},{9,1},{17,25},{25,17},{2,10},{10... | collective-permute-start | bytes 208904 | tf_op jit(solution)/shard_map/ppermute | solution.py:123
  56.6 2.5 %collective-permute-done.19.refs_1_.refs_3_ = bf16[272,128]{1,0:T(8,128)(2,1)S(1)} collective-permute-done((bf16[272,128]{1,0:T(8,128)(2,1)S(1)}, bf16[272,128]{1,0:T(8,128)(2,1)S(1)}, u32[]{:S(2)}, u32[]{:S(2)}) %collective-permute-start.19) | collective-permute-done | bytes 69664 | tf_op jit(solution)/shard_map/ppermute | solution.py:123
  59.1 0.7 shard_map.67
  59.8 1.3 %collective-permute-done.18.refs_1_.refs_2_ = bf16[272,128]{1,0:T(8,128)(2,1)S(1)} collective-permute-done((bf16[272,128]{1,0:T(8,128)(2,1)S(1)}, bf16[272,128]{1,0:T(8,128)(2,1)S(1)}, u32[]{:S(2)}, u32[]{:S(2)}) %collective-permute-start.18) | collective-permute-done | bytes 69664 | tf_op jit(solution)/shard_map/ppermute | solution.py:123
  61.8 0.6 collective-permute-start.24
  63.2 1.5 %collective-permute-start.21 = (bf16[592,128]{1,0:T(8,128)(2,1)S(1)}, bf16[592,128]{1,0:T(8,128)(2,1)S(1)}, u32[]{:S(2)}, u32[]{:S(2)}) collective-permute-start(bf16[592,128]{1,0:T(8,128)(2,1)S(1)} %shard_map.70.own_ref), channel_id=1, source_target_pairs={{0,2},{1,3},{2,0},{3,1},{4,6},{5,7},{6,4},{7,5},{8,10},{9,11},{10,... | collective-permute-start | bytes 454664 | tf_op jit(solution)/shard_map/ppermute | solution.py:126
  64.8 0.9 collective-permute-start.25
  65.6 3.6 %collective-permute-done.21.got_ref = bf16[592,128]{1,0:T(8,128)(2,1)S(1)} collective-permute-done((bf16[592,128]{1,0:T(8,128)(2,1)S(1)}, bf16[592,128]{1,0:T(8,128)(2,1)S(1)}, u32[]{:S(2)}, u32[]{:S(2)}) %collective-permute-start.21) | collective-permute-done | bytes 151584 | tf_op jit(solution)/shard_map/ppermute | solution.py:126
  69.3 0.9 collective-permute-start.22
  70.2 1.6 %collective-permute-start.26 = (bf16[448,128]{1,0:T(8,128)(2,1)S(1)}, bf16[448,128]{1,0:T(8,128)(2,1)S(1)}, u32[]{:S(2)}, u32[]{:S(2)}) collective-permute-start(bf16[448,128]{1,0:T(8,128)(2,1)S(1)} %shard_map.75.own_ref), channel_id=1, source_target_pairs={{0,2},{1,3},{2,0},{3,1},{4,6},{5,7},{6,4},{7,5},{8,10},{9,11},{10,... | collective-permute-start | bytes 344072 | tf_op jit(solution)/shard_map/ppermute | solution.py:126
  71.7 2.8 %collective-permute-done.22.got_ref = bf16[592,128]{1,0:T(8,128)(2,1)S(1)} collective-permute-done((bf16[592,128]{1,0:T(8,128)(2,1)S(1)}, bf16[592,128]{1,0:T(8,128)(2,1)S(1)}, u32[]{:S(2)}, u32[]{:S(2)}) %collective-permute-start.22) | collective-permute-done | bytes 151584 | tf_op jit(solution)/shard_map/ppermute | solution.py:126
  75.3 0.6 shard_map.77.refs_2_.refs_3_
  75.9 0.6 collective-permute-done.27.refs_1_.refs_2_
  77.1 2.3 %collective-permute-start.29 = (bf16[272,128]{1,0:T(8,128)(2,1)S(1)}, bf16[272,128]{1,0:T(8,128)(2,1)S(1)}, u32[]{:S(2)}, u32[]{:S(2)}) collective-permute-start(bf16[272,128]{1,0:T(8,128)(2,1)S(1)} %get-tuple-element.118), channel_id=1, source_target_pairs={{0,16},{8,24},{16,0},{24,8},{1,17},{9,25},{17,1},{25,9},{2,18},{10... | collective-permute-start | bytes 208904 | tf_op jit(solution)/shard_map/ppermute | solution.py:123
  79.4 2.1 %collective-permute-start.30 = (bf16[272,128]{1,0:T(8,128)(2,1)S(1)}, bf16[272,128]{1,0:T(8,128)(2,1)S(1)}, u32[]{:S(2)}, u32[]{:S(2)}) collective-permute-start(bf16[272,128]{1,0:T(8,128)(2,1)S(1)} %get-tuple-element.119), channel_id=1, source_target_pairs={{0,24},{8,16},{16,8},{24,0},{1,25},{9,17},{17,9},{25,1},{2,26},{10... | collective-permute-start | bytes 208904 | tf_op jit(solution)/shard_map/ppermute | solution.py:123
  82.4 3.7 %collective-permute-done.29.refs_1_ = bf16[272,128]{1,0:T(8,128)(2,1)S(1)} collective-permute-done((bf16[272,128]{1,0:T(8,128)(2,1)S(1)}, bf16[272,128]{1,0:T(8,128)(2,1)S(1)}, u32[]{:S(2)}, u32[]{:S(2)}) %collective-permute-start.29) | collective-permute-done | bytes 69664 | tf_op jit(solution)/shard_map/ppermute | solution.py:123
  86.2 2.0 %collective-permute-start.33 = (bf16[272,128]{1,0:T(8,128)(2,1)S(1)}, bf16[272,128]{1,0:T(8,128)(2,1)S(1)}, u32[]{:S(2)}, u32[]{:S(2)}) collective-permute-start(bf16[272,128]{1,0:T(8,128)(2,1)S(1)} %get-tuple-element.123.refs_0_), channel_id=1, source_target_pairs={{0,24},{8,16},{16,8},{24,0},{1,25},{9,17},{17,9},{25,1},{2,26},{10... | collective-permute-start | bytes 208904 | tf_op jit(solution)/shard_map/ppermute | solution.py:123
  88.1 0.9 collective-permute-start.32
  89.0 1.6 %collective-permute-start.31 = (bf16[272,128]{1,0:T(8,128)(2,1)S(1)}, bf16[272,128]{1,0:T(8,128)(2,1)S(1)}, u32[]{:S(2)}, u32[]{:S(2)}) collective-permute-start(bf16[272,128]{1,0:T(8,128)(2,1)S(1)} %get-tuple-element.123.refs_0_), channel_id=1, source_target_pairs={{0,8},{8,0},{16,24},{24,16},{1,9},{9,1},{17,25},{25,17},{2,10},{10... | collective-permute-start | bytes 208904 | tf_op jit(solution)/shard_map/ppermute | solution.py:123
  90.6 1.9 %collective-permute-done.33.refs_3_ = bf16[272,128]{1,0:T(8,128)(2,1)S(1)} collective-permute-done((bf16[272,128]{1,0:T(8,128)(2,1)S(1)}, bf16[272,128]{1,0:T(8,128)(2,1)S(1)}, u32[]{:S(2)}, u32[]{:S(2)}) %collective-permute-start.33) | collective-permute-done | bytes 69664 | tf_op jit(solution)/shard_map/ppermute | solution.py:123
  92.5 2.1 %collective-permute-done.32.refs_2_ = bf16[272,128]{1,0:T(8,128)(2,1)S(1)} collective-permute-done((bf16[272,128]{1,0:T(8,128)(2,1)S(1)}, bf16[272,128]{1,0:T(8,128)(2,1)S(1)}, u32[]{:S(2)}, u32[]{:S(2)}) %collective-permute-start.32) | collective-permute-done | bytes 69664 | tf_op jit(solution)/shard_map/ppermute | solution.py:123
  95.6 0.6 collective-permute-start.34
  96.1 0.7 shard_map.82
  96.9 1.5 %collective-permute-start.38 = (bf16[592,128]{1,0:T(8,128)(2,1)S(1)}, bf16[592,128]{1,0:T(8,128)(2,1)S(1)}, u32[]{:S(2)}, u32[]{:S(2)}) collective-permute-start(bf16[592,128]{1,0:T(8,128)(2,1)S(1)} %shard_map.86.own_ref), channel_id=1, source_target_pairs={{0,2},{1,3},{2,0},{3,1},{4,6},{5,7},{6,4},{7,5},{8,10},{9,11},{10,... | collective-permute-start | bytes 454664 | tf_op jit(solution)/shard_map/ppermute | solution.py:126
  98.8 1.2 %collective-permute-start.35 = (bf16[448,128]{1,0:T(8,128)(2,1)S(1)}, bf16[448,128]{1,0:T(8,128)(2,1)S(1)}, u32[]{:S(2)}, u32[]{:S(2)}) collective-permute-start(bf16[448,128]{1,0:T(8,128)(2,1)S(1)} %shard_map.84.own_ref), channel_id=1, source_target_pairs={{0,4},{1,5},{2,6},{3,7},{4,0},{5,1},{6,2},{7,3},{8,12},{9,13},{10,... | collective-permute-start | bytes 344072 | tf_op jit(solution)/shard_map/ppermute | solution.py:126
  100.0 2.8 %collective-permute-done.38.got_ref = bf16[592,128]{1,0:T(8,128)(2,1)S(1)} collective-permute-done((bf16[592,128]{1,0:T(8,128)(2,1)S(1)}, bf16[592,128]{1,0:T(8,128)(2,1)S(1)}, u32[]{:S(2)}, u32[]{:S(2)}) %collective-permute-start.38) | collective-permute-done | bytes 151584 | tf_op jit(solution)/shard_map/ppermute | solution.py:126
  102.9 1.2 %collective-permute-start.39 = (bf16[592,128]{1,0:T(8,128)(2,1)S(1)}, bf16[592,128]{1,0:T(8,128)(2,1)S(1)}, u32[]{:S(2)}, u32[]{:S(2)}) collective-permute-start(bf16[592,128]{1,0:T(8,128)(2,1)S(1)} %shard_map.87.own_ref), channel_id=1, source_target_pairs={{0,4},{1,5},{2,6},{3,7},{4,0},{5,1},{6,2},{7,3},{8,12},{9,13},{10,... | collective-permute-start | bytes 454664 | tf_op jit(solution)/shard_map/ppermute | solution.py:126
  104.4 1.3 %collective-permute-start.36 = (bf16[448,128]{1,0:T(8,128)(2,1)S(1)}, bf16[448,128]{1,0:T(8,128)(2,1)S(1)}, u32[]{:S(2)}, u32[]{:S(2)}) collective-permute-start(bf16[448,128]{1,0:T(8,128)(2,1)S(1)} %shard_map.85.own_ref), channel_id=1, source_target_pairs={{0,2},{1,3},{2,0},{3,1},{4,6},{5,7},{6,4},{7,5},{8,10},{9,11},{10,... | collective-permute-start | bytes 344072 | tf_op jit(solution)/shard_map/ppermute | solution.py:126
  105.7 2.4 %collective-permute-done.39.got_ref = bf16[592,128]{1,0:T(8,128)(2,1)S(1)} collective-permute-done((bf16[592,128]{1,0:T(8,128)(2,1)S(1)}, bf16[592,128]{1,0:T(8,128)(2,1)S(1)}, u32[]{:S(2)}, u32[]{:S(2)}) %collective-permute-start.39) | collective-permute-done | bytes 151584 | tf_op jit(solution)/shard_map/ppermute | solution.py:126
  108.3 0.9 collective-permute-done.36.got_ref
  109.4 1.2 collective-permute-done.40.got_ref
  110.7 1.8 %collective-permute-start.43 = (f32[8,128]{1,0:T(8,128)S(1)}, f32[8,128]{1,0:T(8,128)S(1)}, u32[]{:S(2)}, u32[]{:S(2)}) collective-permute-start(f32[8,128]{1,0:T(8,128)S(1)} %get-tuple-element.137.refs_0_), channel_id=1, source_target_pairs={{0,24},{8,16},{16,8},{24,0},{1,25},{9,17},{17,9},{25,1},{2,26},{10... | collective-permute-start | bytes 12296 | tf_op jit(solution)/shard_map/ppermute | solution.py:123
  112.6 2.6 %collective-permute-start.41 = (f32[8,128]{1,0:T(8,128)S(1)}, f32[8,128]{1,0:T(8,128)S(1)}, u32[]{:S(2)}, u32[]{:S(2)}) collective-permute-start(f32[8,128]{1,0:T(8,128)S(1)} %get-tuple-element.137.refs_0_), channel_id=1, source_target_pairs={{0,8},{8,0},{16,24},{24,16},{1,9},{9,1},{17,25},{25,17},{2,10},{10... | collective-permute-start | bytes 12296 | tf_op jit(solution)/shard_map/ppermute | solution.py:123
  115.1 1.0 collective-permute-done.43.refs_3_
  116.1 0.9 collective-permute-done.42.refs_2_
  117.1 1.2 %shard_map.93 = (f32[256,128]{1,0:T(8,128)}, f32[2048,128]{1,0:T(8,128)}) custom-call(f32[8,128]{1,0:T(8,128)S(1)} %get-tuple-element.137.refs_0_, f32[8,128]{1,0:T(8,128)S(1)} %collective-permute-done.41.refs_1_, f32[8,128]{1,0:T(8,128)S(1)} %collective-permute-done.42.refs_2_, f32[8,128]{1,0:T(8,128)S(1)} %collective-permute-done.43.refs_3_, ...), custom_call_target="tpu_custom_call" | custom-call | tf_op jit(solution)/shard_map/pallas_call | solution.py:93
  (94 shorter events, 9.2 us)
Async XLA Ops:
  0.6 1.2 %copy-start.2 = (f32[2048,128]{1,0:T(8,128)S(1)}, f32[2048,128]{1,0:T(8,128)}, u32[]{:S(2)}) copy-start(f32[2048,128]{1,0:T(8,128)} %t_ref.1) | copy-start | bytes 3145732
  2.2 2.2 %copy-start = (bf16[2048,1024]{1,0:T(8,128)(2,1)S(1)}, bf16[2048,1024]{1,0:T(8,128)(2,1)}, u32[]{:S(2)}) copy-start(bf16[2048,1024]{1,0:T(8,128)(2,1)} %a_ref.35) | copy-start | bytes 12582916
  5.5 20.4 %copy-start.1 = (bf16[2048,1024]{1,0:T(8,128)(2,1)S(1)}, bf16[2048,1024]{1,0:T(8,128)(2,1)}, u32[]{:S(2)}) copy-start(bf16[2048,1024]{1,0:T(8,128)(2,1)} %a_ref.35) | copy-start | bytes 12582916
  5.6 7.7 %collective-permute-start.2 = (f16[272,128]{1,0:T(8,128)(2,1)S(1)}, f16[272,128]{1,0:T(8,128)(2,1)S(1)}, u32[]{:S(2)}, u32[]{:S(2)}) collective-permute-start(f16[272,128]{1,0:T(8,128)(2,1)S(1)} %convert_element_type.40), channel_id=1, source_target_pairs={{0,24},{8,16},{16,8},{24,0},{1,25},{9,17},{17,9},{25,1},{2,26},{10... | collective-permute-start | bytes 208904 | tf_op jit(solution)/shard_map/ppermute | solution.py:123
  10.7 5.9 %collective-permute-start.1 = (f16[272,128]{1,0:T(8,128)(2,1)S(1)}, f16[272,128]{1,0:T(8,128)(2,1)S(1)}, u32[]{:S(2)}, u32[]{:S(2)}) collective-permute-start(f16[272,128]{1,0:T(8,128)(2,1)S(1)} %convert_element_type.38), channel_id=1, source_target_pairs={{0,16},{8,24},{16,0},{24,8},{1,17},{9,25},{17,1},{25,9},{2,18},{10... | collective-permute-start | bytes 208904 | tf_op jit(solution)/shard_map/ppermute | solution.py:123
  10.8 5.8 %collective-permute-start = (f16[272,128]{1,0:T(8,128)(2,1)S(1)}, f16[272,128]{1,0:T(8,128)(2,1)S(1)}, u32[]{:S(2)}, u32[]{:S(2)}) collective-permute-start(f16[272,128]{1,0:T(8,128)(2,1)S(1)} %convert_element_type.36), channel_id=1, source_target_pairs={{0,8},{8,0},{16,24},{24,16},{1,9},{9,1},{17,25},{25,17},{2,10},{10... | collective-permute-start | bytes 208904 | tf_op jit(solution)/shard_map/ppermute | solution.py:123
  16.7 6.8 %collective-permute-start.5 = (bf16[272,128]{1,0:T(8,128)(2,1)S(1)}, bf16[272,128]{1,0:T(8,128)(2,1)S(1)}, u32[]{:S(2)}, u32[]{:S(2)}) collective-permute-start(bf16[272,128]{1,0:T(8,128)(2,1)S(1)} %get-tuple-element.80.refs_0_), channel_id=1, source_target_pairs={{0,24},{8,16},{16,8},{24,0},{1,25},{9,17},{17,9},{25,1},{2,26},{10... | collective-permute-start | bytes 208904 | tf_op jit(solution)/shard_map/ppermute | solution.py:123
  19.5 6.4 %collective-permute-start.4 = (bf16[272,128]{1,0:T(8,128)(2,1)S(1)}, bf16[272,128]{1,0:T(8,128)(2,1)S(1)}, u32[]{:S(2)}, u32[]{:S(2)}) collective-permute-start(bf16[272,128]{1,0:T(8,128)(2,1)S(1)} %get-tuple-element.80.refs_0_), channel_id=1, source_target_pairs={{0,16},{8,24},{16,0},{24,8},{1,17},{9,25},{17,1},{25,9},{2,18},{10... | collective-permute-start | bytes 208904 | tf_op jit(solution)/shard_map/ppermute | solution.py:123
  19.5 6.4 %collective-permute-start.3 = (bf16[272,128]{1,0:T(8,128)(2,1)S(1)}, bf16[272,128]{1,0:T(8,128)(2,1)S(1)}, u32[]{:S(2)}, u32[]{:S(2)}) collective-permute-start(bf16[272,128]{1,0:T(8,128)(2,1)S(1)} %get-tuple-element.80.refs_0_), channel_id=1, source_target_pairs={{0,8},{8,0},{16,24},{24,16},{1,9},{9,1},{17,25},{25,17},{2,10},{10... | collective-permute-start | bytes 208904 | tf_op jit(solution)/shard_map/ppermute | solution.py:123
  26.5 1.8 %collective-permute-start.6 = (f32[592,128]{1,0:T(8,128)S(1)}, f32[592,128]{1,0:T(8,128)S(1)}, u32[]{:S(2)}, u32[]{:S(2)}) collective-permute-start(f32[592,128]{1,0:T(8,128)S(1)} %get-tuple-element.83), channel_id=1, source_target_pairs={{0,1},{1,0},{2,3},{3,2},{4,5},{5,4},{6,7},{7,6},{8,9},{9,8},{10,11... | collective-permute-start | bytes 909320 | tf_op jit(solution)/shard_map/ppermute | solution.py:126
  27.0 2.9 %collective-permute-start.10 = (f32[448,128]{1,0:T(8,128)S(1)}, f32[448,128]{1,0:T(8,128)S(1)}, u32[]{:S(2)}, u32[]{:S(2)}) collective-permute-start(f32[448,128]{1,0:T(8,128)S(1)} %shard_map.59), channel_id=1, source_target_pairs={{0,1},{1,0},{2,3},{3,2},{4,5},{5,4},{6,7},{7,6},{8,9},{9,8},{10,11... | collective-permute-start | bytes 688136 | tf_op jit(solution)/shard_map/ppermute | solution.py:126
  28.3 5.9 %collective-permute-start.7 = (bf16[592,128]{1,0:T(8,128)(2,1)S(1)}, bf16[592,128]{1,0:T(8,128)(2,1)S(1)}, u32[]{:S(2)}, u32[]{:S(2)}) collective-permute-start(bf16[592,128]{1,0:T(8,128)(2,1)S(1)} %shard_map.56.own_ref), channel_id=1, source_target_pairs={{0,2},{1,3},{2,0},{3,1},{4,6},{5,7},{6,4},{7,5},{8,10},{9,11},{10,... | collective-permute-start | bytes 454664 | tf_op jit(solution)/shard_map/ppermute | solution.py:126
  30.0 6.0 %collective-permute-start.11 = (bf16[448,128]{1,0:T(8,128)(2,1)S(1)}, bf16[448,128]{1,0:T(8,128)(2,1)S(1)}, u32[]{:S(2)}, u32[]{:S(2)}) collective-permute-start(bf16[448,128]{1,0:T(8,128)(2,1)S(1)} %shard_map.60.own_ref), channel_id=1, source_target_pairs={{0,4},{1,5},{2,6},{3,7},{4,0},{5,1},{6,2},{7,3},{8,12},{9,13},{10,... | collective-permute-start | bytes 344072 | tf_op jit(solution)/shard_map/ppermute | solution.py:126
  34.3 5.3 %collective-permute-start.8 = (bf16[592,128]{1,0:T(8,128)(2,1)S(1)}, bf16[592,128]{1,0:T(8,128)(2,1)S(1)}, u32[]{:S(2)}, u32[]{:S(2)}) collective-permute-start(bf16[592,128]{1,0:T(8,128)(2,1)S(1)} %shard_map.57.own_ref), channel_id=1, source_target_pairs={{0,4},{1,5},{2,6},{3,7},{4,0},{5,1},{6,2},{7,3},{8,12},{9,13},{10,... | collective-permute-start | bytes 454664 | tf_op jit(solution)/shard_map/ppermute | solution.py:126
  36.0 4.9 %collective-permute-start.12 = (bf16[448,128]{1,0:T(8,128)(2,1)S(1)}, bf16[448,128]{1,0:T(8,128)(2,1)S(1)}, u32[]{:S(2)}, u32[]{:S(2)}) collective-permute-start(bf16[448,128]{1,0:T(8,128)(2,1)S(1)} %shard_map.61.own_ref), channel_id=1, source_target_pairs={{0,2},{1,3},{2,0},{3,1},{4,6},{5,7},{6,4},{7,5},{8,10},{9,11},{10,... | collective-permute-start | bytes 344072 | tf_op jit(solution)/shard_map/ppermute | solution.py:126
  39.6 2.7 %collective-permute-start.9 = (bf16[576,128]{1,0:T(8,128)(2,1)S(1)}, bf16[576,128]{1,0:T(8,128)(2,1)S(1)}, u32[]{:S(2)}, u32[]{:S(2)}) collective-permute-start(bf16[576,128]{1,0:T(8,128)(2,1)S(1)} %get-tuple-element.87.refs_0_), channel_id=1, source_target_pairs={{0,1},{1,0},{2,3},{3,2},{4,5},{5,4},{6,7},{7,6},{8,9},{9,8},{10,11... | collective-permute-start | bytes 442376 | tf_op jit(solution)/shard_map/ppermute | solution.py:126
  40.9 1.4 %collective-permute-start.13 = (bf16[464,128]{1,0:T(8,128)(2,1)S(1)}, bf16[464,128]{1,0:T(8,128)(2,1)S(1)}, u32[]{:S(2)}, u32[]{:S(2)}) collective-permute-start(bf16[464,128]{1,0:T(8,128)(2,1)S(1)} %get-tuple-element.91.refs_1_.refs_0_), channel_id=1, source_target_pairs={{0,1},{1,0},{2,3},{3,2},{4,5},{5,4},{6,7},{7,6},{8,9},{9,8},{10,11... | collective-permute-start | bytes 356360 | tf_op jit(solution)/shard_map/ppermute | solution.py:126
  42.9 9.2 %copy-start.3 = (f32[128]{0:T(128)S(1)}, f32[128]{0:T(128)}, u32[]{:S(2)}) copy-start(f32[128]{0:T(128)} %param.5) | copy-start | bytes 1540
  42.9 6.9 %collective-permute-start.16 = (f16[272,128]{1,0:T(8,128)(2,1)S(1)}, f16[272,128]{1,0:T(8,128)(2,1)S(1)}, u32[]{:S(2)}, u32[]{:S(2)}) collective-permute-start(f16[272,128]{1,0:T(8,128)(2,1)S(1)} %convert_element_type.46), channel_id=1, source_target_pairs={{0,24},{8,16},{16,8},{24,0},{1,25},{9,17},{17,9},{25,1},{2,26},{10... | collective-permute-start | bytes 208904 | tf_op jit(solution)/shard_map/ppermute | solution.py:123
  44.7 7.3 %collective-permute-start.15 = (f16[272,128]{1,0:T(8,128)(2,1)S(1)}, f16[272,128]{1,0:T(8,128)(2,1)S(1)}, u32[]{:S(2)}, u32[]{:S(2)}) collective-permute-start(f16[272,128]{1,0:T(8,128)(2,1)S(1)} %convert_element_type.44), channel_id=1, source_target_pairs={{0,16},{8,24},{16,0},{24,8},{1,17},{9,25},{17,1},{25,9},{2,18},{10... | collective-permute-start | bytes 208904 | tf_op jit(solution)/shard_map/ppermute | solution.py:123
  44.7 7.3 %collective-permute-start.14 = (f16[272,128]{1,0:T(8,128)(2,1)S(1)}, f16[272,128]{1,0:T(8,128)(2,1)S(1)}, u32[]{:S(2)}, u32[]{:S(2)}) collective-permute-start(f16[272,128]{1,0:T(8,128)(2,1)S(1)} %convert_element_type.42), channel_id=1, source_target_pairs={{0,8},{8,0},{16,24},{24,16},{1,9},{9,1},{17,25},{25,17},{2,10},{10... | collective-permute-start | bytes 208904 | tf_op jit(solution)/shard_map/ppermute | solution.py:123
  52.2 6.9 %collective-permute-start.19 = (bf16[272,128]{1,0:T(8,128)(2,1)S(1)}, bf16[272,128]{1,0:T(8,128)(2,1)S(1)}, u32[]{:S(2)}, u32[]{:S(2)}) collective-permute-start(bf16[272,128]{1,0:T(8,128)(2,1)S(1)} %get-tuple-element.99.refs_0_), channel_id=1, source_target_pairs={{0,24},{8,16},{16,8},{24,0},{1,25},{9,17},{17,9},{25,1},{2,26},{10... | collective-permute-start | bytes 208904 | tf_op jit(solution)/shard_map/ppermute | solution.py:123
  53.9 7.2 %collective-permute-start.18 = (bf16[272,128]{1,0:T(8,128)(2,1)S(1)}, bf16[272,128]{1,0:T(8,128)(2,1)S(1)}, u32[]{:S(2)}, u32[]{:S(2)}) collective-permute-start(bf16[272,128]{1,0:T(8,128)(2,1)S(1)} %get-tuple-element.99.refs_0_), channel_id=1, source_target_pairs={{0,16},{8,24},{16,0},{24,8},{1,17},{9,25},{17,1},{25,9},{2,18},{10... | collective-permute-start | bytes 208904 | tf_op jit(solution)/shard_map/ppermute | solution.py:123
  53.9 7.2 %collective-permute-start.17 = (bf16[272,128]{1,0:T(8,128)(2,1)S(1)}, bf16[272,128]{1,0:T(8,128)(2,1)S(1)}, u32[]{:S(2)}, u32[]{:S(2)}) collective-permute-start(bf16[272,128]{1,0:T(8,128)(2,1)S(1)} %get-tuple-element.99.refs_0_), channel_id=1, source_target_pairs={{0,8},{8,0},{16,24},{24,16},{1,9},{9,1},{17,25},{25,17},{2,10},{10... | collective-permute-start | bytes 208904 | tf_op jit(solution)/shard_map/ppermute | solution.py:123
  61.5 1.7 %collective-permute-start.20 = (f32[592,128]{1,0:T(8,128)S(1)}, f32[592,128]{1,0:T(8,128)S(1)}, u32[]{:S(2)}, u32[]{:S(2)}) collective-permute-start(f32[592,128]{1,0:T(8,128)S(1)} %get-tuple-element.104), channel_id=1, source_target_pairs={{0,1},{1,0},{2,3},{3,2},{4,5},{5,4},{6,7},{7,6},{8,9},{9,8},{10,11... | collective-permute-start | bytes 909320 | tf_op jit(solution)/shard_map/ppermute | solution.py:126
  61.8 2.9 %collective-permute-start.24 = (f32[448,128]{1,0:T(8,128)S(1)}, f32[448,128]{1,0:T(8,128)S(1)}, u32[]{:S(2)}, u32[]{:S(2)}) collective-permute-start(f32[448,128]{1,0:T(8,128)S(1)} %shard_map.73), channel_id=1, source_target_pairs={{0,1},{1,0},{2,3},{3,2},{4,5},{5,4},{6,7},{7,6},{8,9},{9,8},{10,11... | collective-permute-start | bytes 688136 | tf_op jit(solution)/shard_map/ppermute | solution.py:126
  63.2 6.0 %collective-permute-start.21 = (bf16[592,128]{1,0:T(8,128)(2,1)S(1)}, bf16[592,128]{1,0:T(8,128)(2,1)S(1)}, u32[]{:S(2)}, u32[]{:S(2)}) collective-permute-start(bf16[592,128]{1,0:T(8,128)(2,1)S(1)} %shard_map.70.own_ref), channel_id=1, source_target_pairs={{0,2},{1,3},{2,0},{3,1},{4,6},{5,7},{6,4},{7,5},{8,10},{9,11},{10,... | collective-permute-start | bytes 454664 | tf_op jit(solution)/shard_map/ppermute | solution.py:126
  64.8 5.4 %collective-permute-start.25 = (bf16[448,128]{1,0:T(8,128)(2,1)S(1)}, bf16[448,128]{1,0:T(8,128)(2,1)S(1)}, u32[]{:S(2)}, u32[]{:S(2)}) collective-permute-start(bf16[448,128]{1,0:T(8,128)(2,1)S(1)} %shard_map.74.own_ref), channel_id=1, source_target_pairs={{0,4},{1,5},{2,6},{3,7},{4,0},{5,1},{6,2},{7,3},{8,12},{9,13},{10,... | collective-permute-start | bytes 344072 | tf_op jit(solution)/shard_map/ppermute | solution.py:126
  69.3 5.3 %collective-permute-start.22 = (bf16[592,128]{1,0:T(8,128)(2,1)S(1)}, bf16[592,128]{1,0:T(8,128)(2,1)S(1)}, u32[]{:S(2)}, u32[]{:S(2)}) collective-permute-start(bf16[592,128]{1,0:T(8,128)(2,1)S(1)} %shard_map.71.own_ref), channel_id=1, source_target_pairs={{0,4},{1,5},{2,6},{3,7},{4,0},{5,1},{6,2},{7,3},{8,12},{9,13},{10,... | collective-permute-start | bytes 454664 | tf_op jit(solution)/shard_map/ppermute | solution.py:126
  70.2 4.9 %collective-permute-start.26 = (bf16[448,128]{1,0:T(8,128)(2,1)S(1)}, bf16[448,128]{1,0:T(8,128)(2,1)S(1)}, u32[]{:S(2)}, u32[]{:S(2)}) collective-permute-start(bf16[448,128]{1,0:T(8,128)(2,1)S(1)} %shard_map.75.own_ref), channel_id=1, source_target_pairs={{0,2},{1,3},{2,0},{3,1},{4,6},{5,7},{6,4},{7,5},{8,10},{9,11},{10,... | collective-permute-start | bytes 344072 | tf_op jit(solution)/shard_map/ppermute | solution.py:126
  74.6 1.9 %collective-permute-start.23 = (bf16[576,128]{1,0:T(8,128)(2,1)S(1)}, bf16[576,128]{1,0:T(8,128)(2,1)S(1)}, u32[]{:S(2)}, u32[]{:S(2)}) collective-permute-start(bf16[576,128]{1,0:T(8,128)(2,1)S(1)} %get-tuple-element.109.refs_0_), channel_id=1, source_target_pairs={{0,1},{1,0},{2,3},{3,2},{4,5},{5,4},{6,7},{7,6},{8,9},{9,8},{10,11... | collective-permute-start | bytes 442376 | tf_op jit(solution)/shard_map/ppermute | solution.py:126
  75.1 1.4 %collective-permute-start.27 = (bf16[464,128]{1,0:T(8,128)(2,1)S(1)}, bf16[464,128]{1,0:T(8,128)(2,1)S(1)}, u32[]{:S(2)}, u32[]{:S(2)}) collective-permute-start(bf16[464,128]{1,0:T(8,128)(2,1)S(1)} %get-tuple-element.115.refs_1_.refs_0_), channel_id=1, source_target_pairs={{0,1},{1,0},{2,3},{3,2},{4,5},{5,4},{6,7},{7,6},{8,9},{9,8},{10,11... | collective-permute-start | bytes 356360 | tf_op jit(solution)/shard_map/ppermute | solution.py:126
  77.1 5.3 %collective-permute-start.28 = (bf16[272,128]{1,0:T(8,128)(2,1)S(1)}, bf16[272,128]{1,0:T(8,128)(2,1)S(1)}, u32[]{:S(2)}, u32[]{:S(2)}) collective-permute-start(bf16[272,128]{1,0:T(8,128)(2,1)S(1)} %get-tuple-element.117), channel_id=1, source_target_pairs={{0,8},{8,0},{16,24},{24,16},{1,9},{9,1},{17,25},{25,17},{2,10},{10... | collective-permute-start | bytes 208904 | tf_op jit(solution)/shard_map/ppermute | solution.py:123
  77.1 8.9 %collective-permute-start.29 = (bf16[272,128]{1,0:T(8,128)(2,1)S(1)}, bf16[272,128]{1,0:T(8,128)(2,1)S(1)}, u32[]{:S(2)}, u32[]{:S(2)}) collective-permute-start(bf16[272,128]{1,0:T(8,128)(2,1)S(1)} %get-tuple-element.118), channel_id=1, source_target_pairs={{0,16},{8,24},{16,0},{24,8},{1,17},{9,25},{17,1},{25,9},{2,18},{10... | collective-permute-start | bytes 208904 | tf_op jit(solution)/shard_map/ppermute | solution.py:123
  79.4 6.7 %collective-permute-start.30 = (bf16[272,128]{1,0:T(8,128)(2,1)S(1)}, bf16[272,128]{1,0:T(8,128)(2,1)S(1)}, u32[]{:S(2)}, u32[]{:S(2)}) collective-permute-start(bf16[272,128]{1,0:T(8,128)(2,1)S(1)} %get-tuple-element.119), channel_id=1, source_target_pairs={{0,24},{8,16},{16,8},{24,0},{1,25},{9,17},{17,9},{25,1},{2,26},{10... | collective-permute-start | bytes 208904 | tf_op jit(solution)/shard_map/ppermute | solution.py:123
  86.2 6.3 %collective-permute-start.33 = (bf16[272,128]{1,0:T(8,128)(2,1)S(1)}, bf16[272,128]{1,0:T(8,128)(2,1)S(1)}, u32[]{:S(2)}, u32[]{:S(2)}) collective-permute-start(bf16[272,128]{1,0:T(8,128)(2,1)S(1)} %get-tuple-element.123.refs_0_), channel_id=1, source_target_pairs={{0,24},{8,16},{16,8},{24,0},{1,25},{9,17},{17,9},{25,1},{2,26},{10... | collective-permute-start | bytes 208904 | tf_op jit(solution)/shard_map/ppermute | solution.py:123
  88.1 6.4 %collective-permute-start.32 = (bf16[272,128]{1,0:T(8,128)(2,1)S(1)}, bf16[272,128]{1,0:T(8,128)(2,1)S(1)}, u32[]{:S(2)}, u32[]{:S(2)}) collective-permute-start(bf16[272,128]{1,0:T(8,128)(2,1)S(1)} %get-tuple-element.123.refs_0_), channel_id=1, source_target_pairs={{0,16},{8,24},{16,0},{24,8},{1,17},{9,25},{17,1},{25,9},{2,18},{10... | collective-permute-start | bytes 208904 | tf_op jit(solution)/shard_map/ppermute | solution.py:123
  89.0 5.6 %collective-permute-start.31 = (bf16[272,128]{1,0:T(8,128)(2,1)S(1)}, bf16[272,128]{1,0:T(8,128)(2,1)S(1)}, u32[]{:S(2)}, u32[]{:S(2)}) collective-permute-start(bf16[272,128]{1,0:T(8,128)(2,1)S(1)} %get-tuple-element.123.refs_0_), channel_id=1, source_target_pairs={{0,8},{8,0},{16,24},{24,16},{1,9},{9,1},{17,25},{25,17},{2,10},{10... | collective-permute-start | bytes 208904 | tf_op jit(solution)/shard_map/ppermute | solution.py:123
  95.1 1.8 %collective-permute-start.37 = (f32[592,128]{1,0:T(8,128)S(1)}, f32[592,128]{1,0:T(8,128)S(1)}, u32[]{:S(2)}, u32[]{:S(2)}) collective-permute-start(f32[592,128]{1,0:T(8,128)S(1)} %get-tuple-element.127), channel_id=1, source_target_pairs={{0,1},{1,0},{2,3},{3,2},{4,5},{5,4},{6,7},{7,6},{8,9},{9,8},{10,11... | collective-permute-start | bytes 909320 | tf_op jit(solution)/shard_map/ppermute | solution.py:126
  95.6 3.1 %collective-permute-start.34 = (f32[448,128]{1,0:T(8,128)S(1)}, f32[448,128]{1,0:T(8,128)S(1)}, u32[]{:S(2)}, u32[]{:S(2)}) collective-permute-start(f32[448,128]{1,0:T(8,128)S(1)} %shard_map.83), channel_id=1, source_target_pairs={{0,1},{1,0},{2,3},{3,2},{4,5},{5,4},{6,7},{7,6},{8,9},{9,8},{10,11... | collective-permute-start | bytes 688136 | tf_op jit(solution)/shard_map/ppermute | solution.py:126
  96.9 5.9 %collective-permute-start.38 = (bf16[592,128]{1,0:T(8,128)(2,1)S(1)}, bf16[592,128]{1,0:T(8,128)(2,1)S(1)}, u32[]{:S(2)}, u32[]{:S(2)}) collective-permute-start(bf16[592,128]{1,0:T(8,128)(2,1)S(1)} %shard_map.86.own_ref), channel_id=1, source_target_pairs={{0,2},{1,3},{2,0},{3,1},{4,6},{5,7},{6,4},{7,5},{8,10},{9,11},{10,... | collective-permute-start | bytes 454664 | tf_op jit(solution)/shard_map/ppermute | solution.py:126
  98.6 13.9 %collective-permute-start.46 = (f32[1024,128]{1,0:T(8,128)S(1)}, f32[1024,128]{1,0:T(8,128)S(1)}, u32[]{:S(2)}, u32[]{:S(2)}) collective-permute-start(f32[1024,128]{1,0:T(8,128)S(1)} %get-tuple-element.147.refs_11_), channel_id=1, source_target_pairs={{0,1},{1,0},{2,3},{3,2},{4,5},{5,4},{6,7},{7,6},{8,9},{9,8},{10,11... | collective-permute-start | bytes 1572872 | tf_op jit(solution)/shard_map/ppermute | solution.py:126
  98.8 5.6 %collective-permute-start.35 = (bf16[448,128]{1,0:T(8,128)(2,1)S(1)}, bf16[448,128]{1,0:T(8,128)(2,1)S(1)}, u32[]{:S(2)}, u32[]{:S(2)}) collective-permute-start(bf16[448,128]{1,0:T(8,128)(2,1)S(1)} %shard_map.84.own_ref), channel_id=1, source_target_pairs={{0,4},{1,5},{2,6},{3,7},{4,0},{5,1},{6,2},{7,3},{8,12},{9,13},{10,... | collective-permute-start | bytes 344072 | tf_op jit(solution)/shard_map/ppermute | solution.py:126
  102.9 5.3 %collective-permute-start.39 = (bf16[592,128]{1,0:T(8,128)(2,1)S(1)}, bf16[592,128]{1,0:T(8,128)(2,1)S(1)}, u32[]{:S(2)}, u32[]{:S(2)}) collective-permute-start(bf16[592,128]{1,0:T(8,128)(2,1)S(1)} %shard_map.87.own_ref), channel_id=1, source_target_pairs={{0,4},{1,5},{2,6},{3,7},{4,0},{5,1},{6,2},{7,3},{8,12},{9,13},{10,... | collective-permute-start | bytes 454664 | tf_op jit(solution)/shard_map/ppermute | solution.py:126
  104.4 4.9 %collective-permute-start.36 = (bf16[448,128]{1,0:T(8,128)(2,1)S(1)}, bf16[448,128]{1,0:T(8,128)(2,1)S(1)}, u32[]{:S(2)}, u32[]{:S(2)}) collective-permute-start(bf16[448,128]{1,0:T(8,128)(2,1)S(1)} %shard_map.85.own_ref), channel_id=1, source_target_pairs={{0,2},{1,3},{2,0},{3,1},{4,6},{5,7},{6,4},{7,5},{8,10},{9,11},{10,... | collective-permute-start | bytes 344072 | tf_op jit(solution)/shard_map/ppermute | solution.py:126
  108.3 8.8 %collective-permute-start.44 = (f32[576,128]{1,0:T(8,128)S(1)}, f32[576,128]{1,0:T(8,128)S(1)}, u32[]{:S(2)}, u32[]{:S(2)}) collective-permute-start(f32[576,128]{1,0:T(8,128)S(1)} %get-tuple-element.138.refs_4_), channel_id=1, source_target_pairs={{0,1},{1,0},{2,3},{3,2},{4,5},{5,4},{6,7},{7,6},{8,9},{9,8},{10,11... | collective-permute-start | bytes 884744 | tf_op jit(solution)/shard_map/ppermute | solution.py:126
  109.3 1.2 %collective-permute-start.40 = (f32[8,128]{1,0:T(8,128)S(1)}, f32[8,128]{1,0:T(8,128)S(1)}, u32[]{:S(2)}, u32[]{:S(2)}) collective-permute-start(f32[8,128]{1,0:T(8,128)S(1)} %get-tuple-element.135.own_ref), channel_id=1, source_target_pairs={{0,1},{1,0},{2,3},{3,2},{4,5},{5,4},{6,7},{7,6},{8,9},{9,8},{10,11... | collective-permute-start | bytes 12296 | tf_op jit(solution)/shard_map/ppermute | solution.py:126
  110.6 6.5 %collective-permute-start.45 = (f32[448,128]{1,0:T(8,128)S(1)}, f32[448,128]{1,0:T(8,128)S(1)}, u32[]{:S(2)}, u32[]{:S(2)}) collective-permute-start(f32[448,128]{1,0:T(8,128)S(1)} %get-tuple-element.139.refs_5_), channel_id=1, source_target_pairs={{0,1},{1,0},{2,3},{3,2},{4,5},{5,4},{6,7},{7,6},{8,9},{9,8},{10,11... | collective-permute-start | bytes 688136 | tf_op jit(solution)/shard_map/ppermute | solution.py:126
  110.7 5.4 %collective-permute-start.43 = (f32[8,128]{1,0:T(8,128)S(1)}, f32[8,128]{1,0:T(8,128)S(1)}, u32[]{:S(2)}, u32[]{:S(2)}) collective-permute-start(f32[8,128]{1,0:T(8,128)S(1)} %get-tuple-element.137.refs_0_), channel_id=1, source_target_pairs={{0,24},{8,16},{16,8},{24,0},{1,25},{9,17},{17,9},{25,1},{2,26},{10... | collective-permute-start | bytes 12296 | tf_op jit(solution)/shard_map/ppermute | solution.py:123
  112.6 4.5 %collective-permute-start.42 = (f32[8,128]{1,0:T(8,128)S(1)}, f32[8,128]{1,0:T(8,128)S(1)}, u32[]{:S(2)}, u32[]{:S(2)}) collective-permute-start(f32[8,128]{1,0:T(8,128)S(1)} %get-tuple-element.137.refs_0_), channel_id=1, source_target_pairs={{0,16},{8,24},{16,0},{24,8},{1,17},{9,25},{17,1},{25,9},{2,18},{10... | collective-permute-start | bytes 12296 | tf_op jit(solution)/shard_map/ppermute | solution.py:123
  112.6 4.5 %collective-permute-start.41 = (f32[8,128]{1,0:T(8,128)S(1)}, f32[8,128]{1,0:T(8,128)S(1)}, u32[]{:S(2)}, u32[]{:S(2)}) collective-permute-start(f32[8,128]{1,0:T(8,128)S(1)} %get-tuple-element.137.refs_0_), channel_id=1, source_target_pairs={{0,8},{8,0},{16,24},{24,16},{1,9},{9,1},{17,25},{25,17},{2,10},{10... | collective-permute-start | bytes 12296 | tf_op jit(solution)/shard_map/ppermute | solution.py:123
